TPU v7x, 32 devices: a whole 2x2x4 slice. The times are simulated.
32 devices in a mesh: tm: 8 (over z, core), mesh: 4 (over y, x).
Axes of the slice: x: 2, y: 2, z: 4, core: 2. Of those that a mesh axis runs over, the one named last changes fastest.
Arguments:
- diag_blocks: float32 [8, 512, 128], P('tm', 'mesh'), may hold values from -5 to 10, as said below
- coupling: float32 [8, 512, 128], P('tm', 'mesh'), may hold values from -4 to 1.2, as said below
- arrow_cols: float32 [8, 64, 512], P('tm', None, 'mesh'), may hold values from -0.01640625 to 0.01640625
- rhs: float32 [8, 512], P('tm', 'mesh'), may hold values from -3 to 3
- tip_rhs: float32 [64], replicated, may hold values from -6 to 6
- tip_diag: float32 [64], replicated, may hold values from 4 to 6
- config_shift: float32 [4], replicated, may hold values from 0.001 to 0.3
- config_coupling: float32 [4], replicated, may hold values from 0.99 to 1
- pattern: int32 [8, 4], P('tm', 'mesh'), may hold values 0 or 1
Outputs:
- log_diag: float32 [4, 8, 512], P(None, 'tm', 'mesh')
- forward: float32 [4, 8, 512], P(None, 'tm', 'mesh')
- tip_log: float32 [4, 64], replicated
- tip_forward: float32 [4, 64], replicated
Inputs may be any that keep to these rules, and one draw needn't show every extreme that they name: Every tile of diag_blocks is symmetric, and for every setting in the stated ranges the block matrix with diagonal tiles A[t,i] + config_shift[c] I and coupling tiles B[c,t,i] is positive definite. Every tile of coupling is symmetric.
All inputs are finite; a program needn't handle non-finite values. No bound on the sum of `pattern` on one device may be relied on, other than what follows from the above.
Results may differ from a plain program's by a relative error of at most 0.0003.
Values sent between devices are 32-bit elements; how exact they have to be, the bound alone decides.
No kernel may reach another device: no remote copies, remote signals or barrier semaphores. Data moves between devices by JAX's collectives and lax.ppermute only.
A program may use at most 128 MiB of HBM per device.

v0:
```python
import jax
import jax.numpy as jnp
from jax import lax
from jax.sharding import PartitionSpec as P


def shifted(value, axis, steps):
    count = lax.axis_size(axis)
    initial, last = (max(0, -steps), min(count, count - steps))
    return lax.ppermute(value, axis, [(source, source + steps) for source in range(initial, last)])


def lower_solve(low, right):
    return lax.linalg.triangular_solve(low, right, left_side=True, lower=True)


def block_step(prev, blocks, shift_vec, couple_vec):
    low_prev, arrow_prev, solved_prev = prev
    diag_tile, couple_tile, arrow_tile, right_tile, mask_tile, first = blocks
    high = lax.Precision.HIGHEST
    dtype = diag_tile.dtype
    tip = arrow_tile.shape[-1]
    eye = jnp.eye(diag_tile.shape[-1], dtype=dtype)
    low_prev = low_prev + (1.0 - first) * eye
    scaled = couple_tile * (couple_vec * first * mask_tile.astype(dtype))[:, None, None]
    temp = lower_solve(low_prev, jnp.swapaxes(scaled, 1, 2))
    factor_c = jnp.swapaxes(temp, 1, 2)
    schur = (
        diag_tile
        + shift_vec[:, None, None] * eye
        - jnp.einsum("nij,nkj->nik", factor_c, factor_c, precision=high)
    )
    low = jnp.linalg.cholesky(schur)
    arrow_in = arrow_tile - jnp.einsum("nij,njk->nik", factor_c, arrow_prev, precision=high)
    inner = right_tile - jnp.einsum("nij,nj->ni", factor_c, solved_prev, precision=high)
    joined = lower_solve(low, jnp.concatenate([arrow_in, inner[..., None]], axis=-1))
    arrow = joined[..., :tip]
    solved = joined[..., tip]
    cross = jnp.einsum("nik,nil->nkl", arrow, arrow, precision=high)
    cross_rhs = jnp.einsum("nik,ni->nk", arrow, solved, precision=high)
    log_entries = jnp.log(jnp.diagonal(low, axis1=1, axis2=2))
    return ((low, arrow, solved), (log_entries, cross, cross_rhs))


def run_blocks(carry, blocks, shift_vec, couple_vec):

    def one(state, step_blocks):
        low_c, arrow_c, solved_c, cross_sum, rhs_sum = state
        new, (log_entries, cross, cross_rhs) = block_step(
            (low_c, arrow_c, solved_c), step_blocks, shift_vec, couple_vec
        )
        return (new + (cross_sum + cross, rhs_sum + cross_rhs), (log_entries, new[2]))

    return lax.scan(one, carry, blocks)


def pack_state(low, arrow, solved):
    lead = low.shape[:-2]
    return jnp.concatenate(
        [low.reshape(lead + (-1,)), arrow.reshape(lead + (-1,)), solved], axis=-1
    )


def unpack_state(packed, tile, tip):
    lead = packed.shape[:-1]
    low = packed[..., : tile * tile].reshape(lead + (tile, tile))
    arrow = packed[..., tile * tile : tile * tile + tile * tip].reshape(lead + (tile, tip))
    solved = packed[..., tile * tile + tile * tip :]
    return (low, arrow, solved)


def shards(
    diag_blocks,
    coupling,
    arrow_cols,
    rhs,
    tip_rhs,
    tip_diag,
    config_shift,
    config_coupling,
    pattern,
):
    blocks_here = diag_blocks.shape[0]
    nodes_here = diag_blocks.shape[1]
    tile = diag_blocks.shape[2]
    tip = arrow_cols.shape[1]
    ntile = nodes_here // tile
    configs = config_shift.shape[0]
    diag_all = diag_blocks.reshape(blocks_here, ntile, tile, tile)
    couple_all = coupling.reshape(blocks_here, ntile, tile, tile)
    arrow_all = arrow_cols.reshape(blocks_here, tip, ntile, tile).transpose(0, 2, 3, 1)
    right_all = rhs.reshape(blocks_here, ntile, tile)
    position = lax.axis_index("tm")
    groups = lax.axis_size("tm")
    first_dev = jnp.where(position == 0, 0.0, 1.0).astype(jnp.float32)
    firsts = jnp.where(jnp.arange(blocks_here) == 0, first_dev, 1.0)
    blocks = (diag_all, couple_all, arrow_all, right_all, pattern, firsts)
    width_state = tile * tile + tile * tip + tile

    def sweep(packed, shift_value, couple_value):
        low_prev, arrow_prev, solved_prev = unpack_state(packed, tile, tip)
        shift_vec = jnp.full((ntile,), shift_value, jnp.float32)
        couple_vec = jnp.full((ntile,), couple_value, jnp.float32)
        init = (
            low_prev,
            arrow_prev,
            solved_prev,
            jnp.zeros((ntile, tip, tip), jnp.float32),
            jnp.zeros((ntile, tip), jnp.float32),
        )
        final, (logs, solved) = run_blocks(init, blocks, shift_vec, couple_vec)
        outputs = (
            logs.reshape(blocks_here, nodes_here),
            solved.reshape(blocks_here, nodes_here),
            jnp.sum(final[3], axis=0),
            jnp.sum(final[4], axis=0),
        )
        return (pack_state(final[0], final[1], final[2]), outputs)

    empty = (
        jnp.zeros((configs, blocks_here, nodes_here), jnp.float32),
        jnp.zeros((configs, blocks_here, nodes_here), jnp.float32),
        jnp.zeros((configs, tip, tip), jnp.float32),
        jnp.zeros((configs, tip), jnp.float32),
    )
    state_init = jnp.zeros((ntile, width_state), jnp.float32)
    empty_one = (
        jnp.zeros((blocks_here, nodes_here), jnp.float32),
        jnp.zeros((blocks_here, nodes_here), jnp.float32),
        jnp.zeros((tip, tip), jnp.float32),
        jnp.zeros((tip,), jnp.float32),
    )

    def section(step, carry):
        state, results = carry
        setting = step - position
        active = (setting >= 0) & (setting < configs)
        picked = jnp.clip(setting, 0, configs - 1)

        def run_one(current):
            return sweep(current, config_shift[picked], config_coupling[picked])

        def skip_one(current):
            return (current, empty_one)

        new_state, produced = lax.cond(active, run_one, skip_one, state)
        results = jax.tree.map(lambda old, added: old.at[picked].add(added), results, produced)
        state = shifted(new_state, "tm", 1)
        return (state, results)

    _, results = lax.fori_loop(0, groups + configs - 1, section, (state_init, empty))
    log_diag, forward, cross_part, rhs_part = results
    cross, cross_rhs = lax.psum((cross_part, rhs_part), ("tm", "mesh"))
    precision_tip = jnp.diag(tip_diag)[None] - cross
    low_tip = jnp.linalg.cholesky(precision_tip)
    tip_forward = lower_solve(low_tip, (tip_rhs[None] - cross_rhs)[..., None])[..., 0]
    tip_log = jnp.log(jnp.diagonal(low_tip, axis1=1, axis2=2))
    return (log_diag, forward, tip_log, tip_forward)


def solution(mesh):
    in_specs = (
        P("tm", "mesh", None),
        P("tm", "mesh", None),
        P("tm", None, "mesh"),
        P("tm", "mesh"),
        P(),
        P(),
        P(),
        P(),
        P("tm", "mesh"),
    )
    out_specs = (P(None, "tm", "mesh"), P(None, "tm", "mesh"), P(), P())
    return jax.shard_map(shards, mesh=mesh, in_specs=in_specs, out_specs=out_specs, check_vma=False)
```

profile of v0, /device:TPU:0, one launch (start us, length us, event | category | flops | bytes accessed | tf_op | source)
XLA Modules:
  0.0 707.8 jit_solution(13189389293875381549)
XLA Ops:
  8.3 399.5 %while.29 = (s32[]{:T(128)}, f32[1,24704]{1,0:T(1,128)S(1)}, f32[4,1,128]{2,1,0:T(1,128)S(1)}, f32[4,1,128]{2,1,0:T(1,128)S(1)}, f32[4,64,64]{1,2,0:T(8,128)S(1)...) while((s32[]{:T(128)}, f32[1,24704]{1,0:T(1,128)S(1)}, ...), condition=%wide.region_7.8_spmd, body=%wide.region_0.7_spmd.sunk | while | flops 82667304 | bytes 3033308 | solution.py:151
  8.3 42.6 %conditional.2 = (f32[1,24704]{1,0:T(1,128)S(1)}, f32[1,1,128]{2,1,0:T(1,128)S(1)}, f32[1,1,128]{2,1,0:T(1,128)S(1)}, f32[1,64,64]{2,1,0:T(8,128)S(1)}, f32[1,64]{1,0:T(1,128)S(1)}) conditional(s32[]{:T(128)} %convert_element_type.17, f32[1,24704]{1,0:T(1,128)S(1)} %get-tuple-element.619, (f32[1,1,128,128]{2,3,1,0:T(8,128)S(1)}, s32[]{:T(128)}, ...), branch_computations={%region_1.1_spmd, %region_2.4_spmd} | conditional | flops 82658440 | bytes 2222492 | solution.py:146
  8.4 1.2 dynamic_slice.22
  10.9 9.8 %custom-call.15 = f32[1,1,128,128]{2,3,1,0:T(8,128)S(1)} custom-call(f32[1,1,128,128]{3,2,1,0:T(8,128)S(1)} %add_select_fusion), custom_call_target="InvertDiagBlocksLowerTriangular" | custom-call | tf_op jit(solution)/shard_map/while/body/eval_jaxpr/cond/branch_1_fun/while/body/eval_jaxpr/triangular_solve | solution.py:14
  20.7 1.1 fusion.4
  21.8 1.2 dynamic_slice.21
  24.0 11.7 %custom-call.16 = f32[1,128,128]{2,1,0:T(8,128)S(1)} custom-call(f32[1,128,128]{2,1,0:T(8,128)S(1)} %fusion.3), custom_call_target="Cholesky" | custom-call | tf_op jit(solution)/shard_map/while/body/eval_jaxpr/cond/branch_1_fun/while/body/eval_jaxpr/jit(cholesky)/cholesky | solution.py:33
  37.0 9.8 %custom-call.17 = f32[1,1,128,128]{2,3,1,0:T(8,128)S(1)} custom-call(f32[1,1,128,128]{3,2,1,0:T(8,128)S(1)} %get-tuple-element.473), custom_call_target="InvertDiagBlocksLowerTriangular" | custom-call | tf_op jit(solution)/shard_map/while/body/eval_jaxpr/cond/branch_1_fun/while/body/eval_jaxpr/triangular_solve | solution.py:14
  49.7 1.3 gather_fusion
  51.0 1.3 collective-permute-start
  55.9 42.6 %conditional.2 = (f32[1,24704]{1,0:T(1,128)S(1)}, f32[1,1,128]{2,1,0:T(1,128)S(1)}, f32[1,1,128]{2,1,0:T(1,128)S(1)}, f32[1,64,64]{2,1,0:T(8,128)S(1)}, f32[1,64]{1,0:T(1,128)S(1)}) conditional(s32[]{:T(128)} %convert_element_type.17, f32[1,24704]{1,0:T(1,128)S(1)} %get-tuple-element.619, (f32[1,1,128,128]{2,3,1,0:T(8,128)S(1)}, s32[]{:T(128)}, ...), branch_computations={%region_1.1_spmd, %region_2.4_spmd} | conditional | flops 82658440 | bytes 2222492 | solution.py:146
  56.0 1.2 dynamic_slice.22
  58.4 9.8 %custom-call.15 = f32[1,1,128,128]{2,3,1,0:T(8,128)S(1)} custom-call(f32[1,1,128,128]{3,2,1,0:T(8,128)S(1)} %add_select_fusion), custom_call_target="InvertDiagBlocksLowerTriangular" | custom-call | tf_op jit(solution)/shard_map/while/body/eval_jaxpr/cond/branch_1_fun/while/body/eval_jaxpr/triangular_solve | solution.py:14
  68.3 1.1 fusion.4
  69.4 1.2 dynamic_slice.21
  71.6 11.7 %custom-call.16 = f32[1,128,128]{2,1,0:T(8,128)S(1)} custom-call(f32[1,128,128]{2,1,0:T(8,128)S(1)} %fusion.3), custom_call_target="Cholesky" | custom-call | tf_op jit(solution)/shard_map/while/body/eval_jaxpr/cond/branch_1_fun/while/body/eval_jaxpr/jit(cholesky)/cholesky | solution.py:33
  84.6 9.8 %custom-call.17 = f32[1,1,128,128]{2,3,1,0:T(8,128)S(1)} custom-call(f32[1,1,128,128]{3,2,1,0:T(8,128)S(1)} %get-tuple-element.473), custom_call_target="InvertDiagBlocksLowerTriangular" | custom-call | tf_op jit(solution)/shard_map/while/body/eval_jaxpr/cond/branch_1_fun/while/body/eval_jaxpr/triangular_solve | solution.py:14
  97.3 1.3 gather_fusion
  98.6 1.3 collective-permute-start
  103.5 42.6 %conditional.2 = (f32[1,24704]{1,0:T(1,128)S(1)}, f32[1,1,128]{2,1,0:T(1,128)S(1)}, f32[1,1,128]{2,1,0:T(1,128)S(1)}, f32[1,64,64]{2,1,0:T(8,128)S(1)}, f32[1,64]{1,0:T(1,128)S(1)}) conditional(s32[]{:T(128)} %convert_element_type.17, f32[1,24704]{1,0:T(1,128)S(1)} %get-tuple-element.619, (f32[1,1,128,128]{2,3,1,0:T(8,128)S(1)}, s32[]{:T(128)}, ...), branch_computations={%region_1.1_spmd, %region_2.4_spmd} | conditional | flops 82658440 | bytes 2222492 | solution.py:146
  103.5 1.2 dynamic_slice.22
  106.0 9.8 %custom-call.15 = f32[1,1,128,128]{2,3,1,0:T(8,128)S(1)} custom-call(f32[1,1,128,128]{3,2,1,0:T(8,128)S(1)} %add_select_fusion), custom_call_target="InvertDiagBlocksLowerTriangular" | custom-call | tf_op jit(solution)/shard_map/while/body/eval_jaxpr/cond/branch_1_fun/while/body/eval_jaxpr/triangular_solve | solution.py:14
  115.8 1.1 fusion.4
  117.0 1.2 dynamic_slice.21
  119.2 11.7 %custom-call.16 = f32[1,128,128]{2,1,0:T(8,128)S(1)} custom-call(f32[1,128,128]{2,1,0:T(8,128)S(1)} %fusion.3), custom_call_target="Cholesky" | custom-call | tf_op jit(solution)/shard_map/while/body/eval_jaxpr/cond/branch_1_fun/while/body/eval_jaxpr/jit(cholesky)/cholesky | solution.py:33
  132.1 9.8 %custom-call.17 = f32[1,1,128,128]{2,3,1,0:T(8,128)S(1)} custom-call(f32[1,1,128,128]{3,2,1,0:T(8,128)S(1)} %get-tuple-element.473), custom_call_target="InvertDiagBlocksLowerTriangular" | custom-call | tf_op jit(solution)/shard_map/while/body/eval_jaxpr/cond/branch_1_fun/while/body/eval_jaxpr/triangular_solve | solution.py:14
  144.9 1.3 gather_fusion
  146.2 1.3 collective-permute-start
  151.1 42.6 %conditional.2 = (f32[1,24704]{1,0:T(1,128)S(1)}, f32[1,1,128]{2,1,0:T(1,128)S(1)}, f32[1,1,128]{2,1,0:T(1,128)S(1)}, f32[1,64,64]{2,1,0:T(8,128)S(1)}, f32[1,64]{1,0:T(1,128)S(1)}) conditional(s32[]{:T(128)} %convert_element_type.17, f32[1,24704]{1,0:T(1,128)S(1)} %get-tuple-element.619, (f32[1,1,128,128]{2,3,1,0:T(8,128)S(1)}, s32[]{:T(128)}, ...), branch_computations={%region_1.1_spmd, %region_2.4_spmd} | conditional | flops 82658440 | bytes 2222492 | solution.py:146
  151.1 1.2 dynamic_slice.22
  153.6 9.8 %custom-call.15 = f32[1,1,128,128]{2,3,1,0:T(8,128)S(1)} custom-call(f32[1,1,128,128]{3,2,1,0:T(8,128)S(1)} %add_select_fusion), custom_call_target="InvertDiagBlocksLowerTriangular" | custom-call | tf_op jit(solution)/shard_map/while/body/eval_jaxpr/cond/branch_1_fun/while/body/eval_jaxpr/triangular_solve | solution.py:14
  163.4 1.1 fusion.4
  164.6 1.2 dynamic_slice.21
  166.8 11.7 %custom-call.16 = f32[1,128,128]{2,1,0:T(8,128)S(1)} custom-call(f32[1,128,128]{2,1,0:T(8,128)S(1)} %fusion.3), custom_call_target="Cholesky" | custom-call | tf_op jit(solution)/shard_map/while/body/eval_jaxpr/cond/branch_1_fun/while/body/eval_jaxpr/jit(cholesky)/cholesky | solution.py:33
  179.7 9.8 %custom-call.17 = f32[1,1,128,128]{2,3,1,0:T(8,128)S(1)} custom-call(f32[1,1,128,128]{3,2,1,0:T(8,128)S(1)} %get-tuple-element.473), custom_call_target="InvertDiagBlocksLowerTriangular" | custom-call | tf_op jit(solution)/shard_map/while/body/eval_jaxpr/cond/branch_1_fun/while/body/eval_jaxpr/triangular_solve | solution.py:14
  192.5 1.3 gather_fusion
  193.8 1.3 collective-permute-start
  198.8 44.9 %collective-permute-start = (f32[1,24704]{1,0:T(1,128)S(1)}, f32[1,24704]{1,0:T(1,128)S(1)}, u32[]{:S(2)}, u32[]{:S(2)}) collective-permute-start(f32[1,24704]{1,0:T(1,128)S(1)} %get-tuple-element.579), channel_id=1, source_target_pairs={{0,4},{4,8},{8,12},{12,16},{16,20},{20,24},{24,28},{1,5},{5,9},{9,... | collective-permute-start | bytes 296456 | tf_op jit(solution)/shard_map/while/body/eval_jaxpr/ppermute | solution.py:10
  247.4 2.4 collective-permute-start
  253.5 44.9 %collective-permute-start = (f32[1,24704]{1,0:T(1,128)S(1)}, f32[1,24704]{1,0:T(1,128)S(1)}, u32[]{:S(2)}, u32[]{:S(2)}) collective-permute-start(f32[1,24704]{1,0:T(1,128)S(1)} %get-tuple-element.579), channel_id=1, source_target_pairs={{0,4},{4,8},{8,12},{12,16},{16,20},{20,24},{24,28},{1,5},{5,9},{9,... | collective-permute-start | bytes 296456 | tf_op jit(solution)/shard_map/while/body/eval_jaxpr/ppermute | solution.py:10
  302.1 2.4 collective-permute-start
  308.2 41.8 %collective-permute-start = (f32[1,24704]{1,0:T(1,128)S(1)}, f32[1,24704]{1,0:T(1,128)S(1)}, u32[]{:S(2)}, u32[]{:S(2)}) collective-permute-start(f32[1,24704]{1,0:T(1,128)S(1)} %get-tuple-element.579), channel_id=1, source_target_pairs={{0,4},{4,8},{8,12},{12,16},{16,20},{20,24},{24,28},{1,5},{5,9},{9,... | collective-permute-start | bytes 296456 | tf_op jit(solution)/shard_map/while/body/eval_jaxpr/ppermute | solution.py:10
  353.7 2.4 collective-permute-start
  359.7 44.5 %collective-permute-start = (f32[1,24704]{1,0:T(1,128)S(1)}, f32[1,24704]{1,0:T(1,128)S(1)}, u32[]{:S(2)}, u32[]{:S(2)}) collective-permute-start(f32[1,24704]{1,0:T(1,128)S(1)} %get-tuple-element.579), channel_id=1, source_target_pairs={{0,4},{4,8},{8,12},{12,16},{16,20},{20,24},{24,28},{1,5},{5,9},{9,... | collective-permute-start | bytes 296456 | tf_op jit(solution)/shard_map/while/body/eval_jaxpr/ppermute | solution.py:10
  408.6 160.1 %psum.15 = f32[4,64]{1,0:T(4,128)S(1)} all-reduce(f32[4,64]{1,0:T(4,128)S(1)} %get-tuple-element.430), channel_id=1, replica_groups=mesh['tm'=8,'mesh'=4] {'tm','mesh'}, use_global_device_ids=true, to_apply=%region_11.12 | all-reduce | flops 256 | bytes 2048 | tf_op jit(solution)/shard_map/psum | solution.py:153
  568.8 83.7 %all-reduce.2.cloned.1.call-done = f32[4,64,64]{1,2,0:T(8,128)} async-done(((f32[4,64,64]{1,2,0:T(8,128)}), f32[4,64,64]{1,2,0:T(8,128)}) %all-reduce.2.cloned.1.call-update) | async-done | bytes 65552 | tf_op jit(solution)/shard_map/psum | solution.py:153
  654.5 23.5 %custom-call.20 = f32[4,64,64]{2,1,0:T(8,128)S(1)} custom-call(f32[4,64,64]{2,1,0:T(8,128)S(1)} %fusion.24), custom_call_target="Cholesky" | custom-call | tf_op jit(solution)/shard_map/jit(cholesky)/cholesky | solution.py:155
  678.2 19.7 %custom-call.21 = f32[4,1,64,64]{2,3,1,0:T(8,128)S(1)} custom-call(f32[4,1,64,64]{3,2,1,0:T(8,128)S(1)} %get-tuple-element.475), custom_call_target="InvertDiagBlocksLowerTriangular" | custom-call | tf_op jit(solution)/shard_map/triangular_solve | solution.py:14
  (334 shorter events, 66.7 us)
Async XLA Ops:
  7.2 645.3 %all-reduce.2.cloned.1.call-start = ((), (), s32[]{:S(2)}) async-start(), calls=%async_computation | async-start | bytes 262144 | tf_op jit(solution)/shard_map/psum | solution.py:153
  8.3 400.3 %copy-start.5 = (f32[64]{0:T(128)S(1)}, f32[64]{0:T(128)}, u32[]{:S(2)}) copy-start(f32[64]{0:T(128)} %param.26) | copy-start | bytes 772
  8.3 560.4 %copy-start.6 = (f32[64]{0:T(128)S(1)}, f32[64]{0:T(128)}, u32[]{:S(2)}) copy-start(f32[64]{0:T(128)} %param.25) | copy-start | bytes 772
  8.3 44.1 %copy-start.1 = (s32[3]{0:T(128)S(1)}, s32[3]{0:T(128)}, u32[]{:S(2)}) copy-start(s32[3]{0:T(128)} %get-tuple-element.659) | copy-start | bytes 40 | tf_op jit(solution)/shard_map/while
  8.3 45.5 %copy-start.2 = (s32[2]{0:T(128)S(1)}, s32[2]{0:T(128)}, u32[]{:S(2)}) copy-start(s32[2]{0:T(128)} %get-tuple-element.661) | copy-start | bytes 28 | tf_op jit(solution)/shard_map/while
  51.0 4.9 collective-permute-start
  55.9 44.1 %copy-start.1 = (s32[3]{0:T(128)S(1)}, s32[3]{0:T(128)}, u32[]{:S(2)}) copy-start(s32[3]{0:T(128)} %get-tuple-element.659) | copy-start | bytes 40 | tf_op jit(solution)/shard_map/while
  55.9 45.5 %copy-start.2 = (s32[2]{0:T(128)S(1)}, s32[2]{0:T(128)}, u32[]{:S(2)}) copy-start(s32[2]{0:T(128)} %get-tuple-element.661) | copy-start | bytes 28 | tf_op jit(solution)/shard_map/while
  98.6 4.9 collective-permute-start
  103.5 44.1 %copy-start.1 = (s32[3]{0:T(128)S(1)}, s32[3]{0:T(128)}, u32[]{:S(2)}) copy-start(s32[3]{0:T(128)} %get-tuple-element.659) | copy-start | bytes 40 | tf_op jit(solution)/shard_map/while
  103.5 45.5 %copy-start.2 = (s32[2]{0:T(128)S(1)}, s32[2]{0:T(128)}, u32[]{:S(2)}) copy-start(s32[2]{0:T(128)} %get-tuple-element.661) | copy-start | bytes 28 | tf_op jit(solution)/shard_map/while
  146.2 4.9 collective-permute-start
  151.1 44.1 %copy-start.1 = (s32[3]{0:T(128)S(1)}, s32[3]{0:T(128)}, u32[]{:S(2)}) copy-start(s32[3]{0:T(128)} %get-tuple-element.659) | copy-start | bytes 40 | tf_op jit(solution)/shard_map/while
  151.1 45.5 %copy-start.2 = (s32[2]{0:T(128)S(1)}, s32[2]{0:T(128)}, u32[]{:S(2)}) copy-start(s32[2]{0:T(128)} %get-tuple-element.661) | copy-start | bytes 28 | tf_op jit(solution)/shard_map/while
  193.8 4.9 collective-permute-start
  198.7 45.1 %copy-start.1 = (s32[3]{0:T(128)S(1)}, s32[3]{0:T(128)}, u32[]{:S(2)}) copy-start(s32[3]{0:T(128)} %get-tuple-element.659) | copy-start | bytes 40 | tf_op jit(solution)/shard_map/while
  198.7 46.6 %copy-start.2 = (s32[2]{0:T(128)S(1)}, s32[2]{0:T(128)}, u32[]{:S(2)}) copy-start(s32[2]{0:T(128)} %get-tuple-element.661) | copy-start | bytes 28 | tf_op jit(solution)/shard_map/while
  198.8 48.5 %collective-permute-start = (f32[1,24704]{1,0:T(1,128)S(1)}, f32[1,24704]{1,0:T(1,128)S(1)}, u32[]{:S(2)}, u32[]{:S(2)}) collective-permute-start(f32[1,24704]{1,0:T(1,128)S(1)} %get-tuple-element.579), channel_id=1, source_target_pairs={{0,4},{4,8},{8,12},{12,16},{16,20},{20,24},{24,28},{1,5},{5,9},{9,... | collective-permute-start | bytes 296456 | tf_op jit(solution)/shard_map/while/body/eval_jaxpr/ppermute | solution.py:10
  247.3 2.6 copy-start.1
  247.3 4.0 copy-start.2
  247.4 5.9 collective-permute-start
  253.4 45.1 %copy-start.1 = (s32[3]{0:T(128)S(1)}, s32[3]{0:T(128)}, u32[]{:S(2)}) copy-start(s32[3]{0:T(128)} %get-tuple-element.659) | copy-start | bytes 40 | tf_op jit(solution)/shard_map/while
  253.4 46.6 %copy-start.2 = (s32[2]{0:T(128)S(1)}, s32[2]{0:T(128)}, u32[]{:S(2)}) copy-start(s32[2]{0:T(128)} %get-tuple-element.661) | copy-start | bytes 28 | tf_op jit(solution)/shard_map/while
  253.5 48.5 %collective-permute-start = (f32[1,24704]{1,0:T(1,128)S(1)}, f32[1,24704]{1,0:T(1,128)S(1)}, u32[]{:S(2)}, u32[]{:S(2)}) collective-permute-start(f32[1,24704]{1,0:T(1,128)S(1)} %get-tuple-element.579), channel_id=1, source_target_pairs={{0,4},{4,8},{8,12},{12,16},{16,20},{20,24},{24,28},{1,5},{5,9},{9,... | collective-permute-start | bytes 296456 | tf_op jit(solution)/shard_map/while/body/eval_jaxpr/ppermute | solution.py:10
  302.0 2.6 copy-start.1
  302.0 4.0 copy-start.2
  302.1 5.9 collective-permute-start
  308.1 42.0 %copy-start.1 = (s32[3]{0:T(128)S(1)}, s32[3]{0:T(128)}, u32[]{:S(2)}) copy-start(s32[3]{0:T(128)} %get-tuple-element.659) | copy-start | bytes 40 | tf_op jit(solution)/shard_map/while
  308.1 43.4 %copy-start.2 = (s32[2]{0:T(128)S(1)}, s32[2]{0:T(128)}, u32[]{:S(2)}) copy-start(s32[2]{0:T(128)} %get-tuple-element.661) | copy-start | bytes 28 | tf_op jit(solution)/shard_map/while
  308.2 45.3 %collective-permute-start = (f32[1,24704]{1,0:T(1,128)S(1)}, f32[1,24704]{1,0:T(1,128)S(1)}, u32[]{:S(2)}, u32[]{:S(2)}) collective-permute-start(f32[1,24704]{1,0:T(1,128)S(1)} %get-tuple-element.579), channel_id=1, source_target_pairs={{0,4},{4,8},{8,12},{12,16},{16,20},{20,24},{24,28},{1,5},{5,9},{9,... | collective-permute-start | bytes 296456 | tf_op jit(solution)/shard_map/while/body/eval_jaxpr/ppermute | solution.py:10
  353.6 2.6 copy-start.1
  353.6 4.0 copy-start.2
  353.7 5.9 collective-permute-start
  359.6 44.7 %copy-start.1 = (s32[3]{0:T(128)S(1)}, s32[3]{0:T(128)}, u32[]{:S(2)}) copy-start(s32[3]{0:T(128)} %get-tuple-element.659) | copy-start | bytes 40 | tf_op jit(solution)/shard_map/while
  359.7 46.2 %copy-start.2 = (s32[2]{0:T(128)S(1)}, s32[2]{0:T(128)}, u32[]{:S(2)}) copy-start(s32[2]{0:T(128)} %get-tuple-element.661) | copy-start | bytes 28 | tf_op jit(solution)/shard_map/while
  359.7 48.1 %collective-permute-start = (f32[1,24704]{1,0:T(1,128)S(1)}, f32[1,24704]{1,0:T(1,128)S(1)}, u32[]{:S(2)}, u32[]{:S(2)}) collective-permute-start(f32[1,24704]{1,0:T(1,128)S(1)} %get-tuple-element.579), channel_id=1, source_target_pairs={{0,4},{4,8},{8,12},{12,16},{16,20},{20,24},{24,28},{1,5},{5,9},{9,... | collective-permute-start | bytes 296456 | tf_op jit(solution)/shard_map/while/body/eval_jaxpr/ppermute | solution.py:10
  407.8 0.7 copy-start
  407.9 293.1 %copy-start.3 = (f32[4,1,128]{2,1,0:T(1,128)}, f32[4,1,128]{2,1,0:T(1,128)S(1)}, u32[]{:S(2)}) copy-start(f32[4,1,128]{2,1,0:T(1,128)S(1)} %get-tuple-element.439) | copy-start | bytes 6148
  407.9 293.1 %copy-start.4 = (f32[4,1,128]{2,1,0:T(1,128)}, f32[4,1,128]{2,1,0:T(1,128)S(1)}, u32[]{:S(2)}) copy-start(f32[4,1,128]{2,1,0:T(1,128)S(1)} %get-tuple-element.440) | copy-start | bytes 6148
Sparse Core Ops, SparseCore 0:
  408.6 243.8 all-reduce.1
where the time goes:
time: 709 us; the launch traced here: 708 us
  other arithmetic  212 us (30%)
  starting transfers between devices  188 us (27%)
  blocking collectives  160 us (23%)
  waiting for transfers between devices  83.7 us (12%)
  local copies, waits for them, and re-layouts  23.4 us (3%)
  matrix products  18.2 us (3%)
  between operations  14.2 us (2%)
  loops' own time  7.3 us (1%)
    ppermute x11, starting transfers between devices, shifted(): lax.ppermute(value, axis, [(source, source + steps) for source in range(i...  188 us
    psum x1, blocking collectives, shards(): cross, cross_rhs = lax.psum((cross_part, rhs_part), ('tm', 'mesh'))  160 us
    another operation x18, other arithmetic, lower_solve(): return lax.linalg.triangular_solve(low, right, left_side=True, lower=True)  101 us
    psum x1, waiting for transfers between devices, shards(): cross, cross_rhs = lax.psum((cross_part, rhs_part), ('tm', 'mesh'))  83.7 us
    another operation x12, other arithmetic, block_step(): low = jnp.linalg.cholesky(schur)  49.5 us
    another operation x44, other arithmetic  29 us
    another operation x4, other arithmetic, shards(): low_tip = jnp.linalg.cholesky(precision_tip)  23.6 us
  transfers between devices with their start and end apart: 12, of which 1 were waited for; matrix products, arithmetic and copies ran while one was open for 5% of the time, Pallas kernels for 0%

commit v1 on v0

v1 whole, which is shorter than its diff:
```python
import functools

import jax
import jax.numpy as jnp
from jax import lax
from jax.experimental import pallas as pl
from jax.experimental.pallas import tpu as pltpu
from jax.sharding import PartitionSpec as P

F32 = jnp.float32
BF16 = jnp.bfloat16
NN = (((1,), (0,)), ((), ()))
NT = (((1,), (1,)), ((), ()))
TN = (((0,), (0,)), ((), ()))
SUB = 8
STRIP = 32
GROUP = 4
FACTORS = 5
SPAN = 1.8
SMALL = 4e-4


def identity(size):
    row = lax.broadcasted_iota(jnp.int32, (size, size), 0)
    col = lax.broadcasted_iota(jnp.int32, (size, size), 1)
    return (row == col).astype(F32)


def product(left, right, dims=NN):
    return lax.dot_general(left, right, dims, preferred_element_type=F32)


def exact(left, right, dims=NN):
    return lax.dot_general(
        left, right, dims, precision=lax.Precision.HIGHEST, preferred_element_type=F32
    )


def halves(value):
    high = value.astype(BF16)
    return high, (value - high.astype(F32)).astype(BF16)


def fine(left, right, dims=NN):
    (axis_left,), (axis_right,) = dims[0]
    high_l, low_l = halves(left)
    high_r, low_r = halves(right)
    return product(
        jnp.concatenate([high_l, low_l, high_l], axis=axis_left),
        jnp.concatenate([high_r, high_r, low_r], axis=axis_right),
        dims,
    )


def largest_sum(matrix):
    return jnp.max(jnp.sum(jnp.abs(matrix), axis=0, keepdims=True), axis=1, keepdims=True)


def invert(mat_ref, inv_ref, count):
    size = mat_ref.shape[-1]
    eye = identity(size)
    total = None
    for n in range(count):
        mat = mat_ref[n]
        scale = SPAN / largest_sum(mat)
        error = eye - mat * scale
        value = eye + error
        power = error.astype(BF16)
        for _ in range(FACTORS - 1):
            power = product(power, power).astype(BF16)
            value = value + product(value.astype(BF16), power)
        value = value * scale
        rest = eye - fine(mat, value)
        low = rest.astype(BF16)
        inv_ref[n] = value + fine(value, rest + product(low, low))
        square = rest * rest
        total = square if total is None else total + square
    settled = jnp.sum(total) < SMALL * count

    @pl.when(jnp.logical_not(settled))
    def _():
        for n in range(count):
            mat = mat_ref[n]
            inv_ref[n] = eye / largest_sum(mat)

            def unsettled(carry):
                step, norm = carry
                return (step < 80) & jnp.logical_not(norm < 1e-7)

            def improve(carry, n=n):
                step, _ = carry
                value = inv_ref[n]
                rest = eye - exact(mat_ref[n], value)
                inv_ref[n] = value + exact(value, rest)
                return step + 1, jnp.sum(rest * rest)

            lax.while_loop(unsettled, improve, (jnp.int32(0), jnp.float32(1.0)))


def eliminate(inverse, after, before, middle):
    rows = jnp.concatenate([after, before, middle], axis=0)
    return fine(fine(rows, inverse), rows, NT)


def local_kernel(
    where_ref,
    shift_ref,
    couple_ref,
    own_ref,
    one_ref,
    two_ref,
    three_ref,
    diag_ref,
    cross_ref,
    back_ref,
    right_ref,
    left_ref,
    state_ref,
    raw_ref,
    mat_ref,
    inv_ref,
):
    tile = own_ref.shape[1]
    setting = where_ref[0]
    shift = shift_ref[setting]
    couple = couple_ref[setting]
    for step, ref in enumerate((own_ref, one_ref, two_ref, three_ref)):
        raw_ref[setting ^ step] = ref[...]
    eye = identity(tile)
    diag = [raw_ref[n, 0:tile, :] + shift * eye for n in range(GROUP)]
    cross = [raw_ref[n, tile : 2 * tile, :] * couple for n in range(GROUP)]
    right = [raw_ref[n, 2 * tile :, :] for n in range(GROUP)]
    one, two, end = slice(0, tile), slice(tile, 2 * tile), slice(2 * tile, None)

    mat_ref[0] = diag[0]
    mat_ref[1] = diag[2]
    invert(mat_ref, inv_ref, 2)
    gram = eliminate(inv_ref[0], cross[1], cross[0], right[0])
    diag01 = diag[1] - gram[one, one]
    cross01 = -gram[one, two]
    cross01_t = -gram[two, one]
    back01 = -gram[two, two]
    right01 = right[1] - gram[end, one]
    left01 = -gram[end, two]
    gram = eliminate(inv_ref[1], cross[3], cross[2], right[2])
    diag23 = diag[3] - gram[one, one]
    cross23 = -gram[one, two]
    back23 = -gram[two, two]
    right23 = right[3] - gram[end, one]
    left23 = -gram[end, two]

    mat_ref[0] = diag01
    mat_ref[1] = diag01 + back23
    invert(mat_ref, inv_ref, 2)
    gram2 = eliminate(inv_ref[0], cross[2], cross01_t, right01)
    gram3 = eliminate(inv_ref[1], cross23, cross01_t, right01 + left23)
    diag_ref[0] = diag[0]
    diag_ref[1] = diag01
    diag_ref[2] = diag[2] - gram2[one, one]
    diag03 = diag23 - gram3[one, one]
    diag_ref[3] = diag03
    cross_ref[0] = cross[0]
    cross_ref[1] = cross01
    cross_ref[2] = -gram2[one, two]
    cross_ref[3] = -gram3[one, two]
    back_ref[0] = jnp.zeros_like(eye)
    back_ref[1] = back01
    back_ref[2] = back01 - gram2[two, two]
    back_ref[3] = back01 - gram3[two, two]
    right_ref[0] = right[0]
    right_ref[1] = right01
    right_ref[2] = right[2] - gram2[end, one]
    right03 = right23 - gram3[end, one]
    right_ref[3] = right03
    left_ref[0] = jnp.zeros_like(right[0])
    left_ref[1] = left01
    left_ref[2] = left01 - gram2[end, two]
    left_ref[3] = left01 - gram3[end, two]
    state_ref[0:tile, :] = diag03
    state_ref[tile:, :] = right03


def padded(rows, size):
    return jnp.concatenate([rows, jnp.zeros((size - rows.shape[0], size), F32)], axis=0)


def joined(where_ref, state_ref, parts, order, mat_ref, inv_ref):
    diag_ref, cross_ref, back_ref, right_ref, left_ref = parts
    tile = diag_ref.shape[-1]
    lone = jnp.where(where_ref[1] == 0, 1.0, 0.0).astype(F32)
    base = state_ref[0:tile, :] + lone * identity(tile)
    for place, n in enumerate(order):
        mat_ref[place] = base + back_ref[n]
    invert(mat_ref, inv_ref, len(order))
    results = []
    for place, n in enumerate(order):
        cross = cross_ref[n]
        middle = padded(state_ref[tile:, :] + left_ref[n], tile)
        update = fine(fine(cross, inv_ref[place]), jnp.concatenate([cross, middle], axis=0), NT)
        start = jnp.concatenate([diag_ref[n], padded(right_ref[n], tile).T], axis=1)
        results.append(start - update)
    return results


def advance_kernel(
    where_ref, state_ref, diag_ref, cross_ref, back_ref, right_ref, left_ref, out_ref, mat_ref, inv_ref
):
    tile = diag_ref.shape[-1]
    parts = (diag_ref, cross_ref, back_ref, right_ref, left_ref)
    (last,) = joined(where_ref, state_ref, parts, (GROUP - 1,), mat_ref, inv_ref)
    out_ref[0:tile, :] = last[:, 0:tile]
    out_ref[tile:, :] = last[:, tile:].T[0 : state_ref.shape[0] - tile, :]


def splat(value, lane):
    return jnp.broadcast_to(value[:, lane : lane + 1], value.shape)


def factor(refs, size, batch):
    lane = lax.broadcasted_iota(jnp.int32, (SUB, 128), 1)
    pivots = jnp.ones((SUB, 128), F32)
    for strip in range(0, size, STRIP):
        if strip:
            for b in range(batch):
                done = [ref[pl.ds(b, strip, stride=SUB), :] for ref in refs]
                left = done[0][:, strip : strip + STRIP]
                update = fine(left, jnp.concatenate(done, axis=1), TN)
                spot = pl.ds(strip * SUB + b, STRIP, stride=SUB)
                for p, ref in enumerate(refs):
                    ref[spot, :] = ref[spot, :] - update[:, 128 * p : 128 * (p + 1)]
        rows = [[ref[(strip + i) * SUB : (strip + i + 1) * SUB, :] for ref in refs] for i in range(STRIP)]
        for panel in range(0, STRIP, SUB):
            base = strip + panel
            block = {
                (i, m): splat(rows[panel + i][0], base + m) for i in range(SUB) for m in range(i, SUB)
            }
            for k in range(SUB):
                pivot = block[k, k]
                root = lax.rsqrt(pivot)
                pivots = jnp.where(lane == base + k, pivot, pivots)
                scaled = {m: block[k, m] * root for m in range(k + 1, SUB)}
                ready = [piece * root for piece in rows[panel + k]]
                rows[panel + k] = ready
                for i in range(k + 1, SUB):
                    for m in range(i, SUB):
                        block[i, m] = block[i, m] - scaled[i] * scaled[m]
                    rows[panel + i] = [
                        piece - scaled[i] * own for piece, own in zip(rows[panel + i], ready)
                    ]
            for i in range(panel + SUB, STRIP):
                for k in range(panel, panel + SUB):
                    ready = rows[k]
                    weight = splat(ready[0], strip + i)
                    rows[i] = [piece - weight * own for piece, own in zip(rows[i], ready)]
        for i in range(STRIP):
            for p, ref in enumerate(refs):
                ref[(strip + i) * SUB : (strip + i + 1) * SUB, :] = rows[i][p]
    return pivots


def final_kernel(
    tip,
    where_ref,
    state_ref,
    diag_ref,
    cross_ref,
    back_ref,
    right_ref,
    left_ref,
    small_ref,
    sums_ref,
    mat_ref,
    inv_ref,
    rows_ref,
    ends_ref,
):
    tile = diag_ref.shape[-1]
    parts = (diag_ref, cross_ref, back_ref, right_ref, left_ref)
    order = tuple(range(GROUP))
    for b, value in enumerate(joined(where_ref, state_ref, parts, order, mat_ref, inv_ref)):
        rows_ref[pl.ds(b, tile, stride=SUB), :] = value[:, 0:tile]
        ends_ref[pl.ds(b, tile, stride=SUB), :] = value[:, tile:]
    pivots = factor((rows_ref, ends_ref), tile, GROUP)
    small_ref[0:GROUP, :] = 0.5 * jnp.log(pivots[0:GROUP, :])
    solved = [ends_ref[pl.ds(b, tile, stride=SUB), :] for b in range(GROUP)]
    everything = jnp.concatenate(solved, axis=0)
    sums_ref[...] = fine(everything[:, 0:tip], everything, TN)
    for b in range(GROUP):
        small_ref[GROUP + b : GROUP + b + 1, :] = solved[b].T[tip : tip + 1, :]


def tip_kernel(small_ref, sums_ref, prior_ref, out_ref, rows_ref):
    tip = sums_ref.shape[0]
    rows_ref[pl.ds(0, tip, stride=SUB), :] = prior_ref[...] - sums_ref[...]
    pivots = factor((rows_ref,), tip, 1)
    out_ref[0 : 2 * GROUP, :] = small_ref[...]
    out_ref[2 * GROUP : 2 * GROUP + 1, :] = 0.5 * jnp.log(pivots[0:1, :])
    solved = rows_ref[pl.ds(0, tip, stride=SUB), :]
    solved = jnp.concatenate([solved, jnp.zeros((128 - tip, 128), F32)], axis=0).T
    out_ref[2 * GROUP + 1 : 2 * GROUP + 2, :] = solved[tip : tip + 1, :]
    out_ref[2 * GROUP + 2 :, :] = jnp.zeros((6, 128), F32)


def place_kernel(where_ref, own_ref, one_ref, two_ref, three_ref, log_ref, solved_ref, tip_log_ref, tip_ref):
    node = where_ref[0]
    tip = tip_ref.shape[1]
    for step, ref in enumerate((own_ref, one_ref, two_ref, three_ref)):
        setting = pl.ds(node ^ step, 1)
        log_ref[setting, :] = ref[pl.ds(node, 1), :]
        solved_ref[setting, :] = ref[pl.ds(node + GROUP, 1), :]
        tip_log_ref[setting, :] = ref[2 * GROUP : 2 * GROUP + 1, 0:tip]
        tip_ref[setting, :] = ref[2 * GROUP + 1 : 2 * GROUP + 2, 0:tip]


def call(body, inputs, shapes, scratch=(), scalars=0):
    vmem = pl.BlockSpec(memory_space=pltpu.VMEM)
    smem = pl.BlockSpec(memory_space=pltpu.SMEM)
    return pl.pallas_call(
        body,
        out_shape=tuple(jax.ShapeDtypeStruct(shape, F32) for shape in shapes),
        in_specs=[smem] * scalars + [vmem] * (len(inputs) - scalars),
        out_specs=tuple(vmem for _ in shapes),
        scratch_shapes=[pltpu.VMEM(shape, F32) for shape in scratch],
        compiler_params=pltpu.CompilerParams(vmem_limit_bytes=40 * 1024 * 1024),
    )(*inputs)


def crossed(value, axis, step):
    size = lax.axis_size(axis)
    return lax.ppermute(value, axis, [(source, source ^ step) for source in range(size)])


def shards(
    diag_blocks,
    coupling,
    arrow_cols,
    rhs,
    tip_rhs,
    tip_diag,
    config_shift,
    config_coupling,
    pattern,
):
    tile = diag_blocks.shape[2]
    tip = arrow_cols.shape[1]
    groups = lax.axis_size("tm")
    spans = groups // GROUP
    assert config_shift.shape[0] == GROUP and diag_blocks.shape[:2] == (1, tile)
    position = lax.axis_index("tm")
    where = jnp.stack([position % GROUP, position // GROUP]).astype(jnp.int32)
    active = jnp.where(position == 0, 0.0, pattern[0, 0].astype(F32))
    side = tip + 2 * SUB
    raw = jnp.concatenate(
        [diag_blocks[0], coupling[0] * active, arrow_cols[0], rhs, jnp.zeros((2 * SUB - 1, tile), F32)], axis=0
    )
    two = crossed(raw, "tm", 2)
    one = crossed(raw, "tm", 1)
    three = crossed(two, "tm", 1)
    square = (GROUP, tile, tile)
    band = (GROUP, side, tile)
    pair = (GROUP, tile, tile)
    *parts, state = call(
        local_kernel,
        (where, config_shift, config_coupling, raw, one, two, three),
        (square, square, square, band, band, (tile + side, tile)),
        ((GROUP,) + raw.shape, pair, pair),
        3,
    )
    for span in range(spans - 1):
        state = lax.ppermute(state, "tm", [(source, source + GROUP) for source in range(groups - GROUP)])
        if span < spans - 2:
            (state,) = call(
                advance_kernel, (where, state, *parts), ((tile + side, tile),), (pair, pair), 1
            )
    if spans == 1:
        state = jnp.zeros_like(state)
    small, sums = call(
        functools.partial(final_kernel, tip),
        (where, state, *parts),
        ((2 * GROUP, tile), (tip, tile)),
        (pair, pair, (SUB * tile, tile), (SUB * tile, tile)),
        1,
    )
    for axis, first in (("tm", GROUP), ("mesh", 1)):
        step = first
        while step < lax.axis_size(axis):
            sums = sums + crossed(sums, axis, step)
            step *= 2
    prior = jnp.concatenate([jnp.diag(tip_diag), tip_rhs[:, None], jnp.zeros((tip, 128 - tip - 1), F32)], axis=1)
    (packed,) = call(tip_kernel, (small, sums, prior), ((4 * GROUP, tile),), ((SUB * tip, 128),))
    log_diag, solved, tip_log, tip_forward = call(
        place_kernel,
        (where, packed, crossed(packed, "tm", 1), crossed(packed, "tm", 2), crossed(packed, "tm", 3)),
        ((GROUP, tile), (GROUP, tile), (GROUP, tip), (GROUP, tip)),
        (),
        1,
    )
    return (log_diag[:, None, :], solved[:, None, :], tip_log, tip_forward)


def solution(mesh):
    in_specs = (
        P("tm", "mesh", None),
        P("tm", "mesh", None),
        P("tm", None, "mesh"),
        P("tm", "mesh"),
        P(),
        P(),
        P(),
        P(),
        P("tm", "mesh"),
    )
    out_specs = (P(None, "tm", "mesh"), P(None, "tm", "mesh"), P(), P())
    return jax.shard_map(shards, mesh=mesh, in_specs=in_specs, out_specs=out_specs, check_vma=False)
```

time: 709 us -> 86.6 us (0.12)
  other arithmetic: 212 us -> 1.12 us
  blocking collectives: 160 us -> 0 us
  starting transfers between devices: 188 us -> 42.8 us
  waiting for transfers between devices: 83.7 us -> 17.2 us
  local copies, waits for them, and re-layouts: 23.4 us -> 1.62 us
  Pallas kernels: 0 us -> 21.4 us
  matrix products: 18.2 us -> 0 us
  between operations: 14.2 us -> 1.38 us
  loops' own time: 7.3 us -> 0 us
    another operation x78 -> x1, other arithmetic: 203 us -> 0.07 us  [shards(): where = jnp.stack([position % GROUP, position // GROUP]).astype(jnp.int32)]
    psum x1 -> x0, blocking collectives: 160 us -> none  [shards(): cross, cross_rhs = lax.psum((cross_part, rhs_part), ('tm', 'mesh'))]
    ppermute x11 -> x10, starting transfers between devices: 188 us -> 42.8 us  [the longest x9 38.1 us: crossed(): lax.ppermute(value, axis, [(source, source ^ step) for source in range(si...]
    psum x1 -> x0, waiting for transfers between devices: 83.7 us -> none  [shards(): cross, cross_rhs = lax.psum((cross_part, rhs_part), ('tm', 'mesh'))]
    pallas_call x0 -> x4, Pallas kernels: none -> 21.4 us  [call(): pl.pallas_call(body, out_shape=tuple((jax.ShapeDtypeStruct(shape, F32) fo...]
    ppermute x11 -> x10, waiting for transfers between devices: 0.03 us -> 17.2 us  [the longest x9 14.7 us: crossed(): lax.ppermute(value, axis, [(source, source ^ step) for source in range(si...]
    dot_general x20 -> x0, matrix products: 12 us -> none  [the longest x4 4.11 us: block_step(): jnp.einsum('nij,njk->nik', factor_c, arrow_prev, precision=high)]
    dynamic_slice x8 -> x0, local copies, waits for them, and re-layouts: 9.89 us -> none  [run_one(): return sweep(current, config_shift[picked], config_coupling[picked])]
  transfers between devices with their start and end apart: 12 -> 10, of which waited for: 1 -> 8; matrix products, arithmetic and copies ran while one was open for 5% -> 0% of each run, Pallas kernels for 0% -> 0%
where the time goes in v1:
time: 86.6 us; the launch traced here: 85.5 us
  starting transfers between devices  42.8 us (49%)
  Pallas kernels  21.4 us (25%)
  waiting for transfers between devices  17.2 us (20%)
  local copies, waits for them, and re-layouts  1.62 us (2%)
  between operations  1.38 us (2%)
  other arithmetic  1.12 us (1%)
    ppermute x9, starting transfers between devices, crossed(): lax.ppermute(value, axis, [(source, source ^ step) for source in range(si...  38.1 us
    pallas_call x4, Pallas kernels, call(): pl.pallas_call(body, out_shape=tuple((jax.ShapeDtypeStruct(shape, F32) fo...  21.4 us
    ppermute x9, waiting for transfers between devices, crossed(): lax.ppermute(value, axis, [(source, source ^ step) for source in range(si...  14.7 us
    ppermute x1, starting transfers between devices, shards(): lax.ppermute(state, 'tm', [(source, source + GROUP) for source in range(g...  4.66 us
    ppermute x1, waiting for transfers between devices, shards(): lax.ppermute(state, 'tm', [(source, source + GROUP) for source in range(g...  2.51 us
  transfers between devices with their start and end apart: 10, of which 8 were waited for; matrix products, arithmetic and copies ran while one was open for 0% of the time, Pallas kernels for 0%

profile of v1, /device:TPU:0, one launch (start us, length us, event | category | flops | bytes accessed | tf_op | source)
XLA Modules:
  0.0 85.5 jit_solution(9668068573634296194)
XLA Ops:
  1.3 0.0 copy-start.2
  1.3 0.0 copy-start.3
  1.3 0.9 %multiply_bitcast_fusion = f32[128,128]{1,0:T(8,128)S(1)} fusion(f32[1,128,128]{2,1,0:T(8,128)} %param.10, f32[]{:T(128)S(6)} %select_n.22), kind=kLoop, calls=%fused_computation | loop fusion | flops 16384 | bytes 131076 | tf_op jit(solution)/shard_map/mul | solution.py:354
  2.2 0.0 copy-start.4
  2.2 0.0 copy-done.2
  2.2 0.0 copy-done.3
  2.2 0.6 copy-done.4
  2.8 0.1 concatenate.6.own_ref
  3.0 3.1 %collective-permute-start.1 = (f32[336,128]{1,0:T(8,128)S(1)}, f32[336,128]{1,0:T(8,128)S(1)}, u32[]{:S(2)}, u32[]{:S(2)}) collective-permute-start(f32[336,128]{1,0:T(8,128)S(1)} %concatenate.6.own_ref), channel_id=1, source_target_pairs={{0,8},{4,12},{8,0},{12,4},{16,24},{20,28},{24,16},{28,20},{1,9},{5... | collective-permute-start | bytes 516104 | tf_op jit(solution)/shard_map/ppermute | solution.py:330
  6.1 0.0 collective-permute-start
  6.1 4.4 %collective-permute-done.1.two_ref = f32[336,128]{1,0:T(8,128)S(1)} collective-permute-done((f32[336,128]{1,0:T(8,128)S(1)}, f32[336,128]{1,0:T(8,128)S(1)}, u32[]{:S(2)}, u32[]{:S(2)}) %collective-permute-start.1) | collective-permute-done | bytes 172064 | tf_op jit(solution)/shard_map/ppermute | solution.py:330
  10.4 0.0 collective-permute-start.2
  10.4 0.0 copy-start
  10.5 0.0 copy-start.1
  10.5 0.1 pad_add_fusion.where_ref
  10.5 0.0 collective-permute-done.one_ref
  10.5 1.3 %collective-permute-done.2.three_ref = f32[336,128]{1,0:T(8,128)S(1)} collective-permute-done((f32[336,128]{1,0:T(8,128)S(1)}, f32[336,128]{1,0:T(8,128)S(1)}, u32[]{:S(2)}, u32[]{:S(2)}) %collective-permute-start.2) | collective-permute-done | bytes 172064 | tf_op jit(solution)/shard_map/ppermute | solution.py:330
  11.9 0.0 copy-done
  11.9 0.0 copy-done.1
  11.9 6.5 %shard_map.120 = (f32[4,128,128]{2,1,0:T(8,128)S(1)}, f32[4,128,128]{2,1,0:T(8,128)S(1)}, f32[4,128,128]{2,1,0:T(8,128)S(1)}, f32[4,80,128]{2,1,0:T(8,128)S(1)},...) custom-call(s32[2]{0:T(128)S(1)} %pad_add_fusion.where_ref, f32[4]{0:T(128)S(1)} %copy-done, f32[4]{0:T(128)S(1)} %copy-done.1, ...), custom_call_target="tpu_custom_call" | custom-call | tf_op jit(solution)/shard_map/pallas_call | solution.py:318
  18.3 4.7 %collective-permute-start.3 = (f32[208,128]{1,0:T(8,128)S(1)}, f32[208,128]{1,0:T(8,128)S(1)}, u32[]{:S(2)}, u32[]{:S(2)}) collective-permute-start(f32[208,128]{1,0:T(8,128)S(1)} %get-tuple-element.16), channel_id=1, source_target_pairs={{0,16},{4,20},{8,24},{12,28},{1,17},{5,21},{9,25},{13,29},{2,18},{... | collective-permute-start | bytes 319496 | tf_op jit(solution)/shard_map/ppermute | solution.py:370
  23.0 2.5 %collective-permute-done.3.state_ref = f32[208,128]{1,0:T(8,128)S(1)} collective-permute-done((f32[208,128]{1,0:T(8,128)S(1)}, f32[208,128]{1,0:T(8,128)S(1)}, u32[]{:S(2)}, u32[]{:S(2)}) %collective-permute-start.3) | collective-permute-done | bytes 106528 | tf_op jit(solution)/shard_map/ppermute | solution.py:370
  25.5 11.2 %shard_map.121 = (f32[8,128]{1,0:T(8,128)S(1)}, f32[64,128]{1,0:T(8,128)S(1)}) custom-call(s32[2]{0:T(128)S(1)} %pad_add_fusion.where_ref, f32[208,128]{1,0:T(8,128)S(1)} %collective-permute-done.3.state_ref, f32[4,128,128]{2,1,0:T(8,128)S(1)} %get-tuple-element.17.diag_ref, f32[4,128,128]{2,1,0:T(8,128)S(1)} %get-tuple-element.18.cross_ref, ...), custom_call_target="tpu_custom_call" | custom-call | tf_op jit(solution)/shard_map/pallas_call | solution.py:318
  36.7 0.0 copy-start.5
  36.8 16.5 %collective-permute-start.4 = (f32[64,128]{1,0:T(8,128)S(1)}, f32[64,128]{1,0:T(8,128)S(1)}, u32[]{:S(2)}, u32[]{:S(2)}) collective-permute-start(f32[64,128]{1,0:T(8,128)S(1)} %get-tuple-element.23), channel_id=1, source_target_pairs={{0,16},{4,20},{8,24},{12,28},{16,0},{20,4},{24,8},{28,12},{1,17},{... | collective-permute-start | bytes 98312 | tf_op jit(solution)/shard_map/ppermute | solution.py:330
  53.3 1.9 %collective-permute-done.4 = f32[64,128]{1,0:T(8,128)S(1)} collective-permute-done((f32[64,128]{1,0:T(8,128)S(1)}, f32[64,128]{1,0:T(8,128)S(1)}, u32[]{:S(2)}, u32[]{:S(2)}) %collective-permute-start.4) | collective-permute-done | bytes 32800 | tf_op jit(solution)/shard_map/ppermute | solution.py:330
  55.2 1.5 %collective-permute-start.5 = (f32[64,128]{1,0:T(8,128)S(1)}, f32[64,128]{1,0:T(8,128)S(1)}, u32[]{:S(2)}, u32[]{:S(2)}) collective-permute-start(f32[64,128]{1,0:T(8,128)S(1)} %add.15), channel_id=1, source_target_pairs={{0,1},{1,0},{2,3},{3,2},{4,5},{5,4},{6,7},{7,6},{8,9},{9,8},{10,11... | collective-permute-start | bytes 98312 | tf_op jit(solution)/shard_map/ppermute | solution.py:330
  56.7 0.0 copy-done.5
  56.7 0.1 fusion
  56.7 0.0 copy-start.6
  56.7 0.7 copy-done.6
  57.4 0.1 copy.13
  57.5 0.1 pad.2.clone
  57.6 1.5 %collective-permute-done.5 = f32[64,128]{1,0:T(8,128)S(1)} collective-permute-done((f32[64,128]{1,0:T(8,128)S(1)}, f32[64,128]{1,0:T(8,128)S(1)}, u32[]{:S(2)}, u32[]{:S(2)}) %collective-permute-start.5) | collective-permute-done | bytes 32800 | tf_op jit(solution)/shard_map/ppermute | solution.py:330
  59.1 1.2 %collective-permute-start.6 = (f32[64,128]{1,0:T(8,128)S(1)}, f32[64,128]{1,0:T(8,128)S(1)}, u32[]{:S(2)}, u32[]{:S(2)}) collective-permute-start(f32[64,128]{1,0:T(8,128)S(1)} %add.16), channel_id=1, source_target_pairs={{0,2},{1,3},{2,0},{3,1},{4,6},{5,7},{6,4},{7,5},{8,10},{9,11},{10,... | collective-permute-start | bytes 98312 | tf_op jit(solution)/shard_map/ppermute | solution.py:330
  60.3 0.1 maximum_maximum_fusion.prior_ref
  60.4 2.6 %collective-permute-done.6 = f32[64,128]{1,0:T(8,128)S(1)} collective-permute-done((f32[64,128]{1,0:T(8,128)S(1)}, f32[64,128]{1,0:T(8,128)S(1)}, u32[]{:S(2)}, u32[]{:S(2)}) %collective-permute-start.6) | collective-permute-done | bytes 32800 | tf_op jit(solution)/shard_map/ppermute | solution.py:330
  63.0 2.6 %shard_map.122.own_ref = f32[16,128]{1,0:T(8,128)S(1)} custom-call(f32[8,128]{1,0:T(8,128)S(1)} %get-tuple-element.22.small_ref, f32[64,128]{1,0:T(8,128)S(1)} %add.17.sums_ref, f32[64,128]{1,0:T(8,128)S(1)} %maximum_maximum_fusion.prior_ref), custom_call_target="tpu_custom_call" | custom-call | tf_op jit(solution)/shard_map/pallas_call | solution.py:318
  65.6 2.2 %collective-permute-start.7 = (f32[16,128]{1,0:T(8,128)S(1)}, f32[16,128]{1,0:T(8,128)S(1)}, u32[]{:S(2)}, u32[]{:S(2)}) collective-permute-start(f32[16,128]{1,0:T(8,128)S(1)} %shard_map.122.own_ref), channel_id=1, source_target_pairs={{0,4},{4,0},{8,12},{12,8},{16,20},{20,16},{24,28},{28,24},{1,5},{5... | collective-permute-start | bytes 24584 | tf_op jit(solution)/shard_map/ppermute | solution.py:330
  67.8 13.5 %collective-permute-start.8 = (f32[16,128]{1,0:T(8,128)S(1)}, f32[16,128]{1,0:T(8,128)S(1)}, u32[]{:S(2)}, u32[]{:S(2)}) collective-permute-start(f32[16,128]{1,0:T(8,128)S(1)} %shard_map.122.own_ref), channel_id=1, source_target_pairs={{0,8},{4,12},{8,0},{12,4},{16,24},{20,28},{24,16},{28,20},{1,9},{5... | collective-permute-start | bytes 24584 | tf_op jit(solution)/shard_map/ppermute | solution.py:330
  81.3 0.1 collective-permute-start.9
  81.4 0.0 collective-permute-done.7.one_ref
  81.4 1.6 %collective-permute-done.8.two_ref = f32[16,128]{1,0:T(8,128)S(1)} collective-permute-done((f32[16,128]{1,0:T(8,128)S(1)}, f32[16,128]{1,0:T(8,128)S(1)}, u32[]{:S(2)}, u32[]{:S(2)}) %collective-permute-start.8) | collective-permute-done | bytes 8224 | tf_op jit(solution)/shard_map/ppermute | solution.py:330
  83.0 1.4 %collective-permute-done.9.three_ref = f32[16,128]{1,0:T(8,128)S(1)} collective-permute-done((f32[16,128]{1,0:T(8,128)S(1)}, f32[16,128]{1,0:T(8,128)S(1)}, u32[]{:S(2)}, u32[]{:S(2)}) %collective-permute-start.9) | collective-permute-done | bytes 8224 | tf_op jit(solution)/shard_map/ppermute | solution.py:330
  84.4 1.1 %shard_map.123 = (f32[4,128]{1,0:T(4,128)}, f32[4,128]{1,0:T(4,128)}, f32[4,64]{1,0:T(4,128)}, f32[4,64]{1,0:T(4,128)}) custom-call(s32[2]{0:T(128)S(1)} %pad_add_fusion.where_ref, f32[16,128]{1,0:T(8,128)S(1)} %shard_map.122.own_ref, f32[16,128]{1,0:T(8,128)S(1)} %collective-permute-done.7.one_ref, f32[16,128]{1,0:T(8,128)S(1)} %collective-permute-done.8.two_ref, ...), custom_call_target="tpu_custom_call" | custom-call | tf_op jit(solution)/shard_map/pallas_call | solution.py:318
  (5 shorter events, 0.0 us)
Async XLA Ops:
  1.3 0.9 %copy-start.2 = (f32[1,128,128]{2,1,0:T(8,128)S(1)}, f32[1,128,128]{2,1,0:T(8,128)}, u32[]{:S(2)}) copy-start(f32[1,128,128]{2,1,0:T(8,128)} %param.9) | copy-start | bytes 196612
  1.3 0.9 %copy-start.3 = (f32[1,64,128]{2,1,0:T(8,128)S(1)}, f32[1,64,128]{2,1,0:T(8,128)}, u32[]{:S(2)}) copy-start(f32[1,64,128]{2,1,0:T(8,128)} %param.11) | copy-start | bytes 98308
  2.2 0.7 copy-start.4
  3.0 7.5 %collective-permute-start.1 = (f32[336,128]{1,0:T(8,128)S(1)}, f32[336,128]{1,0:T(8,128)S(1)}, u32[]{:S(2)}, u32[]{:S(2)}) collective-permute-start(f32[336,128]{1,0:T(8,128)S(1)} %concatenate.6.own_ref), channel_id=1, source_target_pairs={{0,8},{4,12},{8,0},{12,4},{16,24},{20,28},{24,16},{28,20},{1,9},{5... | collective-permute-start | bytes 516104 | tf_op jit(solution)/shard_map/ppermute | solution.py:330
  6.1 4.5 %collective-permute-start = (f32[336,128]{1,0:T(8,128)S(1)}, f32[336,128]{1,0:T(8,128)S(1)}, u32[]{:S(2)}, u32[]{:S(2)}) collective-permute-start(f32[336,128]{1,0:T(8,128)S(1)} %concatenate.6.own_ref), channel_id=1, source_target_pairs={{0,4},{4,0},{8,12},{12,8},{16,20},{20,16},{24,28},{28,24},{1,5},{5... | collective-permute-start | bytes 516104 | tf_op jit(solution)/shard_map/ppermute | solution.py:330
  10.4 1.4 %collective-permute-start.2 = (f32[336,128]{1,0:T(8,128)S(1)}, f32[336,128]{1,0:T(8,128)S(1)}, u32[]{:S(2)}, u32[]{:S(2)}) collective-permute-start(f32[336,128]{1,0:T(8,128)S(1)} %collective-permute-done.1.two_ref), channel_id=1, source_target_pairs={{0,4},{4,0},{8,12},{12,8},{16,20},{20,16},{24,28},{28,24},{1,5},{5... | collective-permute-start | bytes 516104 | tf_op jit(solution)/shard_map/ppermute | solution.py:330
  10.4 1.4 %copy-start = (f32[4]{0:T(128)S(1)}, f32[4]{0:T(128)}, u32[]{:S(2)}) copy-start(f32[4]{0:T(128)} %shift_ref.1) | copy-start | bytes 52
  10.5 1.4 %copy-start.1 = (f32[4]{0:T(128)S(1)}, f32[4]{0:T(128)}, u32[]{:S(2)}) copy-start(f32[4]{0:T(128)} %couple_ref.1) | copy-start | bytes 52
  18.3 7.2 %collective-permute-start.3 = (f32[208,128]{1,0:T(8,128)S(1)}, f32[208,128]{1,0:T(8,128)S(1)}, u32[]{:S(2)}, u32[]{:S(2)}) collective-permute-start(f32[208,128]{1,0:T(8,128)S(1)} %get-tuple-element.16), channel_id=1, source_target_pairs={{0,16},{4,20},{8,24},{12,28},{1,17},{5,21},{9,25},{13,29},{2,18},{... | collective-permute-start | bytes 319496 | tf_op jit(solution)/shard_map/ppermute | solution.py:370
  36.7 19.9 %copy-start.5 = (f32[64]{0:T(128)S(1)}, f32[64]{0:T(128)}, u32[]{:S(2)}) copy-start(f32[64]{0:T(128)} %param.14) | copy-start | bytes 772
  36.8 18.4 %collective-permute-start.4 = (f32[64,128]{1,0:T(8,128)S(1)}, f32[64,128]{1,0:T(8,128)S(1)}, u32[]{:S(2)}, u32[]{:S(2)}) collective-permute-start(f32[64,128]{1,0:T(8,128)S(1)} %get-tuple-element.23), channel_id=1, source_target_pairs={{0,16},{4,20},{8,24},{12,28},{16,0},{20,4},{24,8},{28,12},{1,17},{... | collective-permute-start | bytes 98312 | tf_op jit(solution)/shard_map/ppermute | solution.py:330
  55.2 3.9 %collective-permute-start.5 = (f32[64,128]{1,0:T(8,128)S(1)}, f32[64,128]{1,0:T(8,128)S(1)}, u32[]{:S(2)}, u32[]{:S(2)}) collective-permute-start(f32[64,128]{1,0:T(8,128)S(1)} %add.15), channel_id=1, source_target_pairs={{0,1},{1,0},{2,3},{3,2},{4,5},{5,4},{6,7},{7,6},{8,9},{9,8},{10,11... | collective-permute-start | bytes 98312 | tf_op jit(solution)/shard_map/ppermute | solution.py:330
  56.7 0.7 copy-start.6
  59.1 3.9 %collective-permute-start.6 = (f32[64,128]{1,0:T(8,128)S(1)}, f32[64,128]{1,0:T(8,128)S(1)}, u32[]{:S(2)}, u32[]{:S(2)}) collective-permute-start(f32[64,128]{1,0:T(8,128)S(1)} %add.16), channel_id=1, source_target_pairs={{0,2},{1,3},{2,0},{3,1},{4,6},{5,7},{6,4},{7,5},{8,10},{9,11},{10,... | collective-permute-start | bytes 98312 | tf_op jit(solution)/shard_map/ppermute | solution.py:330
  65.6 15.8 %collective-permute-start.7 = (f32[16,128]{1,0:T(8,128)S(1)}, f32[16,128]{1,0:T(8,128)S(1)}, u32[]{:S(2)}, u32[]{:S(2)}) collective-permute-start(f32[16,128]{1,0:T(8,128)S(1)} %shard_map.122.own_ref), channel_id=1, source_target_pairs={{0,4},{4,0},{8,12},{12,8},{16,20},{20,16},{24,28},{28,24},{1,5},{5... | collective-permute-start | bytes 24584 | tf_op jit(solution)/shard_map/ppermute | solution.py:330
  67.8 15.2 %collective-permute-start.8 = (f32[16,128]{1,0:T(8,128)S(1)}, f32[16,128]{1,0:T(8,128)S(1)}, u32[]{:S(2)}, u32[]{:S(2)}) collective-permute-start(f32[16,128]{1,0:T(8,128)S(1)} %shard_map.122.own_ref), channel_id=1, source_target_pairs={{0,8},{4,12},{8,0},{12,4},{16,24},{20,28},{24,16},{28,20},{1,9},{5... | collective-permute-start | bytes 24584 | tf_op jit(solution)/shard_map/ppermute | solution.py:330
  81.3 3.1 %collective-permute-start.9 = (f32[16,128]{1,0:T(8,128)S(1)}, f32[16,128]{1,0:T(8,128)S(1)}, u32[]{:S(2)}, u32[]{:S(2)}) collective-permute-start(f32[16,128]{1,0:T(8,128)S(1)} %shard_map.122.own_ref), channel_id=1, source_target_pairs={{0,12},{4,8},{8,4},{12,0},{16,28},{20,24},{24,20},{28,16},{1,13},{... | collective-permute-start | bytes 24584 | tf_op jit(solution)/shard_map/ppermute | solution.py:330

commit v2 on v1

v2 whole, which is shorter than its diff:
```python
import functools

import jax
import jax.numpy as jnp
from jax import lax
from jax.experimental import pallas as pl
from jax.experimental.pallas import tpu as pltpu
from jax.sharding import PartitionSpec as P

F32 = jnp.float32
BF16 = jnp.bfloat16
NN = (((1,), (0,)), ((), ()))
NT = (((1,), (1,)), ((), ()))
TN = (((0,), (0,)), ((), ()))
SUB = 8
STRIP = 32
GROUP = 4
SPAN = 2.8
SMALL = 9e-4


def identity(size):
    row = lax.broadcasted_iota(jnp.int32, (size, size), 0)
    col = lax.broadcasted_iota(jnp.int32, (size, size), 1)
    return (row == col).astype(F32)


def product(left, right, dims=NN):
    return lax.dot_general(left, right, dims, preferred_element_type=F32)


def exact(left, right, dims=NN):
    return lax.dot_general(
        left, right, dims, precision=lax.Precision.HIGHEST, preferred_element_type=F32
    )


def halves(value):
    high = value.astype(BF16)
    return high, (value - high.astype(F32)).astype(BF16)


def fine(left, right, dims=NN):
    (axis_left,), (axis_right,) = dims[0]
    high_l, low_l = halves(left)
    high_r, low_r = halves(right)
    return product(
        jnp.concatenate([high_l, low_l, high_l], axis=axis_left),
        jnp.concatenate([high_r, high_r, low_r], axis=axis_right),
        dims,
    )


def largest_sum(matrix):
    return jnp.max(jnp.sum(jnp.abs(matrix), axis=0, keepdims=True), axis=1, keepdims=True)


def converged(mat, mat_ref, inv_ref):
    eye = identity(mat.shape[-1])
    mat_ref[...] = mat
    inv_ref[...] = eye / largest_sum(mat)

    def unsettled(carry):
        step, norm = carry
        return (step < 80) & jnp.logical_not(norm < 1e-7)

    def improve(carry):
        step, _ = carry
        value = inv_ref[...]
        rest = eye - exact(mat_ref[...], value)
        inv_ref[...] = value + exact(value, rest)
        return step + 1, jnp.sum(rest * rest)

    lax.while_loop(unsettled, improve, (jnp.int32(0), jnp.float32(1.0)))
    return inv_ref[...]


def series(mat, factors):
    eye = identity(mat.shape[-1])
    scale = SPAN / largest_sum(mat)
    error = eye - mat * scale
    value = eye + error
    power = error.astype(BF16)
    for _ in range(factors - 1):
        power = product(power, power).astype(BF16)
        value = value + product(value.astype(BF16), power)
    return value * scale


def quotients(mats, lefts, rights, factors, refs):
    results, total = [], 0.0
    if refs:
        for mat, left, right in zip(mats, lefts, rights):
            results.append(fine(fine(left, converged(mat, *refs)), right, NT))
        return results, total
    eye = identity(mats[0].shape[-1])
    starts = [series(mat, factors) for mat in mats]
    for mat, start, left, right in zip(mats, starts, lefts, rights):
        rest = eye - fine(mat, start)
        first = fine(left, start)
        low = rest.astype(BF16)
        first = first + fine(first, rest + product(low, low))
        results.append(fine(first, right, NT))
        total = total + rest * rest
    return results, total


def pack_kernel(where_ref, pattern_ref, diag_ref, couple_ref, arrow_ref, rhs_ref, out_ref):
    tile = diag_ref.shape[0]
    tip = arrow_ref.shape[0]
    row = lax.broadcasted_iota(jnp.int32, (tile, tile), 0)
    col = lax.broadcasted_iota(jnp.int32, (tile, tile), 1)
    couple = couple_ref[...]
    out_ref[0:tile, :] = jnp.where(row >= col, diag_ref[...], couple)
    out_ref[tile : tile + tip, :] = arrow_ref[...]
    first = (where_ref[0] == 0) & (where_ref[1] == 0)
    active = jnp.where(first, 0, pattern_ref[0, 0]).astype(F32)
    middle = jnp.sum(jnp.where(row == col, couple, 0.0), axis=0, keepdims=True)
    filler = jnp.zeros((2 * SUB - 3, tile), F32)
    out_ref[tile + tip :, :] = jnp.concatenate(
        [rhs_ref[...], middle, jnp.full((1, tile), active), filler], axis=0
    )


def local_kernel(
    tip,
    where_ref,
    shift_ref,
    couple_ref,
    own_ref,
    one_ref,
    two_ref,
    three_ref,
    diag_ref,
    cross_ref,
    back_ref,
    right_ref,
    left_ref,
    state_ref,
    raw_ref,
    mat_ref,
    inv_ref,
):
    tile = own_ref.shape[1]
    side = own_ref.shape[0] - tile
    half = tile // 2
    setting = where_ref[0]
    shift = shift_ref[setting]
    couple = couple_ref[setting]
    for step, ref in enumerate((own_ref, one_ref, two_ref, three_ref)):
        raw_ref[setting ^ step] = ref[...]
    eye = identity(tile)
    row = lax.broadcasted_iota(jnp.int32, (tile, tile), 0)
    col = lax.broadcasted_iota(jnp.int32, (tile, tile), 1)
    used = lax.broadcasted_iota(jnp.int32, (side, tile), 0) <= tip
    diag, cross, right = [], [], []
    for n in range(GROUP):
        both = raw_ref[n, 0:tile, :]
        turned = both.T
        middle = raw_ref[n, tile + tip + 1 : tile + tip + 2, :]
        active = raw_ref[n, tile + tip + 2 : tile + tip + 3, :]
        diag.append(jnp.where(row >= col, both, turned) + shift * eye)
        tie = jnp.where(row < col, both, jnp.where(row > col, turned, middle))
        cross.append(tie * (couple * active))
        right.append(jnp.where(used, raw_ref[n, tile:, :], 0.0))
    one, two, end = slice(0, tile), slice(tile, 2 * tile), slice(2 * tile, None)

    def run(refs):
        low = jnp.concatenate([cross[1], cross[0], right[0]], axis=0)
        high = jnp.concatenate([cross[3], cross[2], right[2]], axis=0)
        (gram, gram23), total = quotients((diag[0], diag[2]), (low, high), (low, high), 4, refs)
        diag01 = diag[1] - gram[one, one]
        cross01 = -gram[one, two]
        cross01_t = -gram[two, one]
        back01 = -gram[two, two]
        right01 = right[1] - gram[end, one]
        left01 = -gram[end, two]
        diag23 = diag[3] - gram23[one, one]
        cross23 = -gram23[one, two]
        back23 = -gram23[two, two]
        right23 = right[3] - gram23[end, one]
        left23 = -gram23[end, two]

        low = jnp.concatenate([cross[2], cross01_t, right01], axis=0)
        high = jnp.concatenate([cross23, cross01_t, right01 + left23], axis=0)
        (gram2, gram3), more = quotients((diag01, diag01 + back23), (low, high), (low, high), 4, refs)
        diag_ref[0] = diag[0]
        diag_ref[1] = diag01
        diag_ref[2] = diag[2] - gram2[one, one]
        diag03 = diag23 - gram3[one, one]
        diag_ref[3] = diag03
        cross_ref[0] = cross[0]
        cross_ref[1] = cross01
        cross_ref[2] = -gram2[one, two]
        cross_ref[3] = -gram3[one, two]
        back_ref[0] = jnp.zeros_like(eye)
        back_ref[1] = back01
        back_ref[2] = back01 - gram2[two, two]
        back_ref[3] = back01 - gram3[two, two]
        right_ref[0] = right[0]
        right_ref[1] = right01
        right_ref[2] = right[2] - gram2[end, one]
        right03 = right23 - gram3[end, one]
        right_ref[3] = right03
        left_ref[0] = jnp.zeros_like(right[0])
        left_ref[1] = left01
        left_ref[2] = left01 - gram2[end, two]
        left_ref[3] = left01 - gram3[end, two]
        send(state_ref, diag03, right03)
        return total + more

    settled = jnp.sum(run(None)) < SMALL * 4

    @pl.when(jnp.logical_not(settled))
    def _():
        run((mat_ref, inv_ref))


def send(state_ref, diag, right):
    half = diag.shape[0] // 2
    mid = half + half // 2
    count = state_ref.shape[0] - mid
    state_ref[0:half, :] = diag[0:half, :]
    state_ref[half:mid, :] = jnp.concatenate([diag[half:mid, half:], diag[mid:, half:]], axis=1)
    state_ref[mid:, :] = right[0:count, :]


def receive(state_ref):
    tile = state_ref.shape[1]
    half = tile // 2
    mid = half + half // 2
    top = state_ref[0:half, :]
    corner = state_ref[half:mid, :]
    corner = jnp.concatenate([corner[:, 0:half], corner[:, half:]], axis=0)
    bottom = jnp.concatenate([top[:, half:].T, corner], axis=1)
    return jnp.concatenate([top, bottom], axis=0), state_ref[mid:, :]


def padded(rows, size):
    return jnp.concatenate([rows, jnp.zeros((size - rows.shape[0], size), F32)], axis=0)


def joined(where_ref, state_ref, parts, order, refs):
    diag_ref, cross_ref, back_ref, right_ref, left_ref = parts
    tile = diag_ref.shape[-1]
    lone = jnp.where(where_ref[1] == 0, 1.0, 0.0).astype(F32)
    base, came = receive(state_ref)
    base = base + lone * identity(tile)
    mats = [base + back_ref[n] for n in order]
    crosses = [cross_ref[n] for n in order]
    came = padded(came, tile)
    middles = [came + padded(left_ref[n], tile) for n in order]
    rights = [jnp.concatenate([cross, middle], axis=0) for cross, middle in zip(crosses, middles)]
    updates, total = quotients(mats, crosses, rights, 5, refs)
    results = []
    for n, update in zip(order, updates):
        start = jnp.concatenate([diag_ref[n], padded(right_ref[n], tile).T], axis=1)
        results.append(start - update)
    return results, total


def advance_kernel(
    where_ref, state_ref, diag_ref, cross_ref, back_ref, right_ref, left_ref, out_ref, mat_ref, inv_ref
):
    tile = diag_ref.shape[-1]
    parts = (diag_ref, cross_ref, back_ref, right_ref, left_ref)

    def run(refs):
        (last,), total = joined(where_ref, state_ref, parts, (GROUP - 1,), refs)
        send(out_ref, last[:, 0:tile], last[:, tile:].T)
        return total

    settled = jnp.sum(run(None)) < SMALL

    @pl.when(jnp.logical_not(settled))
    def _():
        run((mat_ref, inv_ref))


def splat(value, lane):
    return jnp.broadcast_to(value[:, lane : lane + 1], value.shape)


def factor(refs, size, batch, tip):
    lane = lax.broadcasted_iota(jnp.int32, (SUB, 128), 1)
    pivots = jnp.ones((SUB, 128), F32)
    column = jnp.zeros((SUB, 128), F32)
    for strip in range(0, size, STRIP):
        if strip:
            for b in range(batch):
                done = [ref[pl.ds(b, strip, stride=SUB), :] for ref in refs]
                left = done[0][:, strip : strip + STRIP]
                update = fine(left, jnp.concatenate(done, axis=1), TN)
                spot = pl.ds(strip * SUB + b, STRIP, stride=SUB)
                for p, ref in enumerate(refs):
                    ref[spot, :] = ref[spot, :] - update[:, 128 * p : 128 * (p + 1)]
        rows = [[ref[(strip + i) * SUB : (strip + i + 1) * SUB, :] for ref in refs] for i in range(STRIP)]
        for panel in range(0, STRIP, SUB):
            base = strip + panel
            block = {
                (i, m): splat(rows[panel + i][0], base + m) for i in range(SUB) for m in range(i, SUB)
            }
            for k in range(SUB):
                pivot = block[k, k]
                root = lax.rsqrt(pivot)
                pivots = jnp.where(lane == base + k, pivot, pivots)
                scaled = {m: block[k, m] * root for m in range(k + 1, SUB)}
                ready = [piece * root for piece in rows[panel + k]]
                column = jnp.where(lane == base + k, splat(ready[-1], tip), column)
                rows[panel + k] = ready
                for i in range(k + 1, SUB):
                    for m in range(i, SUB):
                        block[i, m] = block[i, m] - scaled[i] * scaled[m]
                    rows[panel + i] = [
                        piece - scaled[i] * own for piece, own in zip(rows[panel + i], ready)
                    ]
            for i in range(panel + SUB, STRIP):
                for k in range(panel, panel + SUB):
                    ready = rows[k]
                    weight = splat(ready[0], strip + i)
                    rows[i] = [piece - weight * own for piece, own in zip(rows[i], ready)]
        for i in range(STRIP):
            for p, ref in enumerate(refs):
                ref[(strip + i) * SUB : (strip + i + 1) * SUB, :] = rows[i][p]
    return pivots, column


def final_kernel(
    tip,
    where_ref,
    state_ref,
    diag_ref,
    cross_ref,
    back_ref,
    right_ref,
    left_ref,
    small_ref,
    sums_ref,
    mat_ref,
    inv_ref,
    rows_ref,
    ends_ref,
):
    tile = diag_ref.shape[-1]
    parts = (diag_ref, cross_ref, back_ref, right_ref, left_ref)

    def run(refs):
        values, total = joined(where_ref, state_ref, parts, range(GROUP), refs)
        for b, value in enumerate(values):
            rows_ref[pl.ds(b, tile, stride=SUB), :] = value[:, 0:tile]
            ends_ref[pl.ds(b, tile, stride=SUB), :] = value[:, tile:]
        return total

    settled = jnp.sum(run(None)) < SMALL * GROUP

    @pl.when(jnp.logical_not(settled))
    def _():
        run((mat_ref, inv_ref))

    pivots, column = factor((rows_ref, ends_ref), tile, GROUP, tip)
    small_ref[0:GROUP, :] = 0.5 * jnp.log(pivots[0:GROUP, :])
    small_ref[GROUP:, :] = column[0:GROUP, :]
    solved = [ends_ref[pl.ds(b, tile, stride=SUB), :] for b in range(GROUP)]
    everything = jnp.concatenate(solved, axis=0)
    sums_ref[...] = fine(everything[:, 0:tip], everything, TN)


def tip_kernel(place_ref, small_ref, diag_ref, rhs_ref, own_ref, one_ref, two_ref, three_ref, out_ref, sums_ref, rows_ref):
    tip = own_ref.shape[0]
    for step, ref in enumerate((own_ref, one_ref, two_ref, three_ref)):
        sums_ref[place_ref[0] ^ step] = ref[...]
    row = lax.broadcasted_iota(jnp.int32, (tip, 128), 0)
    col = lax.broadcasted_iota(jnp.int32, (tip, 128), 1)
    filler = jnp.zeros((1, 128 - tip), F32)
    prior = jnp.where(row == col, jnp.concatenate([diag_ref[...], filler], axis=1), 0.0)
    right = jnp.where(row == col, jnp.concatenate([rhs_ref[...], filler], axis=1), 0.0)
    prior = prior + jnp.where(col == tip, jnp.sum(right, axis=1, keepdims=True), 0.0)
    total = (sums_ref[0] + sums_ref[1]) + (sums_ref[2] + sums_ref[3])
    rows_ref[pl.ds(0, tip, stride=SUB), :] = prior - total
    pivots, column = factor((rows_ref,), tip, 1, tip)
    out_ref[0 : 2 * GROUP, :] = small_ref[...]
    out_ref[2 * GROUP :, :] = jnp.concatenate(
        [0.5 * jnp.log(pivots[0:1, :]), column[0:1, :], jnp.zeros((6, 128), F32)], axis=0
    )


def place_kernel(where_ref, own_ref, one_ref, two_ref, three_ref, log_ref, solved_ref, tip_log_ref, tip_ref):
    node = where_ref[0]
    tip = tip_ref.shape[1]
    for step, ref in enumerate((own_ref, one_ref, two_ref, three_ref)):
        setting = pl.ds(node ^ step, 1)
        log_ref[setting, :] = ref[pl.ds(node, 1), :]
        solved_ref[setting, :] = ref[pl.ds(node + GROUP, 1), :]
        tip_log_ref[setting, :] = ref[2 * GROUP : 2 * GROUP + 1, 0:tip]
        tip_ref[setting, :] = ref[2 * GROUP + 1 : 2 * GROUP + 2, 0:tip]


def call(body, inputs, shapes, scratch=(), scalars=0):
    vmem = pl.BlockSpec(memory_space=pltpu.VMEM)
    smem = pl.BlockSpec(memory_space=pltpu.SMEM)
    return pl.pallas_call(
        body,
        out_shape=tuple(jax.ShapeDtypeStruct(shape, F32) for shape in shapes),
        in_specs=[smem] * scalars + [vmem] * (len(inputs) - scalars),
        out_specs=tuple(vmem for _ in shapes),
        scratch_shapes=[pltpu.VMEM(shape, F32) for shape in scratch],
        compiler_params=pltpu.CompilerParams(vmem_limit_bytes=40 * 1024 * 1024),
    )(*inputs)


def crossed(value, axis, step):
    size = lax.axis_size(axis)
    return lax.ppermute(value, axis, [(source, source ^ step) for source in range(size)])


def shards(
    diag_blocks,
    coupling,
    arrow_cols,
    rhs,
    tip_rhs,
    tip_diag,
    config_shift,
    config_coupling,
    pattern,
):
    tile = diag_blocks.shape[2]
    tip = arrow_cols.shape[1]
    groups = lax.axis_size("tm")
    spans = groups // GROUP
    assert config_shift.shape[0] == GROUP and diag_blocks.shape[:2] == (1, tile)
    position = lax.axis_index("tm")
    where = jnp.stack([position & (GROUP - 1), position >> 2]).astype(jnp.int32)
    side = tip + 2 * SUB
    (raw,) = call(
        pack_kernel,
        (where, pattern, diag_blocks[0], coupling[0], arrow_cols[0], rhs),
        ((tile + side, tile),),
        (),
        2,
    )
    two = crossed(raw, "tm", 2)
    one = crossed(raw, "tm", 1)
    three = crossed(two, "tm", 1)
    square = (GROUP, tile, tile)
    band = (GROUP, side, tile)
    packed_state = (3 * tile // 4 + tip + SUB, tile)
    *parts, state = call(
        functools.partial(local_kernel, tip),
        (where, config_shift, config_coupling, raw, one, two, three),
        (square, square, square, band, band, packed_state),
        ((GROUP,) + raw.shape, (tile, tile), (tile, tile)),
        3,
    )
    for span in range(spans - 1):
        state = lax.ppermute(state, "tm", [(source, source + GROUP) for source in range(groups - GROUP)])
        if span < spans - 2:
            (state,) = call(
                advance_kernel, (where, state, *parts), (packed_state,), ((tile, tile), (tile, tile)), 1
            )
    if spans == 1:
        state = jnp.zeros_like(state)
    small, sums = call(
        functools.partial(final_kernel, tip),
        (where, state, *parts),
        ((2 * GROUP, tile), (tip, tile)),
        ((tile, tile), (tile, tile), (SUB * tile, tile), (SUB * tile, tile)),
        1,
    )
    for axis, first in (("tm", GROUP), ("mesh", 4)):
        step = first
        while step < lax.axis_size(axis):
            sums = sums + crossed(sums, axis, step)
            step *= 2
    place = (lax.axis_index("mesh") & 3).astype(jnp.int32)[None]
    (packed,) = call(
        tip_kernel,
        (place, small, tip_diag[None], tip_rhs[None], sums) + tuple(crossed(sums, "mesh", n) for n in (1, 2, 3)),
        ((4 * GROUP, tile),),
        ((4, tip, 128), (SUB * tip, 128)),
        1,
    )
    log_diag, solved, tip_log, tip_forward = call(
        place_kernel,
        (where, packed, crossed(packed, "tm", 1), crossed(packed, "tm", 2), crossed(packed, "tm", 3)),
        ((GROUP, tile), (GROUP, tile), (GROUP, tip), (GROUP, tip)),
        (),
        1,
    )
    return (log_diag[:, None, :], solved[:, None, :], tip_log, tip_forward)


def solution(mesh):
    in_specs = (
        P("tm", "mesh", None),
        P("tm", "mesh", None),
        P("tm", None, "mesh"),
        P("tm", "mesh"),
        P(),
        P(),
        P(),
        P(),
        P("tm", "mesh"),
    )
    out_specs = (P(None, "tm", "mesh"), P(None, "tm", "mesh"), P(), P())
    return jax.shard_map(shards, mesh=mesh, in_specs=in_specs, out_specs=out_specs, check_vma=False)
```

time: 86.6 us -> 59.5 us (0.69)
  starting transfers between devices: 42.8 us -> 14.9 us
  local copies, waits for them, and re-layouts: 1.62 us -> 3.77 us
  Pallas kernels: 21.4 us -> 22.6 us
  waiting for transfers between devices: 17.2 us -> 16 us
  other arithmetic: 1.12 us -> 0.08 us
    ppermute x9 -> x10, starting transfers between devices: 38.1 us -> 10.3 us  [crossed(): lax.ppermute(value, axis, [(source, source ^ step) for source in range(si...]
    unnamed x14 -> x16, local copies, waits for them, and re-layouts: 1.31 us -> 3.77 us
    pallas_call x4 -> x5, Pallas kernels: 21.4 us -> 22.6 us  [call(): pl.pallas_call(body, out_shape=tuple((jax.ShapeDtypeStruct(shape, F32) fo...]
    mul x1 -> x0, other arithmetic: 0.88 us -> none  [shards(): coupling[0] * active]
    ppermute x9 -> x10, waiting for transfers between devices: 14.7 us -> 13.9 us  [crossed(): lax.ppermute(value, axis, [(source, source ^ step) for source in range(si...]
  transfers between devices with their start and end apart: 10 -> 11, of which waited for: 8 -> 8; matrix products, arithmetic and copies ran while one was open for 0% -> 0% of each run, Pallas kernels for 0% -> 0%
where the time goes in v2:
time: 59.5 us; the launch traced here: 58.7 us
  Pallas kernels  22.6 us (38%)
  waiting for transfers between devices  16 us (27%)
  starting transfers between devices  14.9 us (25%)
  local copies, waits for them, and re-layouts  3.77 us (6%)
  between operations  1.33 us (2%)
    pallas_call x5, Pallas kernels, call(): pl.pallas_call(body, out_shape=tuple((jax.ShapeDtypeStruct(shape, F32) fo...  22.6 us
    ppermute x10, waiting for transfers between devices, crossed(): lax.ppermute(value, axis, [(source, source ^ step) for source in range(si...  13.9 us
    ppermute x10, starting transfers between devices, crossed(): lax.ppermute(value, axis, [(source, source ^ step) for source in range(si...  10.3 us
    ppermute x1, starting transfers between devices, shards(): lax.ppermute(state, 'tm', [(source, source + GROUP) for source in range(g...  4.66 us
    unnamed x16, local copies, waits for them, and re-layouts  3.77 us
    ppermute x1, waiting for transfers between devices, shards(): lax.ppermute(state, 'tm', [(source, source + GROUP) for source in range(g...  2.11 us
  transfers between devices with their start and end apart: 11, of which 8 were waited for; matrix products, arithmetic and copies ran while one was open for 0% of the time, Pallas kernels for 0%

profile of v2, /device:TPU:0, one launch (start us, length us, event | category | flops | bytes accessed | tf_op | source)
XLA Modules:
  0.0 58.7 jit_solution(6215393635643159836)
XLA Ops:
  1.3 0.1 pad_add_fusion.where_ref
  1.4 0.0 copy-start.3
  1.4 0.7 %copy-done.3 = f32[1,128]{1,0:T(1,128)S(1)} copy-done((f32[1,128]{1,0:T(1,128)S(1)}, f32[1,128]{1,0:T(1,128)}, u32[]{:S(2)}) %copy-start.3) | copy-done | bytes 536
  2.0 0.0 copy-start
  2.0 0.8 %copy-done = f32[1,128,128]{2,1,0:T(8,128)S(1)} copy-done((f32[1,128,128]{2,1,0:T(8,128)S(1)}, f32[1,128,128]{2,1,0:T(8,128)}, u32[]{:S(2)}) %copy-start) | copy-done | bytes 65560
  2.9 0.0 copy-start.1
  2.9 0.8 %copy-done.1 = f32[1,128,128]{2,1,0:T(8,128)S(1)} copy-done((f32[1,128,128]{2,1,0:T(8,128)S(1)}, f32[1,128,128]{2,1,0:T(8,128)}, u32[]{:S(2)}) %copy-start.1) | copy-done | bytes 65560
  3.7 0.0 copy-start.2
  3.7 0.8 %copy-done.2 = f32[1,64,128]{2,1,0:T(8,128)S(1)} copy-done((f32[1,64,128]{2,1,0:T(8,128)S(1)}, f32[1,64,128]{2,1,0:T(8,128)}, u32[]{:S(2)}) %copy-start.2) | copy-done | bytes 32792
  4.5 0.0 copy-start.4
  4.5 0.0 copy-start.5
  4.5 0.6 shard_map.120.own_ref
  5.0 3.1 %collective-permute-start.1 = (f32[208,128]{1,0:T(8,128)S(1)}, f32[208,128]{1,0:T(8,128)S(1)}, u32[]{:S(2)}, u32[]{:S(2)}) collective-permute-start(f32[208,128]{1,0:T(8,128)S(1)} %shard_map.120.own_ref), channel_id=1, source_target_pairs={{0,8},{4,12},{8,0},{12,4},{16,24},{20,28},{24,16},{28,20},{1,9},{5... | collective-permute-start | bytes 319496 | tf_op jit(solution)/shard_map/ppermute | solution.py:413
  8.1 0.0 collective-permute-start
  8.1 3.0 %collective-permute-done.1.two_ref = f32[208,128]{1,0:T(8,128)S(1)} collective-permute-done((f32[208,128]{1,0:T(8,128)S(1)}, f32[208,128]{1,0:T(8,128)S(1)}, u32[]{:S(2)}, u32[]{:S(2)}) %collective-permute-start.1) | collective-permute-done | bytes 106528 | tf_op jit(solution)/shard_map/ppermute | solution.py:413
  11.1 0.0 collective-permute-start.2
  11.1 0.0 collective-permute-done.one_ref
  11.1 1.3 %collective-permute-done.2.three_ref = f32[208,128]{1,0:T(8,128)S(1)} collective-permute-done((f32[208,128]{1,0:T(8,128)S(1)}, f32[208,128]{1,0:T(8,128)S(1)}, u32[]{:S(2)}, u32[]{:S(2)}) %collective-permute-start.2) | collective-permute-done | bytes 106528 | tf_op jit(solution)/shard_map/ppermute | solution.py:413
  12.4 0.0 copy-done.4
  12.4 0.0 copy-done.5
  12.4 4.7 %shard_map.121 = (f32[4,128,128]{2,1,0:T(8,128)S(1)}, f32[4,128,128]{2,1,0:T(8,128)S(1)}, f32[4,128,128]{2,1,0:T(8,128)S(1)}, f32[4,80,128]{2,1,0:T(8,128)S(1)},...) custom-call(s32[2]{0:T(128)S(1)} %pad_add_fusion.where_ref, f32[4]{0:T(128)S(1)} %copy-done.4, f32[4]{0:T(128)S(1)} %copy-done.5, ...), custom_call_target="tpu_custom_call" | custom-call | tf_op jit(solution)/shard_map/pallas_call | solution.py:401
  17.1 4.7 %collective-permute-start.3 = (f32[168,128]{1,0:T(8,128)S(1)}, f32[168,128]{1,0:T(8,128)S(1)}, u32[]{:S(2)}, u32[]{:S(2)}) collective-permute-start(f32[168,128]{1,0:T(8,128)S(1)} %get-tuple-element.16), channel_id=1, source_target_pairs={{0,16},{4,20},{8,24},{12,28},{1,17},{5,21},{9,25},{13,29},{2,18},{... | collective-permute-start | bytes 258056 | tf_op jit(solution)/shard_map/ppermute | solution.py:456
  21.8 2.1 %collective-permute-done.3.state_ref = f32[168,128]{1,0:T(8,128)S(1)} collective-permute-done((f32[168,128]{1,0:T(8,128)S(1)}, f32[168,128]{1,0:T(8,128)S(1)}, u32[]{:S(2)}, u32[]{:S(2)}) %collective-permute-start.3) | collective-permute-done | bytes 86048 | tf_op jit(solution)/shard_map/ppermute | solution.py:456
  23.9 13.5 %shard_map.122 = (f32[8,128]{1,0:T(8,128)S(1)}, f32[64,128]{1,0:T(8,128)S(1)}) custom-call(s32[2]{0:T(128)S(1)} %pad_add_fusion.where_ref, f32[168,128]{1,0:T(8,128)S(1)} %collective-permute-done.3.state_ref, f32[4,128,128]{2,1,0:T(8,128)S(1)} %get-tuple-element.17.diag_ref, f32[4,128,128]{2,1,0:T(8,128)S(1)} %get-tuple-element.18.cross_ref, ...), custom_call_target="tpu_custom_call" | custom-call | tf_op jit(solution)/shard_map/pallas_call | solution.py:401
  37.4 0.2 collective-permute-start.4
  37.7 4.7 %collective-permute-done.4 = f32[64,128]{1,0:T(8,128)S(1)} collective-permute-done((f32[64,128]{1,0:T(8,128)S(1)}, f32[64,128]{1,0:T(8,128)S(1)}, u32[]{:S(2)}, u32[]{:S(2)}) %collective-permute-start.4) | collective-permute-done | bytes 32800 | tf_op jit(solution)/shard_map/ppermute | solution.py:413
  42.3 2.4 %collective-permute-start.7 = (f32[64,128]{1,0:T(8,128)S(1)}, f32[64,128]{1,0:T(8,128)S(1)}, u32[]{:S(2)}, u32[]{:S(2)}) collective-permute-start(f32[64,128]{1,0:T(8,128)S(1)} %add.3.own_ref), channel_id=1, source_target_pairs={{0,3},{1,2},{2,1},{3,0},{4,7},{5,6},{6,5},{7,4},{8,11},{9,10},{10,... | collective-permute-start | bytes 98312 | tf_op jit(solution)/shard_map/ppermute | solution.py:413
  44.8 0.5 collective-permute-start.6
  45.3 0.5 collective-permute-start.5
  45.8 1.3 %collective-permute-done.7.three_ref = f32[64,128]{1,0:T(8,128)S(1)} collective-permute-done((f32[64,128]{1,0:T(8,128)S(1)}, f32[64,128]{1,0:T(8,128)S(1)}, u32[]{:S(2)}, u32[]{:S(2)}) %collective-permute-start.7) | collective-permute-done | bytes 32800 | tf_op jit(solution)/shard_map/ppermute | solution.py:413
  47.1 1.5 %collective-permute-done.6.two_ref = f32[64,128]{1,0:T(8,128)S(1)} collective-permute-done((f32[64,128]{1,0:T(8,128)S(1)}, f32[64,128]{1,0:T(8,128)S(1)}, u32[]{:S(2)}, u32[]{:S(2)}) %collective-permute-start.6) | collective-permute-done | bytes 32800 | tf_op jit(solution)/shard_map/ppermute | solution.py:413
  48.7 0.5 collective-permute-done.5.one_ref
  49.2 0.0 copy-start.6
  49.2 0.0 copy-start.7
  49.2 0.7 %copy-done.6 = f32[64]{0:T(128)S(1)} copy-done((f32[64]{0:T(128)S(1)}, f32[64]{0:T(128)}, u32[]{:S(2)}) %copy-start.6) | copy-done | bytes 280
  49.9 0.0 copy-done.7
  49.9 2.6 %shard_map.123.own_ref = f32[16,128]{1,0:T(8,128)S(1)} custom-call(s32[1]{0:T(128)} %bitcast.2.place_ref, f32[8,128]{1,0:T(8,128)S(1)} %get-tuple-element.22.small_ref, f32[1,64]{1,0:T(1,128)S(1)} %bitcast.17, f32[1,64]{1,0:T(1,128)S(1)} %bitcast.18, f32[64,128]{1,0:T(8,128)S(1)} %add.3.own_ref, f32[64,128]{1,0:T(8,128)S(1)} %collective-permute-done.5.one_ref, ...), custom_call_target="tpu_custom_call" | custom-call | tf_op jit(solution)/shard_map/pallas_call | solution.py:401
  52.5 0.1 collective-permute-start.10
  52.6 3.3 %collective-permute-start.9 = (f32[16,128]{1,0:T(8,128)S(1)}, f32[16,128]{1,0:T(8,128)S(1)}, u32[]{:S(2)}, u32[]{:S(2)}) collective-permute-start(f32[16,128]{1,0:T(8,128)S(1)} %shard_map.123.own_ref), channel_id=1, source_target_pairs={{0,8},{4,12},{8,0},{12,4},{16,24},{20,28},{24,16},{28,20},{1,9},{5... | collective-permute-start | bytes 24584 | tf_op jit(solution)/shard_map/ppermute | solution.py:413
  55.9 0.0 collective-permute-start.8
  56.0 0.0 collective-permute-done.10.three_ref
  56.0 1.6 %collective-permute-done.9.two_ref = f32[16,128]{1,0:T(8,128)S(1)} collective-permute-done((f32[16,128]{1,0:T(8,128)S(1)}, f32[16,128]{1,0:T(8,128)S(1)}, u32[]{:S(2)}, u32[]{:S(2)}) %collective-permute-start.9) | collective-permute-done | bytes 8224 | tf_op jit(solution)/shard_map/ppermute | solution.py:413
  57.6 0.0 collective-permute-done.8.one_ref
  57.6 1.1 %shard_map.124 = (f32[4,128]{1,0:T(4,128)}, f32[4,128]{1,0:T(4,128)}, f32[4,64]{1,0:T(4,128)}, f32[4,64]{1,0:T(4,128)}) custom-call(s32[2]{0:T(128)S(1)} %pad_add_fusion.where_ref, f32[16,128]{1,0:T(8,128)S(1)} %shard_map.123.own_ref, f32[16,128]{1,0:T(8,128)S(1)} %collective-permute-done.8.one_ref, f32[16,128]{1,0:T(8,128)S(1)} %collective-permute-done.9.two_ref, ...), custom_call_target="tpu_custom_call" | custom-call | tf_op jit(solution)/shard_map/pallas_call | solution.py:401
  (1 shorter events, 0.0 us)
Async XLA Ops:
  1.4 0.7 %copy-start.3 = (f32[1,128]{1,0:T(1,128)S(1)}, f32[1,128]{1,0:T(1,128)}, u32[]{:S(2)}) copy-start(f32[1,128]{1,0:T(1,128)} %rhs_ref.1) | copy-start | bytes 1540
  2.0 0.8 %copy-start = (f32[1,128,128]{2,1,0:T(8,128)S(1)}, f32[1,128,128]{2,1,0:T(8,128)}, u32[]{:S(2)}) copy-start(f32[1,128,128]{2,1,0:T(8,128)} %param.9) | copy-start | bytes 196612
  2.9 0.8 %copy-start.1 = (f32[1,128,128]{2,1,0:T(8,128)S(1)}, f32[1,128,128]{2,1,0:T(8,128)}, u32[]{:S(2)}) copy-start(f32[1,128,128]{2,1,0:T(8,128)} %param.10) | copy-start | bytes 196612
  3.7 0.8 %copy-start.2 = (f32[1,64,128]{2,1,0:T(8,128)S(1)}, f32[1,64,128]{2,1,0:T(8,128)}, u32[]{:S(2)}) copy-start(f32[1,64,128]{2,1,0:T(8,128)} %param.11) | copy-start | bytes 98308
  4.5 8.0 %copy-start.4 = (f32[4]{0:T(128)S(1)}, f32[4]{0:T(128)}, u32[]{:S(2)}) copy-start(f32[4]{0:T(128)} %shift_ref.1) | copy-start | bytes 52
  4.5 8.0 %copy-start.5 = (f32[4]{0:T(128)S(1)}, f32[4]{0:T(128)}, u32[]{:S(2)}) copy-start(f32[4]{0:T(128)} %couple_ref.1) | copy-start | bytes 52
  5.0 6.1 %collective-permute-start.1 = (f32[208,128]{1,0:T(8,128)S(1)}, f32[208,128]{1,0:T(8,128)S(1)}, u32[]{:S(2)}, u32[]{:S(2)}) collective-permute-start(f32[208,128]{1,0:T(8,128)S(1)} %shard_map.120.own_ref), channel_id=1, source_target_pairs={{0,8},{4,12},{8,0},{12,4},{16,24},{20,28},{24,16},{28,20},{1,9},{5... | collective-permute-start | bytes 319496 | tf_op jit(solution)/shard_map/ppermute | solution.py:413
  8.1 3.0 %collective-permute-start = (f32[208,128]{1,0:T(8,128)S(1)}, f32[208,128]{1,0:T(8,128)S(1)}, u32[]{:S(2)}, u32[]{:S(2)}) collective-permute-start(f32[208,128]{1,0:T(8,128)S(1)} %shard_map.120.own_ref), channel_id=1, source_target_pairs={{0,4},{4,0},{8,12},{12,8},{16,20},{20,16},{24,28},{28,24},{1,5},{5... | collective-permute-start | bytes 319496 | tf_op jit(solution)/shard_map/ppermute | solution.py:413
  11.1 1.3 %collective-permute-start.2 = (f32[208,128]{1,0:T(8,128)S(1)}, f32[208,128]{1,0:T(8,128)S(1)}, u32[]{:S(2)}, u32[]{:S(2)}) collective-permute-start(f32[208,128]{1,0:T(8,128)S(1)} %collective-permute-done.1.two_ref), channel_id=1, source_target_pairs={{0,4},{4,0},{8,12},{12,8},{16,20},{20,16},{24,28},{28,24},{1,5},{5... | collective-permute-start | bytes 319496 | tf_op jit(solution)/shard_map/ppermute | solution.py:413
  17.1 6.8 %collective-permute-start.3 = (f32[168,128]{1,0:T(8,128)S(1)}, f32[168,128]{1,0:T(8,128)S(1)}, u32[]{:S(2)}, u32[]{:S(2)}) collective-permute-start(f32[168,128]{1,0:T(8,128)S(1)} %get-tuple-element.16), channel_id=1, source_target_pairs={{0,16},{4,20},{8,24},{12,28},{1,17},{5,21},{9,25},{13,29},{2,18},{... | collective-permute-start | bytes 258056 | tf_op jit(solution)/shard_map/ppermute | solution.py:456
  37.4 4.9 %collective-permute-start.4 = (f32[64,128]{1,0:T(8,128)S(1)}, f32[64,128]{1,0:T(8,128)S(1)}, u32[]{:S(2)}, u32[]{:S(2)}) collective-permute-start(f32[64,128]{1,0:T(8,128)S(1)} %get-tuple-element.23), channel_id=1, source_target_pairs={{0,16},{4,20},{8,24},{12,28},{16,0},{20,4},{24,8},{28,12},{1,17},{... | collective-permute-start | bytes 98312 | tf_op jit(solution)/shard_map/ppermute | solution.py:413
  42.3 4.8 %collective-permute-start.7 = (f32[64,128]{1,0:T(8,128)S(1)}, f32[64,128]{1,0:T(8,128)S(1)}, u32[]{:S(2)}, u32[]{:S(2)}) collective-permute-start(f32[64,128]{1,0:T(8,128)S(1)} %add.3.own_ref), channel_id=1, source_target_pairs={{0,3},{1,2},{2,1},{3,0},{4,7},{5,6},{6,5},{7,4},{8,11},{9,10},{10,... | collective-permute-start | bytes 98312 | tf_op jit(solution)/shard_map/ppermute | solution.py:413
  44.8 3.9 %collective-permute-start.6 = (f32[64,128]{1,0:T(8,128)S(1)}, f32[64,128]{1,0:T(8,128)S(1)}, u32[]{:S(2)}, u32[]{:S(2)}) collective-permute-start(f32[64,128]{1,0:T(8,128)S(1)} %add.3.own_ref), channel_id=1, source_target_pairs={{0,2},{1,3},{2,0},{3,1},{4,6},{5,7},{6,4},{7,5},{8,10},{9,11},{10,... | collective-permute-start | bytes 98312 | tf_op jit(solution)/shard_map/ppermute | solution.py:413
  45.3 3.9 %collective-permute-start.5 = (f32[64,128]{1,0:T(8,128)S(1)}, f32[64,128]{1,0:T(8,128)S(1)}, u32[]{:S(2)}, u32[]{:S(2)}) collective-permute-start(f32[64,128]{1,0:T(8,128)S(1)} %add.3.own_ref), channel_id=1, source_target_pairs={{0,1},{1,0},{2,3},{3,2},{4,5},{5,4},{6,7},{7,6},{8,9},{9,8},{10,11... | collective-permute-start | bytes 98312 | tf_op jit(solution)/shard_map/ppermute | solution.py:413
  49.2 0.7 %copy-start.6 = (f32[64]{0:T(128)S(1)}, f32[64]{0:T(128)}, u32[]{:S(2)}) copy-start(f32[64]{0:T(128)} %param.14) | copy-start | bytes 772
  49.2 0.7 %copy-start.7 = (f32[64]{0:T(128)S(1)}, f32[64]{0:T(128)}, u32[]{:S(2)}) copy-start(f32[64]{0:T(128)} %param.13) | copy-start | bytes 772
  52.5 3.5 %collective-permute-start.10 = (f32[16,128]{1,0:T(8,128)S(1)}, f32[16,128]{1,0:T(8,128)S(1)}, u32[]{:S(2)}, u32[]{:S(2)}) collective-permute-start(f32[16,128]{1,0:T(8,128)S(1)} %shard_map.123.own_ref), channel_id=1, source_target_pairs={{0,12},{4,8},{8,4},{12,0},{16,28},{20,24},{24,20},{28,16},{1,13},{... | collective-permute-start | bytes 24584 | tf_op jit(solution)/shard_map/ppermute | solution.py:413
  52.6 4.9 %collective-permute-start.9 = (f32[16,128]{1,0:T(8,128)S(1)}, f32[16,128]{1,0:T(8,128)S(1)}, u32[]{:S(2)}, u32[]{:S(2)}) collective-permute-start(f32[16,128]{1,0:T(8,128)S(1)} %shard_map.123.own_ref), channel_id=1, source_target_pairs={{0,8},{4,12},{8,0},{12,4},{16,24},{20,28},{24,16},{28,20},{1,9},{5... | collective-permute-start | bytes 24584 | tf_op jit(solution)/shard_map/ppermute | solution.py:413
  55.9 1.6 %collective-permute-start.8 = (f32[16,128]{1,0:T(8,128)S(1)}, f32[16,128]{1,0:T(8,128)S(1)}, u32[]{:S(2)}, u32[]{:S(2)}) collective-permute-start(f32[16,128]{1,0:T(8,128)S(1)} %shard_map.123.own_ref), channel_id=1, source_target_pairs={{0,4},{4,0},{8,12},{12,8},{16,20},{20,16},{24,28},{28,24},{1,5},{5... | collective-permute-start | bytes 24584 | tf_op jit(solution)/shard_map/ppermute | solution.py:413

commit v3 on v2

--- a/solution.py
+++ b/solution.py
@@ -105,20 +105,48 @@
     return results, total
 
 
-def pack_kernel(where_ref, pattern_ref, diag_ref, couple_ref, arrow_ref, rhs_ref, out_ref):
+def pack_kernel(
+    where_ref,
+    pattern_hbm,
+    diag_hbm,
+    couple_hbm,
+    arrow_hbm,
+    rhs_hbm,
+    out_ref,
+    pattern_ref,
+    diag_ref,
+    couple_ref,
+    rhs_ref,
+    sems,
+):
     tile = diag_ref.shape[0]
-    tip = arrow_ref.shape[0]
+    tip = arrow_hbm.shape[1]
+    copies = [
+        pltpu.make_async_copy(source, target, sems.at[n])
+        for n, (source, target) in enumerate(
+            (
+                (diag_hbm.at[0], diag_ref),
+                (couple_hbm.at[0], couple_ref),
+                (arrow_hbm.at[0], out_ref.at[tile : tile + tip, :]),
+                (rhs_hbm, rhs_ref),
+                (pattern_hbm, pattern_ref),
+            )
+        )
+    ]
+    for copy in copies:
+        copy.start()
+    for copy in copies:
+        copy.wait()
     row = lax.broadcasted_iota(jnp.int32, (tile, tile), 0)
     col = lax.broadcasted_iota(jnp.int32, (tile, tile), 1)
     couple = couple_ref[...]
     out_ref[0:tile, :] = jnp.where(row >= col, diag_ref[...], couple)
-    out_ref[tile : tile + tip, :] = arrow_ref[...]
     first = (where_ref[0] == 0) & (where_ref[1] == 0)
-    active = jnp.where(first, 0, pattern_ref[0, 0]).astype(F32)
+    active = jnp.where(first, 0.0, 1.0).astype(F32) * pattern_ref[...].astype(F32)
     middle = jnp.sum(jnp.where(row == col, couple, 0.0), axis=0, keepdims=True)
     filler = jnp.zeros((2 * SUB - 3, tile), F32)
     out_ref[tile + tip :, :] = jnp.concatenate(
-        [rhs_ref[...], middle, jnp.full((1, tile), active), filler], axis=0
+        [rhs_ref[...], middle, jnp.broadcast_to(active, (1, tile)), filler], axis=0
     )
 
 
@@ -127,6 +155,8 @@
     where_ref,
     shift_ref,
     couple_ref,
+    tip_diag_ref,
+    tip_rhs_ref,
     own_ref,
     one_ref,
     two_ref,
@@ -137,6 +167,7 @@
     right_ref,
     left_ref,
     state_ref,
+    prior_ref,
     raw_ref,
     mat_ref,
     inv_ref,
@@ -209,6 +240,14 @@
         send(state_ref, diag03, right03)
         return total + more
 
+    row = lax.broadcasted_iota(jnp.int32, (tip, 128), 0)
+    col = lax.broadcasted_iota(jnp.int32, (tip, 128), 1)
+    filler = jnp.zeros((1, 128 - tip), F32)
+    prior = jnp.where(row == col, jnp.concatenate([tip_diag_ref[...], filler], axis=1), 0.0)
+    column = jnp.where(row == col, jnp.concatenate([tip_rhs_ref[...], filler], axis=1), 0.0)
+    column = jnp.sum(column, axis=1, keepdims=True)
+    prior_ref[...] = prior + jnp.where(col == tip, column, 0.0)
+
     settled = jnp.sum(run(None)) < SMALL * 4
 
     @pl.when(jnp.logical_not(settled))
@@ -245,7 +284,7 @@
     tile = diag_ref.shape[-1]
     lone = jnp.where(where_ref[1] == 0, 1.0, 0.0).astype(F32)
     base, came = receive(state_ref)
-    base = base + lone * identity(tile)
+    base = base + lone * diag_ref[0]
     mats = [base + back_ref[n] for n in order]
     crosses = [cross_ref[n] for n in order]
     came = padded(came, tile)
@@ -365,34 +404,24 @@
     sums_ref[...] = fine(everything[:, 0:tip], everything, TN)
 
 
-def tip_kernel(place_ref, small_ref, diag_ref, rhs_ref, own_ref, one_ref, two_ref, three_ref, out_ref, sums_ref, rows_ref):
-    tip = own_ref.shape[0]
-    for step, ref in enumerate((own_ref, one_ref, two_ref, three_ref)):
-        sums_ref[place_ref[0] ^ step] = ref[...]
-    row = lax.broadcasted_iota(jnp.int32, (tip, 128), 0)
-    col = lax.broadcasted_iota(jnp.int32, (tip, 128), 1)
-    filler = jnp.zeros((1, 128 - tip), F32)
-    prior = jnp.where(row == col, jnp.concatenate([diag_ref[...], filler], axis=1), 0.0)
-    right = jnp.where(row == col, jnp.concatenate([rhs_ref[...], filler], axis=1), 0.0)
-    prior = prior + jnp.where(col == tip, jnp.sum(right, axis=1, keepdims=True), 0.0)
+def tip_kernel(small_ref, prior_ref, sums_ref, out_ref, rows_ref):
+    tip = prior_ref.shape[0]
     total = (sums_ref[0] + sums_ref[1]) + (sums_ref[2] + sums_ref[3])
-    rows_ref[pl.ds(0, tip, stride=SUB), :] = prior - total
+    rows_ref[pl.ds(0, tip, stride=SUB), :] = prior_ref[...] - total
     pivots, column = factor((rows_ref,), tip, 1, tip)
-    out_ref[0 : 2 * GROUP, :] = small_ref[...]
-    out_ref[2 * GROUP :, :] = jnp.concatenate(
-        [0.5 * jnp.log(pivots[0:1, :]), column[0:1, :], jnp.zeros((6, 128), F32)], axis=0
-    )
-
-
-def place_kernel(where_ref, own_ref, one_ref, two_ref, three_ref, log_ref, solved_ref, tip_log_ref, tip_ref):
-    node = where_ref[0]
+    ends = [0.5 * jnp.log(pivots[0:1, :]), column[0:1, :], jnp.zeros((SUB - 4, 128), F32)]
+    for n in range(GROUP):
+        own = [small_ref[n : n + 1, :], small_ref[GROUP + n : GROUP + n + 1, :]]
+        out_ref[n] = jnp.concatenate(own + ends, axis=0)
+
+
+def place_kernel(came_ref, log_ref, solved_ref, tip_log_ref, tip_ref):
     tip = tip_ref.shape[1]
-    for step, ref in enumerate((own_ref, one_ref, two_ref, three_ref)):
-        setting = pl.ds(node ^ step, 1)
-        log_ref[setting, :] = ref[pl.ds(node, 1), :]
-        solved_ref[setting, :] = ref[pl.ds(node + GROUP, 1), :]
-        tip_log_ref[setting, :] = ref[2 * GROUP : 2 * GROUP + 1, 0:tip]
-        tip_ref[setting, :] = ref[2 * GROUP + 1 : 2 * GROUP + 2, 0:tip]
+    for n in range(GROUP):
+        log_ref[n : n + 1, :] = came_ref[n, 0:1, :]
+        solved_ref[n : n + 1, :] = came_ref[n, 1:2, :]
+        tip_log_ref[n : n + 1, :] = came_ref[n, 2:3, 0:tip]
+        tip_ref[n : n + 1, :] = came_ref[n, 3:4, 0:tip]
 
 
 def call(body, inputs, shapes, scratch=(), scalars=0):
@@ -411,6 +440,12 @@
 def crossed(value, axis, step):
     size = lax.axis_size(axis)
     return lax.ppermute(value, axis, [(source, source ^ step) for source in range(size)])
+
+
+def traded(value, axis):
+    size = lax.axis_size(axis)
+    groups = [[first + n for n in range(4)] for first in range(0, size, 4)]
+    return lax.all_to_all(value, axis, 0, 0, axis_index_groups=groups)
 
 
 def shards(
@@ -432,23 +467,30 @@
     position = lax.axis_index("tm")
     where = jnp.stack([position & (GROUP - 1), position >> 2]).astype(jnp.int32)
     side = tip + 2 * SUB
-    (raw,) = call(
+    hbm = pl.BlockSpec(memory_space=pltpu.HBM)
+    raw = pl.pallas_call(
         pack_kernel,
-        (where, pattern, diag_blocks[0], coupling[0], arrow_cols[0], rhs),
-        ((tile + side, tile),),
-        (),
-        2,
-    )
+        out_shape=jax.ShapeDtypeStruct((tile + side, tile), F32),
+        in_specs=[pl.BlockSpec(memory_space=pltpu.SMEM)] + [hbm] * 5,
+        out_specs=pl.BlockSpec(memory_space=pltpu.VMEM),
+        scratch_shapes=[
+            pltpu.VMEM((1, 1), jnp.int32),
+            pltpu.VMEM((tile, tile), F32),
+            pltpu.VMEM((tile, tile), F32),
+            pltpu.VMEM((1, tile), F32),
+            pltpu.SemaphoreType.DMA((5,)),
+        ],
+    )(where, pattern, diag_blocks, coupling, arrow_cols, rhs)
     two = crossed(raw, "tm", 2)
     one = crossed(raw, "tm", 1)
     three = crossed(two, "tm", 1)
     square = (GROUP, tile, tile)
     band = (GROUP, side, tile)
     packed_state = (3 * tile // 4 + tip + SUB, tile)
-    *parts, state = call(
+    *parts, state, prior = call(
         functools.partial(local_kernel, tip),
-        (where, config_shift, config_coupling, raw, one, two, three),
-        (square, square, square, band, band, packed_state),
+        (where, config_shift, config_coupling, tip_diag[None], tip_rhs[None], raw, one, two, three),
+        (square, square, square, band, band, packed_state, (tip, 128)),
         ((GROUP,) + raw.shape, (tile, tile), (tile, tile)),
         3,
     )
@@ -472,20 +514,16 @@
         while step < lax.axis_size(axis):
             sums = sums + crossed(sums, axis, step)
             step *= 2
-    place = (lax.axis_index("mesh") & 3).astype(jnp.int32)[None]
     (packed,) = call(
         tip_kernel,
-        (place, small, tip_diag[None], tip_rhs[None], sums) + tuple(crossed(sums, "mesh", n) for n in (1, 2, 3)),
-        ((4 * GROUP, tile),),
-        ((4, tip, 128), (SUB * tip, 128)),
-        1,
+        (small, prior, traded(jnp.broadcast_to(sums[None], (4, tip, 128)), "mesh")),
+        ((GROUP, SUB, tile),),
+        ((SUB * tip, 128),),
     )
     log_diag, solved, tip_log, tip_forward = call(
         place_kernel,
-        (where, packed, crossed(packed, "tm", 1), crossed(packed, "tm", 2), crossed(packed, "tm", 3)),
+        (traded(packed, "tm"),),
         ((GROUP, tile), (GROUP, tile), (GROUP, tip), (GROUP, tip)),
-        (),
-        1,
     )
     return (log_diag[:, None, :], solved[:, None, :], tip_log, tip_forward)
 

time: 59.5 us -> 60.8 us (1.022)
  blocking collectives: 0 us -> 16.7 us
  waiting for transfers between devices: 16 us -> 8.47 us
  starting transfers between devices: 14.9 us -> 11.3 us
  local copies, waits for them, and re-layouts: 3.77 us -> 1.58 us
  Pallas kernels: 22.6 us -> 20.6 us
    all_to_all x0 -> x2, blocking collectives: none -> 16.7 us  [traded(): return lax.all_to_all(value, axis, 0, 0, axis_index_groups=groups)]
    ppermute x10 -> x4, waiting for transfers between devices: 13.9 us -> 6.38 us  [crossed(): lax.ppermute(value, axis, [(source, source ^ step) for source in range(si...]
    pallas_call x5 -> x4, Pallas kernels: 22.6 us -> 18.1 us  [call(): pl.pallas_call(body, out_shape=tuple((jax.ShapeDtypeStruct(shape, F32) fo...]
    ppermute x10 -> x4, starting transfers between devices: 10.3 us -> 6.63 us  [crossed(): lax.ppermute(value, axis, [(source, source ^ step) for source in range(si...]
    pallas_call x0 -> x1, Pallas kernels: none -> 2.42 us  [shards(): pl.pallas_call(pack_kernel, out_shape=jax.ShapeDtypeStruct((tile + side,...]
    unnamed x16 -> x12, local copies, waits for them, and re-layouts: 3.77 us -> 1.57 us
  transfers between devices with their start and end apart: 11 -> 5, of which waited for: 8 -> 4; matrix products, arithmetic and copies ran while one was open for 0% -> 0% of each run, Pallas kernels for 0% -> 0%
where the time goes in v3:
time: 60.8 us; the launch traced here: 60.5 us
  Pallas kernels  20.6 us (34%)
  blocking collectives  16.7 us (27%)
  starting transfers between devices  11.3 us (19%)
  waiting for transfers between devices  8.47 us (14%)
  local copies, waits for them, and re-layouts  1.58 us (3%)
  between operations  1.33 us (2%)
    pallas_call x4, Pallas kernels, call(): pl.pallas_call(body, out_shape=tuple((jax.ShapeDtypeStruct(shape, F32) fo...  18.1 us
    all_to_all x2, blocking collectives, traded(): return lax.all_to_all(value, axis, 0, 0, axis_index_groups=groups)  16.7 us
    ppermute x4, starting transfers between devices, crossed(): lax.ppermute(value, axis, [(source, source ^ step) for source in range(si...  6.63 us
    ppermute x4, waiting for transfers between devices, crossed(): lax.ppermute(value, axis, [(source, source ^ step) for source in range(si...  6.38 us
    ppermute x1, starting transfers between devices, shards(): lax.ppermute(state, 'tm', [(source, source + GROUP) for source in range(g...  4.67 us
    pallas_call x1, Pallas kernels, shards(): pl.pallas_call(pack_kernel, out_shape=jax.ShapeDtypeStruct((tile + side,...  2.42 us
    ppermute x1, waiting for transfers between devices, shards(): lax.ppermute(state, 'tm', [(source, source + GROUP) for source in range(g...  2.09 us
    unnamed x12, local copies, waits for them, and re-layouts  1.57 us
  transfers between devices with their start and end apart: 5, of which 4 were waited for; matrix products, arithmetic and copies ran while one was open for 0% of the time, Pallas kernels for 0%

profile of v3, /device:TPU:0, one launch (start us, length us, event | category | flops | bytes accessed | tf_op | source)
XLA Modules:
  0.0 60.5 jit_solution(13246180383311291397)
XLA Ops:
  1.3 0.6 pad_add_fusion.where_ref
  1.9 0.0 copy-start.4
  1.9 0.0 copy-start.5
  1.9 2.4 %shard_map.120.own_ref = f32[208,128]{1,0:T(8,128)} custom-call(s32[2]{0:T(128)} %pad_add_fusion.where_ref, s32[1,1]{1,0:T(1,128)S(6)} %copy.15.pattern_hbm, f32[1,128,128]{2,1,0:T(8,128)} %diag_hbm.1, f32[1,128,128]{2,1,0:T(8,128)} %couple_hbm.1, f32[1,64,128]{2,1,0:T(8,128)} %arrow_hbm.1, f32[1,128]{1,0:T(1,128)} %rhs_hbm.1), custom_call_target="tpu_custom_call" | custom-call | tf_op jit(solution)/shard_map/pallas_call | solution.py:471
  4.3 3.1 %collective-permute-start.1 = (f32[208,128]{1,0:T(8,128)}, f32[208,128]{1,0:T(8,128)S(1)}, u32[]{:S(2)}, u32[]{:S(2)}) collective-permute-start(f32[208,128]{1,0:T(8,128)} %shard_map.120.own_ref), channel_id=1, source_target_pairs={{0,8},{4,12},{8,0},{12,4},{16,24},{20,28},{24,16},{28,20},{1,9},{5... | collective-permute-start | bytes 319496 | tf_op jit(solution)/shard_map/ppermute | solution.py:442
  7.4 0.0 collective-permute-start
  7.4 3.2 %collective-permute-done.1.two_ref = f32[208,128]{1,0:T(8,128)S(1)} collective-permute-done((f32[208,128]{1,0:T(8,128)}, f32[208,128]{1,0:T(8,128)S(1)}, u32[]{:S(2)}, u32[]{:S(2)}) %collective-permute-start.1) | collective-permute-done | bytes 106528 | tf_op jit(solution)/shard_map/ppermute | solution.py:442
  10.6 0.0 collective-permute-start.2
  10.6 0.0 collective-permute-done.one_ref
  10.6 1.3 %collective-permute-done.2.three_ref = f32[208,128]{1,0:T(8,128)S(1)} collective-permute-done((f32[208,128]{1,0:T(8,128)S(1)}, f32[208,128]{1,0:T(8,128)S(1)}, u32[]{:S(2)}, u32[]{:S(2)}) %collective-permute-start.2) | collective-permute-done | bytes 106528 | tf_op jit(solution)/shard_map/ppermute | solution.py:442
  11.9 0.0 copy-start.1
  11.9 0.0 copy-start.2
  11.9 0.0 copy-start.3
  11.9 0.0 copy-done.4
  11.9 0.0 copy-done.5
  11.9 0.6 %copy-done.1 = s32[2]{0:T(128)S(1)} copy-done((s32[2]{0:T(128)S(1)}, s32[2]{0:T(128)}, u32[]{:S(2)}) %copy-start.1) | copy-done | bytes 32
  12.5 0.0 copy-done.2
  12.6 0.0 copy-done.3
  12.6 0.0 copy-start
  12.6 0.9 %copy-done = f32[208,128]{1,0:T(8,128)S(1)} copy-done((f32[208,128]{1,0:T(8,128)S(1)}, f32[208,128]{1,0:T(8,128)}, u32[]{:S(2)}) %copy-start) | copy-done | bytes 106520
  13.5 4.7 %shard_map.121 = (f32[4,128,128]{2,1,0:T(8,128)S(1)}, f32[4,128,128]{2,1,0:T(8,128)S(1)}, f32[4,128,128]{2,1,0:T(8,128)S(1)}, f32[4,80,128]{2,1,0:T(8,128)S(1)},...) custom-call(s32[2]{0:T(128)S(1)} %copy-done.1, f32[4]{0:T(128)S(1)} %copy-done.2, ...), custom_call_target="tpu_custom_call" | custom-call | tf_op jit(solution)/shard_map/pallas_call | solution.py:430
  18.2 4.7 %collective-permute-start.3 = (f32[168,128]{1,0:T(8,128)S(1)}, f32[168,128]{1,0:T(8,128)S(1)}, u32[]{:S(2)}, u32[]{:S(2)}) collective-permute-start(f32[168,128]{1,0:T(8,128)S(1)} %get-tuple-element.17), channel_id=1, source_target_pairs={{0,16},{4,20},{8,24},{12,28},{1,17},{5,21},{9,25},{13,29},{2,18},{... | collective-permute-start | bytes 258056 | tf_op jit(solution)/shard_map/ppermute | solution.py:498
  22.9 2.1 %collective-permute-done.3.state_ref = f32[168,128]{1,0:T(8,128)S(1)} collective-permute-done((f32[168,128]{1,0:T(8,128)S(1)}, f32[168,128]{1,0:T(8,128)S(1)}, u32[]{:S(2)}, u32[]{:S(2)}) %collective-permute-start.3) | collective-permute-done | bytes 86048 | tf_op jit(solution)/shard_map/ppermute | solution.py:498
  25.0 10.2 %shard_map.122 = (f32[8,128]{1,0:T(8,128)S(1)}, f32[64,128]{1,0:T(8,128)S(1)}) custom-call(s32[2]{0:T(128)S(1)} %copy-done.1, f32[168,128]{1,0:T(8,128)S(1)} %collective-permute-done.3.state_ref, f32[4,128,128]{2,1,0:T(8,128)S(1)} %get-tuple-element.18.diag_ref, f32[4,128,128]{2,1,0:T(8,128)S(1)} %get-tuple-element.19.cross_ref, ...), custom_call_target="tpu_custom_call" | custom-call | tf_op jit(solution)/shard_map/pallas_call | solution.py:430
  35.2 3.5 %collective-permute-start.4 = (f32[64,128]{1,0:T(8,128)S(1)}, f32[64,128]{1,0:T(8,128)S(1)}, u32[]{:S(2)}, u32[]{:S(2)}) collective-permute-start(f32[64,128]{1,0:T(8,128)S(1)} %get-tuple-element.25), channel_id=1, source_target_pairs={{0,16},{4,20},{8,24},{12,28},{16,0},{20,4},{24,8},{28,12},{1,17},{... | collective-permute-start | bytes 98312 | tf_op jit(solution)/shard_map/ppermute | solution.py:442
  38.7 1.9 %collective-permute-done.4 = f32[64,128]{1,0:T(8,128)S(1)} collective-permute-done((f32[64,128]{1,0:T(8,128)S(1)}, f32[64,128]{1,0:T(8,128)S(1)}, u32[]{:S(2)}, u32[]{:S(2)}) %collective-permute-start.4) | collective-permute-done | bytes 32800 | tf_op jit(solution)/shard_map/ppermute | solution.py:442
  40.6 8.5 %all_to_all.10.sums_ref = f32[4,64,128]{2,1,0:T(8,128)S(1)} all-to-all(f32[4,64,128]{2,1,0:T(8,128)S(1)} %broadcast_in_dim.20), channel_id=1, replica_groups={{0,1,2,3},{4,5,6,7},{8,9,10,11},{12,13,14,15},{16,17,18,19},{20,21,22,2..., dimensions={0} | all-to-all | bytes 262144 | tf_op jit(solution)/shard_map/all_to_all | solution.py:448
  49.2 2.6 %shard_map.123 = f32[4,8,128]{2,1,0:T(8,128)S(1)} custom-call(f32[8,128]{1,0:T(8,128)S(1)} %get-tuple-element.23.small_ref, f32[64,128]{1,0:T(8,128)S(1)} %get-tuple-element.24.prior_ref, f32[4,64,128]{2,1,0:T(8,128)S(1)} %all_to_all.10.sums_ref), custom_call_target="tpu_custom_call" | custom-call | tf_op jit(solution)/shard_map/pallas_call | solution.py:430
  51.8 8.1 %all_to_all.11.came_ref = f32[4,8,128]{2,1,0:T(8,128)S(1)} all-to-all(f32[4,8,128]{2,1,0:T(8,128)S(1)} %shard_map.123), channel_id=1, replica_groups={{0,4,8,12},{16,20,24,28},{1,5,9,13},{17,21,25,29},{2,6,10,14},{18,22,26..., dimensions={0} | all-to-all | bytes 32768 | tf_op jit(solution)/shard_map/all_to_all | solution.py:448
  59.9 0.6 shard_map.124
  (2 shorter events, 0.0 us)
Async XLA Ops:
  1.9 10.0 %copy-start.4 = (f32[64]{0:T(128)S(1)}, f32[64]{0:T(128)}, u32[]{:S(2)}) copy-start(f32[64]{0:T(128)} %param.14) | copy-start | bytes 772
  1.9 10.0 %copy-start.5 = (f32[64]{0:T(128)S(1)}, f32[64]{0:T(128)}, u32[]{:S(2)}) copy-start(f32[64]{0:T(128)} %param.13) | copy-start | bytes 772
  4.3 6.3 %collective-permute-start.1 = (f32[208,128]{1,0:T(8,128)}, f32[208,128]{1,0:T(8,128)S(1)}, u32[]{:S(2)}, u32[]{:S(2)}) collective-permute-start(f32[208,128]{1,0:T(8,128)} %shard_map.120.own_ref), channel_id=1, source_target_pairs={{0,8},{4,12},{8,0},{12,4},{16,24},{20,28},{24,16},{28,20},{1,9},{5... | collective-permute-start | bytes 319496 | tf_op jit(solution)/shard_map/ppermute | solution.py:442
  7.4 3.2 %collective-permute-start = (f32[208,128]{1,0:T(8,128)}, f32[208,128]{1,0:T(8,128)S(1)}, u32[]{:S(2)}, u32[]{:S(2)}) collective-permute-start(f32[208,128]{1,0:T(8,128)} %shard_map.120.own_ref), channel_id=1, source_target_pairs={{0,4},{4,0},{8,12},{12,8},{16,20},{20,16},{24,28},{28,24},{1,5},{5... | collective-permute-start | bytes 319496 | tf_op jit(solution)/shard_map/ppermute | solution.py:442
  10.6 1.3 %collective-permute-start.2 = (f32[208,128]{1,0:T(8,128)S(1)}, f32[208,128]{1,0:T(8,128)S(1)}, u32[]{:S(2)}, u32[]{:S(2)}) collective-permute-start(f32[208,128]{1,0:T(8,128)S(1)} %collective-permute-done.1.two_ref), channel_id=1, source_target_pairs={{0,4},{4,0},{8,12},{12,8},{16,20},{20,16},{24,28},{28,24},{1,5},{5... | collective-permute-start | bytes 319496 | tf_op jit(solution)/shard_map/ppermute | solution.py:442
  11.9 0.7 %copy-start.1 = (s32[2]{0:T(128)S(1)}, s32[2]{0:T(128)}, u32[]{:S(2)}) copy-start(s32[2]{0:T(128)} %pad_add_fusion.where_ref) | copy-start | bytes 28
  11.9 0.7 %copy-start.2 = (f32[4]{0:T(128)S(1)}, f32[4]{0:T(128)}, u32[]{:S(2)}) copy-start(f32[4]{0:T(128)} %shift_ref.1) | copy-start | bytes 52
  11.9 0.7 %copy-start.3 = (f32[4]{0:T(128)S(1)}, f32[4]{0:T(128)}, u32[]{:S(2)}) copy-start(f32[4]{0:T(128)} %couple_ref.1) | copy-start | bytes 52
  12.6 0.9 %copy-start = (f32[208,128]{1,0:T(8,128)S(1)}, f32[208,128]{1,0:T(8,128)}, u32[]{:S(2)}) copy-start(f32[208,128]{1,0:T(8,128)} %shard_map.120.own_ref) | copy-start | bytes 319492
  18.2 6.8 %collective-permute-start.3 = (f32[168,128]{1,0:T(8,128)S(1)}, f32[168,128]{1,0:T(8,128)S(1)}, u32[]{:S(2)}, u32[]{:S(2)}) collective-permute-start(f32[168,128]{1,0:T(8,128)S(1)} %get-tuple-element.17), channel_id=1, source_target_pairs={{0,16},{4,20},{8,24},{12,28},{1,17},{5,21},{9,25},{13,29},{2,18},{... | collective-permute-start | bytes 258056 | tf_op jit(solution)/shard_map/ppermute | solution.py:498
  35.2 5.4 %collective-permute-start.4 = (f32[64,128]{1,0:T(8,128)S(1)}, f32[64,128]{1,0:T(8,128)S(1)}, u32[]{:S(2)}, u32[]{:S(2)}) collective-permute-start(f32[64,128]{1,0:T(8,128)S(1)} %get-tuple-element.25), channel_id=1, source_target_pairs={{0,16},{4,20},{8,24},{12,28},{16,0},{20,4},{24,8},{28,12},{1,17},{... | collective-permute-start | bytes 98312 | tf_op jit(solution)/shard_map/ppermute | solution.py:442

commit v4 on v3

--- a/solution.py
+++ b/solution.py
@@ -87,11 +87,11 @@
     return value * scale
 
 
-def quotients(mats, lefts, rights, factors, refs):
+def quotients(mats, lefts, rights, factors, refs, dims=NT):
     results, total = [], 0.0
     if refs:
         for mat, left, right in zip(mats, lefts, rights):
-            results.append(fine(fine(left, converged(mat, *refs)), right, NT))
+            results.append(fine(fine(left, converged(mat, *refs)), right, dims))
         return results, total
     eye = identity(mats[0].shape[-1])
     starts = [series(mat, factors) for mat in mats]
@@ -100,13 +100,12 @@
         first = fine(left, start)
         low = rest.astype(BF16)
         first = first + fine(first, rest + product(low, low))
-        results.append(fine(first, right, NT))
+        results.append(fine(first, right, dims))
         total = total + rest * rest
     return results, total
 
 
 def pack_kernel(
-    where_ref,
     pattern_hbm,
     diag_hbm,
     couple_hbm,
@@ -141,8 +140,7 @@
     col = lax.broadcasted_iota(jnp.int32, (tile, tile), 1)
     couple = couple_ref[...]
     out_ref[0:tile, :] = jnp.where(row >= col, diag_ref[...], couple)
-    first = (where_ref[0] == 0) & (where_ref[1] == 0)
-    active = jnp.where(first, 0.0, 1.0).astype(F32) * pattern_ref[...].astype(F32)
+    active = jnp.where(lax.axis_index("tm") == 0, 0.0, 1.0).astype(F32) * pattern_ref[...].astype(F32)
     middle = jnp.sum(jnp.where(row == col, couple, 0.0), axis=0, keepdims=True)
     filler = jnp.zeros((2 * SUB - 3, tile), F32)
     out_ref[tile + tip :, :] = jnp.concatenate(
@@ -152,11 +150,10 @@
 
 def local_kernel(
     tip,
-    where_ref,
     shift_ref,
     couple_ref,
-    tip_diag_ref,
-    tip_rhs_ref,
+    tip_diag_hbm,
+    tip_rhs_hbm,
     own_ref,
     one_ref,
     two_ref,
@@ -171,11 +168,19 @@
     raw_ref,
     mat_ref,
     inv_ref,
+    tip_diag_ref,
+    tip_rhs_ref,
+    sems,
 ):
     tile = own_ref.shape[1]
     side = own_ref.shape[0] - tile
-    half = tile // 2
-    setting = where_ref[0]
+    copies = [
+        pltpu.make_async_copy(tip_diag_hbm, tip_diag_ref, sems.at[0]),
+        pltpu.make_async_copy(tip_rhs_hbm, tip_rhs_ref, sems.at[1]),
+    ]
+    for copy in copies:
+        copy.start()
+    setting = lax.axis_index("tm") & (GROUP - 1)
     shift = shift_ref[setting]
     couple = couple_ref[setting]
     for step, ref in enumerate((own_ref, one_ref, two_ref, three_ref)):
@@ -240,6 +245,9 @@
         send(state_ref, diag03, right03)
         return total + more
 
+    settled = jnp.sum(run(None)) < SMALL * 4
+    for copy in copies:
+        copy.wait()
     row = lax.broadcasted_iota(jnp.int32, (tip, 128), 0)
     col = lax.broadcasted_iota(jnp.int32, (tip, 128), 1)
     filler = jnp.zeros((1, 128 - tip), F32)
@@ -247,8 +255,6 @@
     column = jnp.where(row == col, jnp.concatenate([tip_rhs_ref[...], filler], axis=1), 0.0)
     column = jnp.sum(column, axis=1, keepdims=True)
     prior_ref[...] = prior + jnp.where(col == tip, column, 0.0)
-
-    settled = jnp.sum(run(None)) < SMALL * 4
 
     @pl.when(jnp.logical_not(settled))
     def _():
@@ -279,10 +285,10 @@
     return jnp.concatenate([rows, jnp.zeros((size - rows.shape[0], size), F32)], axis=0)
 
 
-def joined(where_ref, state_ref, parts, order, refs):
+def joined(state_ref, parts, order, refs):
     diag_ref, cross_ref, back_ref, right_ref, left_ref = parts
     tile = diag_ref.shape[-1]
-    lone = jnp.where(where_ref[1] == 0, 1.0, 0.0).astype(F32)
+    lone = jnp.where(lax.axis_index("tm") < GROUP, 1.0, 0.0).astype(F32)
     base, came = receive(state_ref)
     base = base + lone * diag_ref[0]
     mats = [base + back_ref[n] for n in order]
@@ -299,13 +305,13 @@
 
 
 def advance_kernel(
-    where_ref, state_ref, diag_ref, cross_ref, back_ref, right_ref, left_ref, out_ref, mat_ref, inv_ref
+    state_ref, diag_ref, cross_ref, back_ref, right_ref, left_ref, out_ref, mat_ref, inv_ref
 ):
     tile = diag_ref.shape[-1]
     parts = (diag_ref, cross_ref, back_ref, right_ref, left_ref)
 
     def run(refs):
-        (last,), total = joined(where_ref, state_ref, parts, (GROUP - 1,), refs)
+        (last,), total = joined(state_ref, parts, (GROUP - 1,), refs)
         send(out_ref, last[:, 0:tile], last[:, tile:].T)
         return total
 
@@ -364,9 +370,28 @@
     return pivots, column
 
 
+def halved(values, refs):
+    tile = values[0].shape[0]
+    half = tile // 2
+    col = lax.broadcasted_iota(jnp.int32, (half, tile), 1)
+    mats, lefts, rights = [], [], []
+    for one, two in zip(values[0::2], values[1::2]):
+        for rows, target in ((slice(0, half), mats), (slice(half, tile), lefts)):
+            first = jnp.where(col < half, one[rows, 0:tile], 0.0)
+            second = jnp.where(col < half, two[rows, 0:tile], 0.0)
+            target.append(jnp.concatenate([first, pltpu.roll(second, half, 1)], axis=0))
+        rights.append(jnp.concatenate([one[0:half, :], two[0:half, :]], axis=0))
+    updates, total = quotients(mats, lefts, rights, 5, refs, NN)
+    uppers = [value[0:half, :] for value in values]
+    lowers = []
+    for place, value in enumerate(values):
+        first = (place % 2) * half
+        lowers.append(value[half:, :] - updates[place // 2][first : first + half, :])
+    return uppers, lowers, total
+
+
 def final_kernel(
     tip,
-    where_ref,
     state_ref,
     diag_ref,
     cross_ref,
@@ -381,58 +406,74 @@
     ends_ref,
 ):
     tile = diag_ref.shape[-1]
+    half = tile // 2
     parts = (diag_ref, cross_ref, back_ref, right_ref, left_ref)
 
     def run(refs):
-        values, total = joined(where_ref, state_ref, parts, range(GROUP), refs)
-        for b, value in enumerate(values):
-            rows_ref[pl.ds(b, tile, stride=SUB), :] = value[:, 0:tile]
-            ends_ref[pl.ds(b, tile, stride=SUB), :] = value[:, tile:]
-        return total
-
-    settled = jnp.sum(run(None)) < SMALL * GROUP
+        values, total = joined(state_ref, parts, range(GROUP), refs)
+        uppers, lowers, more = halved(values, refs)
+        for b, value in enumerate(uppers):
+            rows_ref[pl.ds(b, half, stride=SUB), :] = value[:, 0:tile]
+            ends_ref[pl.ds(b, half, stride=SUB), :] = value[:, tile:]
+        for b, value in enumerate(lowers):
+            rows_ref[pl.ds(GROUP + b, half, stride=SUB), :] = pltpu.roll(value[:, 0:tile], half, 1)
+            ends_ref[pl.ds(GROUP + b, half, stride=SUB), :] = value[:, tile:]
+        return total, more
+
+    total, more = run(None)
+    settled = (jnp.sum(total) < SMALL * GROUP) & (jnp.sum(more) < SMALL * GROUP)
 
     @pl.when(jnp.logical_not(settled))
     def _():
         run((mat_ref, inv_ref))
 
-    pivots, column = factor((rows_ref, ends_ref), tile, GROUP, tip)
-    small_ref[0:GROUP, :] = 0.5 * jnp.log(pivots[0:GROUP, :])
-    small_ref[GROUP:, :] = column[0:GROUP, :]
-    solved = [ends_ref[pl.ds(b, tile, stride=SUB), :] for b in range(GROUP)]
-    everything = jnp.concatenate(solved, axis=0)
+    pivots, column = factor((rows_ref, ends_ref), half, 2 * GROUP, tip)
+    for n, value in enumerate((0.5 * jnp.log(pivots), column)):
+        spot = slice(n * GROUP, (n + 1) * GROUP)
+        small_ref[spot, 0:half] = value[0:GROUP, 0:half]
+        small_ref[spot, half:] = value[GROUP:, 0:half]
+    everything = jnp.concatenate(
+        [ends_ref[pl.ds(b, half, stride=SUB), :] for b in range(2 * GROUP)], axis=0
+    )
     sums_ref[...] = fine(everything[:, 0:tip], everything, TN)
 
 
-def tip_kernel(small_ref, prior_ref, sums_ref, out_ref, rows_ref):
+def tip_kernel(small_ref, prior_ref, *refs):
+    *came, out_ref, sums_ref, rows_ref = refs
     tip = prior_ref.shape[0]
-    total = (sums_ref[0] + sums_ref[1]) + (sums_ref[2] + sums_ref[3])
+    place = lax.axis_index("tm") & GROUP | lax.axis_index("mesh") & 3
+    for step, ref in enumerate(came):
+        sums_ref[place ^ step] = ref[...]
+    total = sums_ref[0]
+    for n in range(1, len(came)):
+        total = total + sums_ref[n]
     rows_ref[pl.ds(0, tip, stride=SUB), :] = prior_ref[...] - total
     pivots, column = factor((rows_ref,), tip, 1, tip)
-    ends = [0.5 * jnp.log(pivots[0:1, :]), column[0:1, :], jnp.zeros((SUB - 4, 128), F32)]
-    for n in range(GROUP):
-        own = [small_ref[n : n + 1, :], small_ref[GROUP + n : GROUP + n + 1, :]]
-        out_ref[n] = jnp.concatenate(own + ends, axis=0)
-
-
-def place_kernel(came_ref, log_ref, solved_ref, tip_log_ref, tip_ref):
+    out_ref[0 : 2 * GROUP, :] = small_ref[...]
+    out_ref[2 * GROUP :, :] = jnp.concatenate(
+        [0.5 * jnp.log(pivots[0:1, :]), column[0:1, :], jnp.zeros((SUB - 2, 128), F32)], axis=0
+    )
+
+
+def place_kernel(own_ref, one_ref, two_ref, three_ref, log_ref, solved_ref, tip_log_ref, tip_ref):
+    node = lax.axis_index("tm") & (GROUP - 1)
     tip = tip_ref.shape[1]
-    for n in range(GROUP):
-        log_ref[n : n + 1, :] = came_ref[n, 0:1, :]
-        solved_ref[n : n + 1, :] = came_ref[n, 1:2, :]
-        tip_log_ref[n : n + 1, :] = came_ref[n, 2:3, 0:tip]
-        tip_ref[n : n + 1, :] = came_ref[n, 3:4, 0:tip]
-
-
-def call(body, inputs, shapes, scratch=(), scalars=0):
-    vmem = pl.BlockSpec(memory_space=pltpu.VMEM)
-    smem = pl.BlockSpec(memory_space=pltpu.SMEM)
+    for step, ref in enumerate((own_ref, one_ref, two_ref, three_ref)):
+        setting = pl.ds(node ^ step, 1)
+        log_ref[setting, :] = ref[pl.ds(node, 1), :]
+        solved_ref[setting, :] = ref[pl.ds(node + GROUP, 1), :]
+        tip_log_ref[setting, :] = ref[2 * GROUP : 2 * GROUP + 1, 0:tip]
+        tip_ref[setting, :] = ref[2 * GROUP + 1 : 2 * GROUP + 2, 0:tip]
+
+
+def call(body, inputs, shapes, scratch=(), spaces=()):
+    spaces = tuple(spaces) + (pltpu.VMEM,) * (len(inputs) - len(spaces))
     return pl.pallas_call(
         body,
         out_shape=tuple(jax.ShapeDtypeStruct(shape, F32) for shape in shapes),
-        in_specs=[smem] * scalars + [vmem] * (len(inputs) - scalars),
-        out_specs=tuple(vmem for _ in shapes),
-        scratch_shapes=[pltpu.VMEM(shape, F32) for shape in scratch],
+        in_specs=[pl.BlockSpec(memory_space=space) for space in spaces],
+        out_specs=tuple(pl.BlockSpec(memory_space=pltpu.VMEM) for _ in shapes),
+        scratch_shapes=[pltpu.VMEM(piece, F32) if isinstance(piece, tuple) else piece for piece in scratch],
         compiler_params=pltpu.CompilerParams(vmem_limit_bytes=40 * 1024 * 1024),
     )(*inputs)
 
@@ -442,10 +483,14 @@
     return lax.ppermute(value, axis, [(source, source ^ step) for source in range(size)])
 
 
-def traded(value, axis):
-    size = lax.axis_size(axis)
-    groups = [[first + n for n in range(4)] for first in range(0, size, 4)]
-    return lax.all_to_all(value, axis, 0, 0, axis_index_groups=groups)
+def across(value, far, near):
+    rows, columns = lax.axis_size("tm"), lax.axis_size("mesh")
+    pairs = [
+        (row * columns + column, (row ^ far) * columns + (column ^ near))
+        for row in range(rows)
+        for column in range(columns)
+    ]
+    return lax.ppermute(value, ("tm", "mesh"), pairs)
 
 
 def shards(
@@ -464,65 +509,58 @@
     groups = lax.axis_size("tm")
     spans = groups // GROUP
     assert config_shift.shape[0] == GROUP and diag_blocks.shape[:2] == (1, tile)
-    position = lax.axis_index("tm")
-    where = jnp.stack([position & (GROUP - 1), position >> 2]).astype(jnp.int32)
     side = tip + 2 * SUB
-    hbm = pl.BlockSpec(memory_space=pltpu.HBM)
-    raw = pl.pallas_call(
+    square = (GROUP, tile, tile)
+    band = (GROUP, side, tile)
+    packed_state = (3 * tile // 4 + tip + SUB, tile)
+    pair = ((tile, tile), (tile, tile))
+    (raw,) = call(
         pack_kernel,
-        out_shape=jax.ShapeDtypeStruct((tile + side, tile), F32),
-        in_specs=[pl.BlockSpec(memory_space=pltpu.SMEM)] + [hbm] * 5,
-        out_specs=pl.BlockSpec(memory_space=pltpu.VMEM),
-        scratch_shapes=[
-            pltpu.VMEM((1, 1), jnp.int32),
-            pltpu.VMEM((tile, tile), F32),
-            pltpu.VMEM((tile, tile), F32),
-            pltpu.VMEM((1, tile), F32),
-            pltpu.SemaphoreType.DMA((5,)),
-        ],
-    )(where, pattern, diag_blocks, coupling, arrow_cols, rhs)
+        (pattern, diag_blocks, coupling, arrow_cols, rhs),
+        ((tile + side, tile),),
+        (pltpu.VMEM((1, 1), jnp.int32), *pair, (1, tile), pltpu.SemaphoreType.DMA((5,))),
+        (pltpu.HBM,) * 5,
+    )
     two = crossed(raw, "tm", 2)
     one = crossed(raw, "tm", 1)
     three = crossed(two, "tm", 1)
-    square = (GROUP, tile, tile)
-    band = (GROUP, side, tile)
-    packed_state = (3 * tile // 4 + tip + SUB, tile)
     *parts, state, prior = call(
         functools.partial(local_kernel, tip),
-        (where, config_shift, config_coupling, tip_diag[None], tip_rhs[None], raw, one, two, three),
+        (config_shift, config_coupling, tip_diag[None], tip_rhs[None], raw, one, two, three),
         (square, square, square, band, band, packed_state, (tip, 128)),
-        ((GROUP,) + raw.shape, (tile, tile), (tile, tile)),
-        3,
+        ((GROUP,) + raw.shape, *pair, (1, tip), (1, tip), pltpu.SemaphoreType.DMA((2,))),
+        (pltpu.SMEM, pltpu.SMEM, pltpu.HBM, pltpu.HBM),
     )
     for span in range(spans - 1):
         state = lax.ppermute(state, "tm", [(source, source + GROUP) for source in range(groups - GROUP)])
         if span < spans - 2:
-            (state,) = call(
-                advance_kernel, (where, state, *parts), (packed_state,), ((tile, tile), (tile, tile)), 1
-            )
+            (state,) = call(advance_kernel, (state, *parts), (packed_state,), pair)
     if spans == 1:
         state = jnp.zeros_like(state)
+    half = SUB * tile // 2
     small, sums = call(
         functools.partial(final_kernel, tip),
-        (where, state, *parts),
+        (state, *parts),
         ((2 * GROUP, tile), (tip, tile)),
-        ((tile, tile), (tile, tile), (SUB * tile, tile), (SUB * tile, tile)),
-        1,
-    )
-    for axis, first in (("tm", GROUP), ("mesh", 4)):
+        (*pair, (half, tile), (half, tile)),
+    )
+    for axis, first in (("tm", 2 * GROUP), ("mesh", 4)):
         step = first
         while step < lax.axis_size(axis):
             sums = sums + crossed(sums, axis, step)
             step *= 2
+    near = [sums] + [crossed(sums, "mesh", n) for n in range(1, 4)]
+    if spans > 1:
+        near += [crossed(sums, "tm", GROUP)] + [across(sums, GROUP, n) for n in range(1, 4)]
     (packed,) = call(
         tip_kernel,
-        (small, prior, traded(jnp.broadcast_to(sums[None], (4, tip, 128)), "mesh")),
-        ((GROUP, SUB, tile),),
-        ((SUB * tip, 128),),
+        (small, prior, *near),
+        ((4 * GROUP, tile),),
+        ((len(near), tip, 128), (SUB * tip, 128)),
     )
     log_diag, solved, tip_log, tip_forward = call(
         place_kernel,
-        (traded(packed, "tm"),),
+        (packed,) + tuple(crossed(packed, "tm", n) for n in range(1, 4)),
         ((GROUP, tile), (GROUP, tile), (GROUP, tip), (GROUP, tip)),
     )
     return (log_diag[:, None, :], solved[:, None, :], tip_log, tip_forward)

time: 60.8 us -> 56.4 us (0.928)
  blocking collectives: 16.7 us -> 0 us
  starting transfers between devices: 11.3 us -> 23 us
  Pallas kernels: 20.6 us -> 16.9 us
  waiting for transfers between devices: 8.47 us -> 11.3 us
  local copies, waits for them, and re-layouts: 1.58 us -> 3.12 us
    all_to_all x2 -> x0, blocking collectives: 16.7 us -> none  [traded(): return lax.all_to_all(value, axis, 0, 0, axis_index_groups=groups)]
    ppermute x0 -> x3, starting transfers between devices: none -> 8.23 us  [across(): return lax.ppermute(value, ('tm', 'mesh'), pairs)]
    ppermute x4 -> x10, starting transfers between devices: 6.63 us -> 10.1 us  [crossed(): lax.ppermute(value, axis, [(source, source ^ step) for source in range(si...]
    ppermute x4 -> x10, waiting for transfers between devices: 6.38 us -> 9.15 us  [crossed(): lax.ppermute(value, axis, [(source, source ^ step) for source in range(si...]
    pallas_call x1 -> x0, Pallas kernels: 2.42 us -> none  [shards(): pl.pallas_call(pack_kernel, out_shape=jax.ShapeDtypeStruct((tile + side,...]
    unnamed x12 -> x16, local copies, waits for them, and re-layouts: 1.57 us -> 3.12 us
    pallas_call x4 -> x5, Pallas kernels: 18.1 us -> 16.9 us  [call(): pl.pallas_call(body, out_shape=tuple((jax.ShapeDtypeStruct(shape, F32) fo...]
  transfers between devices with their start and end apart: 5 -> 14, of which waited for: 4 -> 7; matrix products, arithmetic and copies ran while one was open for 0% -> 0% of each run, Pallas kernels for 0% -> 0%
where the time goes in v4:
time: 56.4 us; the launch traced here: 55.6 us
  starting transfers between devices  23 us (41%)
  Pallas kernels  16.9 us (30%)
  waiting for transfers between devices  11.3 us (20%)
  local copies, waits for them, and re-layouts  3.12 us (6%)
  between operations  1.36 us (2%)
    pallas_call x5, Pallas kernels, call(): pl.pallas_call(body, out_shape=tuple((jax.ShapeDtypeStruct(shape, F32) fo...  16.9 us
    ppermute x10, starting transfers between devices, crossed(): lax.ppermute(value, axis, [(source, source ^ step) for source in range(si...  10.1 us
    ppermute x10, waiting for transfers between devices, crossed(): lax.ppermute(value, axis, [(source, source ^ step) for source in range(si...  9.15 us
    ppermute x3, starting transfers between devices, across(): return lax.ppermute(value, ('tm', 'mesh'), pairs)  8.23 us
    ppermute x1, starting transfers between devices, shards(): lax.ppermute(state, 'tm', [(source, source + GROUP) for source in range(g...  4.66 us
    unnamed x16, local copies, waits for them, and re-layouts  3.12 us
    ppermute x1, waiting for transfers between devices, shards(): lax.ppermute(state, 'tm', [(source, source + GROUP) for source in range(g...  2.11 us
  transfers between devices with their start and end apart: 14, of which 7 were waited for; matrix products, arithmetic and copies ran while one was open for 0% of the time, Pallas kernels for 0%

profile of v4, /device:TPU:0, one launch (start us, length us, event | category | flops | bytes accessed | tf_op | source)
XLA Modules:
  0.0 55.6 jit_solution(2053956418702958507)
XLA Ops:
  0.6 0.0 copy-start.3
  1.3 0.0 copy-done.3
  1.3 0.0 copy-start
  1.3 0.8 %copy-done = f32[1,128,128]{2,1,0:T(8,128)S(1)} copy-done((f32[1,128,128]{2,1,0:T(8,128)S(1)}, f32[1,128,128]{2,1,0:T(8,128)}, u32[]{:S(2)}) %copy-start) | copy-done | bytes 65560
  2.2 0.0 copy-start.1
  2.2 0.8 %copy-done.1 = f32[1,128,128]{2,1,0:T(8,128)S(1)} copy-done((f32[1,128,128]{2,1,0:T(8,128)S(1)}, f32[1,128,128]{2,1,0:T(8,128)}, u32[]{:S(2)}) %copy-start.1) | copy-done | bytes 65560
  3.0 0.0 copy-start.2
  3.0 0.8 %copy-done.2 = f32[1,64,128]{2,1,0:T(8,128)S(1)} copy-done((f32[1,64,128]{2,1,0:T(8,128)S(1)}, f32[1,64,128]{2,1,0:T(8,128)}, u32[]{:S(2)}) %copy-start.2) | copy-done | bytes 32792
  3.8 0.0 copy-start.7
  3.8 0.3 shard_map.120.own_ref
  4.1 3.1 %collective-permute-start.1 = (f32[208,128]{1,0:T(8,128)S(1)}, f32[208,128]{1,0:T(8,128)S(1)}, u32[]{:S(2)}, u32[]{:S(2)}) collective-permute-start(f32[208,128]{1,0:T(8,128)S(1)} %shard_map.120.own_ref), channel_id=1, source_target_pairs={{0,8},{4,12},{8,0},{12,4},{16,24},{20,28},{24,16},{28,20},{1,9},{5... | collective-permute-start | bytes 319496 | tf_op jit(solution)/shard_map/ppermute | solution.py:483
  7.2 0.0 collective-permute-start
  7.2 3.0 %collective-permute-done.1.two_ref = f32[208,128]{1,0:T(8,128)S(1)} collective-permute-done((f32[208,128]{1,0:T(8,128)S(1)}, f32[208,128]{1,0:T(8,128)S(1)}, u32[]{:S(2)}, u32[]{:S(2)}) %collective-permute-start.1) | collective-permute-done | bytes 106528 | tf_op jit(solution)/shard_map/ppermute | solution.py:483
  10.1 0.0 collective-permute-start.2
  10.2 0.0 collective-permute-done.one_ref
  10.2 1.3 %collective-permute-done.2.three_ref = f32[208,128]{1,0:T(8,128)S(1)} collective-permute-done((f32[208,128]{1,0:T(8,128)S(1)}, f32[208,128]{1,0:T(8,128)S(1)}, u32[]{:S(2)}, u32[]{:S(2)}) %collective-permute-start.2) | collective-permute-done | bytes 106528 | tf_op jit(solution)/shard_map/ppermute | solution.py:483
  11.5 0.0 copy-start.4
  11.5 0.0 copy-start.5
  11.5 0.0 copy-done.7
  11.5 0.6 %copy-done.4 = f32[4]{0:T(128)S(1)} copy-done((f32[4]{0:T(128)S(1)}, f32[4]{0:T(128)}, u32[]{:S(2)}) %copy-start.4) | copy-done | bytes 40
  12.1 0.0 copy-done.5
  12.1 0.0 copy-done.6
  12.1 4.8 %shard_map.121 = (f32[4,128,128]{2,1,0:T(8,128)S(1)}, f32[4,128,128]{2,1,0:T(8,128)S(1)}, f32[4,128,128]{2,1,0:T(8,128)S(1)}, f32[4,80,128]{2,1,0:T(8,128)S(1)},...) custom-call(f32[4]{0:T(128)S(1)} %copy-done.4, f32[4]{0:T(128)S(1)} %copy-done.5, ...), custom_call_target="tpu_custom_call" | custom-call | tf_op jit(solution)/shard_map/pallas_call | solution.py:471
  17.0 4.7 %collective-permute-start.3 = (f32[168,128]{1,0:T(8,128)S(1)}, f32[168,128]{1,0:T(8,128)S(1)}, u32[]{:S(2)}, u32[]{:S(2)}) collective-permute-start(f32[168,128]{1,0:T(8,128)S(1)} %get-tuple-element.17), channel_id=1, source_target_pairs={{0,16},{4,20},{8,24},{12,28},{1,17},{5,21},{9,25},{13,29},{2,18},{... | collective-permute-start | bytes 258056 | tf_op jit(solution)/shard_map/ppermute | solution.py:535
  21.7 2.1 %collective-permute-done.3.state_ref = f32[168,128]{1,0:T(8,128)S(1)} collective-permute-done((f32[168,128]{1,0:T(8,128)S(1)}, f32[168,128]{1,0:T(8,128)S(1)}, u32[]{:S(2)}, u32[]{:S(2)}) %collective-permute-start.3) | collective-permute-done | bytes 86048 | tf_op jit(solution)/shard_map/ppermute | solution.py:535
  23.8 8.5 %shard_map.122 = (f32[8,128]{1,0:T(8,128)S(1)}, f32[64,128]{1,0:T(8,128)S(1)}) custom-call(f32[168,128]{1,0:T(8,128)S(1)} %collective-permute-done.3.state_ref, f32[4,128,128]{2,1,0:T(8,128)S(1)} %get-tuple-element.18.diag_ref, f32[4,128,128]{2,1,0:T(8,128)S(1)} %get-tuple-element.19.cross_ref, f32[4,128,128]{2,1,0:T(8,128)S(1)} %get-tuple-element.20.back_ref, ...), custom_call_target="tpu_custom_call" | custom-call | tf_op jit(solution)/shard_map/pallas_call | solution.py:471
  32.3 5.4 %collective-permute-start.10 = (f32[64,128]{1,0:T(8,128)S(1)}, f32[64,128]{1,0:T(8,128)S(1)}, u32[]{:S(2)}, u32[]{:S(2)}) collective-permute-start(f32[64,128]{1,0:T(8,128)S(1)} %get-tuple-element.25.refs_0_), channel_id=1, source_target_pairs={{0,19},{1,18},{2,17},{3,16},{4,23},{5,22},{6,21},{7,20},{8,27},{9,... | collective-permute-start | bytes 98312 | tf_op jit(solution)/shard_map/ppermute | solution.py:493
  37.7 0.0 collective-permute-start.9
  37.7 2.8 %collective-permute-start.8 = (f32[64,128]{1,0:T(8,128)S(1)}, f32[64,128]{1,0:T(8,128)S(1)}, u32[]{:S(2)}, u32[]{:S(2)}) collective-permute-start(f32[64,128]{1,0:T(8,128)S(1)} %get-tuple-element.25.refs_0_), channel_id=1, source_target_pairs={{0,17},{1,16},{2,19},{3,18},{4,21},{5,20},{6,23},{7,22},{8,25},{9,... | collective-permute-start | bytes 98312 | tf_op jit(solution)/shard_map/ppermute | solution.py:493
  40.6 0.2 collective-permute-start.7
  40.7 2.3 %collective-permute-start.6 = (f32[64,128]{1,0:T(8,128)S(1)}, f32[64,128]{1,0:T(8,128)S(1)}, u32[]{:S(2)}, u32[]{:S(2)}) collective-permute-start(f32[64,128]{1,0:T(8,128)S(1)} %get-tuple-element.25.refs_0_), channel_id=1, source_target_pairs={{0,3},{1,2},{2,1},{3,0},{4,7},{5,6},{6,5},{7,4},{8,11},{9,10},{10,... | collective-permute-start | bytes 98312 | tf_op jit(solution)/shard_map/ppermute | solution.py:483
  43.0 0.0 collective-permute-done.10.refs_7_
  43.0 0.6 %collective-permute-start.5 = (f32[64,128]{1,0:T(8,128)S(1)}, f32[64,128]{1,0:T(8,128)S(1)}, u32[]{:S(2)}, u32[]{:S(2)}) collective-permute-start(f32[64,128]{1,0:T(8,128)S(1)} %get-tuple-element.25.refs_0_), channel_id=1, source_target_pairs={{0,2},{1,3},{2,0},{3,1},{4,6},{5,7},{6,4},{7,5},{8,10},{9,11},{10,... | collective-permute-start | bytes 98312 | tf_op jit(solution)/shard_map/ppermute | solution.py:483
  43.6 0.0 collective-permute-done.9.refs_6_
  43.6 0.6 %collective-permute-start.4 = (f32[64,128]{1,0:T(8,128)S(1)}, f32[64,128]{1,0:T(8,128)S(1)}, u32[]{:S(2)}, u32[]{:S(2)}) collective-permute-start(f32[64,128]{1,0:T(8,128)S(1)} %get-tuple-element.25.refs_0_), channel_id=1, source_target_pairs={{0,1},{1,0},{2,3},{3,2},{4,5},{5,4},{6,7},{7,6},{8,9},{9,8},{10,11... | collective-permute-start | bytes 98312 | tf_op jit(solution)/shard_map/ppermute | solution.py:483
  44.2 0.0 collective-permute-done.8.refs_5_
  44.2 1.6 %collective-permute-done.7.refs_4_ = f32[64,128]{1,0:T(8,128)S(1)} collective-permute-done((f32[64,128]{1,0:T(8,128)S(1)}, f32[64,128]{1,0:T(8,128)S(1)}, u32[]{:S(2)}, u32[]{:S(2)}) %collective-permute-start.7) | collective-permute-done | bytes 32800 | tf_op jit(solution)/shard_map/ppermute | solution.py:483
  45.8 0.0 collective-permute-done.6.refs_3_
  45.8 1.1 %collective-permute-done.5.refs_2_ = f32[64,128]{1,0:T(8,128)S(1)} collective-permute-done((f32[64,128]{1,0:T(8,128)S(1)}, f32[64,128]{1,0:T(8,128)S(1)}, u32[]{:S(2)}, u32[]{:S(2)}) %collective-permute-start.5) | collective-permute-done | bytes 32800 | tf_op jit(solution)/shard_map/ppermute | solution.py:483
  46.9 0.6 %collective-permute-done.4.refs_1_ = f32[64,128]{1,0:T(8,128)S(1)} collective-permute-done((f32[64,128]{1,0:T(8,128)S(1)}, f32[64,128]{1,0:T(8,128)S(1)}, u32[]{:S(2)}, u32[]{:S(2)}) %collective-permute-start.4) | collective-permute-done | bytes 32800 | tf_op jit(solution)/shard_map/ppermute | solution.py:483
  47.5 2.6 %shard_map.123.own_ref = f32[16,128]{1,0:T(8,128)S(1)} custom-call(f32[8,128]{1,0:T(8,128)S(1)} %get-tuple-element.23.small_ref, f32[64,128]{1,0:T(8,128)S(1)} %get-tuple-element.24.prior_ref, f32[64,128]{1,0:T(8,128)S(1)} %get-tuple-element.25.refs_0_, f32[64,128]{1,0:T(8,128)S(1)} %collective-permute-done.4.refs_1_, ...), custom_call_target="tpu_custom_call" | custom-call | tf_op jit(solution)/shard_map/pallas_call | solution.py:471
  50.1 0.7 %collective-permute-start.13 = (f32[16,128]{1,0:T(8,128)S(1)}, f32[16,128]{1,0:T(8,128)S(1)}, u32[]{:S(2)}, u32[]{:S(2)}) collective-permute-start(f32[16,128]{1,0:T(8,128)S(1)} %shard_map.123.own_ref), channel_id=1, source_target_pairs={{0,12},{4,8},{8,4},{12,0},{16,28},{20,24},{24,20},{28,16},{1,13},{... | collective-permute-start | bytes 24584 | tf_op jit(solution)/shard_map/ppermute | solution.py:483
  50.7 2.6 %collective-permute-start.12 = (f32[16,128]{1,0:T(8,128)S(1)}, f32[16,128]{1,0:T(8,128)S(1)}, u32[]{:S(2)}, u32[]{:S(2)}) collective-permute-start(f32[16,128]{1,0:T(8,128)S(1)} %shard_map.123.own_ref), channel_id=1, source_target_pairs={{0,8},{4,12},{8,0},{12,4},{16,24},{20,28},{24,16},{28,20},{1,9},{5... | collective-permute-start | bytes 24584 | tf_op jit(solution)/shard_map/ppermute | solution.py:483
  53.4 0.0 collective-permute-start.11
  53.4 0.0 collective-permute-done.13.three_ref
  53.4 1.6 %collective-permute-done.12.two_ref = f32[16,128]{1,0:T(8,128)S(1)} collective-permute-done((f32[16,128]{1,0:T(8,128)S(1)}, f32[16,128]{1,0:T(8,128)S(1)}, u32[]{:S(2)}, u32[]{:S(2)}) %collective-permute-start.12) | collective-permute-done | bytes 8224 | tf_op jit(solution)/shard_map/ppermute | solution.py:483
  55.0 0.0 collective-permute-done.11.one_ref
  55.0 0.6 %shard_map.124 = (f32[4,128]{1,0:T(4,128)}, f32[4,128]{1,0:T(4,128)}, f32[4,64]{1,0:T(4,128)}, f32[4,64]{1,0:T(4,128)}) custom-call(f32[16,128]{1,0:T(8,128)S(1)} %shard_map.123.own_ref, f32[16,128]{1,0:T(8,128)S(1)} %collective-permute-done.11.one_ref, f32[16,128]{1,0:T(8,128)S(1)} %collective-permute-done.12.two_ref, ...), custom_call_target="tpu_custom_call" | custom-call | tf_op jit(solution)/shard_map/pallas_call | solution.py:471
  (1 shorter events, 0.0 us)
Async XLA Ops:
  0.6 0.7 %copy-start.3 = (f32[1,128]{1,0:T(1,128)S(1)}, f32[1,128]{1,0:T(1,128)}, u32[]{:S(2)}) copy-start(f32[1,128]{1,0:T(1,128)} %rhs_hbm.1) | copy-start | bytes 1540
  1.3 0.8 %copy-start = (f32[1,128,128]{2,1,0:T(8,128)S(1)}, f32[1,128,128]{2,1,0:T(8,128)}, u32[]{:S(2)}) copy-start(f32[1,128,128]{2,1,0:T(8,128)} %diag_hbm.1) | copy-start | bytes 196612
  2.2 0.8 %copy-start.1 = (f32[1,128,128]{2,1,0:T(8,128)S(1)}, f32[1,128,128]{2,1,0:T(8,128)}, u32[]{:S(2)}) copy-start(f32[1,128,128]{2,1,0:T(8,128)} %couple_hbm.1) | copy-start | bytes 196612
  3.0 0.8 %copy-start.2 = (f32[1,64,128]{2,1,0:T(8,128)S(1)}, f32[1,64,128]{2,1,0:T(8,128)}, u32[]{:S(2)}) copy-start(f32[1,64,128]{2,1,0:T(8,128)} %arrow_hbm.1) | copy-start | bytes 98308
  3.8 7.7 %copy-start.7 = (f32[64]{0:T(128)S(1)}, f32[64]{0:T(128)}, u32[]{:S(2)}) copy-start(f32[64]{0:T(128)} %param.13) | copy-start | bytes 772
  4.1 6.1 %collective-permute-start.1 = (f32[208,128]{1,0:T(8,128)S(1)}, f32[208,128]{1,0:T(8,128)S(1)}, u32[]{:S(2)}, u32[]{:S(2)}) collective-permute-start(f32[208,128]{1,0:T(8,128)S(1)} %shard_map.120.own_ref), channel_id=1, source_target_pairs={{0,8},{4,12},{8,0},{12,4},{16,24},{20,28},{24,16},{28,20},{1,9},{5... | collective-permute-start | bytes 319496 | tf_op jit(solution)/shard_map/ppermute | solution.py:483
  7.2 3.0 %collective-permute-start = (f32[208,128]{1,0:T(8,128)S(1)}, f32[208,128]{1,0:T(8,128)S(1)}, u32[]{:S(2)}, u32[]{:S(2)}) collective-permute-start(f32[208,128]{1,0:T(8,128)S(1)} %shard_map.120.own_ref), channel_id=1, source_target_pairs={{0,4},{4,0},{8,12},{12,8},{16,20},{20,16},{24,28},{28,24},{1,5},{5... | collective-permute-start | bytes 319496 | tf_op jit(solution)/shard_map/ppermute | solution.py:483
  10.1 1.3 %collective-permute-start.2 = (f32[208,128]{1,0:T(8,128)S(1)}, f32[208,128]{1,0:T(8,128)S(1)}, u32[]{:S(2)}, u32[]{:S(2)}) collective-permute-start(f32[208,128]{1,0:T(8,128)S(1)} %collective-permute-done.1.two_ref), channel_id=1, source_target_pairs={{0,4},{4,0},{8,12},{12,8},{16,20},{20,16},{24,28},{28,24},{1,5},{5... | collective-permute-start | bytes 319496 | tf_op jit(solution)/shard_map/ppermute | solution.py:483
  11.5 0.7 %copy-start.4 = (f32[4]{0:T(128)S(1)}, f32[4]{0:T(128)}, u32[]{:S(2)}) copy-start(f32[4]{0:T(128)} %shift_ref.1) | copy-start | bytes 52
  11.5 0.7 %copy-start.5 = (f32[4]{0:T(128)S(1)}, f32[4]{0:T(128)}, u32[]{:S(2)}) copy-start(f32[4]{0:T(128)} %couple_ref.1) | copy-start | bytes 52
  11.5 0.7 %copy-start.6 = (f32[64]{0:T(128)S(1)}, f32[64]{0:T(128)}, u32[]{:S(2)}) copy-start(f32[64]{0:T(128)} %param.14) | copy-start | bytes 772
  17.0 6.8 %collective-permute-start.3 = (f32[168,128]{1,0:T(8,128)S(1)}, f32[168,128]{1,0:T(8,128)S(1)}, u32[]{:S(2)}, u32[]{:S(2)}) collective-permute-start(f32[168,128]{1,0:T(8,128)S(1)} %get-tuple-element.17), channel_id=1, source_target_pairs={{0,16},{4,20},{8,24},{12,28},{1,17},{5,21},{9,25},{13,29},{2,18},{... | collective-permute-start | bytes 258056 | tf_op jit(solution)/shard_map/ppermute | solution.py:535
  32.3 10.7 %collective-permute-start.10 = (f32[64,128]{1,0:T(8,128)S(1)}, f32[64,128]{1,0:T(8,128)S(1)}, u32[]{:S(2)}, u32[]{:S(2)}) collective-permute-start(f32[64,128]{1,0:T(8,128)S(1)} %get-tuple-element.25.refs_0_), channel_id=1, source_target_pairs={{0,19},{1,18},{2,17},{3,16},{4,23},{5,22},{6,21},{7,20},{8,27},{9,... | collective-permute-start | bytes 98312 | tf_op jit(solution)/shard_map/ppermute | solution.py:493
  37.7 5.9 %collective-permute-start.9 = (f32[64,128]{1,0:T(8,128)S(1)}, f32[64,128]{1,0:T(8,128)S(1)}, u32[]{:S(2)}, u32[]{:S(2)}) collective-permute-start(f32[64,128]{1,0:T(8,128)S(1)} %get-tuple-element.25.refs_0_), channel_id=1, source_target_pairs={{0,18},{1,19},{2,16},{3,17},{4,22},{5,23},{6,20},{7,21},{8,26},{9,... | collective-permute-start | bytes 98312 | tf_op jit(solution)/shard_map/ppermute | solution.py:493
  37.7 6.5 %collective-permute-start.8 = (f32[64,128]{1,0:T(8,128)S(1)}, f32[64,128]{1,0:T(8,128)S(1)}, u32[]{:S(2)}, u32[]{:S(2)}) collective-permute-start(f32[64,128]{1,0:T(8,128)S(1)} %get-tuple-element.25.refs_0_), channel_id=1, source_target_pairs={{0,17},{1,16},{2,19},{3,18},{4,21},{5,20},{6,23},{7,22},{8,25},{9,... | collective-permute-start | bytes 98312 | tf_op jit(solution)/shard_map/ppermute | solution.py:493
  40.6 5.3 %collective-permute-start.7 = (f32[64,128]{1,0:T(8,128)S(1)}, f32[64,128]{1,0:T(8,128)S(1)}, u32[]{:S(2)}, u32[]{:S(2)}) collective-permute-start(f32[64,128]{1,0:T(8,128)S(1)} %get-tuple-element.25.refs_0_), channel_id=1, source_target_pairs={{0,16},{4,20},{8,24},{12,28},{16,0},{20,4},{24,8},{28,12},{1,17},{... | collective-permute-start | bytes 98312 | tf_op jit(solution)/shard_map/ppermute | solution.py:483
  40.7 5.1 %collective-permute-start.6 = (f32[64,128]{1,0:T(8,128)S(1)}, f32[64,128]{1,0:T(8,128)S(1)}, u32[]{:S(2)}, u32[]{:S(2)}) collective-permute-start(f32[64,128]{1,0:T(8,128)S(1)} %get-tuple-element.25.refs_0_), channel_id=1, source_target_pairs={{0,3},{1,2},{2,1},{3,0},{4,7},{5,6},{6,5},{7,4},{8,11},{9,10},{10,... | collective-permute-start | bytes 98312 | tf_op jit(solution)/shard_map/ppermute | solution.py:483
  43.0 3.9 %collective-permute-start.5 = (f32[64,128]{1,0:T(8,128)S(1)}, f32[64,128]{1,0:T(8,128)S(1)}, u32[]{:S(2)}, u32[]{:S(2)}) collective-permute-start(f32[64,128]{1,0:T(8,128)S(1)} %get-tuple-element.25.refs_0_), channel_id=1, source_target_pairs={{0,2},{1,3},{2,0},{3,1},{4,6},{5,7},{6,4},{7,5},{8,10},{9,11},{10,... | collective-permute-start | bytes 98312 | tf_op jit(solution)/shard_map/ppermute | solution.py:483
  43.6 3.9 %collective-permute-start.4 = (f32[64,128]{1,0:T(8,128)S(1)}, f32[64,128]{1,0:T(8,128)S(1)}, u32[]{:S(2)}, u32[]{:S(2)}) collective-permute-start(f32[64,128]{1,0:T(8,128)S(1)} %get-tuple-element.25.refs_0_), channel_id=1, source_target_pairs={{0,1},{1,0},{2,3},{3,2},{4,5},{5,4},{6,7},{7,6},{8,9},{9,8},{10,11... | collective-permute-start | bytes 98312 | tf_op jit(solution)/shard_map/ppermute | solution.py:483
  50.1 3.4 %collective-permute-start.13 = (f32[16,128]{1,0:T(8,128)S(1)}, f32[16,128]{1,0:T(8,128)S(1)}, u32[]{:S(2)}, u32[]{:S(2)}) collective-permute-start(f32[16,128]{1,0:T(8,128)S(1)} %shard_map.123.own_ref), channel_id=1, source_target_pairs={{0,12},{4,8},{8,4},{12,0},{16,28},{20,24},{24,20},{28,16},{1,13},{... | collective-permute-start | bytes 24584 | tf_op jit(solution)/shard_map/ppermute | solution.py:483
  50.7 4.3 %collective-permute-start.12 = (f32[16,128]{1,0:T(8,128)S(1)}, f32[16,128]{1,0:T(8,128)S(1)}, u32[]{:S(2)}, u32[]{:S(2)}) collective-permute-start(f32[16,128]{1,0:T(8,128)S(1)} %shard_map.123.own_ref), channel_id=1, source_target_pairs={{0,8},{4,12},{8,0},{12,4},{16,24},{20,28},{24,16},{28,20},{1,9},{5... | collective-permute-start | bytes 24584 | tf_op jit(solution)/shard_map/ppermute | solution.py:483
  53.4 1.6 %collective-permute-start.11 = (f32[16,128]{1,0:T(8,128)S(1)}, f32[16,128]{1,0:T(8,128)S(1)}, u32[]{:S(2)}, u32[]{:S(2)}) collective-permute-start(f32[16,128]{1,0:T(8,128)S(1)} %shard_map.123.own_ref), channel_id=1, source_target_pairs={{0,4},{4,0},{8,12},{12,8},{16,20},{20,16},{24,28},{28,24},{1,5},{5... | collective-permute-start | bytes 24584 | tf_op jit(solution)/shard_map/ppermute | solution.py:483

commit v5 on v4

--- a/solution.py
+++ b/solution.py
@@ -16,7 +16,7 @@
 STRIP = 32
 GROUP = 4
 SPAN = 2.8
-SMALL = 9e-4
+SMALL = 2.5e-9
 
 
 def identity(size):
@@ -88,72 +88,29 @@
 
 
 def quotients(mats, lefts, rights, factors, refs, dims=NT):
-    results, total = [], 0.0
+    results = []
     if refs:
         for mat, left, right in zip(mats, lefts, rights):
             results.append(fine(fine(left, converged(mat, *refs)), right, dims))
-        return results, total
+        return results, jnp.float32(0.0)
     eye = identity(mats[0].shape[-1])
     starts = [series(mat, factors) for mat in mats]
+    linear, square = 0.0, 0.0
     for mat, start, left, right in zip(mats, starts, lefts, rights):
         rest = eye - fine(mat, start)
         first = fine(left, start)
         low = rest.astype(BF16)
-        first = first + fine(first, rest + product(low, low))
+        twice = product(low, low)
+        first = first + fine(first, rest + twice)
         results.append(fine(first, right, dims))
-        total = total + rest * rest
-    return results, total
-
-
-def pack_kernel(
-    pattern_hbm,
-    diag_hbm,
-    couple_hbm,
-    arrow_hbm,
-    rhs_hbm,
-    out_ref,
-    pattern_ref,
-    diag_ref,
-    couple_ref,
-    rhs_ref,
-    sems,
-):
-    tile = diag_ref.shape[0]
-    tip = arrow_hbm.shape[1]
-    copies = [
-        pltpu.make_async_copy(source, target, sems.at[n])
-        for n, (source, target) in enumerate(
-            (
-                (diag_hbm.at[0], diag_ref),
-                (couple_hbm.at[0], couple_ref),
-                (arrow_hbm.at[0], out_ref.at[tile : tile + tip, :]),
-                (rhs_hbm, rhs_ref),
-                (pattern_hbm, pattern_ref),
-            )
-        )
-    ]
-    for copy in copies:
-        copy.start()
-    for copy in copies:
-        copy.wait()
-    row = lax.broadcasted_iota(jnp.int32, (tile, tile), 0)
-    col = lax.broadcasted_iota(jnp.int32, (tile, tile), 1)
-    couple = couple_ref[...]
-    out_ref[0:tile, :] = jnp.where(row >= col, diag_ref[...], couple)
-    active = jnp.where(lax.axis_index("tm") == 0, 0.0, 1.0).astype(F32) * pattern_ref[...].astype(F32)
-    middle = jnp.sum(jnp.where(row == col, couple, 0.0), axis=0, keepdims=True)
-    filler = jnp.zeros((2 * SUB - 3, tile), F32)
-    out_ref[tile + tip :, :] = jnp.concatenate(
-        [rhs_ref[...], middle, jnp.broadcast_to(active, (1, tile)), filler], axis=0
-    )
+        linear = linear + rest * rest
+        square = square + twice * twice
+    return results, jnp.sum(linear) * jnp.sum(square)
 
 
 def local_kernel(
     tip,
-    shift_ref,
-    couple_ref,
-    tip_diag_hbm,
-    tip_rhs_hbm,
+    extra_ref,
     own_ref,
     one_ref,
     two_ref,
@@ -168,21 +125,15 @@
     raw_ref,
     mat_ref,
     inv_ref,
-    tip_diag_ref,
-    tip_rhs_ref,
-    sems,
 ):
     tile = own_ref.shape[1]
     side = own_ref.shape[0] - tile
-    copies = [
-        pltpu.make_async_copy(tip_diag_hbm, tip_diag_ref, sems.at[0]),
-        pltpu.make_async_copy(tip_rhs_hbm, tip_rhs_ref, sems.at[1]),
-    ]
-    for copy in copies:
-        copy.start()
+    spare = tile + tip + 1
     setting = lax.axis_index("tm") & (GROUP - 1)
-    shift = shift_ref[setting]
-    couple = couple_ref[setting]
+    lane = lax.broadcasted_iota(jnp.int32, (1, tile), 1)
+    settings = extra_ref[1:2, :]
+    shift = jnp.sum(jnp.where(lane == setting, settings, 0.0), axis=1, keepdims=True)
+    couple = jnp.sum(jnp.where(lane == setting + GROUP, settings, 0.0), axis=1, keepdims=True)
     for step, ref in enumerate((own_ref, one_ref, two_ref, three_ref)):
         raw_ref[setting ^ step] = ref[...]
     eye = identity(tile)
@@ -193,8 +144,8 @@
     for n in range(GROUP):
         both = raw_ref[n, 0:tile, :]
         turned = both.T
-        middle = raw_ref[n, tile + tip + 1 : tile + tip + 2, :]
-        active = raw_ref[n, tile + tip + 2 : tile + tip + 3, :]
+        middle = raw_ref[n, spare : spare + 1, :]
+        active = raw_ref[n, spare + 1 : spare + 2, :]
         diag.append(jnp.where(row >= col, both, turned) + shift * eye)
         tie = jnp.where(row < col, both, jnp.where(row > col, turned, middle))
         cross.append(tie * (couple * active))
@@ -243,17 +194,14 @@
         left_ref[2] = left01 - gram2[end, two]
         left_ref[3] = left01 - gram3[end, two]
         send(state_ref, diag03, right03)
-        return total + more
-
-    settled = jnp.sum(run(None)) < SMALL * 4
-    for copy in copies:
-        copy.wait()
+        return (total < SMALL) & (more < SMALL)
+
+    settled = run(None)
+    tips = extra_ref[0:1, :]
     row = lax.broadcasted_iota(jnp.int32, (tip, 128), 0)
     col = lax.broadcasted_iota(jnp.int32, (tip, 128), 1)
-    filler = jnp.zeros((1, 128 - tip), F32)
-    prior = jnp.where(row == col, jnp.concatenate([tip_diag_ref[...], filler], axis=1), 0.0)
-    column = jnp.where(row == col, jnp.concatenate([tip_rhs_ref[...], filler], axis=1), 0.0)
-    column = jnp.sum(column, axis=1, keepdims=True)
+    prior = jnp.where(row == col, tips, 0.0)
+    column = jnp.sum(jnp.where(row + tip == col, tips, 0.0), axis=1, keepdims=True)
     prior_ref[...] = prior + jnp.where(col == tip, column, 0.0)
 
     @pl.when(jnp.logical_not(settled))
@@ -313,9 +261,9 @@
     def run(refs):
         (last,), total = joined(state_ref, parts, (GROUP - 1,), refs)
         send(out_ref, last[:, 0:tile], last[:, tile:].T)
-        return total
-
-    settled = jnp.sum(run(None)) < SMALL
+        return total < SMALL
+
+    settled = run(None)
 
     @pl.when(jnp.logical_not(settled))
     def _():
@@ -381,7 +329,7 @@
             second = jnp.where(col < half, two[rows, 0:tile], 0.0)
             target.append(jnp.concatenate([first, pltpu.roll(second, half, 1)], axis=0))
         rights.append(jnp.concatenate([one[0:half, :], two[0:half, :]], axis=0))
-    updates, total = quotients(mats, lefts, rights, 5, refs, NN)
+    updates, total = quotients(mats, lefts, rights, 4, refs, NN)
     uppers = [value[0:half, :] for value in values]
     lowers = []
     for place, value in enumerate(values):
@@ -418,10 +366,9 @@
         for b, value in enumerate(lowers):
             rows_ref[pl.ds(GROUP + b, half, stride=SUB), :] = pltpu.roll(value[:, 0:tile], half, 1)
             ends_ref[pl.ds(GROUP + b, half, stride=SUB), :] = value[:, tile:]
-        return total, more
-
-    total, more = run(None)
-    settled = (jnp.sum(total) < SMALL * GROUP) & (jnp.sum(more) < SMALL * GROUP)
+        return (total < SMALL) & (more < SMALL)
+
+    settled = run(None)
 
     @pl.when(jnp.logical_not(settled))
     def _():
@@ -441,7 +388,7 @@
 def tip_kernel(small_ref, prior_ref, *refs):
     *came, out_ref, sums_ref, rows_ref = refs
     tip = prior_ref.shape[0]
-    place = lax.axis_index("tm") & GROUP | lax.axis_index("mesh") & 3
+    place = lax.axis_index("mesh") & 3
     for step, ref in enumerate(came):
         sums_ref[place ^ step] = ref[...]
     total = sums_ref[0]
@@ -466,14 +413,14 @@
         tip_ref[setting, :] = ref[2 * GROUP + 1 : 2 * GROUP + 2, 0:tip]
 
 
-def call(body, inputs, shapes, scratch=(), spaces=()):
-    spaces = tuple(spaces) + (pltpu.VMEM,) * (len(inputs) - len(spaces))
+def call(body, inputs, shapes, scratch=()):
+    vmem = pl.BlockSpec(memory_space=pltpu.VMEM)
     return pl.pallas_call(
         body,
         out_shape=tuple(jax.ShapeDtypeStruct(shape, F32) for shape in shapes),
-        in_specs=[pl.BlockSpec(memory_space=space) for space in spaces],
-        out_specs=tuple(pl.BlockSpec(memory_space=pltpu.VMEM) for _ in shapes),
-        scratch_shapes=[pltpu.VMEM(piece, F32) if isinstance(piece, tuple) else piece for piece in scratch],
+        in_specs=[vmem] * len(inputs),
+        out_specs=tuple(vmem for _ in shapes),
+        scratch_shapes=[pltpu.VMEM(shape, F32) for shape in scratch],
         compiler_params=pltpu.CompilerParams(vmem_limit_bytes=40 * 1024 * 1024),
     )(*inputs)
 
@@ -481,16 +428,6 @@
 def crossed(value, axis, step):
     size = lax.axis_size(axis)
     return lax.ppermute(value, axis, [(source, source ^ step) for source in range(size)])
-
-
-def across(value, far, near):
-    rows, columns = lax.axis_size("tm"), lax.axis_size("mesh")
-    pairs = [
-        (row * columns + column, (row ^ far) * columns + (column ^ near))
-        for row in range(rows)
-        for column in range(columns)
-    ]
-    return lax.ppermute(value, ("tm", "mesh"), pairs)
 
 
 def shards(
@@ -514,22 +451,31 @@
     band = (GROUP, side, tile)
     packed_state = (3 * tile // 4 + tip + SUB, tile)
     pair = ((tile, tile), (tile, tile))
-    (raw,) = call(
-        pack_kernel,
-        (pattern, diag_blocks, coupling, arrow_cols, rhs),
-        ((tile + side, tile),),
-        (pltpu.VMEM((1, 1), jnp.int32), *pair, (1, tile), pltpu.SemaphoreType.DMA((5,))),
-        (pltpu.HBM,) * 5,
-    )
+    row = lax.broadcasted_iota(jnp.int32, (tile, tile), 0)
+    col = lax.broadcasted_iota(jnp.int32, (tile, tile), 1)
+    active = jnp.where(lax.axis_index("tm") == 0, 0.0, pattern[0, 0].astype(F32))
+    raw = jnp.concatenate(
+        [
+            jnp.where(row >= col, diag_blocks[0], coupling[0]),
+            arrow_cols[0],
+            rhs,
+            jnp.sum(jnp.where(row == col, coupling[0], 0.0), axis=0, keepdims=True),
+            jnp.full((1, tile), active),
+            jnp.zeros((2 * SUB - 3, tile), F32),
+        ],
+        axis=0,
+    )
+    extra = jnp.concatenate(
+        [tip_diag, tip_rhs, config_shift, config_coupling, jnp.zeros((2 * tile - 2 * tip - 2 * GROUP,), F32)]
+    ).reshape(2, tile)
     two = crossed(raw, "tm", 2)
     one = crossed(raw, "tm", 1)
     three = crossed(two, "tm", 1)
     *parts, state, prior = call(
         functools.partial(local_kernel, tip),
-        (config_shift, config_coupling, tip_diag[None], tip_rhs[None], raw, one, two, three),
+        (extra, raw, one, two, three),
         (square, square, square, band, band, packed_state, (tip, 128)),
-        ((GROUP,) + raw.shape, *pair, (1, tip), (1, tip), pltpu.SemaphoreType.DMA((2,))),
-        (pltpu.SMEM, pltpu.SMEM, pltpu.HBM, pltpu.HBM),
+        ((GROUP,) + raw.shape, *pair),
     )
     for span in range(spans - 1):
         state = lax.ppermute(state, "tm", [(source, source + GROUP) for source in range(groups - GROUP)])
@@ -544,14 +490,12 @@
         ((2 * GROUP, tile), (tip, tile)),
         (*pair, (half, tile), (half, tile)),
     )
-    for axis, first in (("tm", 2 * GROUP), ("mesh", 4)):
+    for axis, first in (("tm", GROUP), ("mesh", 4)):
         step = first
         while step < lax.axis_size(axis):
             sums = sums + crossed(sums, axis, step)
             step *= 2
     near = [sums] + [crossed(sums, "mesh", n) for n in range(1, 4)]
-    if spans > 1:
-        near += [crossed(sums, "tm", GROUP)] + [across(sums, GROUP, n) for n in range(1, 4)]
     (packed,) = call(
         tip_kernel,
         (small, prior, *near),

time: 56.4 us -> 50.9 us (0.902)
  starting transfers between devices: 23 us -> 18.1 us
  local copies, waits for them, and re-layouts: 3.12 us -> 0.88 us
  waiting for transfers between devices: 11.3 us -> 13.1 us
  Pallas kernels: 16.9 us -> 15.8 us
  other arithmetic: 0 us -> 0.92 us
    ppermute x3 -> x0, starting transfers between devices: 8.23 us -> none  [across(): return lax.ppermute(value, ('tm', 'mesh'), pairs)]
    ppermute x10, starting transfers between devices: 10.1 us -> 13.4 us  [crossed(): lax.ppermute(value, axis, [(source, source ^ step) for source in range(si...]
    unnamed x16 -> x12, local copies, waits for them, and re-layouts: 3.12 us -> 0.66 us
    ppermute x10, waiting for transfers between devices: 9.15 us -> 11 us  [crossed(): lax.ppermute(value, axis, [(source, source ^ step) for source in range(si...]
    pallas_call x5 -> x4, Pallas kernels: 16.9 us -> 15.8 us  [call(): pl.pallas_call(body, out_shape=tuple((jax.ShapeDtypeStruct(shape, F32) fo...]
    reduce_sum x0 -> x1, other arithmetic: none -> 0.91 us  [shards(): jnp.sum(jnp.where(row == col, coupling[0], 0.0), axis=0, keepdims=True)]
  transfers between devices with their start and end apart: 14 -> 11, of which waited for: 7 -> 8; matrix products, arithmetic and copies ran while one was open for 0% -> 0% of each run, Pallas kernels for 0% -> 0%
where the time goes in v5:
time: 50.9 us; the launch traced here: 50.3 us
  starting transfers between devices  18.1 us (36%)
  Pallas kernels  15.8 us (31%)
  waiting for transfers between devices  13.1 us (26%)
  between operations  1.41 us (3%)
  other arithmetic  0.92 us (2%)
  local copies, waits for them, and re-layouts  0.88 us (2%)
    pallas_call x4, Pallas kernels, call(): pl.pallas_call(body, out_shape=tuple((jax.ShapeDtypeStruct(shape, F32) fo...  15.8 us
    ppermute x10, starting transfers between devices, crossed(): lax.ppermute(value, axis, [(source, source ^ step) for source in range(si...  13.4 us
    ppermute x10, waiting for transfers between devices, crossed(): lax.ppermute(value, axis, [(source, source ^ step) for source in range(si...  11 us
    ppermute x1, starting transfers between devices, shards(): lax.ppermute(state, 'tm', [(source, source + GROUP) for source in range(g...  4.66 us
    ppermute x1, waiting for transfers between devices, shards(): lax.ppermute(state, 'tm', [(source, source + GROUP) for source in range(g...  2.1 us
  transfers between devices with their start and end apart: 11, of which 8 were waited for; matrix products, arithmetic and copies ran while one was open for 0% of the time, Pallas kernels for 0%

profile of v5, /device:TPU:0, one launch (start us, length us, event | category | flops | bytes accessed | tf_op | source)
XLA Modules:
  0.0 50.3 jit_solution(8254842586286759033)
XLA Ops:
  1.3 0.0 copy-start
  1.3 0.9 %fusion = (f32[128]{0:T(128)S(1)}, f32[128,128]{1,0:T(8,128)S(1)}) fusion(f32[1,128,128]{2,1,0:T(8,128)} %param.10, f32[1,128,128]{2,1,0:T(8,128)} %param.9), kind=kLoop, calls=%fused_computation.2 | loop fusion | flops 81792 | bytes 197120 | tf_op jit(solution)/shard_map/reduce_sum | solution.py:462
  2.2 0.0 copy-start.1
  2.2 0.0 copy-done
  2.2 0.6 %copy-done.1 = f32[1,128]{1,0:T(1,128)S(1)} copy-done((f32[1,128]{1,0:T(1,128)S(1)}, f32[1,128]{1,0:T(1,128)}, u32[]{:S(2)}) %copy-start.1) | copy-done | bytes 536
  2.9 0.0 copy-start.5
  2.9 0.1 concatenate.7.own_ref
  3.0 0.0 copy-start.2
  3.0 0.0 copy-start.3
  3.0 0.0 copy-start.4
  3.1 3.1 %collective-permute-start.1 = (f32[208,128]{1,0:T(8,128)S(1)}, f32[208,128]{1,0:T(8,128)S(1)}, u32[]{:S(2)}, u32[]{:S(2)}) collective-permute-start(f32[208,128]{1,0:T(8,128)S(1)} %concatenate.7.own_ref), channel_id=1, source_target_pairs={{0,8},{4,12},{8,0},{12,4},{16,24},{20,28},{24,16},{28,20},{1,9},{5... | collective-permute-start | bytes 319496 | tf_op jit(solution)/shard_map/ppermute | solution.py:430
  6.1 0.0 collective-permute-start
  6.1 3.0 %collective-permute-done.1.two_ref = f32[208,128]{1,0:T(8,128)S(1)} collective-permute-done((f32[208,128]{1,0:T(8,128)S(1)}, f32[208,128]{1,0:T(8,128)S(1)}, u32[]{:S(2)}, u32[]{:S(2)}) %collective-permute-start.1) | collective-permute-done | bytes 106528 | tf_op jit(solution)/shard_map/ppermute | solution.py:430
  9.1 0.0 collective-permute-start.2
  9.1 0.0 copy-done.5
  9.1 0.0 copy-done.2
  9.1 0.0 copy-done.3
  9.1 0.0 copy-done.4
  9.2 0.1 concatenate.6
  9.2 0.0 collective-permute-done.one_ref
  9.2 1.2 %collective-permute-done.2.three_ref = f32[208,128]{1,0:T(8,128)S(1)} collective-permute-done((f32[208,128]{1,0:T(8,128)S(1)}, f32[208,128]{1,0:T(8,128)S(1)}, u32[]{:S(2)}, u32[]{:S(2)}) %collective-permute-start.2) | collective-permute-done | bytes 106528 | tf_op jit(solution)/shard_map/ppermute | solution.py:430
  10.4 4.2 %shard_map.120 = (f32[4,128,128]{2,1,0:T(8,128)S(1)}, f32[4,128,128]{2,1,0:T(8,128)S(1)}, f32[4,128,128]{2,1,0:T(8,128)S(1)}, f32[4,80,128]{2,1,0:T(8,128)S(1)},...) custom-call(f32[2,128]{1,0:T(2,128)S(1)} %bitcast.17, ...), custom_call_target="tpu_custom_call" | custom-call | tf_op jit(solution)/shard_map/pallas_call | solution.py:418
  14.6 4.7 %collective-permute-start.3 = (f32[168,128]{1,0:T(8,128)S(1)}, f32[168,128]{1,0:T(8,128)S(1)}, u32[]{:S(2)}, u32[]{:S(2)}) collective-permute-start(f32[168,128]{1,0:T(8,128)S(1)} %get-tuple-element.17), channel_id=1, source_target_pairs={{0,16},{4,20},{8,24},{12,28},{1,17},{5,21},{9,25},{13,29},{2,18},{... | collective-permute-start | bytes 258056 | tf_op jit(solution)/shard_map/ppermute | solution.py:481
  19.3 2.1 %collective-permute-done.3.state_ref = f32[168,128]{1,0:T(8,128)S(1)} collective-permute-done((f32[168,128]{1,0:T(8,128)S(1)}, f32[168,128]{1,0:T(8,128)S(1)}, u32[]{:S(2)}, u32[]{:S(2)}) %collective-permute-start.3) | collective-permute-done | bytes 86048 | tf_op jit(solution)/shard_map/ppermute | solution.py:481
  21.4 8.4 %shard_map.121 = (f32[8,128]{1,0:T(8,128)S(1)}, f32[64,128]{1,0:T(8,128)S(1)}) custom-call(f32[168,128]{1,0:T(8,128)S(1)} %collective-permute-done.3.state_ref, f32[4,128,128]{2,1,0:T(8,128)S(1)} %get-tuple-element.18.diag_ref, f32[4,128,128]{2,1,0:T(8,128)S(1)} %get-tuple-element.19.cross_ref, f32[4,128,128]{2,1,0:T(8,128)S(1)} %get-tuple-element.20.back_ref, ...), custom_call_target="tpu_custom_call" | custom-call | tf_op jit(solution)/shard_map/pallas_call | solution.py:418
  29.8 3.5 %collective-permute-start.4 = (f32[64,128]{1,0:T(8,128)S(1)}, f32[64,128]{1,0:T(8,128)S(1)}, u32[]{:S(2)}, u32[]{:S(2)}) collective-permute-start(f32[64,128]{1,0:T(8,128)S(1)} %get-tuple-element.25), channel_id=1, source_target_pairs={{0,16},{4,20},{8,24},{12,28},{16,0},{20,4},{24,8},{28,12},{1,17},{... | collective-permute-start | bytes 98312 | tf_op jit(solution)/shard_map/ppermute | solution.py:430
  33.3 1.9 %collective-permute-done.4 = f32[64,128]{1,0:T(8,128)S(1)} collective-permute-done((f32[64,128]{1,0:T(8,128)S(1)}, f32[64,128]{1,0:T(8,128)S(1)}, u32[]{:S(2)}, u32[]{:S(2)}) %collective-permute-start.4) | collective-permute-done | bytes 32800 | tf_op jit(solution)/shard_map/ppermute | solution.py:430
  35.2 2.5 %collective-permute-start.7 = (f32[64,128]{1,0:T(8,128)S(1)}, f32[64,128]{1,0:T(8,128)S(1)}, u32[]{:S(2)}, u32[]{:S(2)}) collective-permute-start(f32[64,128]{1,0:T(8,128)S(1)} %add.3.refs_0_), channel_id=1, source_target_pairs={{0,3},{1,2},{2,1},{3,0},{4,7},{5,6},{6,5},{7,4},{8,11},{9,10},{10,... | collective-permute-start | bytes 98312 | tf_op jit(solution)/shard_map/ppermute | solution.py:430
  37.7 0.5 %collective-permute-start.6 = (f32[64,128]{1,0:T(8,128)S(1)}, f32[64,128]{1,0:T(8,128)S(1)}, u32[]{:S(2)}, u32[]{:S(2)}) collective-permute-start(f32[64,128]{1,0:T(8,128)S(1)} %add.3.refs_0_), channel_id=1, source_target_pairs={{0,2},{1,3},{2,0},{3,1},{4,6},{5,7},{6,4},{7,5},{8,10},{9,11},{10,... | collective-permute-start | bytes 98312 | tf_op jit(solution)/shard_map/ppermute | solution.py:430
  38.2 0.5 %collective-permute-start.5 = (f32[64,128]{1,0:T(8,128)S(1)}, f32[64,128]{1,0:T(8,128)S(1)}, u32[]{:S(2)}, u32[]{:S(2)}) collective-permute-start(f32[64,128]{1,0:T(8,128)S(1)} %add.3.refs_0_), channel_id=1, source_target_pairs={{0,1},{1,0},{2,3},{3,2},{4,5},{5,4},{6,7},{7,6},{8,9},{9,8},{10,11... | collective-permute-start | bytes 98312 | tf_op jit(solution)/shard_map/ppermute | solution.py:430
  38.7 1.5 %collective-permute-done.7.refs_3_ = f32[64,128]{1,0:T(8,128)S(1)} collective-permute-done((f32[64,128]{1,0:T(8,128)S(1)}, f32[64,128]{1,0:T(8,128)S(1)}, u32[]{:S(2)}, u32[]{:S(2)}) %collective-permute-start.7) | collective-permute-done | bytes 32800 | tf_op jit(solution)/shard_map/ppermute | solution.py:430
  40.2 1.4 %collective-permute-done.6.refs_2_ = f32[64,128]{1,0:T(8,128)S(1)} collective-permute-done((f32[64,128]{1,0:T(8,128)S(1)}, f32[64,128]{1,0:T(8,128)S(1)}, u32[]{:S(2)}, u32[]{:S(2)}) %collective-permute-start.6) | collective-permute-done | bytes 32800 | tf_op jit(solution)/shard_map/ppermute | solution.py:430
  41.6 0.5 %collective-permute-done.5.refs_1_ = f32[64,128]{1,0:T(8,128)S(1)} collective-permute-done((f32[64,128]{1,0:T(8,128)S(1)}, f32[64,128]{1,0:T(8,128)S(1)}, u32[]{:S(2)}, u32[]{:S(2)}) %collective-permute-start.5) | collective-permute-done | bytes 32800 | tf_op jit(solution)/shard_map/ppermute | solution.py:430
  42.1 2.6 %shard_map.122.own_ref = f32[16,128]{1,0:T(8,128)S(1)} custom-call(f32[8,128]{1,0:T(8,128)S(1)} %get-tuple-element.23.small_ref, f32[64,128]{1,0:T(8,128)S(1)} %get-tuple-element.24.prior_ref, f32[64,128]{1,0:T(8,128)S(1)} %add.3.refs_0_, f32[64,128]{1,0:T(8,128)S(1)} %collective-permute-done.5.refs_1_, f32[64,128]{1,0:T(8,128)S(1)} %collective-permute-done.6.refs_2_, ...), custom_call_target="tpu_custom_call" | custom-call | tf_op jit(solution)/shard_map/pallas_call | solution.py:418
  44.7 0.6 %collective-permute-start.10 = (f32[16,128]{1,0:T(8,128)S(1)}, f32[16,128]{1,0:T(8,128)S(1)}, u32[]{:S(2)}, u32[]{:S(2)}) collective-permute-start(f32[16,128]{1,0:T(8,128)S(1)} %shard_map.122.own_ref), channel_id=1, source_target_pairs={{0,12},{4,8},{8,4},{12,0},{16,28},{20,24},{24,20},{28,16},{1,13},{... | collective-permute-start | bytes 24584 | tf_op jit(solution)/shard_map/ppermute | solution.py:430
  45.3 2.7 %collective-permute-start.9 = (f32[16,128]{1,0:T(8,128)S(1)}, f32[16,128]{1,0:T(8,128)S(1)}, u32[]{:S(2)}, u32[]{:S(2)}) collective-permute-start(f32[16,128]{1,0:T(8,128)S(1)} %shard_map.122.own_ref), channel_id=1, source_target_pairs={{0,8},{4,12},{8,0},{12,4},{16,24},{20,28},{24,16},{28,20},{1,9},{5... | collective-permute-start | bytes 24584 | tf_op jit(solution)/shard_map/ppermute | solution.py:430
  48.0 0.0 collective-permute-start.8
  48.1 0.0 collective-permute-done.10.three_ref
  48.1 1.6 %collective-permute-done.9.two_ref = f32[16,128]{1,0:T(8,128)S(1)} collective-permute-done((f32[16,128]{1,0:T(8,128)S(1)}, f32[16,128]{1,0:T(8,128)S(1)}, u32[]{:S(2)}, u32[]{:S(2)}) %collective-permute-start.9) | collective-permute-done | bytes 8224 | tf_op jit(solution)/shard_map/ppermute | solution.py:430
  49.7 0.0 collective-permute-done.8.one_ref
  49.7 0.6 %shard_map.123 = (f32[4,128]{1,0:T(4,128)}, f32[4,128]{1,0:T(4,128)}, f32[4,64]{1,0:T(4,128)}, f32[4,64]{1,0:T(4,128)}) custom-call(f32[16,128]{1,0:T(8,128)S(1)} %shard_map.122.own_ref, f32[16,128]{1,0:T(8,128)S(1)} %collective-permute-done.8.one_ref, f32[16,128]{1,0:T(8,128)S(1)} %collective-permute-done.9.two_ref, ...), custom_call_target="tpu_custom_call" | custom-call | tf_op jit(solution)/shard_map/pallas_call | solution.py:418
  (4 shorter events, 0.0 us)
Async XLA Ops:
  1.3 1.0 %copy-start = (f32[1,64,128]{2,1,0:T(8,128)S(1)}, f32[1,64,128]{2,1,0:T(8,128)}, u32[]{:S(2)}) copy-start(f32[1,64,128]{2,1,0:T(8,128)} %param.11) | copy-start | bytes 98308
  2.2 0.7 %copy-start.1 = (f32[1,128]{1,0:T(1,128)S(1)}, f32[1,128]{1,0:T(1,128)}, u32[]{:S(2)}) copy-start(f32[1,128]{1,0:T(1,128)} %param.12) | copy-start | bytes 1540
  2.9 6.2 %copy-start.5 = (f32[4]{0:T(128)S(1)}, f32[4]{0:T(128)}, u32[]{:S(2)}) copy-start(f32[4]{0:T(128)} %param.16) | copy-start | bytes 52
  3.0 6.1 %copy-start.2 = (f32[64]{0:T(128)S(1)}, f32[64]{0:T(128)}, u32[]{:S(2)}) copy-start(f32[64]{0:T(128)} %param.14) | copy-start | bytes 772
  3.0 6.1 %copy-start.3 = (f32[64]{0:T(128)S(1)}, f32[64]{0:T(128)}, u32[]{:S(2)}) copy-start(f32[64]{0:T(128)} %param.13) | copy-start | bytes 772
  3.0 6.1 %copy-start.4 = (f32[4]{0:T(128)S(1)}, f32[4]{0:T(128)}, u32[]{:S(2)}) copy-start(f32[4]{0:T(128)} %param.15) | copy-start | bytes 52
  3.1 6.1 %collective-permute-start.1 = (f32[208,128]{1,0:T(8,128)S(1)}, f32[208,128]{1,0:T(8,128)S(1)}, u32[]{:S(2)}, u32[]{:S(2)}) collective-permute-start(f32[208,128]{1,0:T(8,128)S(1)} %concatenate.7.own_ref), channel_id=1, source_target_pairs={{0,8},{4,12},{8,0},{12,4},{16,24},{20,28},{24,16},{28,20},{1,9},{5... | collective-permute-start | bytes 319496 | tf_op jit(solution)/shard_map/ppermute | solution.py:430
  6.1 3.1 %collective-permute-start = (f32[208,128]{1,0:T(8,128)S(1)}, f32[208,128]{1,0:T(8,128)S(1)}, u32[]{:S(2)}, u32[]{:S(2)}) collective-permute-start(f32[208,128]{1,0:T(8,128)S(1)} %concatenate.7.own_ref), channel_id=1, source_target_pairs={{0,4},{4,0},{8,12},{12,8},{16,20},{20,16},{24,28},{28,24},{1,5},{5... | collective-permute-start | bytes 319496 | tf_op jit(solution)/shard_map/ppermute | solution.py:430
  9.1 1.3 %collective-permute-start.2 = (f32[208,128]{1,0:T(8,128)S(1)}, f32[208,128]{1,0:T(8,128)S(1)}, u32[]{:S(2)}, u32[]{:S(2)}) collective-permute-start(f32[208,128]{1,0:T(8,128)S(1)} %collective-permute-done.1.two_ref), channel_id=1, source_target_pairs={{0,4},{4,0},{8,12},{12,8},{16,20},{20,16},{24,28},{28,24},{1,5},{5... | collective-permute-start | bytes 319496 | tf_op jit(solution)/shard_map/ppermute | solution.py:430
  14.6 6.8 %collective-permute-start.3 = (f32[168,128]{1,0:T(8,128)S(1)}, f32[168,128]{1,0:T(8,128)S(1)}, u32[]{:S(2)}, u32[]{:S(2)}) collective-permute-start(f32[168,128]{1,0:T(8,128)S(1)} %get-tuple-element.17), channel_id=1, source_target_pairs={{0,16},{4,20},{8,24},{12,28},{1,17},{5,21},{9,25},{13,29},{2,18},{... | collective-permute-start | bytes 258056 | tf_op jit(solution)/shard_map/ppermute | solution.py:481
  29.8 5.4 %collective-permute-start.4 = (f32[64,128]{1,0:T(8,128)S(1)}, f32[64,128]{1,0:T(8,128)S(1)}, u32[]{:S(2)}, u32[]{:S(2)}) collective-permute-start(f32[64,128]{1,0:T(8,128)S(1)} %get-tuple-element.25), channel_id=1, source_target_pairs={{0,16},{4,20},{8,24},{12,28},{16,0},{20,4},{24,8},{28,12},{1,17},{... | collective-permute-start | bytes 98312 | tf_op jit(solution)/shard_map/ppermute | solution.py:430
  35.2 5.0 %collective-permute-start.7 = (f32[64,128]{1,0:T(8,128)S(1)}, f32[64,128]{1,0:T(8,128)S(1)}, u32[]{:S(2)}, u32[]{:S(2)}) collective-permute-start(f32[64,128]{1,0:T(8,128)S(1)} %add.3.refs_0_), channel_id=1, source_target_pairs={{0,3},{1,2},{2,1},{3,0},{4,7},{5,6},{6,5},{7,4},{8,11},{9,10},{10,... | collective-permute-start | bytes 98312 | tf_op jit(solution)/shard_map/ppermute | solution.py:430
  37.7 3.9 %collective-permute-start.6 = (f32[64,128]{1,0:T(8,128)S(1)}, f32[64,128]{1,0:T(8,128)S(1)}, u32[]{:S(2)}, u32[]{:S(2)}) collective-permute-start(f32[64,128]{1,0:T(8,128)S(1)} %add.3.refs_0_), channel_id=1, source_target_pairs={{0,2},{1,3},{2,0},{3,1},{4,6},{5,7},{6,4},{7,5},{8,10},{9,11},{10,... | collective-permute-start | bytes 98312 | tf_op jit(solution)/shard_map/ppermute | solution.py:430
  38.2 3.9 %collective-permute-start.5 = (f32[64,128]{1,0:T(8,128)S(1)}, f32[64,128]{1,0:T(8,128)S(1)}, u32[]{:S(2)}, u32[]{:S(2)}) collective-permute-start(f32[64,128]{1,0:T(8,128)S(1)} %add.3.refs_0_), channel_id=1, source_target_pairs={{0,1},{1,0},{2,3},{3,2},{4,5},{5,4},{6,7},{7,6},{8,9},{9,8},{10,11... | collective-permute-start | bytes 98312 | tf_op jit(solution)/shard_map/ppermute | solution.py:430
  44.7 3.4 %collective-permute-start.10 = (f32[16,128]{1,0:T(8,128)S(1)}, f32[16,128]{1,0:T(8,128)S(1)}, u32[]{:S(2)}, u32[]{:S(2)}) collective-permute-start(f32[16,128]{1,0:T(8,128)S(1)} %shard_map.122.own_ref), channel_id=1, source_target_pairs={{0,12},{4,8},{8,4},{12,0},{16,28},{20,24},{24,20},{28,16},{1,13},{... | collective-permute-start | bytes 24584 | tf_op jit(solution)/shard_map/ppermute | solution.py:430
  45.3 4.4 %collective-permute-start.9 = (f32[16,128]{1,0:T(8,128)S(1)}, f32[16,128]{1,0:T(8,128)S(1)}, u32[]{:S(2)}, u32[]{:S(2)}) collective-permute-start(f32[16,128]{1,0:T(8,128)S(1)} %shard_map.122.own_ref), channel_id=1, source_target_pairs={{0,8},{4,12},{8,0},{12,4},{16,24},{20,28},{24,16},{28,20},{1,9},{5... | collective-permute-start | bytes 24584 | tf_op jit(solution)/shard_map/ppermute | solution.py:430
  48.0 1.6 %collective-permute-start.8 = (f32[16,128]{1,0:T(8,128)S(1)}, f32[16,128]{1,0:T(8,128)S(1)}, u32[]{:S(2)}, u32[]{:S(2)}) collective-permute-start(f32[16,128]{1,0:T(8,128)S(1)} %shard_map.122.own_ref), channel_id=1, source_target_pairs={{0,4},{4,0},{8,12},{12,8},{16,20},{20,16},{24,28},{28,24},{1,5},{5... | collective-permute-start | bytes 24584 | tf_op jit(solution)/shard_map/ppermute | solution.py:430

commit v6 on v5

--- a/solution.py
+++ b/solution.py
@@ -121,7 +121,6 @@
     right_ref,
     left_ref,
     state_ref,
-    prior_ref,
     raw_ref,
     mat_ref,
     inv_ref,
@@ -168,33 +167,51 @@
         right23 = right[3] - gram23[end, one]
         left23 = -gram23[end, two]
 
-        low = jnp.concatenate([cross[2], cross01_t, right01], axis=0)
-        high = jnp.concatenate([cross23, cross01_t, right01 + left23], axis=0)
-        (gram2, gram3), more = quotients((diag01, diag01 + back23), (low, high), (low, high), 4, refs)
-        diag_ref[0] = diag[0]
-        diag_ref[1] = diag01
-        diag_ref[2] = diag[2] - gram2[one, one]
-        diag03 = diag23 - gram3[one, one]
-        diag_ref[3] = diag03
-        cross_ref[0] = cross[0]
-        cross_ref[1] = cross01
-        cross_ref[2] = -gram2[one, two]
-        cross_ref[3] = -gram3[one, two]
-        back_ref[0] = jnp.zeros_like(eye)
-        back_ref[1] = back01
-        back_ref[2] = back01 - gram2[two, two]
-        back_ref[3] = back01 - gram3[two, two]
-        right_ref[0] = right[0]
-        right_ref[1] = right01
-        right_ref[2] = right[2] - gram2[end, one]
-        right03 = right23 - gram3[end, one]
-        right_ref[3] = right03
-        left_ref[0] = jnp.zeros_like(right[0])
-        left_ref[1] = left01
-        left_ref[2] = left01 - gram2[end, two]
-        left_ref[3] = left01 - gram3[end, two]
+        rows = jnp.concatenate([cross23, cross01_t, right01 + left23], axis=0)
+        (gram,), more = quotients((diag01 + back23,), (rows,), (rows,), 4, refs)
+        diag03 = diag23 - gram[one, one]
+        right03 = right23 - gram[end, one]
         send(state_ref, diag03, right03)
+        for n, value in enumerate((diag[0], diag01, diag[2], diag03)):
+            diag_ref[n] = value
+        for n, value in enumerate((cross[0], cross01, cross[2], -gram[one, two])):
+            cross_ref[n] = value
+        nothing = jnp.zeros_like(eye)
+        for n, value in enumerate((nothing, back01, nothing, back01 - gram[two, two])):
+            back_ref[n] = value
+        for n, value in enumerate((right[0], right01, right[2], right03)):
+            right_ref[n] = value
+        nothing = jnp.zeros_like(right01)
+        for n, value in enumerate((nothing, left01, nothing, left01 - gram[end, two])):
+            left_ref[n] = value
         return (total < SMALL) & (more < SMALL)
+
+    settled = run(None)
+
+    @pl.when(jnp.logical_not(settled))
+    def _():
+        run((mat_ref, inv_ref))
+
+
+def middle_kernel(tip, *refs):
+    extra_ref, diag_ref, cross_ref, back_ref, right_ref, left_ref, *refs = refs
+    *out_refs, prior_ref, mat_ref, inv_ref = refs
+    tile = diag_ref.shape[-1]
+    one, two, end = slice(0, tile), slice(tile, 2 * tile), slice(2 * tile, None)
+    rows = jnp.concatenate([cross_ref[2], cross_ref[1].T, right_ref[1]], axis=0)
+
+    def run(refs):
+        (gram,), total = quotients((diag_ref[1],), (rows,), (rows,), 4, refs)
+        values = (
+            diag_ref[2] - gram[one, one],
+            -gram[one, two],
+            back_ref[1] - gram[two, two],
+            right_ref[2] - gram[end, one],
+            left_ref[1] - gram[end, two],
+        )
+        for ref, value in zip(out_refs, values):
+            ref[...] = value
+        return total < SMALL
 
     settled = run(None)
     tips = extra_ref[0:1, :]
@@ -210,23 +227,38 @@
 
 
 def send(state_ref, diag, right):
-    half = diag.shape[0] // 2
-    mid = half + half // 2
-    count = state_ref.shape[0] - mid
-    state_ref[0:half, :] = diag[0:half, :]
-    state_ref[half:mid, :] = jnp.concatenate([diag[half:mid, half:], diag[mid:, half:]], axis=1)
-    state_ref[mid:, :] = right[0:count, :]
+    tile = diag.shape[0]
+    part = tile // 4
+    col = lax.broadcasted_iota(jnp.int32, (part, tile), 1)
+    fold = 2 * part + part // 2
+    state_ref[0:part, :] = diag[0:part, :]
+    corner = pltpu.roll(diag[3 * part :, :], part, 1)
+    state_ref[part : 2 * part, :] = jnp.where(col >= part, diag[part : 2 * part, :], corner)
+    first, second = diag[2 * part : fold, :], diag[fold : 3 * part, :]
+    col = col[0 : part // 2, :]
+    state_ref[2 * part : fold, :] = jnp.where(col >= 2 * part, first, pltpu.roll(second, 2 * part, 1))
+    state_ref[fold:, :] = right[0 : state_ref.shape[0] - fold, :]
 
 
 def receive(state_ref):
     tile = state_ref.shape[1]
-    half = tile // 2
-    mid = half + half // 2
-    top = state_ref[0:half, :]
-    corner = state_ref[half:mid, :]
-    corner = jnp.concatenate([corner[:, 0:half], corner[:, half:]], axis=0)
-    bottom = jnp.concatenate([top[:, half:].T, corner], axis=1)
-    return jnp.concatenate([top, bottom], axis=0), state_ref[mid:, :]
+    part = tile // 4
+    fold = 2 * part + part // 2
+    second = state_ref[part : 2 * part, :]
+    third = state_ref[2 * part : fold, :]
+    upper = jnp.concatenate(
+        [
+            state_ref[0:part, :],
+            second,
+            third,
+            pltpu.roll(third, 2 * part, 1),
+            pltpu.roll(second, 3 * part, 1),
+        ],
+        axis=0,
+    )
+    row = lax.broadcasted_iota(jnp.int32, (tile, tile), 0)
+    col = lax.broadcasted_iota(jnp.int32, (tile, tile), 1)
+    return jnp.where(row <= col, upper, upper.T), state_ref[fold:, :]
 
 
 def padded(rows, size):
@@ -234,29 +266,28 @@
 
 
 def joined(state_ref, parts, order, refs):
-    diag_ref, cross_ref, back_ref, right_ref, left_ref = parts
-    tile = diag_ref.shape[-1]
+    values = [[third[...] if n == 2 else every[n] for n in order] for every, third in zip(parts[:5], parts[5:])]
+    diags, crosses, backs, sides, lefts = values
+    tile = crosses[0].shape[-1]
     lone = jnp.where(lax.axis_index("tm") < GROUP, 1.0, 0.0).astype(F32)
     base, came = receive(state_ref)
-    base = base + lone * diag_ref[0]
-    mats = [base + back_ref[n] for n in order]
-    crosses = [cross_ref[n] for n in order]
+    base = base + lone * parts[0][0]
+    mats = [base + back for back in backs]
     came = padded(came, tile)
-    middles = [came + padded(left_ref[n], tile) for n in order]
-    rights = [jnp.concatenate([cross, middle], axis=0) for cross, middle in zip(crosses, middles)]
+    rights = [
+        jnp.concatenate([cross, came + padded(left, tile)], axis=0) for cross, left in zip(crosses, lefts)
+    ]
     updates, total = quotients(mats, crosses, rights, 5, refs)
     results = []
-    for n, update in zip(order, updates):
-        start = jnp.concatenate([diag_ref[n], padded(right_ref[n], tile).T], axis=1)
+    for diag, side, update in zip(diags, sides, updates):
+        start = jnp.concatenate([diag, padded(side, tile).T], axis=1)
         results.append(start - update)
     return results, total
 
 
-def advance_kernel(
-    state_ref, diag_ref, cross_ref, back_ref, right_ref, left_ref, out_ref, mat_ref, inv_ref
-):
-    tile = diag_ref.shape[-1]
-    parts = (diag_ref, cross_ref, back_ref, right_ref, left_ref)
+def advance_kernel(state_ref, *refs):
+    *parts, out_ref, mat_ref, inv_ref = refs
+    tile = state_ref.shape[1]
 
     def run(refs):
         (last,), total = joined(state_ref, parts, (GROUP - 1,), refs)
@@ -338,24 +369,10 @@
     return uppers, lowers, total
 
 
-def final_kernel(
-    tip,
-    state_ref,
-    diag_ref,
-    cross_ref,
-    back_ref,
-    right_ref,
-    left_ref,
-    small_ref,
-    sums_ref,
-    mat_ref,
-    inv_ref,
-    rows_ref,
-    ends_ref,
-):
-    tile = diag_ref.shape[-1]
+def final_kernel(tip, state_ref, *refs):
+    *parts, small_ref, sums_ref, mat_ref, inv_ref, rows_ref, ends_ref = refs
+    tile = state_ref.shape[1]
     half = tile // 2
-    parts = (diag_ref, cross_ref, back_ref, right_ref, left_ref)
 
     def run(refs):
         values, total = joined(state_ref, parts, range(GROUP), refs)
@@ -382,7 +399,13 @@
     everything = jnp.concatenate(
         [ends_ref[pl.ds(b, half, stride=SUB), :] for b in range(2 * GROUP)], axis=0
     )
-    sums_ref[...] = fine(everything[:, 0:tip], everything, TN)
+    gram = fine(everything[:, 0:tip], everything, TN)
+    mid = tip // 2
+    top, bottom = gram[0:mid, :], gram[mid:, :]
+    col = lax.broadcasted_iota(jnp.int32, (mid, tile), 1)
+    ends = jnp.where(col == tip + mid, pltpu.roll(top, mid, 1), pltpu.roll(bottom, mid + 1, 1))
+    folded = jnp.where(col < tip + mid, pltpu.roll(bottom, mid, 1), ends)
+    sums_ref[...] = jnp.where(col < tip, top, folded)
 
 
 def tip_kernel(small_ref, prior_ref, *refs):
@@ -394,7 +417,12 @@
     total = sums_ref[0]
     for n in range(1, len(came)):
         total = total + sums_ref[n]
-    rows_ref[pl.ds(0, tip, stride=SUB), :] = prior_ref[...] - total
+    mid = tip // 2
+    col = lax.broadcasted_iota(jnp.int32, (mid, 128), 1)
+    top = jnp.where(col < tip, total, pltpu.roll(total, 128 - mid, 1))
+    bottom = jnp.where(col < tip, pltpu.roll(total, 128 - mid, 1), pltpu.roll(total, 127 - mid, 1))
+    rows_ref[pl.ds(0, mid, stride=SUB), :] = prior_ref[0:mid, :] - top
+    rows_ref[pl.ds(SUB * mid, mid, stride=SUB), :] = prior_ref[mid:, :] - bottom
     pivots, column = factor((rows_ref,), tip, 1, tip)
     out_ref[0 : 2 * GROUP, :] = small_ref[...]
     out_ref[2 * GROUP :, :] = jnp.concatenate(
@@ -449,7 +477,7 @@
     side = tip + 2 * SUB
     square = (GROUP, tile, tile)
     band = (GROUP, side, tile)
-    packed_state = (3 * tile // 4 + tip + SUB, tile)
+    packed_state = (5 * tile // 8 + tip + SUB, tile)
     pair = ((tile, tile), (tile, tile))
     row = lax.broadcasted_iota(jnp.int32, (tile, tile), 0)
     col = lax.broadcasted_iota(jnp.int32, (tile, tile), 1)
@@ -471,12 +499,19 @@
     two = crossed(raw, "tm", 2)
     one = crossed(raw, "tm", 1)
     three = crossed(two, "tm", 1)
-    *parts, state, prior = call(
+    *parts, state = call(
         functools.partial(local_kernel, tip),
         (extra, raw, one, two, three),
-        (square, square, square, band, band, packed_state, (tip, 128)),
+        (square, square, square, band, band, packed_state),
         ((GROUP,) + raw.shape, *pair),
     )
+    *thirds, prior = call(
+        functools.partial(middle_kernel, tip),
+        (extra, *parts),
+        ((tile, tile), (tile, tile), (tile, tile), (side, tile), (side, tile), (tip, 128)),
+        pair,
+    )
+    parts = (*parts, *thirds)
     for span in range(spans - 1):
         state = lax.ppermute(state, "tm", [(source, source + GROUP) for source in range(groups - GROUP)])
         if span < spans - 2:
@@ -487,7 +522,7 @@
     small, sums = call(
         functools.partial(final_kernel, tip),
         (state, *parts),
-        ((2 * GROUP, tile), (tip, tile)),
+        ((2 * GROUP, tile), (tip // 2, tile)),
         (*pair, (half, tile), (half, tile)),
     )
     for axis, first in (("tm", GROUP), ("mesh", 4)):
@@ -500,7 +535,7 @@
         tip_kernel,
         (small, prior, *near),
         ((4 * GROUP, tile),),
-        ((len(near), tip, 128), (SUB * tip, 128)),
+        ((len(near), tip // 2, 128), (SUB * tip, 128)),
     )
     log_diag, solved, tip_log, tip_forward = call(
         place_kernel,

time: 50.9 us -> 49.8 us (0.978)
  waiting for transfers between devices: 13.1 us -> 11.2 us
  Pallas kernels: 15.8 us -> 16.8 us
    ppermute x1, waiting for transfers between devices: 2.1 us -> 0.54 us  [shards(): lax.ppermute(state, 'tm', [(source, source + GROUP) for source in range(g...]
    pallas_call x4 -> x5, Pallas kernels: 15.8 us -> 16.8 us  [call(): pl.pallas_call(body, out_shape=tuple((jax.ShapeDtypeStruct(shape, F32) fo...]
  transfers between devices with their start and end apart: 11 -> 11, of which waited for: 8 -> 8; matrix products, arithmetic and copies ran while one was open for 0% -> 0% of each run, Pallas kernels for 0% -> 3%
where the time goes in v6:
time: 49.8 us; the launch traced here: 49.1 us
  starting transfers between devices  17.9 us (36%)
  Pallas kernels  16.8 us (34%)
  waiting for transfers between devices  11.2 us (22%)
  between operations  1.42 us (3%)
  other arithmetic  0.91 us (2%)
  local copies, waits for them, and re-layouts  0.88 us (2%)
    pallas_call x5, Pallas kernels, call(): pl.pallas_call(body, out_shape=tuple((jax.ShapeDtypeStruct(shape, F32) fo...  16.8 us
    ppermute x10, starting transfers between devices, crossed(): lax.ppermute(value, axis, [(source, source ^ step) for source in range(si...  13.2 us
    ppermute x10, waiting for transfers between devices, crossed(): lax.ppermute(value, axis, [(source, source ^ step) for source in range(si...  10.7 us
    ppermute x1, starting transfers between devices, shards(): lax.ppermute(state, 'tm', [(source, source + GROUP) for source in range(g...  4.66 us
  transfers between devices with their start and end apart: 11, of which 8 were waited for; matrix products, arithmetic and copies ran while one was open for 0% of the time, Pallas kernels for 3%

profile of v6, /device:TPU:0, one launch (start us, length us, event | category | flops | bytes accessed | tf_op | source)
XLA Modules:
  0.0 49.1 jit_solution(16241051991502863276)
XLA Ops:
  1.3 0.0 copy-start
  1.3 0.9 %fusion = (f32[128]{0:T(128)S(1)}, f32[128,128]{1,0:T(8,128)S(1)}) fusion(f32[1,128,128]{2,1,0:T(8,128)} %param.10, f32[1,128,128]{2,1,0:T(8,128)} %param.9), kind=kLoop, calls=%fused_computation.2 | loop fusion | flops 81792 | bytes 197120 | tf_op jit(solution)/shard_map/reduce_sum | solution.py:490
  2.2 0.0 copy-start.1
  2.2 0.0 copy-done
  2.2 0.6 %copy-done.1 = f32[1,128]{1,0:T(1,128)S(1)} copy-done((f32[1,128]{1,0:T(1,128)S(1)}, f32[1,128]{1,0:T(1,128)}, u32[]{:S(2)}) %copy-start.1) | copy-done | bytes 536
  2.9 0.0 copy-start.5
  2.9 0.1 concatenate.7.own_ref
  3.0 0.0 copy-start.2
  3.0 0.0 copy-start.3
  3.0 0.0 copy-start.4
  3.1 3.1 %collective-permute-start.1 = (f32[208,128]{1,0:T(8,128)S(1)}, f32[208,128]{1,0:T(8,128)S(1)}, u32[]{:S(2)}, u32[]{:S(2)}) collective-permute-start(f32[208,128]{1,0:T(8,128)S(1)} %concatenate.7.own_ref), channel_id=1, source_target_pairs={{0,8},{4,12},{8,0},{12,4},{16,24},{20,28},{24,16},{28,20},{1,9},{5... | collective-permute-start | bytes 319496 | tf_op jit(solution)/shard_map/ppermute | solution.py:458
  6.1 0.0 collective-permute-start
  6.1 3.0 %collective-permute-done.1.two_ref = f32[208,128]{1,0:T(8,128)S(1)} collective-permute-done((f32[208,128]{1,0:T(8,128)S(1)}, f32[208,128]{1,0:T(8,128)S(1)}, u32[]{:S(2)}, u32[]{:S(2)}) %collective-permute-start.1) | collective-permute-done | bytes 106528 | tf_op jit(solution)/shard_map/ppermute | solution.py:458
  9.1 0.0 collective-permute-start.2
  9.1 0.0 copy-done.5
  9.1 0.0 copy-done.2
  9.1 0.0 copy-done.3
  9.1 0.0 copy-done.4
  9.2 0.1 concatenate.6
  9.2 0.0 collective-permute-done.one_ref
  9.2 1.2 %collective-permute-done.2.three_ref = f32[208,128]{1,0:T(8,128)S(1)} collective-permute-done((f32[208,128]{1,0:T(8,128)S(1)}, f32[208,128]{1,0:T(8,128)S(1)}, u32[]{:S(2)}, u32[]{:S(2)}) %collective-permute-start.2) | collective-permute-done | bytes 106528 | tf_op jit(solution)/shard_map/ppermute | solution.py:458
  10.4 3.7 %shard_map.120 = (f32[4,128,128]{2,1,0:T(8,128)S(1)}, f32[4,128,128]{2,1,0:T(8,128)S(1)}, f32[4,128,128]{2,1,0:T(8,128)S(1)}, f32[4,80,128]{2,1,0:T(8,128)S(1)},...) custom-call(f32[2,128]{1,0:T(2,128)S(1)} %bitcast.17, f32[208,128]{1,0:T(8,128)S(1)} %concatenate.7.own_ref, ...), custom_call_target="tpu_custom_call" | custom-call | tf_op jit(solution)/shard_map/pallas_call | solution.py:446
  14.2 4.7 %collective-permute-start.3 = (f32[152,128]{1,0:T(8,128)S(1)}, f32[152,128]{1,0:T(8,128)S(1)}, u32[]{:S(2)}, u32[]{:S(2)}) collective-permute-start(f32[152,128]{1,0:T(8,128)S(1)} %get-tuple-element.22), channel_id=1, source_target_pairs={{0,16},{4,20},{8,24},{12,28},{1,17},{5,21},{9,25},{13,29},{2,18},{... | collective-permute-start | bytes 233480 | tf_op jit(solution)/shard_map/ppermute | solution.py:516
  18.8 1.5 %shard_map.121 = (f32[128,128]{1,0:T(8,128)S(1)}, f32[128,128]{1,0:T(8,128)S(1)}, f32[128,128]{1,0:T(8,128)S(1)}, f32[80,128]{1,0:T(8,128)S(1)}, f32[80,128]{1,0:T(8,128)S(1)}, /*index=5*/f32[64,128]{1,0:T(8,128)S(1)}) custom-call(f32[2,128]{1,0:T(2,128)S(1)} %bitcast.18, f32[4,128,128]{2,1,0:T(8,128)S(1)} %get-tuple-element.23.refs_1_.refs_0_, ...), custom_call_target="tpu_custom_call" | custom-call | tf_op jit(solution)/shard_map/pallas_call | solution.py:446
  20.3 0.5 %collective-permute-done.3.state_ref = f32[152,128]{1,0:T(8,128)S(1)} collective-permute-done((f32[152,128]{1,0:T(8,128)S(1)}, f32[152,128]{1,0:T(8,128)S(1)}, u32[]{:S(2)}, u32[]{:S(2)}) %collective-permute-start.3) | collective-permute-done | bytes 77856 | tf_op jit(solution)/shard_map/ppermute | solution.py:516
  20.8 8.4 %shard_map.122 = (f32[8,128]{1,0:T(8,128)S(1)}, f32[32,128]{1,0:T(8,128)S(1)}) custom-call(f32[152,128]{1,0:T(8,128)S(1)} %collective-permute-done.3.state_ref, f32[4,128,128]{2,1,0:T(8,128)S(1)} %get-tuple-element.23.refs_1_.refs_0_, f32[4,128,128]{2,1,0:T(8,128)S(1)} %get-tuple-element.24.refs_2_.refs_1_, ...), custom_call_target="tpu_custom_call" | custom-call | tf_op jit(solution)/shard_map/pallas_call | solution.py:446
  29.3 3.5 %collective-permute-start.4 = (f32[32,128]{1,0:T(8,128)S(1)}, f32[32,128]{1,0:T(8,128)S(1)}, u32[]{:S(2)}, u32[]{:S(2)}) collective-permute-start(f32[32,128]{1,0:T(8,128)S(1)} %get-tuple-element.35), channel_id=1, source_target_pairs={{0,16},{4,20},{8,24},{12,28},{16,0},{20,4},{24,8},{28,12},{1,17},{... | collective-permute-start | bytes 49160 | tf_op jit(solution)/shard_map/ppermute | solution.py:458
  32.7 1.7 %collective-permute-done.4 = f32[32,128]{1,0:T(8,128)S(1)} collective-permute-done((f32[32,128]{1,0:T(8,128)S(1)}, f32[32,128]{1,0:T(8,128)S(1)}, u32[]{:S(2)}, u32[]{:S(2)}) %collective-permute-start.4) | collective-permute-done | bytes 16416 | tf_op jit(solution)/shard_map/ppermute | solution.py:458
  34.4 2.4 %collective-permute-start.7 = (f32[32,128]{1,0:T(8,128)S(1)}, f32[32,128]{1,0:T(8,128)S(1)}, u32[]{:S(2)}, u32[]{:S(2)}) collective-permute-start(f32[32,128]{1,0:T(8,128)S(1)} %add.3.refs_0_), channel_id=1, source_target_pairs={{0,3},{1,2},{2,1},{3,0},{4,7},{5,6},{6,5},{7,4},{8,11},{9,10},{10,... | collective-permute-start | bytes 49160 | tf_op jit(solution)/shard_map/ppermute | solution.py:458
  36.9 0.5 %collective-permute-start.6 = (f32[32,128]{1,0:T(8,128)S(1)}, f32[32,128]{1,0:T(8,128)S(1)}, u32[]{:S(2)}, u32[]{:S(2)}) collective-permute-start(f32[32,128]{1,0:T(8,128)S(1)} %add.3.refs_0_), channel_id=1, source_target_pairs={{0,2},{1,3},{2,0},{3,1},{4,6},{5,7},{6,4},{7,5},{8,10},{9,11},{10,... | collective-permute-start | bytes 49160 | tf_op jit(solution)/shard_map/ppermute | solution.py:458
  37.4 0.5 %collective-permute-start.5 = (f32[32,128]{1,0:T(8,128)S(1)}, f32[32,128]{1,0:T(8,128)S(1)}, u32[]{:S(2)}, u32[]{:S(2)}) collective-permute-start(f32[32,128]{1,0:T(8,128)S(1)} %add.3.refs_0_), channel_id=1, source_target_pairs={{0,1},{1,0},{2,3},{3,2},{4,5},{5,4},{6,7},{7,6},{8,9},{9,8},{10,11... | collective-permute-start | bytes 49160 | tf_op jit(solution)/shard_map/ppermute | solution.py:458
  37.9 1.1 %collective-permute-done.7.refs_3_ = f32[32,128]{1,0:T(8,128)S(1)} collective-permute-done((f32[32,128]{1,0:T(8,128)S(1)}, f32[32,128]{1,0:T(8,128)S(1)}, u32[]{:S(2)}, u32[]{:S(2)}) %collective-permute-start.7) | collective-permute-done | bytes 16416 | tf_op jit(solution)/shard_map/ppermute | solution.py:458
  39.1 1.5 %collective-permute-done.6.refs_2_ = f32[32,128]{1,0:T(8,128)S(1)} collective-permute-done((f32[32,128]{1,0:T(8,128)S(1)}, f32[32,128]{1,0:T(8,128)S(1)}, u32[]{:S(2)}, u32[]{:S(2)}) %collective-permute-start.6) | collective-permute-done | bytes 16416 | tf_op jit(solution)/shard_map/ppermute | solution.py:458
  40.6 0.5 %collective-permute-done.5.refs_1_ = f32[32,128]{1,0:T(8,128)S(1)} collective-permute-done((f32[32,128]{1,0:T(8,128)S(1)}, f32[32,128]{1,0:T(8,128)S(1)}, u32[]{:S(2)}, u32[]{:S(2)}) %collective-permute-start.5) | collective-permute-done | bytes 16416 | tf_op jit(solution)/shard_map/ppermute | solution.py:458
  41.1 2.6 %shard_map.123.own_ref = f32[16,128]{1,0:T(8,128)S(1)} custom-call(f32[8,128]{1,0:T(8,128)S(1)} %get-tuple-element.33.small_ref, f32[64,128]{1,0:T(8,128)S(1)} %get-tuple-element.34.prior_ref, f32[32,128]{1,0:T(8,128)S(1)} %add.3.refs_0_, f32[32,128]{1,0:T(8,128)S(1)} %collective-permute-done.5.refs_1_, f32[32,128]{1,0:T(8,128)S(1)} %collective-permute-done.6.refs_2_, ...), custom_call_target="tpu_custom_call" | custom-call | tf_op jit(solution)/shard_map/pallas_call | solution.py:446
  43.8 0.4 collective-permute-start.10
  44.2 2.7 %collective-permute-start.9 = (f32[16,128]{1,0:T(8,128)S(1)}, f32[16,128]{1,0:T(8,128)S(1)}, u32[]{:S(2)}, u32[]{:S(2)}) collective-permute-start(f32[16,128]{1,0:T(8,128)S(1)} %shard_map.123.own_ref), channel_id=1, source_target_pairs={{0,8},{4,12},{8,0},{12,4},{16,24},{20,28},{24,16},{28,20},{1,9},{5... | collective-permute-start | bytes 24584 | tf_op jit(solution)/shard_map/ppermute | solution.py:458
  46.9 0.0 collective-permute-start.8
  46.9 0.0 collective-permute-done.10.three_ref
  46.9 1.6 %collective-permute-done.9.two_ref = f32[16,128]{1,0:T(8,128)S(1)} collective-permute-done((f32[16,128]{1,0:T(8,128)S(1)}, f32[16,128]{1,0:T(8,128)S(1)}, u32[]{:S(2)}, u32[]{:S(2)}) %collective-permute-start.9) | collective-permute-done | bytes 8224 | tf_op jit(solution)/shard_map/ppermute | solution.py:458
  48.5 0.0 collective-permute-done.8.one_ref
  48.5 0.6 %shard_map.124 = (f32[4,128]{1,0:T(4,128)}, f32[4,128]{1,0:T(4,128)}, f32[4,64]{1,0:T(4,128)}, f32[4,64]{1,0:T(4,128)}) custom-call(f32[16,128]{1,0:T(8,128)S(1)} %shard_map.123.own_ref, f32[16,128]{1,0:T(8,128)S(1)} %collective-permute-done.8.one_ref, f32[16,128]{1,0:T(8,128)S(1)} %collective-permute-done.9.two_ref, ...), custom_call_target="tpu_custom_call" | custom-call | tf_op jit(solution)/shard_map/pallas_call | solution.py:446
  (4 shorter events, 0.0 us)
Async XLA Ops:
  1.3 1.0 %copy-start = (f32[1,64,128]{2,1,0:T(8,128)S(1)}, f32[1,64,128]{2,1,0:T(8,128)}, u32[]{:S(2)}) copy-start(f32[1,64,128]{2,1,0:T(8,128)} %param.11) | copy-start | bytes 98308
  2.2 0.7 %copy-start.1 = (f32[1,128]{1,0:T(1,128)S(1)}, f32[1,128]{1,0:T(1,128)}, u32[]{:S(2)}) copy-start(f32[1,128]{1,0:T(1,128)} %param.12) | copy-start | bytes 1540
  2.9 6.2 %copy-start.5 = (f32[4]{0:T(128)S(1)}, f32[4]{0:T(128)}, u32[]{:S(2)}) copy-start(f32[4]{0:T(128)} %param.16) | copy-start | bytes 52
  3.0 6.1 %copy-start.2 = (f32[64]{0:T(128)S(1)}, f32[64]{0:T(128)}, u32[]{:S(2)}) copy-start(f32[64]{0:T(128)} %param.14) | copy-start | bytes 772
  3.0 6.1 %copy-start.3 = (f32[64]{0:T(128)S(1)}, f32[64]{0:T(128)}, u32[]{:S(2)}) copy-start(f32[64]{0:T(128)} %param.13) | copy-start | bytes 772
  3.0 6.1 %copy-start.4 = (f32[4]{0:T(128)S(1)}, f32[4]{0:T(128)}, u32[]{:S(2)}) copy-start(f32[4]{0:T(128)} %param.15) | copy-start | bytes 52
  3.1 6.1 %collective-permute-start.1 = (f32[208,128]{1,0:T(8,128)S(1)}, f32[208,128]{1,0:T(8,128)S(1)}, u32[]{:S(2)}, u32[]{:S(2)}) collective-permute-start(f32[208,128]{1,0:T(8,128)S(1)} %concatenate.7.own_ref), channel_id=1, source_target_pairs={{0,8},{4,12},{8,0},{12,4},{16,24},{20,28},{24,16},{28,20},{1,9},{5... | collective-permute-start | bytes 319496 | tf_op jit(solution)/shard_map/ppermute | solution.py:458
  6.1 3.1 %collective-permute-start = (f32[208,128]{1,0:T(8,128)S(1)}, f32[208,128]{1,0:T(8,128)S(1)}, u32[]{:S(2)}, u32[]{:S(2)}) collective-permute-start(f32[208,128]{1,0:T(8,128)S(1)} %concatenate.7.own_ref), channel_id=1, source_target_pairs={{0,4},{4,0},{8,12},{12,8},{16,20},{20,16},{24,28},{28,24},{1,5},{5... | collective-permute-start | bytes 319496 | tf_op jit(solution)/shard_map/ppermute | solution.py:458
  9.1 1.3 %collective-permute-start.2 = (f32[208,128]{1,0:T(8,128)S(1)}, f32[208,128]{1,0:T(8,128)S(1)}, u32[]{:S(2)}, u32[]{:S(2)}) collective-permute-start(f32[208,128]{1,0:T(8,128)S(1)} %collective-permute-done.1.two_ref), channel_id=1, source_target_pairs={{0,4},{4,0},{8,12},{12,8},{16,20},{20,16},{24,28},{28,24},{1,5},{5... | collective-permute-start | bytes 319496 | tf_op jit(solution)/shard_map/ppermute | solution.py:458
  14.2 6.7 %collective-permute-start.3 = (f32[152,128]{1,0:T(8,128)S(1)}, f32[152,128]{1,0:T(8,128)S(1)}, u32[]{:S(2)}, u32[]{:S(2)}) collective-permute-start(f32[152,128]{1,0:T(8,128)S(1)} %get-tuple-element.22), channel_id=1, source_target_pairs={{0,16},{4,20},{8,24},{12,28},{1,17},{5,21},{9,25},{13,29},{2,18},{... | collective-permute-start | bytes 233480 | tf_op jit(solution)/shard_map/ppermute | solution.py:516
  29.3 5.2 %collective-permute-start.4 = (f32[32,128]{1,0:T(8,128)S(1)}, f32[32,128]{1,0:T(8,128)S(1)}, u32[]{:S(2)}, u32[]{:S(2)}) collective-permute-start(f32[32,128]{1,0:T(8,128)S(1)} %get-tuple-element.35), channel_id=1, source_target_pairs={{0,16},{4,20},{8,24},{12,28},{16,0},{20,4},{24,8},{28,12},{1,17},{... | collective-permute-start | bytes 49160 | tf_op jit(solution)/shard_map/ppermute | solution.py:458
  34.4 4.6 %collective-permute-start.7 = (f32[32,128]{1,0:T(8,128)S(1)}, f32[32,128]{1,0:T(8,128)S(1)}, u32[]{:S(2)}, u32[]{:S(2)}) collective-permute-start(f32[32,128]{1,0:T(8,128)S(1)} %add.3.refs_0_), channel_id=1, source_target_pairs={{0,3},{1,2},{2,1},{3,0},{4,7},{5,6},{6,5},{7,4},{8,11},{9,10},{10,... | collective-permute-start | bytes 49160 | tf_op jit(solution)/shard_map/ppermute | solution.py:458
  36.9 3.7 %collective-permute-start.6 = (f32[32,128]{1,0:T(8,128)S(1)}, f32[32,128]{1,0:T(8,128)S(1)}, u32[]{:S(2)}, u32[]{:S(2)}) collective-permute-start(f32[32,128]{1,0:T(8,128)S(1)} %add.3.refs_0_), channel_id=1, source_target_pairs={{0,2},{1,3},{2,0},{3,1},{4,6},{5,7},{6,4},{7,5},{8,10},{9,11},{10,... | collective-permute-start | bytes 49160 | tf_op jit(solution)/shard_map/ppermute | solution.py:458
  37.4 3.7 %collective-permute-start.5 = (f32[32,128]{1,0:T(8,128)S(1)}, f32[32,128]{1,0:T(8,128)S(1)}, u32[]{:S(2)}, u32[]{:S(2)}) collective-permute-start(f32[32,128]{1,0:T(8,128)S(1)} %add.3.refs_0_), channel_id=1, source_target_pairs={{0,1},{1,0},{2,3},{3,2},{4,5},{5,4},{6,7},{7,6},{8,9},{9,8},{10,11... | collective-permute-start | bytes 49160 | tf_op jit(solution)/shard_map/ppermute | solution.py:458
  43.8 3.2 %collective-permute-start.10 = (f32[16,128]{1,0:T(8,128)S(1)}, f32[16,128]{1,0:T(8,128)S(1)}, u32[]{:S(2)}, u32[]{:S(2)}) collective-permute-start(f32[16,128]{1,0:T(8,128)S(1)} %shard_map.123.own_ref), channel_id=1, source_target_pairs={{0,12},{4,8},{8,4},{12,0},{16,28},{20,24},{24,20},{28,16},{1,13},{... | collective-permute-start | bytes 24584 | tf_op jit(solution)/shard_map/ppermute | solution.py:458
  44.2 4.4 %collective-permute-start.9 = (f32[16,128]{1,0:T(8,128)S(1)}, f32[16,128]{1,0:T(8,128)S(1)}, u32[]{:S(2)}, u32[]{:S(2)}) collective-permute-start(f32[16,128]{1,0:T(8,128)S(1)} %shard_map.123.own_ref), channel_id=1, source_target_pairs={{0,8},{4,12},{8,0},{12,4},{16,24},{20,28},{24,16},{28,20},{1,9},{5... | collective-permute-start | bytes 24584 | tf_op jit(solution)/shard_map/ppermute | solution.py:458
  46.9 1.6 %collective-permute-start.8 = (f32[16,128]{1,0:T(8,128)S(1)}, f32[16,128]{1,0:T(8,128)S(1)}, u32[]{:S(2)}, u32[]{:S(2)}) collective-permute-start(f32[16,128]{1,0:T(8,128)S(1)} %shard_map.123.own_ref), channel_id=1, source_target_pairs={{0,4},{4,0},{8,12},{12,8},{16,20},{20,16},{24,28},{28,24},{1,5},{5... | collective-permute-start | bytes 24584 | tf_op jit(solution)/shard_map/ppermute | solution.py:458

commit v7 on v6

--- a/solution.py
+++ b/solution.py
@@ -121,6 +121,7 @@
     right_ref,
     left_ref,
     state_ref,
+    part_ref,
     raw_ref,
     mat_ref,
     inv_ref,
@@ -167,11 +168,14 @@
         right23 = right[3] - gram23[end, one]
         left23 = -gram23[end, two]
 
+        part = gram[end, end] + gram23[end, end]
         rows = jnp.concatenate([cross23, cross01_t, right01 + left23], axis=0)
         (gram,), more = quotients((diag01 + back23,), (rows,), (rows,), 4, refs)
         diag03 = diag23 - gram[one, one]
         right03 = right23 - gram[end, one]
         send(state_ref, diag03, right03)
+        part = (part + gram[end, end])[0:tip, :]
+        part_ref[...] = jnp.concatenate([part, jnp.zeros((tip, tile - part.shape[1]), F32)], axis=1)
         for n, value in enumerate((diag[0], diag01, diag[2], diag03)):
             diag_ref[n] = value
         for n, value in enumerate((cross[0], cross01, cross[2], -gram[one, two])):
@@ -274,15 +278,14 @@
     base = base + lone * parts[0][0]
     mats = [base + back for back in backs]
     came = padded(came, tile)
-    rights = [
-        jnp.concatenate([cross, came + padded(left, tile)], axis=0) for cross, left in zip(crosses, lefts)
-    ]
-    updates, total = quotients(mats, crosses, rights, 5, refs)
+    middles = [came + padded(left, tile) for left in lefts]
+    rights = [jnp.concatenate([cross, middle], axis=0) for cross, middle in zip(crosses, middles)]
+    updates, total = quotients(mats, crosses[:-1] + rights[-1:], rights, 5, refs)
     results = []
     for diag, side, update in zip(diags, sides, updates):
         start = jnp.concatenate([diag, padded(side, tile).T], axis=1)
-        results.append(start - update)
-    return results, total
+        results.append(start - update[0:tile, :])
+    return results, updates[-1][tile:, tile:], total
 
 
 def advance_kernel(state_ref, *refs):
@@ -290,7 +293,7 @@
     tile = state_ref.shape[1]
 
     def run(refs):
-        (last,), total = joined(state_ref, parts, (GROUP - 1,), refs)
+        (last,), _, total = joined(state_ref, parts, (GROUP - 1,), refs)
         send(out_ref, last[:, 0:tile], last[:, tile:].T)
         return total < SMALL
 
@@ -369,21 +372,63 @@
     return uppers, lowers, total
 
 
-def final_kernel(tip, state_ref, *refs):
-    *parts, small_ref, sums_ref, mat_ref, inv_ref, rows_ref, ends_ref = refs
+def fold(gram):
+    tip, tile = gram.shape
+    mid = tip // 2
+    top, bottom = gram[0:mid, :], gram[mid:, :]
+    col = lax.broadcasted_iota(jnp.int32, (mid, tile), 1)
+    ends = jnp.where(col == tip + mid, pltpu.roll(top, mid, 1), pltpu.roll(bottom, mid + 1, 1))
+    ends = jnp.where(col < tip + mid, pltpu.roll(bottom, mid, 1), ends)
+    return jnp.where(col < tip, top, ends)
+
+
+def unfold(folded):
+    mid, tile = folded.shape
+    near = pltpu.roll(folded, tile - mid, 1)
+    far = pltpu.roll(folded, tile - mid - 1, 1)
+    col = lax.broadcasted_iota(jnp.int32, (mid, tile), 1)
+    top = jnp.where(col < 2 * mid, folded, near)
+    bottom = jnp.where(col < 2 * mid, near, far)
+    return top, bottom
+
+
+def merge_kernel(start, state_ref, *refs):
+    *parts, part_ref, square_ref, side_ref, sums_ref, mat_ref, inv_ref = refs
     tile = state_ref.shape[1]
+    tip = part_ref.shape[0]
+    last = jnp.where(lax.axis_index("tm") >= start, 1.0, 0.0).astype(F32)
+
+    def run(refs):
+        values, share, total = joined(state_ref, parts, range(GROUP), refs)
+        for n, value in enumerate(values):
+            square_ref[n] = value[:, 0:tile]
+            side_ref[n] = value[:, tile:]
+        side = values[-1][:, tile:].T
+        (own,), more = quotients((values[-1][:, 0:tile],), (side[0:tip, :],), (side,), 5, refs)
+        sums_ref[...] = fold(part_ref[...] + share[0:tip, :] + last * own)
+        return (total < SMALL) & (more < SMALL)
+
+    settled = run(None)
+
+    @pl.when(jnp.logical_not(settled))
+    def _():
+        run((mat_ref, inv_ref))
+
+
+def factor_kernel(tip, square_ref, side_ref, small_ref, mat_ref, inv_ref, rows_ref, ends_ref):
+    tile = square_ref.shape[-1]
     half = tile // 2
+    values = [jnp.concatenate([square_ref[n], side_ref[n]], axis=1) for n in range(GROUP)]
 
     def run(refs):
-        values, total = joined(state_ref, parts, range(GROUP), refs)
-        uppers, lowers, more = halved(values, refs)
+        uppers, lowers, total = halved(values, refs)
         for b, value in enumerate(uppers):
             rows_ref[pl.ds(b, half, stride=SUB), :] = value[:, 0:tile]
             ends_ref[pl.ds(b, half, stride=SUB), :] = value[:, tile:]
         for b, value in enumerate(lowers):
             rows_ref[pl.ds(GROUP + b, half, stride=SUB), :] = pltpu.roll(value[:, 0:tile], half, 1)
             ends_ref[pl.ds(GROUP + b, half, stride=SUB), :] = value[:, tile:]
-        return (total < SMALL) & (more < SMALL)
+        return total < SMALL
 
     settled = run(None)
 
@@ -396,49 +441,24 @@
         spot = slice(n * GROUP, (n + 1) * GROUP)
         small_ref[spot, 0:half] = value[0:GROUP, 0:half]
         small_ref[spot, half:] = value[GROUP:, 0:half]
-    everything = jnp.concatenate(
-        [ends_ref[pl.ds(b, half, stride=SUB), :] for b in range(2 * GROUP)], axis=0
-    )
-    gram = fine(everything[:, 0:tip], everything, TN)
+
+
+def tip_kernel(prior_ref, *refs):
+    *came, log_ref, solved_ref, tip_log_ref, tip_ref, all_ref, rows_ref = refs
+    tip = prior_ref.shape[0]
     mid = tip // 2
-    top, bottom = gram[0:mid, :], gram[mid:, :]
-    col = lax.broadcasted_iota(jnp.int32, (mid, tile), 1)
-    ends = jnp.where(col == tip + mid, pltpu.roll(top, mid, 1), pltpu.roll(bottom, mid + 1, 1))
-    folded = jnp.where(col < tip + mid, pltpu.roll(bottom, mid, 1), ends)
-    sums_ref[...] = jnp.where(col < tip, top, folded)
-
-
-def tip_kernel(small_ref, prior_ref, *refs):
-    *came, out_ref, sums_ref, rows_ref = refs
-    tip = prior_ref.shape[0]
-    place = lax.axis_index("mesh") & 3
+    node = lax.axis_index("tm") & (GROUP - 1)
     for step, ref in enumerate(came):
-        sums_ref[place ^ step] = ref[...]
-    total = sums_ref[0]
-    for n in range(1, len(came)):
-        total = total + sums_ref[n]
-    mid = tip // 2
-    col = lax.broadcasted_iota(jnp.int32, (mid, 128), 1)
-    top = jnp.where(col < tip, total, pltpu.roll(total, 128 - mid, 1))
-    bottom = jnp.where(col < tip, pltpu.roll(total, 128 - mid, 1), pltpu.roll(total, 127 - mid, 1))
-    rows_ref[pl.ds(0, mid, stride=SUB), :] = prior_ref[0:mid, :] - top
-    rows_ref[pl.ds(SUB * mid, mid, stride=SUB), :] = prior_ref[mid:, :] - bottom
-    pivots, column = factor((rows_ref,), tip, 1, tip)
-    out_ref[0 : 2 * GROUP, :] = small_ref[...]
-    out_ref[2 * GROUP :, :] = jnp.concatenate(
-        [0.5 * jnp.log(pivots[0:1, :]), column[0:1, :], jnp.zeros((SUB - 2, 128), F32)], axis=0
-    )
-
-
-def place_kernel(own_ref, one_ref, two_ref, three_ref, log_ref, solved_ref, tip_log_ref, tip_ref):
-    node = lax.axis_index("tm") & (GROUP - 1)
-    tip = tip_ref.shape[1]
-    for step, ref in enumerate((own_ref, one_ref, two_ref, three_ref)):
-        setting = pl.ds(node ^ step, 1)
-        log_ref[setting, :] = ref[pl.ds(node, 1), :]
-        solved_ref[setting, :] = ref[pl.ds(node + GROUP, 1), :]
-        tip_log_ref[setting, :] = ref[2 * GROUP : 2 * GROUP + 1, 0:tip]
-        tip_ref[setting, :] = ref[2 * GROUP + 1 : 2 * GROUP + 2, 0:tip]
+        all_ref[node ^ step] = ref[...]
+    for n in range(GROUP):
+        top, bottom = unfold(all_ref[n, 0:mid, :])
+        rows_ref[pl.ds(n, mid, stride=SUB), :] = prior_ref[0:mid, :] - top
+        rows_ref[pl.ds(SUB * mid + n, mid, stride=SUB), :] = prior_ref[mid:, :] - bottom
+        log_ref[n : n + 1, :] = all_ref[n, pl.ds(mid + node, 1), :]
+        solved_ref[n : n + 1, :] = all_ref[n, pl.ds(mid + GROUP + node, 1), :]
+    pivots, column = factor((rows_ref,), tip, GROUP, tip)
+    tip_log_ref[...] = 0.5 * jnp.log(pivots[0:GROUP, 0:tip])
+    tip_ref[...] = column[0:GROUP, 0:tip]
 
 
 def call(body, inputs, shapes, scratch=()):
@@ -499,10 +519,10 @@
     two = crossed(raw, "tm", 2)
     one = crossed(raw, "tm", 1)
     three = crossed(two, "tm", 1)
-    *parts, state = call(
+    *parts, state, part = call(
         functools.partial(local_kernel, tip),
         (extra, raw, one, two, three),
-        (square, square, square, band, band, packed_state),
+        (square, square, square, band, band, packed_state, (tip, tile)),
         ((GROUP,) + raw.shape, *pair),
     )
     *thirds, prior = call(
@@ -519,10 +539,16 @@
     if spans == 1:
         state = jnp.zeros_like(state)
     half = SUB * tile // 2
-    small, sums = call(
-        functools.partial(final_kernel, tip),
-        (state, *parts),
-        ((2 * GROUP, tile), (tip // 2, tile)),
+    squares, sides, sums = call(
+        functools.partial(merge_kernel, groups - GROUP),
+        (state, *parts, part),
+        (square, square, (tip // 2, tile)),
+        pair,
+    )
+    (small,) = call(
+        functools.partial(factor_kernel, tip),
+        (squares, sides),
+        ((2 * GROUP, tile),),
         (*pair, (half, tile), (half, tile)),
     )
     for axis, first in (("tm", GROUP), ("mesh", 4)):
@@ -530,17 +556,14 @@
         while step < lax.axis_size(axis):
             sums = sums + crossed(sums, axis, step)
             step *= 2
-    near = [sums] + [crossed(sums, "mesh", n) for n in range(1, 4)]
-    (packed,) = call(
+    sums, small = lax.optimization_barrier((sums, small))
+    sums = (sums + crossed(sums, "mesh", 1)) + (crossed(sums, "mesh", 2) + crossed(sums, "mesh", 3))
+    found = jnp.concatenate([sums, small], axis=0)
+    log_diag, solved, tip_log, tip_forward = call(
         tip_kernel,
-        (small, prior, *near),
-        ((4 * GROUP, tile),),
-        ((len(near), tip // 2, 128), (SUB * tip, 128)),
-    )
-    log_diag, solved, tip_log, tip_forward = call(
-        place_kernel,
-        (packed,) + tuple(crossed(packed, "tm", n) for n in range(1, 4)),
+        (prior, found) + tuple(crossed(found, "tm", n) for n in range(1, 4)),
         ((GROUP, tile), (GROUP, tile), (GROUP, tip), (GROUP, tip)),
+        ((GROUP,) + found.shape, (SUB * tip, tile)),
     )
     return (log_diag[:, None, :], solved[:, None, :], tip_log, tip_forward)
 

time: 49.8 us -> 51.5 us (1.034)
  Pallas kernels: 16.8 us -> 19.1 us
    pallas_call x5, Pallas kernels: 16.8 us -> 19.1 us  [call(): pl.pallas_call(body, out_shape=tuple((jax.ShapeDtypeStruct(shape, F32) fo...]
  transfers between devices with their start and end apart: 11 -> 11, of which waited for: 8 -> 8; matrix products, arithmetic and copies ran while one was open for 0% -> 0% of each run, Pallas kernels for 3% -> 12%
where the time goes in v7:
time: 51.5 us; the launch traced here: 51.3 us
  Pallas kernels  19.1 us (37%)
  starting transfers between devices  18 us (35%)
  waiting for transfers between devices  11 us (21%)
  between operations  1.44 us (3%)
  other arithmetic  0.93 us (2%)
  local copies, waits for them, and re-layouts  0.88 us (2%)
    pallas_call x5, Pallas kernels, call(): pl.pallas_call(body, out_shape=tuple((jax.ShapeDtypeStruct(shape, F32) fo...  19.1 us
    ppermute x10, starting transfers between devices, crossed(): lax.ppermute(value, axis, [(source, source ^ step) for source in range(si...  13.3 us
    ppermute x10, waiting for transfers between devices, crossed(): lax.ppermute(value, axis, [(source, source ^ step) for source in range(si...  10.5 us
    ppermute x1, starting transfers between devices, shards(): lax.ppermute(state, 'tm', [(source, source + GROUP) for source in range(g...  4.66 us
  transfers between devices with their start and end apart: 11, of which 8 were waited for; matrix products, arithmetic and copies ran while one was open for 0% of the time, Pallas kernels for 12%

profile of v7, /device:TPU:0, one launch (start us, length us, event | category | flops | bytes accessed | tf_op | source)
XLA Modules:
  0.0 51.3 jit_solution(14440693863678247649)
XLA Ops:
  1.3 0.0 copy-start
  1.3 0.9 %fusion = (f32[128]{0:T(128)S(1)}, f32[128,128]{1,0:T(8,128)S(1)}) fusion(f32[1,128,128]{2,1,0:T(8,128)} %param.10, f32[1,128,128]{2,1,0:T(8,128)} %param.9), kind=kLoop, calls=%fused_computation.2 | loop fusion | flops 81792 | bytes 197120 | tf_op jit(solution)/shard_map/reduce_sum | solution.py:510
  2.2 0.0 copy-start.1
  2.2 0.0 copy-done
  2.2 0.6 %copy-done.1 = f32[1,128]{1,0:T(1,128)S(1)} copy-done((f32[1,128]{1,0:T(1,128)S(1)}, f32[1,128]{1,0:T(1,128)}, u32[]{:S(2)}) %copy-start.1) | copy-done | bytes 536
  2.9 0.0 copy-start.5
  2.9 0.1 concatenate.10.own_ref
  3.0 0.0 copy-start.2
  3.0 0.0 copy-start.3
  3.0 0.0 copy-start.4
  3.1 3.1 %collective-permute-start.1 = (f32[208,128]{1,0:T(8,128)S(1)}, f32[208,128]{1,0:T(8,128)S(1)}, u32[]{:S(2)}, u32[]{:S(2)}) collective-permute-start(f32[208,128]{1,0:T(8,128)S(1)} %concatenate.10.own_ref), channel_id=1, source_target_pairs={{0,8},{4,12},{8,0},{12,4},{16,24},{20,28},{24,16},{28,20},{1,9},{5... | collective-permute-start | bytes 319496 | tf_op jit(solution)/shard_map/ppermute | solution.py:478
  6.1 0.0 collective-permute-start
  6.1 3.0 %collective-permute-done.1.two_ref = f32[208,128]{1,0:T(8,128)S(1)} collective-permute-done((f32[208,128]{1,0:T(8,128)S(1)}, f32[208,128]{1,0:T(8,128)S(1)}, u32[]{:S(2)}, u32[]{:S(2)}) %collective-permute-start.1) | collective-permute-done | bytes 106528 | tf_op jit(solution)/shard_map/ppermute | solution.py:478
  9.1 0.0 collective-permute-start.2
  9.1 0.0 copy-done.5
  9.1 0.0 copy-done.2
  9.1 0.0 copy-done.3
  9.1 0.0 copy-done.4
  9.2 0.1 concatenate.9
  9.2 0.0 collective-permute-done.one_ref
  9.2 1.2 %collective-permute-done.2.three_ref = f32[208,128]{1,0:T(8,128)S(1)} collective-permute-done((f32[208,128]{1,0:T(8,128)S(1)}, f32[208,128]{1,0:T(8,128)S(1)}, u32[]{:S(2)}, u32[]{:S(2)}) %collective-permute-start.2) | collective-permute-done | bytes 106528 | tf_op jit(solution)/shard_map/ppermute | solution.py:478
  10.4 4.1 %shard_map.120 = (f32[4,128,128]{2,1,0:T(8,128)S(1)}, f32[4,128,128]{2,1,0:T(8,128)S(1)}, f32[4,128,128]{2,1,0:T(8,128)S(1)}, f32[4,80,128]{2,1,0:T(8,128)S(1)},...) custom-call(f32[2,128]{1,0:T(2,128)S(1)} %bitcast.17, ...), custom_call_target="tpu_custom_call" | custom-call | tf_op jit(solution)/shard_map/pallas_call | solution.py:466
  14.5 4.7 %collective-permute-start.3 = (f32[152,128]{1,0:T(8,128)S(1)}, f32[152,128]{1,0:T(8,128)S(1)}, u32[]{:S(2)}, u32[]{:S(2)}) collective-permute-start(f32[152,128]{1,0:T(8,128)S(1)} %get-tuple-element.32), channel_id=1, source_target_pairs={{0,16},{4,20},{8,24},{12,28},{1,17},{5,21},{9,25},{13,29},{2,18},{... | collective-permute-start | bytes 233480 | tf_op jit(solution)/shard_map/ppermute | solution.py:536
  19.2 1.5 %shard_map.121 = (f32[128,128]{1,0:T(8,128)S(1)}, f32[128,128]{1,0:T(8,128)S(1)}, f32[128,128]{1,0:T(8,128)S(1)}, f32[80,128]{1,0:T(8,128)S(1)}, f32[80,128]{1,0:T(8,128)S(1)}, /*index=5*/f32[64,128]{1,0:T(8,128)S(1)}) custom-call(f32[2,128]{1,0:T(2,128)S(1)} %bitcast.18, f32[4,128,128]{2,1,0:T(8,128)S(1)} %get-tuple-element.26.refs_1_.refs_0_, ...), custom_call_target="tpu_custom_call" | custom-call | tf_op jit(solution)/shard_map/pallas_call | solution.py:466
  20.6 0.5 %collective-permute-done.3.state_ref = f32[152,128]{1,0:T(8,128)S(1)} collective-permute-done((f32[152,128]{1,0:T(8,128)S(1)}, f32[152,128]{1,0:T(8,128)S(1)}, u32[]{:S(2)}, u32[]{:S(2)}) %collective-permute-start.3) | collective-permute-done | bytes 77856 | tf_op jit(solution)/shard_map/ppermute | solution.py:536
  21.2 5.4 %shard_map.122 = (f32[4,128,128]{2,1,0:T(8,128)S(1)}, f32[4,128,128]{2,1,0:T(8,128)S(1)}, f32[32,128]{1,0:T(8,128)S(1)}) custom-call(f32[152,128]{1,0:T(8,128)S(1)} %collective-permute-done.3.state_ref, f32[4,128,128]{2,1,0:T(8,128)S(1)} %get-tuple-element.26.refs_1_.refs_0_, f32[4,128,128]{2,1,0:T(8,128)S(1)} %get-tuple-element.27.refs_2_.refs_1_, ...), custom_call_target="tpu_custom_call" | custom-call | tf_op jit(solution)/shard_map/pallas_call | solution.py:466
  26.5 3.5 %collective-permute-start.4 = (f32[32,128]{1,0:T(8,128)S(1)}, f32[32,128]{1,0:T(8,128)S(1)}, u32[]{:S(2)}, u32[]{:S(2)}) collective-permute-start(f32[32,128]{1,0:T(8,128)S(1)} %get-tuple-element.39), channel_id=1, source_target_pairs={{0,16},{4,20},{8,24},{12,28},{16,0},{20,4},{24,8},{28,12},{1,17},{... | collective-permute-start | bytes 49160 | tf_op jit(solution)/shard_map/ppermute | solution.py:478
  30.0 4.9 %shard_map.123 = f32[8,128]{1,0:T(8,128)S(1)} custom-call(f32[4,128,128]{2,1,0:T(8,128)S(1)} %get-tuple-element.40.square_ref, f32[4,128,128]{2,1,0:T(8,128)S(1)} %get-tuple-element.41.side_ref), custom_call_target="tpu_custom_call" | custom-call | tf_op jit(solution)/shard_map/pallas_call | solution.py:466
  34.9 0.0 collective-permute-done.4
  34.9 1.6 %collective-permute-start.6 = (f32[32,128]{1,0:T(8,128)S(1)}, f32[32,128]{1,0:T(8,128)S(1)}, u32[]{:S(2)}, u32[]{:S(2)}) collective-permute-start(f32[32,128]{1,0:T(8,128)S(1)} %add.12), channel_id=1, source_target_pairs={{0,2},{1,3},{2,0},{3,1},{4,6},{5,7},{6,4},{7,5},{8,10},{9,11},{10,... | collective-permute-start | bytes 49160 | tf_op jit(solution)/shard_map/ppermute | solution.py:478
  36.4 1.4 %collective-permute-start.7 = (f32[32,128]{1,0:T(8,128)S(1)}, f32[32,128]{1,0:T(8,128)S(1)}, u32[]{:S(2)}, u32[]{:S(2)}) collective-permute-start(f32[32,128]{1,0:T(8,128)S(1)} %add.12), channel_id=1, source_target_pairs={{0,3},{1,2},{2,1},{3,0},{4,7},{5,6},{6,5},{7,4},{8,11},{9,10},{10,... | collective-permute-start | bytes 49160 | tf_op jit(solution)/shard_map/ppermute | solution.py:478
  37.9 0.5 %collective-permute-start.5 = (f32[32,128]{1,0:T(8,128)S(1)}, f32[32,128]{1,0:T(8,128)S(1)}, u32[]{:S(2)}, u32[]{:S(2)}) collective-permute-start(f32[32,128]{1,0:T(8,128)S(1)} %add.12), channel_id=1, source_target_pairs={{0,1},{1,0},{2,3},{3,2},{4,5},{5,4},{6,7},{7,6},{8,9},{9,8},{10,11... | collective-permute-start | bytes 49160 | tf_op jit(solution)/shard_map/ppermute | solution.py:478
  38.4 0.3 collective-permute-done.6
  38.7 2.4 %collective-permute-done.7 = f32[32,128]{1,0:T(8,128)S(1)} collective-permute-done((f32[32,128]{1,0:T(8,128)S(1)}, f32[32,128]{1,0:T(8,128)S(1)}, u32[]{:S(2)}, u32[]{:S(2)}) %collective-permute-start.7) | collective-permute-done | bytes 16416 | tf_op jit(solution)/shard_map/ppermute | solution.py:478
  41.1 0.5 %collective-permute-done.5 = f32[32,128]{1,0:T(8,128)S(1)} collective-permute-done((f32[32,128]{1,0:T(8,128)S(1)}, f32[32,128]{1,0:T(8,128)S(1)}, u32[]{:S(2)}, u32[]{:S(2)}) %collective-permute-start.5) | collective-permute-done | bytes 16416 | tf_op jit(solution)/shard_map/ppermute | solution.py:478
  41.6 0.1 collective-permute-start.8
  41.7 3.1 %collective-permute-start.9 = (f32[40,128]{1,0:T(8,128)S(1)}, f32[40,128]{1,0:T(8,128)S(1)}, u32[]{:S(2)}, u32[]{:S(2)}) collective-permute-start(f32[40,128]{1,0:T(8,128)S(1)} %pad_maximum_fusion.refs_0_), channel_id=1, source_target_pairs={{0,8},{4,12},{8,0},{12,4},{16,24},{20,28},{24,16},{28,20},{1,9},{5... | collective-permute-start | bytes 61448 | tf_op jit(solution)/shard_map/ppermute | solution.py:478
  44.8 0.1 collective-permute-start.10
  44.9 0.0 collective-permute-done.8.refs_1_
  44.9 1.7 %collective-permute-done.9.refs_2_ = f32[40,128]{1,0:T(8,128)S(1)} collective-permute-done((f32[40,128]{1,0:T(8,128)S(1)}, f32[40,128]{1,0:T(8,128)S(1)}, u32[]{:S(2)}, u32[]{:S(2)}) %collective-permute-start.9) | collective-permute-done | bytes 20512 | tf_op jit(solution)/shard_map/ppermute | solution.py:478
  46.6 1.4 %collective-permute-done.10.refs_3_ = f32[40,128]{1,0:T(8,128)S(1)} collective-permute-done((f32[40,128]{1,0:T(8,128)S(1)}, f32[40,128]{1,0:T(8,128)S(1)}, u32[]{:S(2)}, u32[]{:S(2)}) %collective-permute-start.10) | collective-permute-done | bytes 20512 | tf_op jit(solution)/shard_map/ppermute | solution.py:478
  48.0 3.3 %shard_map.124 = (f32[4,128]{1,0:T(4,128)}, f32[4,128]{1,0:T(4,128)}, f32[4,64]{1,0:T(4,128)}, f32[4,64]{1,0:T(4,128)}) custom-call(f32[64,128]{1,0:T(8,128)S(1)} %get-tuple-element.31.prior_ref, f32[40,128]{1,0:T(8,128)S(1)} %pad_maximum_fusion.refs_0_, f32[40,128]{1,0:T(8,128)S(1)} %collective-permute-done.8.refs_1_, ...), custom_call_target="tpu_custom_call" | custom-call | tf_op jit(solution)/shard_map/pallas_call | solution.py:466
  (6 shorter events, 0.0 us)
Async XLA Ops:
  1.3 1.0 %copy-start = (f32[1,64,128]{2,1,0:T(8,128)S(1)}, f32[1,64,128]{2,1,0:T(8,128)}, u32[]{:S(2)}) copy-start(f32[1,64,128]{2,1,0:T(8,128)} %param.11) | copy-start | bytes 98308
  2.2 0.7 %copy-start.1 = (f32[1,128]{1,0:T(1,128)S(1)}, f32[1,128]{1,0:T(1,128)}, u32[]{:S(2)}) copy-start(f32[1,128]{1,0:T(1,128)} %param.12) | copy-start | bytes 1540
  2.9 6.2 %copy-start.5 = (f32[4]{0:T(128)S(1)}, f32[4]{0:T(128)}, u32[]{:S(2)}) copy-start(f32[4]{0:T(128)} %param.16) | copy-start | bytes 52
  3.0 6.1 %copy-start.2 = (f32[64]{0:T(128)S(1)}, f32[64]{0:T(128)}, u32[]{:S(2)}) copy-start(f32[64]{0:T(128)} %param.14) | copy-start | bytes 772
  3.0 6.1 %copy-start.3 = (f32[64]{0:T(128)S(1)}, f32[64]{0:T(128)}, u32[]{:S(2)}) copy-start(f32[64]{0:T(128)} %param.13) | copy-start | bytes 772
  3.0 6.1 %copy-start.4 = (f32[4]{0:T(128)S(1)}, f32[4]{0:T(128)}, u32[]{:S(2)}) copy-start(f32[4]{0:T(128)} %param.15) | copy-start | bytes 52
  3.1 6.1 %collective-permute-start.1 = (f32[208,128]{1,0:T(8,128)S(1)}, f32[208,128]{1,0:T(8,128)S(1)}, u32[]{:S(2)}, u32[]{:S(2)}) collective-permute-start(f32[208,128]{1,0:T(8,128)S(1)} %concatenate.10.own_ref), channel_id=1, source_target_pairs={{0,8},{4,12},{8,0},{12,4},{16,24},{20,28},{24,16},{28,20},{1,9},{5... | collective-permute-start | bytes 319496 | tf_op jit(solution)/shard_map/ppermute | solution.py:478
  6.1 3.1 %collective-permute-start = (f32[208,128]{1,0:T(8,128)S(1)}, f32[208,128]{1,0:T(8,128)S(1)}, u32[]{:S(2)}, u32[]{:S(2)}) collective-permute-start(f32[208,128]{1,0:T(8,128)S(1)} %concatenate.10.own_ref), channel_id=1, source_target_pairs={{0,4},{4,0},{8,12},{12,8},{16,20},{20,16},{24,28},{28,24},{1,5},{5... | collective-permute-start | bytes 319496 | tf_op jit(solution)/shard_map/ppermute | solution.py:478
  9.1 1.3 %collective-permute-start.2 = (f32[208,128]{1,0:T(8,128)S(1)}, f32[208,128]{1,0:T(8,128)S(1)}, u32[]{:S(2)}, u32[]{:S(2)}) collective-permute-start(f32[208,128]{1,0:T(8,128)S(1)} %collective-permute-done.1.two_ref), channel_id=1, source_target_pairs={{0,4},{4,0},{8,12},{12,8},{16,20},{20,16},{24,28},{28,24},{1,5},{5... | collective-permute-start | bytes 319496 | tf_op jit(solution)/shard_map/ppermute | solution.py:478
  14.5 6.7 %collective-permute-start.3 = (f32[152,128]{1,0:T(8,128)S(1)}, f32[152,128]{1,0:T(8,128)S(1)}, u32[]{:S(2)}, u32[]{:S(2)}) collective-permute-start(f32[152,128]{1,0:T(8,128)S(1)} %get-tuple-element.32), channel_id=1, source_target_pairs={{0,16},{4,20},{8,24},{12,28},{1,17},{5,21},{9,25},{13,29},{2,18},{... | collective-permute-start | bytes 233480 | tf_op jit(solution)/shard_map/ppermute | solution.py:536
  26.5 8.3 %collective-permute-start.4 = (f32[32,128]{1,0:T(8,128)S(1)}, f32[32,128]{1,0:T(8,128)S(1)}, u32[]{:S(2)}, u32[]{:S(2)}) collective-permute-start(f32[32,128]{1,0:T(8,128)S(1)} %get-tuple-element.39), channel_id=1, source_target_pairs={{0,16},{4,20},{8,24},{12,28},{16,0},{20,4},{24,8},{28,12},{1,17},{... | collective-permute-start | bytes 49160 | tf_op jit(solution)/shard_map/ppermute | solution.py:478
  34.9 3.8 %collective-permute-start.6 = (f32[32,128]{1,0:T(8,128)S(1)}, f32[32,128]{1,0:T(8,128)S(1)}, u32[]{:S(2)}, u32[]{:S(2)}) collective-permute-start(f32[32,128]{1,0:T(8,128)S(1)} %add.12), channel_id=1, source_target_pairs={{0,2},{1,3},{2,0},{3,1},{4,6},{5,7},{6,4},{7,5},{8,10},{9,11},{10,... | collective-permute-start | bytes 49160 | tf_op jit(solution)/shard_map/ppermute | solution.py:478
  36.4 4.6 %collective-permute-start.7 = (f32[32,128]{1,0:T(8,128)S(1)}, f32[32,128]{1,0:T(8,128)S(1)}, u32[]{:S(2)}, u32[]{:S(2)}) collective-permute-start(f32[32,128]{1,0:T(8,128)S(1)} %add.12), channel_id=1, source_target_pairs={{0,3},{1,2},{2,1},{3,0},{4,7},{5,6},{6,5},{7,4},{8,11},{9,10},{10,... | collective-permute-start | bytes 49160 | tf_op jit(solution)/shard_map/ppermute | solution.py:478
  37.9 3.7 %collective-permute-start.5 = (f32[32,128]{1,0:T(8,128)S(1)}, f32[32,128]{1,0:T(8,128)S(1)}, u32[]{:S(2)}, u32[]{:S(2)}) collective-permute-start(f32[32,128]{1,0:T(8,128)S(1)} %add.12), channel_id=1, source_target_pairs={{0,1},{1,0},{2,3},{3,2},{4,5},{5,4},{6,7},{7,6},{8,9},{9,8},{10,11... | collective-permute-start | bytes 49160 | tf_op jit(solution)/shard_map/ppermute | solution.py:478
  41.6 3.3 %collective-permute-start.8 = (f32[40,128]{1,0:T(8,128)S(1)}, f32[40,128]{1,0:T(8,128)S(1)}, u32[]{:S(2)}, u32[]{:S(2)}) collective-permute-start(f32[40,128]{1,0:T(8,128)S(1)} %pad_maximum_fusion.refs_0_), channel_id=1, source_target_pairs={{0,4},{4,0},{8,12},{12,8},{16,20},{20,16},{24,28},{28,24},{1,5},{5... | collective-permute-start | bytes 61448 | tf_op jit(solution)/shard_map/ppermute | solution.py:478
  41.7 4.9 %collective-permute-start.9 = (f32[40,128]{1,0:T(8,128)S(1)}, f32[40,128]{1,0:T(8,128)S(1)}, u32[]{:S(2)}, u32[]{:S(2)}) collective-permute-start(f32[40,128]{1,0:T(8,128)S(1)} %pad_maximum_fusion.refs_0_), channel_id=1, source_target_pairs={{0,8},{4,12},{8,0},{12,4},{16,24},{20,28},{24,16},{28,20},{1,9},{5... | collective-permute-start | bytes 61448 | tf_op jit(solution)/shard_map/ppermute | solution.py:478
  44.8 3.2 %collective-permute-start.10 = (f32[40,128]{1,0:T(8,128)S(1)}, f32[40,128]{1,0:T(8,128)S(1)}, u32[]{:S(2)}, u32[]{:S(2)}) collective-permute-start(f32[40,128]{1,0:T(8,128)S(1)} %pad_maximum_fusion.refs_0_), channel_id=1, source_target_pairs={{0,12},{4,8},{8,4},{12,0},{16,28},{20,24},{24,20},{28,16},{1,13},{... | collective-permute-start | bytes 61448 | tf_op jit(solution)/shard_map/ppermute | solution.py:478

commit v8 on v7

--- a/solution.py
+++ b/solution.py
@@ -393,10 +393,11 @@
 
 
 def merge_kernel(start, state_ref, *refs):
-    *parts, part_ref, square_ref, side_ref, sums_ref, mat_ref, inv_ref = refs
+    *parts, part_ref, square_ref, side_ref, sums_ref, small_ref, mat_ref, inv_ref, rows_ref, ends_ref = refs
     tile = state_ref.shape[1]
     tip = part_ref.shape[0]
-    last = jnp.where(lax.axis_index("tm") >= start, 1.0, 0.0).astype(F32)
+    position = lax.axis_index("tm")
+    last = jnp.where(position >= start, 1.0, 0.0).astype(F32)
 
     def run(refs):
         values, share, total = joined(state_ref, parts, range(GROUP), refs)
@@ -408,17 +409,27 @@
         sums_ref[...] = fold(part_ref[...] + share[0:tip, :] + last * own)
         return (total < SMALL) & (more < SMALL)
 
-    settled = run(None)
-
-    @pl.when(jnp.logical_not(settled))
-    def _():
-        run((mat_ref, inv_ref))
-
-
-def factor_kernel(tip, square_ref, side_ref, small_ref, mat_ref, inv_ref, rows_ref, ends_ref):
-    tile = square_ref.shape[-1]
+    @pl.when(position >= GROUP)
+    def _():
+        settled = run(None)
+
+        @pl.when(jnp.logical_not(settled))
+        def _():
+            run((mat_ref, inv_ref))
+
+    @pl.when(position < GROUP)
+    def _():
+        sums_ref[...] = fold(part_ref[...])
+        values = []
+        for n in range(GROUP):
+            diag, side = [third[...] if n == 2 else every[n] for every, third in zip(parts[0:4:3], parts[5:9:3])]
+            values.append(jnp.concatenate([diag, padded(side, tile).T], axis=1))
+        factored(tip, values, small_ref, (mat_ref, inv_ref), rows_ref, ends_ref)
+
+
+def factored(tip, values, small_ref, spare, rows_ref, ends_ref):
+    tile = values[0].shape[0]
     half = tile // 2
-    values = [jnp.concatenate([square_ref[n], side_ref[n]], axis=1) for n in range(GROUP)]
 
     def run(refs):
         uppers, lowers, total = halved(values, refs)
@@ -434,13 +445,26 @@
 
     @pl.when(jnp.logical_not(settled))
     def _():
-        run((mat_ref, inv_ref))
+        run(spare)
 
     pivots, column = factor((rows_ref, ends_ref), half, 2 * GROUP, tip)
     for n, value in enumerate((0.5 * jnp.log(pivots), column)):
         spot = slice(n * GROUP, (n + 1) * GROUP)
         small_ref[spot, 0:half] = value[0:GROUP, 0:half]
         small_ref[spot, half:] = value[GROUP:, 0:half]
+
+
+def factor_kernel(tip, square_ref, side_ref, early_ref, small_ref, mat_ref, inv_ref, rows_ref, ends_ref):
+    position = lax.axis_index("tm")
+
+    @pl.when(position >= GROUP)
+    def _():
+        values = [jnp.concatenate([square_ref[n], side_ref[n]], axis=1) for n in range(GROUP)]
+        factored(tip, values, small_ref, (mat_ref, inv_ref), rows_ref, ends_ref)
+
+    @pl.when(position < GROUP)
+    def _():
+        small_ref[...] = early_ref[...]
 
 
 def tip_kernel(prior_ref, *refs):
@@ -539,15 +563,15 @@
     if spans == 1:
         state = jnp.zeros_like(state)
     half = SUB * tile // 2
-    squares, sides, sums = call(
+    squares, sides, sums, small = call(
         functools.partial(merge_kernel, groups - GROUP),
         (state, *parts, part),
-        (square, square, (tip // 2, tile)),
-        pair,
+        (square, square, (tip // 2, tile), (2 * GROUP, tile)),
+        (*pair, (half, tile), (half, tile)),
     )
     (small,) = call(
         functools.partial(factor_kernel, tip),
-        (squares, sides),
+        (squares, sides, small),
         ((2 * GROUP, tile),),
         (*pair, (half, tile), (half, tile)),
     )

time: 51.5 us -> 48.5 us (0.942)
  Pallas kernels: 19.1 us -> 13.6 us
  waiting for transfers between devices: 11 us -> 12.8 us
  starting transfers between devices: 18 us -> 18.7 us
    pallas_call x5, Pallas kernels: 19.1 us -> 13.6 us  [call(): pl.pallas_call(body, out_shape=tuple((jax.ShapeDtypeStruct(shape, F32) fo...]
    ppermute x10, waiting for transfers between devices: 10.5 us -> 12.2 us  [crossed(): lax.ppermute(value, axis, [(source, source ^ step) for source in range(si...]
    ppermute x10, starting transfers between devices: 13.3 us -> 14 us  [crossed(): lax.ppermute(value, axis, [(source, source ^ step) for source in range(si...]
  transfers between devices with their start and end apart: 11 -> 11, of which waited for: 8 -> 9; matrix products, arithmetic and copies ran while one was open for 0% -> 0% of each run, Pallas kernels for 12% -> 3%
where the time goes in v8:
time: 48.5 us; the launch traced here: 48.3 us
  starting transfers between devices  18.7 us (39%)
  Pallas kernels  13.6 us (28%)
  waiting for transfers between devices  12.8 us (26%)
  between operations  1.44 us (3%)
  other arithmetic  0.93 us (2%)
  local copies, waits for them, and re-layouts  0.88 us (2%)
    ppermute x10, starting transfers between devices, crossed(): lax.ppermute(value, axis, [(source, source ^ step) for source in range(si...  14 us
    pallas_call x5, Pallas kernels, call(): pl.pallas_call(body, out_shape=tuple((jax.ShapeDtypeStruct(shape, F32) fo...  13.6 us
    ppermute x10, waiting for transfers between devices, crossed(): lax.ppermute(value, axis, [(source, source ^ step) for source in range(si...  12.2 us
    ppermute x1, starting transfers between devices, shards(): lax.ppermute(state, 'tm', [(source, source + GROUP) for source in range(g...  4.66 us
  transfers between devices with their start and end apart: 11, of which 9 were waited for; matrix products, arithmetic and copies ran while one was open for 0% of the time, Pallas kernels for 3%

profile of v8, /device:TPU:0, one launch (start us, length us, event | category | flops | bytes accessed | tf_op | source)
XLA Modules:
  0.0 48.3 jit_solution(13225769676690767121)
XLA Ops:
  1.3 0.0 copy-start
  1.3 0.9 %fusion = (f32[128]{0:T(128)S(1)}, f32[128,128]{1,0:T(8,128)S(1)}) fusion(f32[1,128,128]{2,1,0:T(8,128)} %param.10, f32[1,128,128]{2,1,0:T(8,128)} %param.9), kind=kLoop, calls=%fused_computation.2 | loop fusion | flops 81792 | bytes 197120 | tf_op jit(solution)/shard_map/reduce_sum | solution.py:534
  2.2 0.0 copy-start.1
  2.2 0.0 copy-done
  2.2 0.6 %copy-done.1 = f32[1,128]{1,0:T(1,128)S(1)} copy-done((f32[1,128]{1,0:T(1,128)S(1)}, f32[1,128]{1,0:T(1,128)}, u32[]{:S(2)}) %copy-start.1) | copy-done | bytes 536
  2.9 0.0 copy-start.5
  2.9 0.1 concatenate.10.own_ref
  3.0 0.0 copy-start.2
  3.0 0.0 copy-start.3
  3.0 0.0 copy-start.4
  3.1 3.1 %collective-permute-start.1 = (f32[208,128]{1,0:T(8,128)S(1)}, f32[208,128]{1,0:T(8,128)S(1)}, u32[]{:S(2)}, u32[]{:S(2)}) collective-permute-start(f32[208,128]{1,0:T(8,128)S(1)} %concatenate.10.own_ref), channel_id=1, source_target_pairs={{0,8},{4,12},{8,0},{12,4},{16,24},{20,28},{24,16},{28,20},{1,9},{5... | collective-permute-start | bytes 319496 | tf_op jit(solution)/shard_map/ppermute | solution.py:502
  6.1 0.0 collective-permute-start
  6.1 3.0 %collective-permute-done.1.two_ref = f32[208,128]{1,0:T(8,128)S(1)} collective-permute-done((f32[208,128]{1,0:T(8,128)S(1)}, f32[208,128]{1,0:T(8,128)S(1)}, u32[]{:S(2)}, u32[]{:S(2)}) %collective-permute-start.1) | collective-permute-done | bytes 106528 | tf_op jit(solution)/shard_map/ppermute | solution.py:502
  9.1 0.0 collective-permute-start.2
  9.1 0.0 copy-done.5
  9.1 0.0 copy-done.2
  9.1 0.0 copy-done.3
  9.1 0.0 copy-done.4
  9.2 0.1 concatenate.9
  9.2 0.0 collective-permute-done.one_ref
  9.2 1.2 %collective-permute-done.2.three_ref = f32[208,128]{1,0:T(8,128)S(1)} collective-permute-done((f32[208,128]{1,0:T(8,128)S(1)}, f32[208,128]{1,0:T(8,128)S(1)}, u32[]{:S(2)}, u32[]{:S(2)}) %collective-permute-start.2) | collective-permute-done | bytes 106528 | tf_op jit(solution)/shard_map/ppermute | solution.py:502
  10.4 4.1 %shard_map.120 = (f32[4,128,128]{2,1,0:T(8,128)S(1)}, f32[4,128,128]{2,1,0:T(8,128)S(1)}, f32[4,128,128]{2,1,0:T(8,128)S(1)}, f32[4,80,128]{2,1,0:T(8,128)S(1)},...) custom-call(f32[2,128]{1,0:T(2,128)S(1)} %bitcast.17, ...), custom_call_target="tpu_custom_call" | custom-call | tf_op jit(solution)/shard_map/pallas_call | solution.py:490
  14.5 4.7 %collective-permute-start.3 = (f32[152,128]{1,0:T(8,128)S(1)}, f32[152,128]{1,0:T(8,128)S(1)}, u32[]{:S(2)}, u32[]{:S(2)}) collective-permute-start(f32[152,128]{1,0:T(8,128)S(1)} %get-tuple-element.33), channel_id=1, source_target_pairs={{0,16},{4,20},{8,24},{12,28},{1,17},{5,21},{9,25},{13,29},{2,18},{... | collective-permute-start | bytes 233480 | tf_op jit(solution)/shard_map/ppermute | solution.py:560
  19.2 1.5 %shard_map.121 = (f32[128,128]{1,0:T(8,128)S(1)}, f32[128,128]{1,0:T(8,128)S(1)}, f32[128,128]{1,0:T(8,128)S(1)}, f32[80,128]{1,0:T(8,128)S(1)}, f32[80,128]{1,0:T(8,128)S(1)}, /*index=5*/f32[64,128]{1,0:T(8,128)S(1)}) custom-call(f32[2,128]{1,0:T(2,128)S(1)} %bitcast.18, f32[4,128,128]{2,1,0:T(8,128)S(1)} %get-tuple-element.27.refs_1_.refs_0_, ...), custom_call_target="tpu_custom_call" | custom-call | tf_op jit(solution)/shard_map/pallas_call | solution.py:490
  20.6 0.5 %collective-permute-done.3.state_ref = f32[152,128]{1,0:T(8,128)S(1)} collective-permute-done((f32[152,128]{1,0:T(8,128)S(1)}, f32[152,128]{1,0:T(8,128)S(1)}, u32[]{:S(2)}, u32[]{:S(2)}) %collective-permute-start.3) | collective-permute-done | bytes 77856 | tf_op jit(solution)/shard_map/ppermute | solution.py:560
  21.2 4.8 %shard_map.122 = (f32[4,128,128]{2,1,0:T(8,128)S(1)}, f32[4,128,128]{2,1,0:T(8,128)S(1)}, f32[32,128]{1,0:T(8,128)S(1)}, f32[8,128]{1,0:T(8,128)S(1)}) custom-call(f32[152,128]{1,0:T(8,128)S(1)} %collective-permute-done.3.state_ref, f32[4,128,128]{2,1,0:T(8,128)S(1)} %get-tuple-element.27.refs_1_.refs_0_, ...), custom_call_target="tpu_custom_call" | custom-call | tf_op jit(solution)/shard_map/pallas_call | solution.py:490
  26.0 4.2 %collective-permute-start.4 = (f32[32,128]{1,0:T(8,128)S(1)}, f32[32,128]{1,0:T(8,128)S(1)}, u32[]{:S(2)}, u32[]{:S(2)}) collective-permute-start(f32[32,128]{1,0:T(8,128)S(1)} %get-tuple-element.40), channel_id=1, source_target_pairs={{0,16},{4,20},{8,24},{12,28},{16,0},{20,4},{24,8},{28,12},{1,17},{... | collective-permute-start | bytes 49160 | tf_op jit(solution)/shard_map/ppermute | solution.py:502
  30.2 1.7 %collective-permute-done.4 = f32[32,128]{1,0:T(8,128)S(1)} collective-permute-done((f32[32,128]{1,0:T(8,128)S(1)}, f32[32,128]{1,0:T(8,128)S(1)}, u32[]{:S(2)}, u32[]{:S(2)}) %collective-permute-start.4) | collective-permute-done | bytes 16416 | tf_op jit(solution)/shard_map/ppermute | solution.py:502
  31.9 1.5 %collective-permute-start.6 = (f32[32,128]{1,0:T(8,128)S(1)}, f32[32,128]{1,0:T(8,128)S(1)}, u32[]{:S(2)}, u32[]{:S(2)}) collective-permute-start(f32[32,128]{1,0:T(8,128)S(1)} %add.12), channel_id=1, source_target_pairs={{0,2},{1,3},{2,0},{3,1},{4,6},{5,7},{6,4},{7,5},{8,10},{9,11},{10,... | collective-permute-start | bytes 49160 | tf_op jit(solution)/shard_map/ppermute | solution.py:502
  33.4 1.4 %collective-permute-start.7 = (f32[32,128]{1,0:T(8,128)S(1)}, f32[32,128]{1,0:T(8,128)S(1)}, u32[]{:S(2)}, u32[]{:S(2)}) collective-permute-start(f32[32,128]{1,0:T(8,128)S(1)} %add.12), channel_id=1, source_target_pairs={{0,3},{1,2},{2,1},{3,0},{4,7},{5,6},{6,5},{7,4},{8,11},{9,10},{10,... | collective-permute-start | bytes 49160 | tf_op jit(solution)/shard_map/ppermute | solution.py:502
  34.9 0.5 %collective-permute-start.5 = (f32[32,128]{1,0:T(8,128)S(1)}, f32[32,128]{1,0:T(8,128)S(1)}, u32[]{:S(2)}, u32[]{:S(2)}) collective-permute-start(f32[32,128]{1,0:T(8,128)S(1)} %add.12), channel_id=1, source_target_pairs={{0,1},{1,0},{2,3},{3,2},{4,5},{5,4},{6,7},{7,6},{8,9},{9,8},{10,11... | collective-permute-start | bytes 49160 | tf_op jit(solution)/shard_map/ppermute | solution.py:502
  35.4 0.2 collective-permute-done.6
  35.6 2.4 %collective-permute-done.7 = f32[32,128]{1,0:T(8,128)S(1)} collective-permute-done((f32[32,128]{1,0:T(8,128)S(1)}, f32[32,128]{1,0:T(8,128)S(1)}, u32[]{:S(2)}, u32[]{:S(2)}) %collective-permute-start.7) | collective-permute-done | bytes 16416 | tf_op jit(solution)/shard_map/ppermute | solution.py:502
  38.1 0.5 %collective-permute-done.5 = f32[32,128]{1,0:T(8,128)S(1)} collective-permute-done((f32[32,128]{1,0:T(8,128)S(1)}, f32[32,128]{1,0:T(8,128)S(1)}, u32[]{:S(2)}, u32[]{:S(2)}) %collective-permute-start.5) | collective-permute-done | bytes 16416 | tf_op jit(solution)/shard_map/ppermute | solution.py:502
  38.6 0.1 collective-permute-start.8
  38.7 3.1 %collective-permute-start.9 = (f32[40,128]{1,0:T(8,128)S(1)}, f32[40,128]{1,0:T(8,128)S(1)}, u32[]{:S(2)}, u32[]{:S(2)}) collective-permute-start(f32[40,128]{1,0:T(8,128)S(1)} %pad_maximum_fusion.refs_0_), channel_id=1, source_target_pairs={{0,8},{4,12},{8,0},{12,4},{16,24},{20,28},{24,16},{28,20},{1,9},{5... | collective-permute-start | bytes 61448 | tf_op jit(solution)/shard_map/ppermute | solution.py:502
  41.8 0.1 collective-permute-start.10
  41.9 0.0 collective-permute-done.8.refs_1_
  41.9 1.7 %collective-permute-done.9.refs_2_ = f32[40,128]{1,0:T(8,128)S(1)} collective-permute-done((f32[40,128]{1,0:T(8,128)S(1)}, f32[40,128]{1,0:T(8,128)S(1)}, u32[]{:S(2)}, u32[]{:S(2)}) %collective-permute-start.9) | collective-permute-done | bytes 20512 | tf_op jit(solution)/shard_map/ppermute | solution.py:502
  43.5 1.4 %collective-permute-done.10.refs_3_ = f32[40,128]{1,0:T(8,128)S(1)} collective-permute-done((f32[40,128]{1,0:T(8,128)S(1)}, f32[40,128]{1,0:T(8,128)S(1)}, u32[]{:S(2)}, u32[]{:S(2)}) %collective-permute-start.10) | collective-permute-done | bytes 20512 | tf_op jit(solution)/shard_map/ppermute | solution.py:502
  45.0 3.3 %shard_map.124 = (f32[4,128]{1,0:T(4,128)}, f32[4,128]{1,0:T(4,128)}, f32[4,64]{1,0:T(4,128)}, f32[4,64]{1,0:T(4,128)}) custom-call(f32[64,128]{1,0:T(8,128)S(1)} %get-tuple-element.32.prior_ref, f32[40,128]{1,0:T(8,128)S(1)} %pad_maximum_fusion.refs_0_, f32[40,128]{1,0:T(8,128)S(1)} %collective-permute-done.8.refs_1_, ...), custom_call_target="tpu_custom_call" | custom-call | tf_op jit(solution)/shard_map/pallas_call | solution.py:490
  (7 shorter events, 0.0 us)
Async XLA Ops:
  1.3 1.0 %copy-start = (f32[1,64,128]{2,1,0:T(8,128)S(1)}, f32[1,64,128]{2,1,0:T(8,128)}, u32[]{:S(2)}) copy-start(f32[1,64,128]{2,1,0:T(8,128)} %param.11) | copy-start | bytes 98308
  2.2 0.7 %copy-start.1 = (f32[1,128]{1,0:T(1,128)S(1)}, f32[1,128]{1,0:T(1,128)}, u32[]{:S(2)}) copy-start(f32[1,128]{1,0:T(1,128)} %param.12) | copy-start | bytes 1540
  2.9 6.2 %copy-start.5 = (f32[4]{0:T(128)S(1)}, f32[4]{0:T(128)}, u32[]{:S(2)}) copy-start(f32[4]{0:T(128)} %param.16) | copy-start | bytes 52
  3.0 6.1 %copy-start.2 = (f32[64]{0:T(128)S(1)}, f32[64]{0:T(128)}, u32[]{:S(2)}) copy-start(f32[64]{0:T(128)} %param.14) | copy-start | bytes 772
  3.0 6.1 %copy-start.3 = (f32[64]{0:T(128)S(1)}, f32[64]{0:T(128)}, u32[]{:S(2)}) copy-start(f32[64]{0:T(128)} %param.13) | copy-start | bytes 772
  3.0 6.1 %copy-start.4 = (f32[4]{0:T(128)S(1)}, f32[4]{0:T(128)}, u32[]{:S(2)}) copy-start(f32[4]{0:T(128)} %param.15) | copy-start | bytes 52
  3.1 6.1 %collective-permute-start.1 = (f32[208,128]{1,0:T(8,128)S(1)}, f32[208,128]{1,0:T(8,128)S(1)}, u32[]{:S(2)}, u32[]{:S(2)}) collective-permute-start(f32[208,128]{1,0:T(8,128)S(1)} %concatenate.10.own_ref), channel_id=1, source_target_pairs={{0,8},{4,12},{8,0},{12,4},{16,24},{20,28},{24,16},{28,20},{1,9},{5... | collective-permute-start | bytes 319496 | tf_op jit(solution)/shard_map/ppermute | solution.py:502
  6.1 3.1 %collective-permute-start = (f32[208,128]{1,0:T(8,128)S(1)}, f32[208,128]{1,0:T(8,128)S(1)}, u32[]{:S(2)}, u32[]{:S(2)}) collective-permute-start(f32[208,128]{1,0:T(8,128)S(1)} %concatenate.10.own_ref), channel_id=1, source_target_pairs={{0,4},{4,0},{8,12},{12,8},{16,20},{20,16},{24,28},{28,24},{1,5},{5... | collective-permute-start | bytes 319496 | tf_op jit(solution)/shard_map/ppermute | solution.py:502
  9.1 1.3 %collective-permute-start.2 = (f32[208,128]{1,0:T(8,128)S(1)}, f32[208,128]{1,0:T(8,128)S(1)}, u32[]{:S(2)}, u32[]{:S(2)}) collective-permute-start(f32[208,128]{1,0:T(8,128)S(1)} %collective-permute-done.1.two_ref), channel_id=1, source_target_pairs={{0,4},{4,0},{8,12},{12,8},{16,20},{20,16},{24,28},{28,24},{1,5},{5... | collective-permute-start | bytes 319496 | tf_op jit(solution)/shard_map/ppermute | solution.py:502
  14.5 6.7 %collective-permute-start.3 = (f32[152,128]{1,0:T(8,128)S(1)}, f32[152,128]{1,0:T(8,128)S(1)}, u32[]{:S(2)}, u32[]{:S(2)}) collective-permute-start(f32[152,128]{1,0:T(8,128)S(1)} %get-tuple-element.33), channel_id=1, source_target_pairs={{0,16},{4,20},{8,24},{12,28},{1,17},{5,21},{9,25},{13,29},{2,18},{... | collective-permute-start | bytes 233480 | tf_op jit(solution)/shard_map/ppermute | solution.py:560
  26.0 5.9 %collective-permute-start.4 = (f32[32,128]{1,0:T(8,128)S(1)}, f32[32,128]{1,0:T(8,128)S(1)}, u32[]{:S(2)}, u32[]{:S(2)}) collective-permute-start(f32[32,128]{1,0:T(8,128)S(1)} %get-tuple-element.40), channel_id=1, source_target_pairs={{0,16},{4,20},{8,24},{12,28},{16,0},{20,4},{24,8},{28,12},{1,17},{... | collective-permute-start | bytes 49160 | tf_op jit(solution)/shard_map/ppermute | solution.py:502
  31.9 3.7 %collective-permute-start.6 = (f32[32,128]{1,0:T(8,128)S(1)}, f32[32,128]{1,0:T(8,128)S(1)}, u32[]{:S(2)}, u32[]{:S(2)}) collective-permute-start(f32[32,128]{1,0:T(8,128)S(1)} %add.12), channel_id=1, source_target_pairs={{0,2},{1,3},{2,0},{3,1},{4,6},{5,7},{6,4},{7,5},{8,10},{9,11},{10,... | collective-permute-start | bytes 49160 | tf_op jit(solution)/shard_map/ppermute | solution.py:502
  33.4 4.6 %collective-permute-start.7 = (f32[32,128]{1,0:T(8,128)S(1)}, f32[32,128]{1,0:T(8,128)S(1)}, u32[]{:S(2)}, u32[]{:S(2)}) collective-permute-start(f32[32,128]{1,0:T(8,128)S(1)} %add.12), channel_id=1, source_target_pairs={{0,3},{1,2},{2,1},{3,0},{4,7},{5,6},{6,5},{7,4},{8,11},{9,10},{10,... | collective-permute-start | bytes 49160 | tf_op jit(solution)/shard_map/ppermute | solution.py:502
  34.9 3.7 %collective-permute-start.5 = (f32[32,128]{1,0:T(8,128)S(1)}, f32[32,128]{1,0:T(8,128)S(1)}, u32[]{:S(2)}, u32[]{:S(2)}) collective-permute-start(f32[32,128]{1,0:T(8,128)S(1)} %add.12), channel_id=1, source_target_pairs={{0,1},{1,0},{2,3},{3,2},{4,5},{5,4},{6,7},{7,6},{8,9},{9,8},{10,11... | collective-permute-start | bytes 49160 | tf_op jit(solution)/shard_map/ppermute | solution.py:502
  38.6 3.2 %collective-permute-start.8 = (f32[40,128]{1,0:T(8,128)S(1)}, f32[40,128]{1,0:T(8,128)S(1)}, u32[]{:S(2)}, u32[]{:S(2)}) collective-permute-start(f32[40,128]{1,0:T(8,128)S(1)} %pad_maximum_fusion.refs_0_), channel_id=1, source_target_pairs={{0,4},{4,0},{8,12},{12,8},{16,20},{20,16},{24,28},{28,24},{1,5},{5... | collective-permute-start | bytes 61448 | tf_op jit(solution)/shard_map/ppermute | solution.py:502
  38.7 4.9 %collective-permute-start.9 = (f32[40,128]{1,0:T(8,128)S(1)}, f32[40,128]{1,0:T(8,128)S(1)}, u32[]{:S(2)}, u32[]{:S(2)}) collective-permute-start(f32[40,128]{1,0:T(8,128)S(1)} %pad_maximum_fusion.refs_0_), channel_id=1, source_target_pairs={{0,8},{4,12},{8,0},{12,4},{16,24},{20,28},{24,16},{28,20},{1,9},{5... | collective-permute-start | bytes 61448 | tf_op jit(solution)/shard_map/ppermute | solution.py:502
  41.8 3.2 %collective-permute-start.10 = (f32[40,128]{1,0:T(8,128)S(1)}, f32[40,128]{1,0:T(8,128)S(1)}, u32[]{:S(2)}, u32[]{:S(2)}) collective-permute-start(f32[40,128]{1,0:T(8,128)S(1)} %pad_maximum_fusion.refs_0_), channel_id=1, source_target_pairs={{0,12},{4,8},{8,4},{12,0},{16,28},{20,24},{24,20},{28,16},{1,13},{... | collective-permute-start | bytes 61448 | tf_op jit(solution)/shard_map/ppermute | solution.py:502

commit v9 on v8

--- a/solution.py
+++ b/solution.py
@@ -91,7 +91,8 @@
     results = []
     if refs:
         for mat, left, right in zip(mats, lefts, rights):
-            results.append(fine(fine(left, converged(mat, *refs)), right, dims))
+            first = fine(left, converged(mat, *refs))
+            results.append((fine(first, right, dims), first))
         return results, jnp.float32(0.0)
     eye = identity(mats[0].shape[-1])
     starts = [series(mat, factors) for mat in mats]
@@ -102,7 +103,7 @@
         low = rest.astype(BF16)
         twice = product(low, low)
         first = first + fine(first, rest + twice)
-        results.append(fine(first, right, dims))
+        results.append((fine(first, right, dims), first))
         linear = linear + rest * rest
         square = square + twice * twice
     return results, jnp.sum(linear) * jnp.sum(square)
@@ -152,10 +153,14 @@
         right.append(jnp.where(used, raw_ref[n, tile:, :], 0.0))
     one, two, end = slice(0, tile), slice(tile, 2 * tile), slice(2 * tile, None)
 
+    def share(first, middle):
+        return fine(first[2 * tile : 2 * tile + tip, :], padded(middle, tile), NT)
+
     def run(refs):
         low = jnp.concatenate([cross[1], cross[0], right[0]], axis=0)
         high = jnp.concatenate([cross[3], cross[2], right[2]], axis=0)
-        (gram, gram23), total = quotients((diag[0], diag[2]), (low, high), (low, high), 4, refs)
+        lefts, rights = (low, high), (low[0 : 2 * tile, :], high[0 : 2 * tile, :])
+        ((gram, first), (gram23, first23)), total = quotients((diag[0], diag[2]), lefts, rights, 4, refs)
         diag01 = diag[1] - gram[one, one]
         cross01 = -gram[one, two]
         cross01_t = -gram[two, one]
@@ -168,14 +173,14 @@
         right23 = right[3] - gram23[end, one]
         left23 = -gram23[end, two]
 
-        part = gram[end, end] + gram23[end, end]
-        rows = jnp.concatenate([cross23, cross01_t, right01 + left23], axis=0)
-        (gram,), more = quotients((diag01 + back23,), (rows,), (rows,), 4, refs)
+        part = share(first, right[0]) + share(first23, right[2])
+        middle = right01 + left23
+        rows = jnp.concatenate([cross23, cross01_t, middle], axis=0)
+        ((gram, first),), more = quotients((diag01 + back23,), (rows,), (rows[0 : 2 * tile, :],), 4, refs)
         diag03 = diag23 - gram[one, one]
         right03 = right23 - gram[end, one]
         send(state_ref, diag03, right03)
-        part = (part + gram[end, end])[0:tip, :]
-        part_ref[...] = jnp.concatenate([part, jnp.zeros((tip, tile - part.shape[1]), F32)], axis=1)
+        part_ref[...] = part + share(first, middle)
         for n, value in enumerate((diag[0], diag01, diag[2], diag03)):
             diag_ref[n] = value
         for n, value in enumerate((cross[0], cross01, cross[2], -gram[one, two])):
@@ -205,7 +210,7 @@
     rows = jnp.concatenate([cross_ref[2], cross_ref[1].T, right_ref[1]], axis=0)
 
     def run(refs):
-        (gram,), total = quotients((diag_ref[1],), (rows,), (rows,), 4, refs)
+        ((gram, _),), total = quotients((diag_ref[1],), (rows,), (rows[0 : 2 * tile, :],), 4, refs)
         values = (
             diag_ref[2] - gram[one, one],
             -gram[one, two],
@@ -282,10 +287,10 @@
     rights = [jnp.concatenate([cross, middle], axis=0) for cross, middle in zip(crosses, middles)]
     updates, total = quotients(mats, crosses[:-1] + rights[-1:], rights, 5, refs)
     results = []
-    for diag, side, update in zip(diags, sides, updates):
+    for diag, side, (update, _) in zip(diags, sides, updates):
         start = jnp.concatenate([diag, padded(side, tile).T], axis=1)
         results.append(start - update[0:tile, :])
-    return results, updates[-1][tile:, tile:], total
+    return results, updates[-1][0][tile:, tile:], total
 
 
 def advance_kernel(state_ref, *refs):
@@ -368,7 +373,7 @@
     lowers = []
     for place, value in enumerate(values):
         first = (place % 2) * half
-        lowers.append(value[half:, :] - updates[place // 2][first : first + half, :])
+        lowers.append(value[half:, :] - updates[place // 2][0][first : first + half, :])
     return uppers, lowers, total
 
 
@@ -405,7 +410,7 @@
             square_ref[n] = value[:, 0:tile]
             side_ref[n] = value[:, tile:]
         side = values[-1][:, tile:].T
-        (own,), more = quotients((values[-1][:, 0:tile],), (side[0:tip, :],), (side,), 5, refs)
+        ((own, _),), more = quotients((values[-1][:, 0:tile],), (side[0:tip, :],), (side,), 5, refs)
         sums_ref[...] = fold(part_ref[...] + share[0:tip, :] + last * own)
         return (total < SMALL) & (more < SMALL)
 
@@ -472,8 +477,10 @@
     tip = prior_ref.shape[0]
     mid = tip // 2
     node = lax.axis_index("tm") & (GROUP - 1)
+    count = all_ref.shape[1]
     for step, ref in enumerate(came):
-        all_ref[node ^ step] = ref[...]
+        all_ref[node ^ step] = ref[0:count, :]
+        all_ref[node ^ step ^ 2] = ref[count:, :]
     for n in range(GROUP):
         top, bottom = unfold(all_ref[n, 0:mid, :])
         rows_ref[pl.ds(n, mid, stride=SUB), :] = prior_ref[0:mid, :] - top
@@ -581,13 +588,15 @@
             sums = sums + crossed(sums, axis, step)
             step *= 2
     sums, small = lax.optimization_barrier((sums, small))
-    sums = (sums + crossed(sums, "mesh", 1)) + (crossed(sums, "mesh", 2) + crossed(sums, "mesh", 3))
+    for step in (1, 2):
+        sums = sums + crossed(sums, "mesh", step)
     found = jnp.concatenate([sums, small], axis=0)
+    found = jnp.concatenate([found, crossed(found, "tm", 2)], axis=0)
     log_diag, solved, tip_log, tip_forward = call(
         tip_kernel,
-        (prior, found) + tuple(crossed(found, "tm", n) for n in range(1, 4)),
+        (prior, found, crossed(found, "tm", 1)),
         ((GROUP, tile), (GROUP, tile), (GROUP, tip), (GROUP, tip)),
-        ((GROUP,) + found.shape, (SUB * tip, tile)),
+        ((GROUP, found.shape[0] // 2, tile), (SUB * tip, tile)),
     )
     return (log_diag[:, None, :], solved[:, None, :], tip_log, tip_forward)
 

time: 48.5 us -> 48.8 us (level)
  waiting for transfers between devices: 12.8 us -> 13.9 us
  starting transfers between devices: 18.7 us -> 18.1 us
    ppermute x10 -> x8, waiting for transfers between devices: 12.2 us -> 13.3 us  [crossed(): lax.ppermute(value, axis, [(source, source ^ step) for source in range(si...]
    ppermute x10 -> x8, starting transfers between devices: 14 us -> 13.4 us  [crossed(): lax.ppermute(value, axis, [(source, source ^ step) for source in range(si...]
  transfers between devices with their start and end apart: 11 -> 9, of which waited for: 9 -> 8; matrix products, arithmetic and copies ran while one was open for 0% -> 0% of each run, Pallas kernels for 3% -> 3%
where the time goes in v9:
time: 48.8 us; the launch traced here: 48.6 us
  starting transfers between devices  18.1 us (37%)
  waiting for transfers between devices  13.9 us (28%)
  Pallas kernels  13.4 us (27%)
  between operations  1.42 us (3%)
  other arithmetic  0.93 us (2%)
  local copies, waits for them, and re-layouts  0.88 us (2%)
    ppermute x8, starting transfers between devices, crossed(): lax.ppermute(value, axis, [(source, source ^ step) for source in range(si...  13.4 us
    pallas_call x5, Pallas kernels, call(): pl.pallas_call(body, out_shape=tuple((jax.ShapeDtypeStruct(shape, F32) fo...  13.4 us
    ppermute x8, waiting for transfers between devices, crossed(): lax.ppermute(value, axis, [(source, source ^ step) for source in range(si...  13.3 us
    ppermute x1, starting transfers between devices, shards(): lax.ppermute(state, 'tm', [(source, source + GROUP) for source in range(g...  4.66 us
  transfers between devices with their start and end apart: 9, of which 8 were waited for; matrix products, arithmetic and copies ran while one was open for 0% of the time, Pallas kernels for 3%

profile of v9, /device:TPU:0, one launch (start us, length us, event | category | flops | bytes accessed | tf_op | source)
XLA Modules:
  0.0 48.6 jit_solution(1271451965181633499)
XLA Ops:
  1.3 0.0 copy-start
  1.3 0.9 %fusion = (f32[128]{0:T(128)S(1)}, f32[128,128]{1,0:T(8,128)S(1)}) fusion(f32[1,128,128]{2,1,0:T(8,128)} %param.10, f32[1,128,128]{2,1,0:T(8,128)} %param.9), kind=kLoop, calls=%fused_computation.2 | loop fusion | flops 81792 | bytes 197120 | tf_op jit(solution)/shard_map/reduce_sum | solution.py:541
  2.2 0.0 copy-start.1
  2.2 0.0 copy-done
  2.2 0.6 %copy-done.1 = f32[1,128]{1,0:T(1,128)S(1)} copy-done((f32[1,128]{1,0:T(1,128)S(1)}, f32[1,128]{1,0:T(1,128)}, u32[]{:S(2)}) %copy-start.1) | copy-done | bytes 536
  2.9 0.0 copy-start.5
  2.9 0.1 concatenate.14.own_ref
  3.0 0.0 copy-start.2
  3.0 0.0 copy-start.3
  3.0 0.0 copy-start.4
  3.1 3.1 %collective-permute-start.1 = (f32[208,128]{1,0:T(8,128)S(1)}, f32[208,128]{1,0:T(8,128)S(1)}, u32[]{:S(2)}, u32[]{:S(2)}) collective-permute-start(f32[208,128]{1,0:T(8,128)S(1)} %concatenate.14.own_ref), channel_id=1, source_target_pairs={{0,8},{4,12},{8,0},{12,4},{16,24},{20,28},{24,16},{28,20},{1,9},{5... | collective-permute-start | bytes 319496 | tf_op jit(solution)/shard_map/ppermute | solution.py:509
  6.1 0.0 collective-permute-start
  6.1 3.0 %collective-permute-done.1.two_ref = f32[208,128]{1,0:T(8,128)S(1)} collective-permute-done((f32[208,128]{1,0:T(8,128)S(1)}, f32[208,128]{1,0:T(8,128)S(1)}, u32[]{:S(2)}, u32[]{:S(2)}) %collective-permute-start.1) | collective-permute-done | bytes 106528 | tf_op jit(solution)/shard_map/ppermute | solution.py:509
  9.1 0.0 collective-permute-start.2
  9.1 0.0 copy-done.5
  9.1 0.0 copy-done.2
  9.1 0.0 copy-done.3
  9.1 0.0 copy-done.4
  9.2 0.1 concatenate.13
  9.2 0.0 collective-permute-done.one_ref
  9.2 1.2 %collective-permute-done.2.three_ref = f32[208,128]{1,0:T(8,128)S(1)} collective-permute-done((f32[208,128]{1,0:T(8,128)S(1)}, f32[208,128]{1,0:T(8,128)S(1)}, u32[]{:S(2)}, u32[]{:S(2)}) %collective-permute-start.2) | collective-permute-done | bytes 106528 | tf_op jit(solution)/shard_map/ppermute | solution.py:509
  10.4 3.9 %shard_map.120 = (f32[4,128,128]{2,1,0:T(8,128)S(1)}, f32[4,128,128]{2,1,0:T(8,128)S(1)}, f32[4,128,128]{2,1,0:T(8,128)S(1)}, f32[4,80,128]{2,1,0:T(8,128)S(1)},...) custom-call(f32[2,128]{1,0:T(2,128)S(1)} %bitcast.17, ...), custom_call_target="tpu_custom_call" | custom-call | tf_op jit(solution)/shard_map/pallas_call | solution.py:497
  14.3 4.7 %collective-permute-start.3 = (f32[152,128]{1,0:T(8,128)S(1)}, f32[152,128]{1,0:T(8,128)S(1)}, u32[]{:S(2)}, u32[]{:S(2)}) collective-permute-start(f32[152,128]{1,0:T(8,128)S(1)} %get-tuple-element.33), channel_id=1, source_target_pairs={{0,16},{4,20},{8,24},{12,28},{1,17},{5,21},{9,25},{13,29},{2,18},{... | collective-permute-start | bytes 233480 | tf_op jit(solution)/shard_map/ppermute | solution.py:567
  19.0 1.5 %shard_map.121 = (f32[128,128]{1,0:T(8,128)S(1)}, f32[128,128]{1,0:T(8,128)S(1)}, f32[128,128]{1,0:T(8,128)S(1)}, f32[80,128]{1,0:T(8,128)S(1)}, f32[80,128]{1,0:T(8,128)S(1)}, /*index=5*/f32[64,128]{1,0:T(8,128)S(1)}) custom-call(f32[2,128]{1,0:T(2,128)S(1)} %bitcast.18, f32[4,128,128]{2,1,0:T(8,128)S(1)} %get-tuple-element.27.refs_1_.refs_0_, ...), custom_call_target="tpu_custom_call" | custom-call | tf_op jit(solution)/shard_map/pallas_call | solution.py:497
  20.4 0.5 %collective-permute-done.3.state_ref = f32[152,128]{1,0:T(8,128)S(1)} collective-permute-done((f32[152,128]{1,0:T(8,128)S(1)}, f32[152,128]{1,0:T(8,128)S(1)}, u32[]{:S(2)}, u32[]{:S(2)}) %collective-permute-start.3) | collective-permute-done | bytes 77856 | tf_op jit(solution)/shard_map/ppermute | solution.py:567
  21.0 4.8 %shard_map.122 = (f32[4,128,128]{2,1,0:T(8,128)S(1)}, f32[4,128,128]{2,1,0:T(8,128)S(1)}, f32[32,128]{1,0:T(8,128)S(1)}, f32[8,128]{1,0:T(8,128)S(1)}) custom-call(f32[152,128]{1,0:T(8,128)S(1)} %collective-permute-done.3.state_ref, f32[4,128,128]{2,1,0:T(8,128)S(1)} %get-tuple-element.27.refs_1_.refs_0_, ...), custom_call_target="tpu_custom_call" | custom-call | tf_op jit(solution)/shard_map/pallas_call | solution.py:497
  25.7 4.2 %collective-permute-start.4 = (f32[32,128]{1,0:T(8,128)S(1)}, f32[32,128]{1,0:T(8,128)S(1)}, u32[]{:S(2)}, u32[]{:S(2)}) collective-permute-start(f32[32,128]{1,0:T(8,128)S(1)} %get-tuple-element.40), channel_id=1, source_target_pairs={{0,16},{4,20},{8,24},{12,28},{16,0},{20,4},{24,8},{28,12},{1,17},{... | collective-permute-start | bytes 49160 | tf_op jit(solution)/shard_map/ppermute | solution.py:509
  30.0 1.7 %collective-permute-done.4 = f32[32,128]{1,0:T(8,128)S(1)} collective-permute-done((f32[32,128]{1,0:T(8,128)S(1)}, f32[32,128]{1,0:T(8,128)S(1)}, u32[]{:S(2)}, u32[]{:S(2)}) %collective-permute-start.4) | collective-permute-done | bytes 16416 | tf_op jit(solution)/shard_map/ppermute | solution.py:509
  31.7 1.5 %collective-permute-start.5 = (f32[32,128]{1,0:T(8,128)S(1)}, f32[32,128]{1,0:T(8,128)S(1)}, u32[]{:S(2)}, u32[]{:S(2)}) collective-permute-start(f32[32,128]{1,0:T(8,128)S(1)} %add.9), channel_id=1, source_target_pairs={{0,1},{1,0},{2,3},{3,2},{4,5},{5,4},{6,7},{7,6},{8,9},{9,8},{10,11... | collective-permute-start | bytes 49160 | tf_op jit(solution)/shard_map/ppermute | solution.py:509
  33.2 2.2 %collective-permute-done.5 = f32[32,128]{1,0:T(8,128)S(1)} collective-permute-done((f32[32,128]{1,0:T(8,128)S(1)}, f32[32,128]{1,0:T(8,128)S(1)}, u32[]{:S(2)}, u32[]{:S(2)}) %collective-permute-start.5) | collective-permute-done | bytes 16416 | tf_op jit(solution)/shard_map/ppermute | solution.py:509
  35.4 1.5 %collective-permute-start.6 = (f32[32,128]{1,0:T(8,128)S(1)}, f32[32,128]{1,0:T(8,128)S(1)}, u32[]{:S(2)}, u32[]{:S(2)}) collective-permute-start(f32[32,128]{1,0:T(8,128)S(1)} %add.10), channel_id=1, source_target_pairs={{0,2},{1,3},{2,0},{3,1},{4,6},{5,7},{6,4},{7,5},{8,10},{9,11},{10,... | collective-permute-start | bytes 49160 | tf_op jit(solution)/shard_map/ppermute | solution.py:509
  36.9 2.2 %collective-permute-done.6 = f32[32,128]{1,0:T(8,128)S(1)} collective-permute-done((f32[32,128]{1,0:T(8,128)S(1)}, f32[32,128]{1,0:T(8,128)S(1)}, u32[]{:S(2)}, u32[]{:S(2)}) %collective-permute-start.6) | collective-permute-done | bytes 16416 | tf_op jit(solution)/shard_map/ppermute | solution.py:509
  39.2 3.1 %collective-permute-start.7 = (f32[40,128]{1,0:T(8,128)S(1)}, f32[40,128]{1,0:T(8,128)S(1)}, u32[]{:S(2)}, u32[]{:S(2)}) collective-permute-start(f32[40,128]{1,0:T(8,128)S(1)} %pad_maximum_fusion.1), channel_id=1, source_target_pairs={{0,8},{4,12},{8,0},{12,4},{16,24},{20,28},{24,16},{28,20},{1,9},{5... | collective-permute-start | bytes 61448 | tf_op jit(solution)/shard_map/ppermute | solution.py:509
  42.3 1.8 %collective-permute-done.7 = f32[40,128]{1,0:T(8,128)S(1)} collective-permute-done((f32[40,128]{1,0:T(8,128)S(1)}, f32[40,128]{1,0:T(8,128)S(1)}, u32[]{:S(2)}, u32[]{:S(2)}) %collective-permute-start.7) | collective-permute-done | bytes 20512 | tf_op jit(solution)/shard_map/ppermute | solution.py:509
  44.0 0.0 collective-permute-start.8
  44.0 1.2 %collective-permute-done.8.refs_1_ = f32[80,128]{1,0:T(8,128)S(1)} collective-permute-done((f32[80,128]{1,0:T(8,128)S(1)}, f32[80,128]{1,0:T(8,128)S(1)}, u32[]{:S(2)}, u32[]{:S(2)}) %collective-permute-start.8) | collective-permute-done | bytes 40992 | tf_op jit(solution)/shard_map/ppermute | solution.py:509
  45.3 3.3 %shard_map.124 = (f32[4,128]{1,0:T(4,128)}, f32[4,128]{1,0:T(4,128)}, f32[4,64]{1,0:T(4,128)}, f32[4,64]{1,0:T(4,128)}) custom-call(f32[64,128]{1,0:T(8,128)S(1)} %get-tuple-element.32.prior_ref, f32[80,128]{1,0:T(8,128)S(1)} %pad_maximum_fusion.refs_0_, f32[80,128]{1,0:T(8,128)S(1)} %collective-permute-done.8.refs_1_), custom_call_target="tpu_custom_call" | custom-call | tf_op jit(solution)/shard_map/pallas_call | solution.py:497
  (9 shorter events, 0.0 us)
Async XLA Ops:
  1.3 1.0 %copy-start = (f32[1,64,128]{2,1,0:T(8,128)S(1)}, f32[1,64,128]{2,1,0:T(8,128)}, u32[]{:S(2)}) copy-start(f32[1,64,128]{2,1,0:T(8,128)} %param.11) | copy-start | bytes 98308
  2.2 0.7 %copy-start.1 = (f32[1,128]{1,0:T(1,128)S(1)}, f32[1,128]{1,0:T(1,128)}, u32[]{:S(2)}) copy-start(f32[1,128]{1,0:T(1,128)} %param.12) | copy-start | bytes 1540
  2.9 6.2 %copy-start.5 = (f32[4]{0:T(128)S(1)}, f32[4]{0:T(128)}, u32[]{:S(2)}) copy-start(f32[4]{0:T(128)} %param.16) | copy-start | bytes 52
  3.0 6.1 %copy-start.2 = (f32[64]{0:T(128)S(1)}, f32[64]{0:T(128)}, u32[]{:S(2)}) copy-start(f32[64]{0:T(128)} %param.14) | copy-start | bytes 772
  3.0 6.1 %copy-start.3 = (f32[64]{0:T(128)S(1)}, f32[64]{0:T(128)}, u32[]{:S(2)}) copy-start(f32[64]{0:T(128)} %param.13) | copy-start | bytes 772
  3.0 6.1 %copy-start.4 = (f32[4]{0:T(128)S(1)}, f32[4]{0:T(128)}, u32[]{:S(2)}) copy-start(f32[4]{0:T(128)} %param.15) | copy-start | bytes 52
  3.1 6.1 %collective-permute-start.1 = (f32[208,128]{1,0:T(8,128)S(1)}, f32[208,128]{1,0:T(8,128)S(1)}, u32[]{:S(2)}, u32[]{:S(2)}) collective-permute-start(f32[208,128]{1,0:T(8,128)S(1)} %concatenate.14.own_ref), channel_id=1, source_target_pairs={{0,8},{4,12},{8,0},{12,4},{16,24},{20,28},{24,16},{28,20},{1,9},{5... | collective-permute-start | bytes 319496 | tf_op jit(solution)/shard_map/ppermute | solution.py:509
  6.1 3.1 %collective-permute-start = (f32[208,128]{1,0:T(8,128)S(1)}, f32[208,128]{1,0:T(8,128)S(1)}, u32[]{:S(2)}, u32[]{:S(2)}) collective-permute-start(f32[208,128]{1,0:T(8,128)S(1)} %concatenate.14.own_ref), channel_id=1, source_target_pairs={{0,4},{4,0},{8,12},{12,8},{16,20},{20,16},{24,28},{28,24},{1,5},{5... | collective-permute-start | bytes 319496 | tf_op jit(solution)/shard_map/ppermute | solution.py:509
  9.1 1.3 %collective-permute-start.2 = (f32[208,128]{1,0:T(8,128)S(1)}, f32[208,128]{1,0:T(8,128)S(1)}, u32[]{:S(2)}, u32[]{:S(2)}) collective-permute-start(f32[208,128]{1,0:T(8,128)S(1)} %collective-permute-done.1.two_ref), channel_id=1, source_target_pairs={{0,4},{4,0},{8,12},{12,8},{16,20},{20,16},{24,28},{28,24},{1,5},{5... | collective-permute-start | bytes 319496 | tf_op jit(solution)/shard_map/ppermute | solution.py:509
  14.3 6.7 %collective-permute-start.3 = (f32[152,128]{1,0:T(8,128)S(1)}, f32[152,128]{1,0:T(8,128)S(1)}, u32[]{:S(2)}, u32[]{:S(2)}) collective-permute-start(f32[152,128]{1,0:T(8,128)S(1)} %get-tuple-element.33), channel_id=1, source_target_pairs={{0,16},{4,20},{8,24},{12,28},{1,17},{5,21},{9,25},{13,29},{2,18},{... | collective-permute-start | bytes 233480 | tf_op jit(solution)/shard_map/ppermute | solution.py:567
  25.7 5.9 %collective-permute-start.4 = (f32[32,128]{1,0:T(8,128)S(1)}, f32[32,128]{1,0:T(8,128)S(1)}, u32[]{:S(2)}, u32[]{:S(2)}) collective-permute-start(f32[32,128]{1,0:T(8,128)S(1)} %get-tuple-element.40), channel_id=1, source_target_pairs={{0,16},{4,20},{8,24},{12,28},{16,0},{20,4},{24,8},{28,12},{1,17},{... | collective-permute-start | bytes 49160 | tf_op jit(solution)/shard_map/ppermute | solution.py:509
  31.7 3.7 %collective-permute-start.5 = (f32[32,128]{1,0:T(8,128)S(1)}, f32[32,128]{1,0:T(8,128)S(1)}, u32[]{:S(2)}, u32[]{:S(2)}) collective-permute-start(f32[32,128]{1,0:T(8,128)S(1)} %add.9), channel_id=1, source_target_pairs={{0,1},{1,0},{2,3},{3,2},{4,5},{5,4},{6,7},{7,6},{8,9},{9,8},{10,11... | collective-permute-start | bytes 49160 | tf_op jit(solution)/shard_map/ppermute | solution.py:509
  35.4 3.7 %collective-permute-start.6 = (f32[32,128]{1,0:T(8,128)S(1)}, f32[32,128]{1,0:T(8,128)S(1)}, u32[]{:S(2)}, u32[]{:S(2)}) collective-permute-start(f32[32,128]{1,0:T(8,128)S(1)} %add.10), channel_id=1, source_target_pairs={{0,2},{1,3},{2,0},{3,1},{4,6},{5,7},{6,4},{7,5},{8,10},{9,11},{10,... | collective-permute-start | bytes 49160 | tf_op jit(solution)/shard_map/ppermute | solution.py:509
  39.2 4.9 %collective-permute-start.7 = (f32[40,128]{1,0:T(8,128)S(1)}, f32[40,128]{1,0:T(8,128)S(1)}, u32[]{:S(2)}, u32[]{:S(2)}) collective-permute-start(f32[40,128]{1,0:T(8,128)S(1)} %pad_maximum_fusion.1), channel_id=1, source_target_pairs={{0,8},{4,12},{8,0},{12,4},{16,24},{20,28},{24,16},{28,20},{1,9},{5... | collective-permute-start | bytes 61448 | tf_op jit(solution)/shard_map/ppermute | solution.py:509
  44.0 1.2 %collective-permute-start.8 = (f32[80,128]{1,0:T(8,128)S(1)}, f32[80,128]{1,0:T(8,128)S(1)}, u32[]{:S(2)}, u32[]{:S(2)}) collective-permute-start(f32[80,128]{1,0:T(8,128)S(1)} %pad_maximum_fusion.refs_0_), channel_id=1, source_target_pairs={{0,4},{4,0},{8,12},{12,8},{16,20},{20,16},{24,28},{28,24},{1,5},{5... | collective-permute-start | bytes 122888 | tf_op jit(solution)/shard_map/ppermute | solution.py:509

commit v10 on v9

--- a/solution.py
+++ b/solution.py
@@ -473,14 +473,28 @@
 
 
 def tip_kernel(prior_ref, *refs):
-    *came, log_ref, solved_ref, tip_log_ref, tip_ref, all_ref, rows_ref = refs
+    own_ref, came_ref, log_ref, solved_ref, tip_log_ref, tip_ref, all_ref, rows_ref = refs
     tip = prior_ref.shape[0]
     mid = tip // 2
     node = lax.axis_index("tm") & (GROUP - 1)
-    count = all_ref.shape[1]
-    for step, ref in enumerate(came):
-        all_ref[node ^ step] = ref[0:count, :]
-        all_ref[node ^ step ^ 2] = ref[count:, :]
+    size = 2 * (mid + 2 * GROUP)
+
+    def collect(ref):
+        for step in range(GROUP):
+            first, second = step // 2 * size, step % 2
+            start = first + second * mid
+            all_ref[(node | 1) ^ step, 0:mid, :] = ref[start : start + mid, :]
+            start = first + 2 * mid + second * 2 * GROUP
+            all_ref[(node | 1) ^ step, mid:, :] = ref[start : start + 2 * GROUP, :]
+
+    @pl.when(node & 1 == 1)
+    def _():
+        collect(own_ref)
+
+    @pl.when(node & 1 == 0)
+    def _():
+        collect(came_ref)
+
     for n in range(GROUP):
         top, bottom = unfold(all_ref[n, 0:mid, :])
         rows_ref[pl.ds(n, mid, stride=SUB), :] = prior_ref[0:mid, :] - top
@@ -507,6 +521,16 @@
 def crossed(value, axis, step):
     size = lax.axis_size(axis)
     return lax.ppermute(value, axis, [(source, source ^ step) for source in range(size)])
+
+
+def bridged(value, far, near):
+    rows, columns = lax.axis_size("tm"), lax.axis_size("mesh")
+    pairs = [
+        (row * columns + column, (row ^ far) * columns + (column ^ near))
+        for row in range(1, rows, 2)
+        for column in range(columns)
+    ]
+    return lax.ppermute(value, ("tm", "mesh"), pairs)
 
 
 def shards(
@@ -582,21 +606,25 @@
         ((2 * GROUP, tile),),
         (*pair, (half, tile), (half, tile)),
     )
-    for axis, first in (("tm", GROUP), ("mesh", 4)):
-        step = first
-        while step < lax.axis_size(axis):
-            sums = sums + crossed(sums, axis, step)
-            step *= 2
-    sums, small = lax.optimization_barrier((sums, small))
-    for step in (1, 2):
-        sums = sums + crossed(sums, "mesh", step)
-    found = jnp.concatenate([sums, small], axis=0)
-    found = jnp.concatenate([found, crossed(found, "tm", 2)], axis=0)
+    both = jnp.concatenate([sums, crossed(sums, "tm", 1)], axis=0)
+    step = GROUP
+    while step < groups:
+        both = both + bridged(both, step, 0)
+        step *= 2
+    both, small = lax.optimization_barrier((both, small))
+    step = 4
+    while step < lax.axis_size("mesh"):
+        both = both + bridged(both, 0, step)
+        step *= 2
+    both = (both + bridged(both, 0, 1)) + (bridged(both, 0, 2) + bridged(both, 0, 3))
+    found = jnp.concatenate([both, small, crossed(small, "tm", 1)], axis=0)
+    found = jnp.concatenate([found, bridged(found, 2, 0)], axis=0)
+    came = lax.ppermute(found, "tm", [(source, source - 1) for source in range(1, groups, 2)])
     log_diag, solved, tip_log, tip_forward = call(
         tip_kernel,
-        (prior, found, crossed(found, "tm", 1)),
+        (prior, found, came),
         ((GROUP, tile), (GROUP, tile), (GROUP, tip), (GROUP, tip)),
-        ((GROUP, found.shape[0] // 2, tile), (SUB * tip, tile)),
+        ((GROUP, tip // 2 + 2 * GROUP, tile), (SUB * tip, tile)),
     )
     return (log_diag[:, None, :], solved[:, None, :], tip_log, tip_forward)
 

time: 48.8 us -> 57 us (1.17)
  starting transfers between devices: 18.1 us -> 25.4 us
    ppermute x0 -> x6, waiting for transfers between devices: none -> 7.75 us  [the longest x1 7.73 us: shards(): lax.ppermute(found, 'tm', [(source, source - 1) for source in range(1, gr...]
    ppermute x8 -> x5, waiting for transfers between devices: 13.3 us -> 6.11 us  [crossed(): lax.ppermute(value, axis, [(source, source ^ step) for source in range(si...]
    ppermute x0 -> x6, starting transfers between devices: none -> 4.58 us  [the longest x5 3.29 us: bridged(): return lax.ppermute(value, ('tm', 'mesh'), pairs)]
    ppermute x8 -> x5, starting transfers between devices: 13.4 us -> 16.1 us  [crossed(): lax.ppermute(value, axis, [(source, source ^ step) for source in range(si...]
  transfers between devices with their start and end apart: 9 -> 12, of which waited for: 8 -> 6; matrix products, arithmetic and copies ran while one was open for 0% -> 0% of each run, Pallas kernels for 3% -> 3%
where the time goes in v10:
time: 57 us; the launch traced here: 56.5 us
  starting transfers between devices  25.4 us (45%)
  waiting for transfers between devices  14.4 us (25%)
  Pallas kernels  13.4 us (24%)
  between operations  1.53 us (3%)
  other arithmetic  0.94 us (2%)
  local copies, waits for them, and re-layouts  0.88 us (2%)
    ppermute x5, starting transfers between devices, crossed(): lax.ppermute(value, axis, [(source, source ^ step) for source in range(si...  16.1 us
    pallas_call x5, Pallas kernels, call(): pl.pallas_call(body, out_shape=tuple((jax.ShapeDtypeStruct(shape, F32) fo...  13.4 us
    ppermute x1, waiting for transfers between devices, shards(): lax.ppermute(found, 'tm', [(source, source - 1) for source in range(1, gr...  7.73 us
    ppermute x5, waiting for transfers between devices, crossed(): lax.ppermute(value, axis, [(source, source ^ step) for source in range(si...  6.11 us
    ppermute x1, starting transfers between devices, shards(): lax.ppermute(state, 'tm', [(source, source + GROUP) for source in range(g...  4.66 us
    ppermute x5, starting transfers between devices, bridged(): return lax.ppermute(value, ('tm', 'mesh'), pairs)  3.29 us
    ppermute x1, starting transfers between devices, shards(): lax.ppermute(found, 'tm', [(source, source - 1) for source in range(1, gr...  1.29 us
  transfers between devices with their start and end apart: 12, of which 6 were waited for; matrix products, arithmetic and copies ran while one was open for 0% of the time, Pallas kernels for 3%

profile of v10, /device:TPU:0, one launch (start us, length us, event | category | flops | bytes accessed | tf_op | source)
XLA Modules:
  0.0 56.5 jit_solution(7219908768004543878)
XLA Ops:
  1.3 0.0 copy-start
  1.3 0.9 %fusion = (f32[128]{0:T(128)S(1)}, f32[128,128]{1,0:T(8,128)S(1)}) fusion(f32[1,128,128]{2,1,0:T(8,128)} %param.10, f32[1,128,128]{2,1,0:T(8,128)} %param.9), kind=kLoop, calls=%fused_computation.3 | loop fusion | flops 81792 | bytes 197120 | tf_op jit(solution)/shard_map/reduce_sum | solution.py:565
  2.2 0.0 copy-start.1
  2.2 0.0 copy-done
  2.2 0.6 %copy-done.1 = f32[1,128]{1,0:T(1,128)S(1)} copy-done((f32[1,128]{1,0:T(1,128)S(1)}, f32[1,128]{1,0:T(1,128)}, u32[]{:S(2)}) %copy-start.1) | copy-done | bytes 536
  2.9 0.0 copy-start.5
  2.9 0.1 concatenate.17.own_ref
  3.0 0.0 copy-start.2
  3.0 0.0 copy-start.3
  3.0 0.0 copy-start.4
  3.1 3.1 %collective-permute-start.1 = (f32[208,128]{1,0:T(8,128)S(1)}, f32[208,128]{1,0:T(8,128)S(1)}, u32[]{:S(2)}, u32[]{:S(2)}) collective-permute-start(f32[208,128]{1,0:T(8,128)S(1)} %concatenate.17.own_ref), channel_id=1, source_target_pairs={{0,8},{4,12},{8,0},{12,4},{16,24},{20,28},{24,16},{28,20},{1,9},{5... | collective-permute-start | bytes 319496 | tf_op jit(solution)/shard_map/ppermute | solution.py:523
  6.1 0.0 collective-permute-start
  6.1 3.0 %collective-permute-done.1.two_ref = f32[208,128]{1,0:T(8,128)S(1)} collective-permute-done((f32[208,128]{1,0:T(8,128)S(1)}, f32[208,128]{1,0:T(8,128)S(1)}, u32[]{:S(2)}, u32[]{:S(2)}) %collective-permute-start.1) | collective-permute-done | bytes 106528 | tf_op jit(solution)/shard_map/ppermute | solution.py:523
  9.1 0.0 collective-permute-start.2
  9.1 0.0 copy-done.5
  9.1 0.0 copy-done.2
  9.1 0.0 copy-done.3
  9.1 0.0 copy-done.4
  9.2 0.1 concatenate.16
  9.2 0.0 collective-permute-done.one_ref
  9.2 1.2 %collective-permute-done.2.three_ref = f32[208,128]{1,0:T(8,128)S(1)} collective-permute-done((f32[208,128]{1,0:T(8,128)S(1)}, f32[208,128]{1,0:T(8,128)S(1)}, u32[]{:S(2)}, u32[]{:S(2)}) %collective-permute-start.2) | collective-permute-done | bytes 106528 | tf_op jit(solution)/shard_map/ppermute | solution.py:523
  10.4 3.9 %shard_map.120 = (f32[4,128,128]{2,1,0:T(8,128)S(1)}, f32[4,128,128]{2,1,0:T(8,128)S(1)}, f32[4,128,128]{2,1,0:T(8,128)S(1)}, f32[4,80,128]{2,1,0:T(8,128)S(1)},...) custom-call(f32[2,128]{1,0:T(2,128)S(1)} %bitcast.17, ...), custom_call_target="tpu_custom_call" | custom-call | tf_op jit(solution)/shard_map/pallas_call | solution.py:511
  14.3 4.7 %collective-permute-start.3 = (f32[152,128]{1,0:T(8,128)S(1)}, f32[152,128]{1,0:T(8,128)S(1)}, u32[]{:S(2)}, u32[]{:S(2)}) collective-permute-start(f32[152,128]{1,0:T(8,128)S(1)} %get-tuple-element.33), channel_id=1, source_target_pairs={{0,16},{4,20},{8,24},{12,28},{1,17},{5,21},{9,25},{13,29},{2,18},{... | collective-permute-start | bytes 233480 | tf_op jit(solution)/shard_map/ppermute | solution.py:591
  19.0 1.5 %shard_map.121 = (f32[128,128]{1,0:T(8,128)S(1)}, f32[128,128]{1,0:T(8,128)S(1)}, f32[128,128]{1,0:T(8,128)S(1)}, f32[80,128]{1,0:T(8,128)S(1)}, f32[80,128]{1,0:T(8,128)S(1)}, /*index=5*/f32[64,128]{1,0:T(8,128)S(1)}) custom-call(f32[2,128]{1,0:T(2,128)S(1)} %bitcast.18, f32[4,128,128]{2,1,0:T(8,128)S(1)} %get-tuple-element.27.refs_1_.refs_0_, ...), custom_call_target="tpu_custom_call" | custom-call | tf_op jit(solution)/shard_map/pallas_call | solution.py:511
  20.4 0.5 collective-permute-done.3.state_ref
  21.0 4.8 %shard_map.122 = (f32[4,128,128]{2,1,0:T(8,128)S(1)}, f32[4,128,128]{2,1,0:T(8,128)S(1)}, f32[32,128]{1,0:T(8,128)S(1)}, f32[8,128]{1,0:T(8,128)S(1)}) custom-call(f32[152,128]{1,0:T(8,128)S(1)} %collective-permute-done.3.state_ref, f32[4,128,128]{2,1,0:T(8,128)S(1)} %get-tuple-element.27.refs_1_.refs_0_, ...), custom_call_target="tpu_custom_call" | custom-call | tf_op jit(solution)/shard_map/pallas_call | solution.py:511
  25.7 0.1 collective-permute-start.4
  25.8 1.2 %collective-permute-done.4 = f32[32,128]{1,0:T(8,128)S(1)} collective-permute-done((f32[32,128]{1,0:T(8,128)S(1)}, f32[32,128]{1,0:T(8,128)S(1)}, u32[]{:S(2)}, u32[]{:S(2)}) %collective-permute-start.4) | collective-permute-done | bytes 16416 | tf_op jit(solution)/shard_map/ppermute | solution.py:523
  27.0 0.7 %collective-permute-start.5 = (f32[64,128]{1,0:T(8,128)S(1)}, f32[64,128]{1,0:T(8,128)S(1)}, u32[]{:S(2)}, u32[]{:S(2)}) collective-permute-start(f32[64,128]{1,0:T(8,128)S(1)} %constant_dynamic-update-slice_fusion), channel_id=1, source_target_pairs={{4,20},{5,21},{6,22},{7,23},{12,28},{13,29},{14,30},{15,31},{20,4}... | collective-permute-start | bytes 98312 | tf_op jit(solution)/shard_map/ppermute | solution.py:533
  27.7 0.0 collective-permute-done.5
  27.7 0.7 %collective-permute-start.7 = (f32[64,128]{1,0:T(8,128)S(1)}, f32[64,128]{1,0:T(8,128)S(1)}, u32[]{:S(2)}, u32[]{:S(2)}) collective-permute-start(f32[64,128]{1,0:T(8,128)S(1)} %add.12), channel_id=1, source_target_pairs={{4,6},{5,7},{6,4},{7,5},{12,14},{13,15},{14,12},{15,13},{20,22},{2... | collective-permute-start | bytes 98312 | tf_op jit(solution)/shard_map/ppermute | solution.py:533
  28.4 0.7 %collective-permute-start.8 = (f32[64,128]{1,0:T(8,128)S(1)}, f32[64,128]{1,0:T(8,128)S(1)}, u32[]{:S(2)}, u32[]{:S(2)}) collective-permute-start(f32[64,128]{1,0:T(8,128)S(1)} %add.12), channel_id=1, source_target_pairs={{4,7},{5,6},{6,5},{7,4},{12,15},{13,14},{14,13},{15,12},{20,23},{2... | collective-permute-start | bytes 98312 | tf_op jit(solution)/shard_map/ppermute | solution.py:533
  29.1 0.7 %collective-permute-start.6 = (f32[64,128]{1,0:T(8,128)S(1)}, f32[64,128]{1,0:T(8,128)S(1)}, u32[]{:S(2)}, u32[]{:S(2)}) collective-permute-start(f32[64,128]{1,0:T(8,128)S(1)} %add.12), channel_id=1, source_target_pairs={{4,5},{5,4},{6,7},{7,6},{12,13},{13,12},{14,15},{15,14},{20,21},{2... | collective-permute-start | bytes 98312 | tf_op jit(solution)/shard_map/ppermute | solution.py:533
  29.7 13.0 %collective-permute-start.9 = (f32[8,128]{1,0:T(8,128)S(1)}, f32[8,128]{1,0:T(8,128)S(1)}, u32[]{:S(2)}, u32[]{:S(2)}) collective-permute-start(f32[8,128]{1,0:T(8,128)S(1)} %shard_map.123), channel_id=1, source_target_pairs={{0,4},{4,0},{8,12},{12,8},{16,20},{20,16},{24,28},{28,24},{1,5},{5... | collective-permute-start | bytes 12296 | tf_op jit(solution)/shard_map/ppermute | solution.py:523
  42.7 0.0 collective-permute-done.7
  42.7 0.0 collective-permute-done.8
  42.7 0.0 collective-permute-done.6
  42.7 0.8 %collective-permute-done.9 = f32[8,128]{1,0:T(8,128)S(1)} collective-permute-done((f32[8,128]{1,0:T(8,128)S(1)}, f32[8,128]{1,0:T(8,128)S(1)}, u32[]{:S(2)}, u32[]{:S(2)}) %collective-permute-start.9) | collective-permute-done | bytes 4128 | tf_op jit(solution)/shard_map/ppermute | solution.py:523
  43.5 0.7 %collective-permute-start.10 = (f32[80,128]{1,0:T(8,128)S(1)}, f32[80,128]{1,0:T(8,128)S(1)}, u32[]{:S(2)}, u32[]{:S(2)}) collective-permute-start(f32[80,128]{1,0:T(8,128)S(1)} %pad_maximum_fusion.1), channel_id=1, source_target_pairs={{4,12},{5,13},{6,14},{7,15},{12,4},{13,5},{14,6},{15,7},{20,28},{2... | collective-permute-start | bytes 122888 | tf_op jit(solution)/shard_map/ppermute | solution.py:533
  44.2 0.0 collective-permute-done.10
  44.2 1.3 %collective-permute-start.11 = (f32[160,128]{1,0:T(8,128)S(1)}, f32[160,128]{1,0:T(8,128)S(1)}, u32[]{:S(2)}, u32[]{:S(2)}) collective-permute-start(f32[160,128]{1,0:T(8,128)S(1)} %pad_maximum_fusion.refs_0_), channel_id=1, source_target_pairs={{4,0},{12,8},{20,16},{28,24},{5,1},{13,9},{21,17},{29,25},{6,2},{1... | collective-permute-start | bytes 245768 | tf_op jit(solution)/shard_map/ppermute | solution.py:622
  45.5 7.7 %collective-permute-done.11.refs_1_ = f32[160,128]{1,0:T(8,128)S(1)} collective-permute-done((f32[160,128]{1,0:T(8,128)S(1)}, f32[160,128]{1,0:T(8,128)S(1)}, u32[]{:S(2)}, u32[]{:S(2)}) %collective-permute-start.11) | collective-permute-done | bytes 81952 | tf_op jit(solution)/shard_map/ppermute | solution.py:622
  53.2 3.3 %shard_map.124 = (f32[4,128]{1,0:T(4,128)}, f32[4,128]{1,0:T(4,128)}, f32[4,64]{1,0:T(4,128)}, f32[4,64]{1,0:T(4,128)}) custom-call(f32[64,128]{1,0:T(8,128)S(1)} %get-tuple-element.32.prior_ref, f32[160,128]{1,0:T(8,128)S(1)} %pad_maximum_fusion.refs_0_, f32[160,128]{1,0:T(8,128)S(1)} %collective-permute-done.11.refs_1_), custom_call_target="tpu_custom_call" | custom-call | tf_op jit(solution)/shard_map/pallas_call | solution.py:511
  (10 shorter events, 0.1 us)
Async XLA Ops:
  1.3 1.0 %copy-start = (f32[1,64,128]{2,1,0:T(8,128)S(1)}, f32[1,64,128]{2,1,0:T(8,128)}, u32[]{:S(2)}) copy-start(f32[1,64,128]{2,1,0:T(8,128)} %param.11) | copy-start | bytes 98308
  2.2 0.7 %copy-start.1 = (f32[1,128]{1,0:T(1,128)S(1)}, f32[1,128]{1,0:T(1,128)}, u32[]{:S(2)}) copy-start(f32[1,128]{1,0:T(1,128)} %param.12) | copy-start | bytes 1540
  2.9 6.2 %copy-start.5 = (f32[4]{0:T(128)S(1)}, f32[4]{0:T(128)}, u32[]{:S(2)}) copy-start(f32[4]{0:T(128)} %param.16) | copy-start | bytes 52
  3.0 6.1 %copy-start.2 = (f32[64]{0:T(128)S(1)}, f32[64]{0:T(128)}, u32[]{:S(2)}) copy-start(f32[64]{0:T(128)} %param.14) | copy-start | bytes 772
  3.0 6.1 %copy-start.3 = (f32[64]{0:T(128)S(1)}, f32[64]{0:T(128)}, u32[]{:S(2)}) copy-start(f32[64]{0:T(128)} %param.13) | copy-start | bytes 772
  3.0 6.1 %copy-start.4 = (f32[4]{0:T(128)S(1)}, f32[4]{0:T(128)}, u32[]{:S(2)}) copy-start(f32[4]{0:T(128)} %param.15) | copy-start | bytes 52
  3.1 6.1 %collective-permute-start.1 = (f32[208,128]{1,0:T(8,128)S(1)}, f32[208,128]{1,0:T(8,128)S(1)}, u32[]{:S(2)}, u32[]{:S(2)}) collective-permute-start(f32[208,128]{1,0:T(8,128)S(1)} %concatenate.17.own_ref), channel_id=1, source_target_pairs={{0,8},{4,12},{8,0},{12,4},{16,24},{20,28},{24,16},{28,20},{1,9},{5... | collective-permute-start | bytes 319496 | tf_op jit(solution)/shard_map/ppermute | solution.py:523
  6.1 3.1 %collective-permute-start = (f32[208,128]{1,0:T(8,128)S(1)}, f32[208,128]{1,0:T(8,128)S(1)}, u32[]{:S(2)}, u32[]{:S(2)}) collective-permute-start(f32[208,128]{1,0:T(8,128)S(1)} %concatenate.17.own_ref), channel_id=1, source_target_pairs={{0,4},{4,0},{8,12},{12,8},{16,20},{20,16},{24,28},{28,24},{1,5},{5... | collective-permute-start | bytes 319496 | tf_op jit(solution)/shard_map/ppermute | solution.py:523
  9.1 1.3 %collective-permute-start.2 = (f32[208,128]{1,0:T(8,128)S(1)}, f32[208,128]{1,0:T(8,128)S(1)}, u32[]{:S(2)}, u32[]{:S(2)}) collective-permute-start(f32[208,128]{1,0:T(8,128)S(1)} %collective-permute-done.1.two_ref), channel_id=1, source_target_pairs={{0,4},{4,0},{8,12},{12,8},{16,20},{20,16},{24,28},{28,24},{1,5},{5... | collective-permute-start | bytes 319496 | tf_op jit(solution)/shard_map/ppermute | solution.py:523
  14.3 6.7 %collective-permute-start.3 = (f32[152,128]{1,0:T(8,128)S(1)}, f32[152,128]{1,0:T(8,128)S(1)}, u32[]{:S(2)}, u32[]{:S(2)}) collective-permute-start(f32[152,128]{1,0:T(8,128)S(1)} %get-tuple-element.33), channel_id=1, source_target_pairs={{0,16},{4,20},{8,24},{12,28},{1,17},{5,21},{9,25},{13,29},{2,18},{... | collective-permute-start | bytes 233480 | tf_op jit(solution)/shard_map/ppermute | solution.py:591
  25.7 1.2 %collective-permute-start.4 = (f32[32,128]{1,0:T(8,128)S(1)}, f32[32,128]{1,0:T(8,128)S(1)}, u32[]{:S(2)}, u32[]{:S(2)}) collective-permute-start(f32[32,128]{1,0:T(8,128)S(1)} %get-tuple-element.40), channel_id=1, source_target_pairs={{0,4},{4,0},{8,12},{12,8},{16,20},{20,16},{24,28},{28,24},{1,5},{5... | collective-permute-start | bytes 49160 | tf_op jit(solution)/shard_map/ppermute | solution.py:523
  27.0 0.7 %collective-permute-start.5 = (f32[64,128]{1,0:T(8,128)S(1)}, f32[64,128]{1,0:T(8,128)S(1)}, u32[]{:S(2)}, u32[]{:S(2)}) collective-permute-start(f32[64,128]{1,0:T(8,128)S(1)} %constant_dynamic-update-slice_fusion), channel_id=1, source_target_pairs={{4,20},{5,21},{6,22},{7,23},{12,28},{13,29},{14,30},{15,31},{20,4}... | collective-permute-start | bytes 98312 | tf_op jit(solution)/shard_map/ppermute | solution.py:533
  27.7 15.0 %collective-permute-start.7 = (f32[64,128]{1,0:T(8,128)S(1)}, f32[64,128]{1,0:T(8,128)S(1)}, u32[]{:S(2)}, u32[]{:S(2)}) collective-permute-start(f32[64,128]{1,0:T(8,128)S(1)} %add.12), channel_id=1, source_target_pairs={{4,6},{5,7},{6,4},{7,5},{12,14},{13,15},{14,12},{15,13},{20,22},{2... | collective-permute-start | bytes 98312 | tf_op jit(solution)/shard_map/ppermute | solution.py:533
  28.4 14.3 %collective-permute-start.8 = (f32[64,128]{1,0:T(8,128)S(1)}, f32[64,128]{1,0:T(8,128)S(1)}, u32[]{:S(2)}, u32[]{:S(2)}) collective-permute-start(f32[64,128]{1,0:T(8,128)S(1)} %add.12), channel_id=1, source_target_pairs={{4,7},{5,6},{6,5},{7,4},{12,15},{13,14},{14,13},{15,12},{20,23},{2... | collective-permute-start | bytes 98312 | tf_op jit(solution)/shard_map/ppermute | solution.py:533
  29.1 13.6 %collective-permute-start.6 = (f32[64,128]{1,0:T(8,128)S(1)}, f32[64,128]{1,0:T(8,128)S(1)}, u32[]{:S(2)}, u32[]{:S(2)}) collective-permute-start(f32[64,128]{1,0:T(8,128)S(1)} %add.12), channel_id=1, source_target_pairs={{4,5},{5,4},{6,7},{7,6},{12,13},{13,12},{14,15},{15,14},{20,21},{2... | collective-permute-start | bytes 98312 | tf_op jit(solution)/shard_map/ppermute | solution.py:533
  29.7 13.8 %collective-permute-start.9 = (f32[8,128]{1,0:T(8,128)S(1)}, f32[8,128]{1,0:T(8,128)S(1)}, u32[]{:S(2)}, u32[]{:S(2)}) collective-permute-start(f32[8,128]{1,0:T(8,128)S(1)} %shard_map.123), channel_id=1, source_target_pairs={{0,4},{4,0},{8,12},{12,8},{16,20},{20,16},{24,28},{28,24},{1,5},{5... | collective-permute-start | bytes 12296 | tf_op jit(solution)/shard_map/ppermute | solution.py:523
  43.5 0.7 %collective-permute-start.10 = (f32[80,128]{1,0:T(8,128)S(1)}, f32[80,128]{1,0:T(8,128)S(1)}, u32[]{:S(2)}, u32[]{:S(2)}) collective-permute-start(f32[80,128]{1,0:T(8,128)S(1)} %pad_maximum_fusion.1), channel_id=1, source_target_pairs={{4,12},{5,13},{6,14},{7,15},{12,4},{13,5},{14,6},{15,7},{20,28},{2... | collective-permute-start | bytes 122888 | tf_op jit(solution)/shard_map/ppermute | solution.py:533
  44.2 9.0 %collective-permute-start.11 = (f32[160,128]{1,0:T(8,128)S(1)}, f32[160,128]{1,0:T(8,128)S(1)}, u32[]{:S(2)}, u32[]{:S(2)}) collective-permute-start(f32[160,128]{1,0:T(8,128)S(1)} %pad_maximum_fusion.refs_0_), channel_id=1, source_target_pairs={{4,0},{12,8},{20,16},{28,24},{5,1},{13,9},{21,17},{29,25},{6,2},{1... | collective-permute-start | bytes 245768 | tf_op jit(solution)/shard_map/ppermute | solution.py:622

commit v11 on v9

--- a/solution.py
+++ b/solution.py
@@ -202,15 +202,19 @@
         run((mat_ref, inv_ref))
 
 
-def middle_kernel(tip, *refs):
-    extra_ref, diag_ref, cross_ref, back_ref, right_ref, left_ref, *refs = refs
-    *out_refs, prior_ref, mat_ref, inv_ref = refs
+def middle_kernel(tip, start, *refs):
+    extra_ref, diag_ref, cross_ref, back_ref, right_ref, left_ref, part_ref, *refs = refs
+    *out_refs, far_ref, near_ref, share_ref, prior_ref, mat_ref, inv_ref = refs
     tile = diag_ref.shape[-1]
+    side = right_ref.shape[1]
+    last = jnp.where(lax.axis_index("tm") >= start, 1.0, 0.0).astype(F32)
     one, two, end = slice(0, tile), slice(tile, 2 * tile), slice(2 * tile, None)
     rows = jnp.concatenate([cross_ref[2], cross_ref[1].T, right_ref[1]], axis=0)
+    ends = jnp.concatenate([cross_ref[3].T, padded(right_ref[3], tile)], axis=0)
 
     def run(refs):
-        ((gram, _),), total = quotients((diag_ref[1],), (rows,), (rows[0 : 2 * tile, :],), 4, refs)
+        lefts, rights = (rows, ends), (rows[0 : 2 * tile, :], ends)
+        ((gram, _), (over, _)), total = quotients((diag_ref[1], diag_ref[3]), lefts, rights, 5, refs)
         values = (
             diag_ref[2] - gram[one, one],
             -gram[one, two],
@@ -220,6 +224,9 @@
         )
         for ref, value in zip(out_refs, values):
             ref[...] = value
+        far_ref[...] = back_ref[3] - last * over[one, one]
+        near_ref[...] = left_ref[3] - last * over[tile : tile + side, one]
+        share_ref[...] = part_ref[...] + last * over[tile : tile + tip, two]
         return total < SMALL
 
     settled = run(None)
@@ -274,39 +281,48 @@
     return jnp.concatenate([rows, jnp.zeros((size - rows.shape[0], size), F32)], axis=0)
 
 
-def joined(state_ref, parts, order, refs):
+def joined(state_ref, parts, order, refs, far=None, near=None):
     values = [[third[...] if n == 2 else every[n] for n in order] for every, third in zip(parts[:5], parts[5:])]
     diags, crosses, backs, sides, lefts = values
     tile = crosses[0].shape[-1]
-    lone = jnp.where(lax.axis_index("tm") < GROUP, 1.0, 0.0).astype(F32)
     base, came = receive(state_ref)
-    base = base + lone * parts[0][0]
+    came = padded(came, tile)
     mats = [base + back for back in backs]
-    came = padded(came, tile)
-    middles = [came + padded(left, tile) for left in lefts]
-    rights = [jnp.concatenate([cross, middle], axis=0) for cross, middle in zip(crosses, middles)]
-    updates, total = quotients(mats, crosses[:-1] + rights[-1:], rights, 5, refs)
+    rights = [
+        jnp.concatenate([cross, came + padded(left, tile)], axis=0) for cross, left in zip(crosses, lefts)
+    ]
+    if far is not None:
+        middle = came + padded(near, tile)
+        mats, crosses, rights = mats + [base + far], crosses + [middle], rights + [middle]
+    updates, total = quotients(mats, crosses, rights, 5, refs)
     results = []
     for diag, side, (update, _) in zip(diags, sides, updates):
         start = jnp.concatenate([diag, padded(side, tile).T], axis=1)
-        results.append(start - update[0:tile, :])
-    return results, updates[-1][0][tile:, tile:], total
+        results.append(start - update)
+    return results, updates[-1][0], total
 
 
 def advance_kernel(state_ref, *refs):
     *parts, out_ref, mat_ref, inv_ref = refs
     tile = state_ref.shape[1]
+    position = lax.axis_index("tm")
 
     def run(refs):
         (last,), _, total = joined(state_ref, parts, (GROUP - 1,), refs)
         send(out_ref, last[:, 0:tile], last[:, tile:].T)
         return total < SMALL
 
-    settled = run(None)
-
-    @pl.when(jnp.logical_not(settled))
-    def _():
-        run((mat_ref, inv_ref))
+    @pl.when(position >= GROUP)
+    def _():
+        settled = run(None)
+
+        @pl.when(jnp.logical_not(settled))
+        def _():
+            run((mat_ref, inv_ref))
+
+    @pl.when(position < GROUP)
+    def _():
+        send(out_ref, parts[0][GROUP - 1], parts[3][GROUP - 1])
 
 
 def splat(value, lane):
@@ -397,22 +413,19 @@
     return top, bottom
 
 
-def merge_kernel(start, state_ref, *refs):
-    *parts, part_ref, square_ref, side_ref, sums_ref, small_ref, mat_ref, inv_ref, rows_ref, ends_ref = refs
+def merge_kernel(state_ref, *refs):
+    *parts, far_ref, near_ref, part_ref, square_ref, side_ref, sums_ref, small_ref, mat_ref, inv_ref, rows_ref, ends_ref = refs
     tile = state_ref.shape[1]
     tip = part_ref.shape[0]
     position = lax.axis_index("tm")
-    last = jnp.where(position >= start, 1.0, 0.0).astype(F32)
 
     def run(refs):
-        values, share, total = joined(state_ref, parts, range(GROUP), refs)
+        values, share, total = joined(state_ref, parts, range(GROUP), refs, far_ref[...], near_ref[...])
         for n, value in enumerate(values):
             square_ref[n] = value[:, 0:tile]
             side_ref[n] = value[:, tile:]
-        side = values[-1][:, tile:].T
-        ((own, _),), more = quotients((values[-1][:, 0:tile],), (side[0:tip, :],), (side,), 5, refs)
-        sums_ref[...] = fold(part_ref[...] + share[0:tip, :] + last * own)
-        return (total < SMALL) & (more < SMALL)
+        sums_ref[...] = fold(part_ref[...] + share[0:tip, :])
+        return total < SMALL
 
     @pl.when(position >= GROUP)
     def _():
@@ -557,11 +570,12 @@
         ((GROUP,) + raw.shape, *pair),
     )
     *thirds, prior = call(
-        functools.partial(middle_kernel, tip),
-        (extra, *parts),
-        ((tile, tile), (tile, tile), (tile, tile), (side, tile), (side, tile), (tip, 128)),
+        functools.partial(middle_kernel, tip, groups - GROUP),
+        (extra, *parts, part),
+        ((tile, tile),) * 3 + ((side, tile),) * 2 + ((tile, tile), (side, tile), (tip, tile), (tip, tile)),
         pair,
     )
+    *thirds, far, near, part = thirds
     parts = (*parts, *thirds)
     for span in range(spans - 1):
         state = lax.ppermute(state, "tm", [(source, source + GROUP) for source in range(groups - GROUP)])
@@ -571,8 +585,8 @@
         state = jnp.zeros_like(state)
     half = SUB * tile // 2
     squares, sides, sums, small = call(
-        functools.partial(merge_kernel, groups - GROUP),
-        (state, *parts, part),
+        merge_kernel,
+        (state, *parts, far, near, part),
         (square, square, (tip // 2, tile), (2 * GROUP, tile)),
         (*pair, (half, tile), (half, tile)),
     )
@@ -588,8 +602,7 @@
             sums = sums + crossed(sums, axis, step)
             step *= 2
     sums, small = lax.optimization_barrier((sums, small))
-    for step in (1, 2):
-        sums = sums + crossed(sums, "mesh", step)
+    sums = (sums + crossed(sums, "mesh", 1)) + (crossed(sums, "mesh", 2) + crossed(sums, "mesh", 3))
     found = jnp.concatenate([sums, small], axis=0)
     found = jnp.concatenate([found, crossed(found, "tm", 2)], axis=0)
     log_diag, solved, tip_log, tip_forward = call(

time: 48.8 us -> 47.2 us (0.967)
  waiting for transfers between devices: 13.9 us -> 12.1 us
  Pallas kernels: 13.4 us -> 14.3 us
  starting transfers between devices: 18.1 us -> 17.4 us
    ppermute x8 -> x9, waiting for transfers between devices: 13.3 us -> 12.1 us  [crossed(): lax.ppermute(value, axis, [(source, source ^ step) for source in range(si...]
    pallas_call x5, Pallas kernels: 13.4 us -> 14.3 us  [call(): pl.pallas_call(body, out_shape=tuple((jax.ShapeDtypeStruct(shape, F32) fo...]
    ppermute x8 -> x9, starting transfers between devices: 13.4 us -> 12.8 us  [crossed(): lax.ppermute(value, axis, [(source, source ^ step) for source in range(si...]
    ppermute x1, waiting for transfers between devices: 0.54 us -> 0.01 us  [shards(): lax.ppermute(state, 'tm', [(source, source + GROUP) for source in range(g...]
  transfers between devices with their start and end apart: 9 -> 10, of which waited for: 8 -> 8; matrix products, arithmetic and copies ran while one was open for 0% -> 0% of each run, Pallas kernels for 3% -> 5%
where the time goes in v11:
time: 47.2 us; the launch traced here: 47 us
  starting transfers between devices  17.4 us (37%)
  Pallas kernels  14.3 us (30%)
  waiting for transfers between devices  12.1 us (26%)
  between operations  1.43 us (3%)
  other arithmetic  0.93 us (2%)
  local copies, waits for them, and re-layouts  0.88 us (2%)
    pallas_call x5, Pallas kernels, call(): pl.pallas_call(body, out_shape=tuple((jax.ShapeDtypeStruct(shape, F32) fo...  14.3 us
    ppermute x9, starting transfers between devices, crossed(): lax.ppermute(value, axis, [(source, source ^ step) for source in range(si...  12.8 us
    ppermute x9, waiting for transfers between devices, crossed(): lax.ppermute(value, axis, [(source, source ^ step) for source in range(si...  12.1 us
    ppermute x1, starting transfers between devices, shards(): lax.ppermute(state, 'tm', [(source, source + GROUP) for source in range(g...  4.66 us
  transfers between devices with their start and end apart: 10, of which 8 were waited for; matrix products, arithmetic and copies ran while one was open for 0% of the time, Pallas kernels for 5%

profile of v11, /device:TPU:0, one launch (start us, length us, event | category | flops | bytes accessed | tf_op | source)
XLA Modules:
  0.0 47.0 jit_solution(13992108212325963568)
XLA Ops:
  1.3 0.0 copy-start
  1.3 0.9 %fusion = (f32[128]{0:T(128)S(1)}, f32[128,128]{1,0:T(8,128)S(1)}) fusion(f32[1,128,128]{2,1,0:T(8,128)} %param.10, f32[1,128,128]{2,1,0:T(8,128)} %param.9), kind=kLoop, calls=%fused_computation.2 | loop fusion | flops 81792 | bytes 197120 | tf_op jit(solution)/shard_map/reduce_sum | solution.py:554
  2.2 0.0 copy-start.1
  2.2 0.0 copy-done
  2.2 0.6 %copy-done.1 = f32[1,128]{1,0:T(1,128)S(1)} copy-done((f32[1,128]{1,0:T(1,128)S(1)}, f32[1,128]{1,0:T(1,128)}, u32[]{:S(2)}) %copy-start.1) | copy-done | bytes 536
  2.9 0.0 copy-start.5
  2.9 0.1 concatenate.14.own_ref
  3.0 0.0 copy-start.2
  3.0 0.0 copy-start.3
  3.0 0.0 copy-start.4
  3.1 3.1 %collective-permute-start.1 = (f32[208,128]{1,0:T(8,128)S(1)}, f32[208,128]{1,0:T(8,128)S(1)}, u32[]{:S(2)}, u32[]{:S(2)}) collective-permute-start(f32[208,128]{1,0:T(8,128)S(1)} %concatenate.14.own_ref), channel_id=1, source_target_pairs={{0,8},{4,12},{8,0},{12,4},{16,24},{20,28},{24,16},{28,20},{1,9},{5... | collective-permute-start | bytes 319496 | tf_op jit(solution)/shard_map/ppermute | solution.py:522
  6.1 0.0 collective-permute-start
  6.1 3.0 %collective-permute-done.1.two_ref = f32[208,128]{1,0:T(8,128)S(1)} collective-permute-done((f32[208,128]{1,0:T(8,128)S(1)}, f32[208,128]{1,0:T(8,128)S(1)}, u32[]{:S(2)}, u32[]{:S(2)}) %collective-permute-start.1) | collective-permute-done | bytes 106528 | tf_op jit(solution)/shard_map/ppermute | solution.py:522
  9.1 0.0 collective-permute-start.2
  9.1 0.0 copy-done.5
  9.1 0.0 copy-done.2
  9.1 0.0 copy-done.3
  9.1 0.0 copy-done.4
  9.2 0.1 concatenate.13
  9.2 0.0 collective-permute-done.one_ref
  9.2 1.2 %collective-permute-done.2.three_ref = f32[208,128]{1,0:T(8,128)S(1)} collective-permute-done((f32[208,128]{1,0:T(8,128)S(1)}, f32[208,128]{1,0:T(8,128)S(1)}, u32[]{:S(2)}, u32[]{:S(2)}) %collective-permute-start.2) | collective-permute-done | bytes 106528 | tf_op jit(solution)/shard_map/ppermute | solution.py:522
  10.4 3.9 %shard_map.120 = (f32[4,128,128]{2,1,0:T(8,128)S(1)}, f32[4,128,128]{2,1,0:T(8,128)S(1)}, f32[4,128,128]{2,1,0:T(8,128)S(1)}, f32[4,80,128]{2,1,0:T(8,128)S(1)},...) custom-call(f32[2,128]{1,0:T(2,128)S(1)} %bitcast.17, ...), custom_call_target="tpu_custom_call" | custom-call | tf_op jit(solution)/shard_map/pallas_call | solution.py:510
  14.3 4.7 %collective-permute-start.3 = (f32[152,128]{1,0:T(8,128)S(1)}, f32[152,128]{1,0:T(8,128)S(1)}, u32[]{:S(2)}, u32[]{:S(2)}) collective-permute-start(f32[152,128]{1,0:T(8,128)S(1)} %get-tuple-element.37), channel_id=1, source_target_pairs={{0,16},{4,20},{8,24},{12,28},{1,17},{5,21},{9,25},{13,29},{2,18},{... | collective-permute-start | bytes 233480 | tf_op jit(solution)/shard_map/ppermute | solution.py:581
  19.0 2.3 %shard_map.121 = (f32[128,128]{1,0:T(8,128)S(1)}, f32[128,128]{1,0:T(8,128)S(1)}, f32[128,128]{1,0:T(8,128)S(1)}, f32[80,128]{1,0:T(8,128)S(1)}, f32[80,128]{1,0...) custom-call(f32[2,128]{1,0:T(2,128)S(1)} %bitcast.18, ...), custom_call_target="tpu_custom_call" | custom-call | tf_op jit(solution)/shard_map/pallas_call | solution.py:510
  21.3 0.0 collective-permute-done.3.state_ref
  21.3 4.8 %shard_map.122 = (f32[4,128,128]{2,1,0:T(8,128)S(1)}, f32[4,128,128]{2,1,0:T(8,128)S(1)}, f32[32,128]{1,0:T(8,128)S(1)}, f32[8,128]{1,0:T(8,128)S(1)}) custom-call(f32[152,128]{1,0:T(8,128)S(1)} %collective-permute-done.3.state_ref, f32[4,128,128]{2,1,0:T(8,128)S(1)} %get-tuple-element.30.refs_1_.refs_0_, ...), custom_call_target="tpu_custom_call" | custom-call | tf_op jit(solution)/shard_map/pallas_call | solution.py:510
  26.1 3.1 %collective-permute-start.4 = (f32[32,128]{1,0:T(8,128)S(1)}, f32[32,128]{1,0:T(8,128)S(1)}, u32[]{:S(2)}, u32[]{:S(2)}) collective-permute-start(f32[32,128]{1,0:T(8,128)S(1)} %get-tuple-element.46), channel_id=1, source_target_pairs={{0,16},{4,20},{8,24},{12,28},{16,0},{20,4},{24,8},{28,12},{1,17},{... | collective-permute-start | bytes 49160 | tf_op jit(solution)/shard_map/ppermute | solution.py:522
  29.2 1.7 %collective-permute-done.4 = f32[32,128]{1,0:T(8,128)S(1)} collective-permute-done((f32[32,128]{1,0:T(8,128)S(1)}, f32[32,128]{1,0:T(8,128)S(1)}, u32[]{:S(2)}, u32[]{:S(2)}) %collective-permute-start.4) | collective-permute-done | bytes 16416 | tf_op jit(solution)/shard_map/ppermute | solution.py:522
  30.9 1.5 %collective-permute-start.6 = (f32[32,128]{1,0:T(8,128)S(1)}, f32[32,128]{1,0:T(8,128)S(1)}, u32[]{:S(2)}, u32[]{:S(2)}) collective-permute-start(f32[32,128]{1,0:T(8,128)S(1)} %add.12), channel_id=1, source_target_pairs={{0,2},{1,3},{2,0},{3,1},{4,6},{5,7},{6,4},{7,5},{8,10},{9,11},{10,... | collective-permute-start | bytes 49160 | tf_op jit(solution)/shard_map/ppermute | solution.py:522
  32.5 1.4 %collective-permute-start.7 = (f32[32,128]{1,0:T(8,128)S(1)}, f32[32,128]{1,0:T(8,128)S(1)}, u32[]{:S(2)}, u32[]{:S(2)}) collective-permute-start(f32[32,128]{1,0:T(8,128)S(1)} %add.12), channel_id=1, source_target_pairs={{0,3},{1,2},{2,1},{3,0},{4,7},{5,6},{6,5},{7,4},{8,11},{9,10},{10,... | collective-permute-start | bytes 49160 | tf_op jit(solution)/shard_map/ppermute | solution.py:522
  33.9 0.5 %collective-permute-start.5 = (f32[32,128]{1,0:T(8,128)S(1)}, f32[32,128]{1,0:T(8,128)S(1)}, u32[]{:S(2)}, u32[]{:S(2)}) collective-permute-start(f32[32,128]{1,0:T(8,128)S(1)} %add.12), channel_id=1, source_target_pairs={{0,1},{1,0},{2,3},{3,2},{4,5},{5,4},{6,7},{7,6},{8,9},{9,8},{10,11... | collective-permute-start | bytes 49160 | tf_op jit(solution)/shard_map/ppermute | solution.py:522
  34.4 0.2 collective-permute-done.6
  34.7 2.4 %collective-permute-done.7 = f32[32,128]{1,0:T(8,128)S(1)} collective-permute-done((f32[32,128]{1,0:T(8,128)S(1)}, f32[32,128]{1,0:T(8,128)S(1)}, u32[]{:S(2)}, u32[]{:S(2)}) %collective-permute-start.7) | collective-permute-done | bytes 16416 | tf_op jit(solution)/shard_map/ppermute | solution.py:522
  37.1 0.5 %collective-permute-done.5 = f32[32,128]{1,0:T(8,128)S(1)} collective-permute-done((f32[32,128]{1,0:T(8,128)S(1)}, f32[32,128]{1,0:T(8,128)S(1)}, u32[]{:S(2)}, u32[]{:S(2)}) %collective-permute-start.5) | collective-permute-done | bytes 16416 | tf_op jit(solution)/shard_map/ppermute | solution.py:522
  37.6 3.1 %collective-permute-start.8 = (f32[40,128]{1,0:T(8,128)S(1)}, f32[40,128]{1,0:T(8,128)S(1)}, u32[]{:S(2)}, u32[]{:S(2)}) collective-permute-start(f32[40,128]{1,0:T(8,128)S(1)} %pad_maximum_fusion.1), channel_id=1, source_target_pairs={{0,8},{4,12},{8,0},{12,4},{16,24},{20,28},{24,16},{28,20},{1,9},{5... | collective-permute-start | bytes 61448 | tf_op jit(solution)/shard_map/ppermute | solution.py:522
  40.7 1.8 %collective-permute-done.8 = f32[40,128]{1,0:T(8,128)S(1)} collective-permute-done((f32[40,128]{1,0:T(8,128)S(1)}, f32[40,128]{1,0:T(8,128)S(1)}, u32[]{:S(2)}, u32[]{:S(2)}) %collective-permute-start.8) | collective-permute-done | bytes 20512 | tf_op jit(solution)/shard_map/ppermute | solution.py:522
  42.5 0.0 collective-permute-start.9
  42.5 1.2 %collective-permute-done.9.refs_1_ = f32[80,128]{1,0:T(8,128)S(1)} collective-permute-done((f32[80,128]{1,0:T(8,128)S(1)}, f32[80,128]{1,0:T(8,128)S(1)}, u32[]{:S(2)}, u32[]{:S(2)}) %collective-permute-start.9) | collective-permute-done | bytes 40992 | tf_op jit(solution)/shard_map/ppermute | solution.py:522
  43.7 3.3 %shard_map.124 = (f32[4,128]{1,0:T(4,128)}, f32[4,128]{1,0:T(4,128)}, f32[4,64]{1,0:T(4,128)}, f32[4,64]{1,0:T(4,128)}) custom-call(f32[64,128]{1,0:T(8,128)S(1)} %get-tuple-element.36.prior_ref, f32[80,128]{1,0:T(8,128)S(1)} %pad_maximum_fusion.refs_0_, f32[80,128]{1,0:T(8,128)S(1)} %collective-permute-done.9.refs_1_), custom_call_target="tpu_custom_call" | custom-call | tf_op jit(solution)/shard_map/pallas_call | solution.py:510
  (8 shorter events, 0.0 us)
Async XLA Ops:
  1.3 1.0 %copy-start = (f32[1,64,128]{2,1,0:T(8,128)S(1)}, f32[1,64,128]{2,1,0:T(8,128)}, u32[]{:S(2)}) copy-start(f32[1,64,128]{2,1,0:T(8,128)} %param.11) | copy-start | bytes 98308
  2.2 0.7 %copy-start.1 = (f32[1,128]{1,0:T(1,128)S(1)}, f32[1,128]{1,0:T(1,128)}, u32[]{:S(2)}) copy-start(f32[1,128]{1,0:T(1,128)} %param.12) | copy-start | bytes 1540
  2.9 6.2 %copy-start.5 = (f32[4]{0:T(128)S(1)}, f32[4]{0:T(128)}, u32[]{:S(2)}) copy-start(f32[4]{0:T(128)} %param.16) | copy-start | bytes 52
  3.0 6.1 %copy-start.2 = (f32[64]{0:T(128)S(1)}, f32[64]{0:T(128)}, u32[]{:S(2)}) copy-start(f32[64]{0:T(128)} %param.14) | copy-start | bytes 772
  3.0 6.1 %copy-start.3 = (f32[64]{0:T(128)S(1)}, f32[64]{0:T(128)}, u32[]{:S(2)}) copy-start(f32[64]{0:T(128)} %param.13) | copy-start | bytes 772
  3.0 6.1 %copy-start.4 = (f32[4]{0:T(128)S(1)}, f32[4]{0:T(128)}, u32[]{:S(2)}) copy-start(f32[4]{0:T(128)} %param.15) | copy-start | bytes 52
  3.1 6.1 %collective-permute-start.1 = (f32[208,128]{1,0:T(8,128)S(1)}, f32[208,128]{1,0:T(8,128)S(1)}, u32[]{:S(2)}, u32[]{:S(2)}) collective-permute-start(f32[208,128]{1,0:T(8,128)S(1)} %concatenate.14.own_ref), channel_id=1, source_target_pairs={{0,8},{4,12},{8,0},{12,4},{16,24},{20,28},{24,16},{28,20},{1,9},{5... | collective-permute-start | bytes 319496 | tf_op jit(solution)/shard_map/ppermute | solution.py:522
  6.1 3.1 %collective-permute-start = (f32[208,128]{1,0:T(8,128)S(1)}, f32[208,128]{1,0:T(8,128)S(1)}, u32[]{:S(2)}, u32[]{:S(2)}) collective-permute-start(f32[208,128]{1,0:T(8,128)S(1)} %concatenate.14.own_ref), channel_id=1, source_target_pairs={{0,4},{4,0},{8,12},{12,8},{16,20},{20,16},{24,28},{28,24},{1,5},{5... | collective-permute-start | bytes 319496 | tf_op jit(solution)/shard_map/ppermute | solution.py:522
  9.1 1.3 %collective-permute-start.2 = (f32[208,128]{1,0:T(8,128)S(1)}, f32[208,128]{1,0:T(8,128)S(1)}, u32[]{:S(2)}, u32[]{:S(2)}) collective-permute-start(f32[208,128]{1,0:T(8,128)S(1)} %collective-permute-done.1.two_ref), channel_id=1, source_target_pairs={{0,4},{4,0},{8,12},{12,8},{16,20},{20,16},{24,28},{28,24},{1,5},{5... | collective-permute-start | bytes 319496 | tf_op jit(solution)/shard_map/ppermute | solution.py:522
  14.3 7.0 %collective-permute-start.3 = (f32[152,128]{1,0:T(8,128)S(1)}, f32[152,128]{1,0:T(8,128)S(1)}, u32[]{:S(2)}, u32[]{:S(2)}) collective-permute-start(f32[152,128]{1,0:T(8,128)S(1)} %get-tuple-element.37), channel_id=1, source_target_pairs={{0,16},{4,20},{8,24},{12,28},{1,17},{5,21},{9,25},{13,29},{2,18},{... | collective-permute-start | bytes 233480 | tf_op jit(solution)/shard_map/ppermute | solution.py:581
  26.1 4.8 %collective-permute-start.4 = (f32[32,128]{1,0:T(8,128)S(1)}, f32[32,128]{1,0:T(8,128)S(1)}, u32[]{:S(2)}, u32[]{:S(2)}) collective-permute-start(f32[32,128]{1,0:T(8,128)S(1)} %get-tuple-element.46), channel_id=1, source_target_pairs={{0,16},{4,20},{8,24},{12,28},{16,0},{20,4},{24,8},{28,12},{1,17},{... | collective-permute-start | bytes 49160 | tf_op jit(solution)/shard_map/ppermute | solution.py:522
  30.9 3.7 %collective-permute-start.6 = (f32[32,128]{1,0:T(8,128)S(1)}, f32[32,128]{1,0:T(8,128)S(1)}, u32[]{:S(2)}, u32[]{:S(2)}) collective-permute-start(f32[32,128]{1,0:T(8,128)S(1)} %add.12), channel_id=1, source_target_pairs={{0,2},{1,3},{2,0},{3,1},{4,6},{5,7},{6,4},{7,5},{8,10},{9,11},{10,... | collective-permute-start | bytes 49160 | tf_op jit(solution)/shard_map/ppermute | solution.py:522
  32.5 4.6 %collective-permute-start.7 = (f32[32,128]{1,0:T(8,128)S(1)}, f32[32,128]{1,0:T(8,128)S(1)}, u32[]{:S(2)}, u32[]{:S(2)}) collective-permute-start(f32[32,128]{1,0:T(8,128)S(1)} %add.12), channel_id=1, source_target_pairs={{0,3},{1,2},{2,1},{3,0},{4,7},{5,6},{6,5},{7,4},{8,11},{9,10},{10,... | collective-permute-start | bytes 49160 | tf_op jit(solution)/shard_map/ppermute | solution.py:522
  33.9 3.7 %collective-permute-start.5 = (f32[32,128]{1,0:T(8,128)S(1)}, f32[32,128]{1,0:T(8,128)S(1)}, u32[]{:S(2)}, u32[]{:S(2)}) collective-permute-start(f32[32,128]{1,0:T(8,128)S(1)} %add.12), channel_id=1, source_target_pairs={{0,1},{1,0},{2,3},{3,2},{4,5},{5,4},{6,7},{7,6},{8,9},{9,8},{10,11... | collective-permute-start | bytes 49160 | tf_op jit(solution)/shard_map/ppermute | solution.py:522
  37.6 4.9 %collective-permute-start.8 = (f32[40,128]{1,0:T(8,128)S(1)}, f32[40,128]{1,0:T(8,128)S(1)}, u32[]{:S(2)}, u32[]{:S(2)}) collective-permute-start(f32[40,128]{1,0:T(8,128)S(1)} %pad_maximum_fusion.1), channel_id=1, source_target_pairs={{0,8},{4,12},{8,0},{12,4},{16,24},{20,28},{24,16},{28,20},{1,9},{5... | collective-permute-start | bytes 61448 | tf_op jit(solution)/shard_map/ppermute | solution.py:522
  42.5 1.2 %collective-permute-start.9 = (f32[80,128]{1,0:T(8,128)S(1)}, f32[80,128]{1,0:T(8,128)S(1)}, u32[]{:S(2)}, u32[]{:S(2)}) collective-permute-start(f32[80,128]{1,0:T(8,128)S(1)} %pad_maximum_fusion.refs_0_), channel_id=1, source_target_pairs={{0,4},{4,0},{8,12},{12,8},{16,20},{20,16},{24,28},{28,24},{1,5},{5... | collective-permute-start | bytes 122888 | tf_op jit(solution)/shard_map/ppermute | solution.py:522

commit v12 on v11

--- a/solution.py
+++ b/solution.py
@@ -81,10 +81,13 @@
     error = eye - mat * scale
     value = eye + error
     power = error.astype(BF16)
-    for _ in range(factors - 1):
-        power = product(power, power).astype(BF16)
-        value = value + product(value.astype(BF16), power)
-    return value * scale
+    power = product(power, power).astype(BF16)
+    size = mat.shape[0]
+    for _ in range(factors - 2):
+        both = product(jnp.concatenate([power, value.astype(BF16)], axis=0), power)
+        power = both[0:size, :].astype(BF16)
+        value = value + both[size:, :]
+    return (value + product(value.astype(BF16), power)) * scale
 
 
 def quotients(mats, lefts, rights, factors, refs, dims=NT):
@@ -98,8 +101,10 @@
     starts = [series(mat, factors) for mat in mats]
     linear, square = 0.0, 0.0
     for mat, start, left, right in zip(mats, starts, lefts, rights):
-        rest = eye - fine(mat, start)
-        first = fine(left, start)
+        size = mat.shape[0]
+        both = fine(jnp.concatenate([mat, left], axis=0), start)
+        rest = eye - both[0:size, :]
+        first = both[size:, :]
         low = rest.astype(BF16)
         twice = product(low, low)
         first = first + fine(first, rest + twice)
@@ -204,7 +209,7 @@
 
 def middle_kernel(tip, start, *refs):
     extra_ref, diag_ref, cross_ref, back_ref, right_ref, left_ref, part_ref, *refs = refs
-    *out_refs, far_ref, near_ref, share_ref, prior_ref, mat_ref, inv_ref = refs
+    *out_refs, far_ref, near_ref, share_ref, prior_ref, columns_ref, mat_ref, inv_ref = refs
     tile = diag_ref.shape[-1]
     side = right_ref.shape[1]
     last = jnp.where(lax.axis_index("tm") >= start, 1.0, 0.0).astype(F32)
@@ -224,12 +229,16 @@
         )
         for ref, value in zip(out_refs, values):
             ref[...] = value
+        columns_ref[2] = padded(values[3], tile).T
         far_ref[...] = back_ref[3] - last * over[one, one]
         near_ref[...] = left_ref[3] - last * over[tile : tile + side, one]
         share_ref[...] = part_ref[...] + last * over[tile : tile + tip, two]
         return total < SMALL
 
     settled = run(None)
+    for n in range(GROUP):
+        if n != 2:
+            columns_ref[n] = padded(right_ref[n], tile).T
     tips = extra_ref[0:1, :]
     row = lax.broadcasted_iota(jnp.int32, (tip, 128), 0)
     col = lax.broadcasted_iota(jnp.int32, (tip, 128), 1)
@@ -281,9 +290,9 @@
     return jnp.concatenate([rows, jnp.zeros((size - rows.shape[0], size), F32)], axis=0)
 
 
-def joined(state_ref, parts, order, refs, far=None, near=None):
+def joined(state_ref, parts, columns, order, refs, far=None, near=None):
     values = [[third[...] if n == 2 else every[n] for n in order] for every, third in zip(parts[:5], parts[5:])]
-    diags, crosses, backs, sides, lefts = values
+    diags, crosses, backs, _, lefts = values
     tile = crosses[0].shape[-1]
     base, came = receive(state_ref)
     came = padded(came, tile)
@@ -296,19 +305,18 @@
         mats, crosses, rights = mats + [base + far], crosses + [middle], rights + [middle]
     updates, total = quotients(mats, crosses, rights, 5, refs)
     results = []
-    for diag, side, (update, _) in zip(diags, sides, updates):
-        start = jnp.concatenate([diag, padded(side, tile).T], axis=1)
-        results.append(start - update)
+    for n, diag, (update, _) in zip(order, diags, updates):
+        results.append(jnp.concatenate([diag, columns[n]], axis=1) - update)
     return results, updates[-1][0], total
 
 
 def advance_kernel(state_ref, *refs):
-    *parts, out_ref, mat_ref, inv_ref = refs
+    *parts, columns_ref, out_ref, mat_ref, inv_ref = refs
     tile = state_ref.shape[1]
     position = lax.axis_index("tm")
 
     def run(refs):
-        (last,), _, total = joined(state_ref, parts, (GROUP - 1,), refs)
+        (last,), _, total = joined(state_ref, parts, columns_ref, (GROUP - 1,), refs)
         send(out_ref, last[:, 0:tile], last[:, tile:].T)
         return total < SMALL
 
@@ -414,13 +422,16 @@
 
 
 def merge_kernel(state_ref, *refs):
-    *parts, far_ref, near_ref, part_ref, square_ref, side_ref, sums_ref, small_ref, mat_ref, inv_ref, rows_ref, ends_ref = refs
+    *parts, columns_ref, far_ref, near_ref, part_ref = refs[:-8]
+    square_ref, side_ref, sums_ref, small_ref, mat_ref, inv_ref, rows_ref, ends_ref = refs[-8:]
     tile = state_ref.shape[1]
     tip = part_ref.shape[0]
     position = lax.axis_index("tm")
 
     def run(refs):
-        values, share, total = joined(state_ref, parts, range(GROUP), refs, far_ref[...], near_ref[...])
+        values, share, total = joined(
+            state_ref, parts, columns_ref, range(GROUP), refs, far_ref[...], near_ref[...]
+        )
         for n, value in enumerate(values):
             square_ref[n] = value[:, 0:tile]
             side_ref[n] = value[:, tile:]
@@ -440,8 +451,8 @@
         sums_ref[...] = fold(part_ref[...])
         values = []
         for n in range(GROUP):
-            diag, side = [third[...] if n == 2 else every[n] for every, third in zip(parts[0:4:3], parts[5:9:3])]
-            values.append(jnp.concatenate([diag, padded(side, tile).T], axis=1))
+            diag = parts[5][...] if n == 2 else parts[0][n]
+            values.append(jnp.concatenate([diag, columns_ref[n]], axis=1))
         factored(tip, values, small_ref, (mat_ref, inv_ref), rows_ref, ends_ref)
 
 
@@ -569,24 +580,24 @@
         (square, square, square, band, band, packed_state, (tip, tile)),
         ((GROUP,) + raw.shape, *pair),
     )
-    *thirds, prior = call(
+    thirds = call(
         functools.partial(middle_kernel, tip, groups - GROUP),
         (extra, *parts, part),
-        ((tile, tile),) * 3 + ((side, tile),) * 2 + ((tile, tile), (side, tile), (tip, tile), (tip, tile)),
+        ((tile, tile),) * 3 + ((side, tile),) * 2 + ((tile, tile), (side, tile), (tip, tile), (tip, tile), square),
         pair,
     )
-    *thirds, far, near, part = thirds
+    thirds, (far, near, part, prior, columns) = thirds[:5], thirds[5:]
     parts = (*parts, *thirds)
     for span in range(spans - 1):
         state = lax.ppermute(state, "tm", [(source, source + GROUP) for source in range(groups - GROUP)])
         if span < spans - 2:
-            (state,) = call(advance_kernel, (state, *parts), (packed_state,), pair)
+            (state,) = call(advance_kernel, (state, *parts, columns), (packed_state,), pair)
     if spans == 1:
         state = jnp.zeros_like(state)
     half = SUB * tile // 2
     squares, sides, sums, small = call(
         merge_kernel,
-        (state, *parts, far, near, part),
+        (state, *parts, columns, far, near, part),
         (square, square, (tip // 2, tile), (2 * GROUP, tile)),
         (*pair, (half, tile), (half, tile)),
     )

time: 47.2 us -> 47.8 us (1.013)
  no operation moved by 1% of the time
where the time goes in v12:
time: 47.8 us; the launch traced here: 47.6 us
  starting transfers between devices  17.7 us (37%)
  Pallas kernels  14.6 us (31%)
  waiting for transfers between devices  12.1 us (25%)
  between operations  1.43 us (3%)
  other arithmetic  0.93 us (2%)
  local copies, waits for them, and re-layouts  0.88 us (2%)
    pallas_call x5, Pallas kernels, call(): pl.pallas_call(body, out_shape=tuple((jax.ShapeDtypeStruct(shape, F32) fo...  14.6 us
    ppermute x9, starting transfers between devices, crossed(): lax.ppermute(value, axis, [(source, source ^ step) for source in range(si...  13.1 us
    ppermute x9, waiting for transfers between devices, crossed(): lax.ppermute(value, axis, [(source, source ^ step) for source in range(si...  12.1 us
    ppermute x1, starting transfers between devices, shards(): lax.ppermute(state, 'tm', [(source, source + GROUP) for source in range(g...  4.66 us
  transfers between devices with their start and end apart: 10, of which 8 were waited for; matrix products, arithmetic and copies ran while one was open for 0% of the time, Pallas kernels for 5%

profile of v12, /device:TPU:0, one launch (start us, length us, event | category | flops | bytes accessed | tf_op | source)
XLA Modules:
  0.0 47.6 jit_solution(3325127446705851808)
XLA Ops:
  1.3 0.0 copy-start
  1.3 0.9 %fusion = (f32[128]{0:T(128)S(1)}, f32[128,128]{1,0:T(8,128)S(1)}) fusion(f32[1,128,128]{2,1,0:T(8,128)} %param.10, f32[1,128,128]{2,1,0:T(8,128)} %param.9), kind=kLoop, calls=%fused_computation.2 | loop fusion | flops 81792 | bytes 197120 | tf_op jit(solution)/shard_map/reduce_sum | solution.py:565
  2.2 0.0 copy-start.1
  2.2 0.0 copy-done
  2.2 0.6 %copy-done.1 = f32[1,128]{1,0:T(1,128)S(1)} copy-done((f32[1,128]{1,0:T(1,128)S(1)}, f32[1,128]{1,0:T(1,128)}, u32[]{:S(2)}) %copy-start.1) | copy-done | bytes 536
  2.9 0.0 copy-start.5
  2.9 0.1 concatenate.14.own_ref
  3.0 0.0 copy-start.2
  3.0 0.0 copy-start.3
  3.0 0.0 copy-start.4
  3.1 3.1 %collective-permute-start.1 = (f32[208,128]{1,0:T(8,128)S(1)}, f32[208,128]{1,0:T(8,128)S(1)}, u32[]{:S(2)}, u32[]{:S(2)}) collective-permute-start(f32[208,128]{1,0:T(8,128)S(1)} %concatenate.14.own_ref), channel_id=1, source_target_pairs={{0,8},{4,12},{8,0},{12,4},{16,24},{20,28},{24,16},{28,20},{1,9},{5... | collective-permute-start | bytes 319496 | tf_op jit(solution)/shard_map/ppermute | solution.py:533
  6.1 0.0 collective-permute-start
  6.1 3.0 %collective-permute-done.1.two_ref = f32[208,128]{1,0:T(8,128)S(1)} collective-permute-done((f32[208,128]{1,0:T(8,128)S(1)}, f32[208,128]{1,0:T(8,128)S(1)}, u32[]{:S(2)}, u32[]{:S(2)}) %collective-permute-start.1) | collective-permute-done | bytes 106528 | tf_op jit(solution)/shard_map/ppermute | solution.py:533
  9.1 0.0 collective-permute-start.2
  9.1 0.0 copy-done.5
  9.1 0.0 copy-done.2
  9.1 0.0 copy-done.3
  9.1 0.0 copy-done.4
  9.2 0.1 concatenate.13
  9.2 0.0 collective-permute-done.one_ref
  9.2 1.2 %collective-permute-done.2.three_ref = f32[208,128]{1,0:T(8,128)S(1)} collective-permute-done((f32[208,128]{1,0:T(8,128)S(1)}, f32[208,128]{1,0:T(8,128)S(1)}, u32[]{:S(2)}, u32[]{:S(2)}) %collective-permute-start.2) | collective-permute-done | bytes 106528 | tf_op jit(solution)/shard_map/ppermute | solution.py:533
  10.4 3.8 %shard_map.120 = (f32[4,128,128]{2,1,0:T(8,128)S(1)}, f32[4,128,128]{2,1,0:T(8,128)S(1)}, f32[4,128,128]{2,1,0:T(8,128)S(1)}, f32[4,80,128]{2,1,0:T(8,128)S(1)},...) custom-call(f32[2,128]{1,0:T(2,128)S(1)} %bitcast.17, ...), custom_call_target="tpu_custom_call" | custom-call | tf_op jit(solution)/shard_map/pallas_call | solution.py:521
  14.3 4.7 %collective-permute-start.3 = (f32[152,128]{1,0:T(8,128)S(1)}, f32[152,128]{1,0:T(8,128)S(1)}, u32[]{:S(2)}, u32[]{:S(2)}) collective-permute-start(f32[152,128]{1,0:T(8,128)S(1)} %get-tuple-element.38), channel_id=1, source_target_pairs={{0,16},{4,20},{8,24},{12,28},{1,17},{5,21},{9,25},{13,29},{2,18},{... | collective-permute-start | bytes 233480 | tf_op jit(solution)/shard_map/ppermute | solution.py:592
  18.9 2.4 %shard_map.121 = (f32[128,128]{1,0:T(8,128)S(1)}, f32[128,128]{1,0:T(8,128)S(1)}, f32[128,128]{1,0:T(8,128)S(1)}, f32[80,128]{1,0:T(8,128)S(1)}, f32[80,128]{1,0...) custom-call(f32[2,128]{1,0:T(2,128)S(1)} %bitcast.18, ...), custom_call_target="tpu_custom_call" | custom-call | tf_op jit(solution)/shard_map/pallas_call | solution.py:521
  21.4 0.0 collective-permute-done.3.state_ref
  21.4 5.0 %shard_map.122 = (f32[4,128,128]{2,1,0:T(8,128)S(1)}, f32[4,128,128]{2,1,0:T(8,128)S(1)}, f32[32,128]{1,0:T(8,128)S(1)}, f32[8,128]{1,0:T(8,128)S(1)}) custom-call(f32[152,128]{1,0:T(8,128)S(1)} %collective-permute-done.3.state_ref, f32[4,128,128]{2,1,0:T(8,128)S(1)} %get-tuple-element.31.refs_1_.refs_0_, ...), custom_call_target="tpu_custom_call" | custom-call | tf_op jit(solution)/shard_map/pallas_call | solution.py:521
  26.4 3.4 %collective-permute-start.4 = (f32[32,128]{1,0:T(8,128)S(1)}, f32[32,128]{1,0:T(8,128)S(1)}, u32[]{:S(2)}, u32[]{:S(2)}) collective-permute-start(f32[32,128]{1,0:T(8,128)S(1)} %get-tuple-element.48), channel_id=1, source_target_pairs={{0,16},{4,20},{8,24},{12,28},{16,0},{20,4},{24,8},{28,12},{1,17},{... | collective-permute-start | bytes 49160 | tf_op jit(solution)/shard_map/ppermute | solution.py:533
  29.8 1.7 %collective-permute-done.4 = f32[32,128]{1,0:T(8,128)S(1)} collective-permute-done((f32[32,128]{1,0:T(8,128)S(1)}, f32[32,128]{1,0:T(8,128)S(1)}, u32[]{:S(2)}, u32[]{:S(2)}) %collective-permute-start.4) | collective-permute-done | bytes 16416 | tf_op jit(solution)/shard_map/ppermute | solution.py:533
  31.5 1.5 %collective-permute-start.6 = (f32[32,128]{1,0:T(8,128)S(1)}, f32[32,128]{1,0:T(8,128)S(1)}, u32[]{:S(2)}, u32[]{:S(2)}) collective-permute-start(f32[32,128]{1,0:T(8,128)S(1)} %add.12), channel_id=1, source_target_pairs={{0,2},{1,3},{2,0},{3,1},{4,6},{5,7},{6,4},{7,5},{8,10},{9,11},{10,... | collective-permute-start | bytes 49160 | tf_op jit(solution)/shard_map/ppermute | solution.py:533
  33.0 1.4 %collective-permute-start.7 = (f32[32,128]{1,0:T(8,128)S(1)}, f32[32,128]{1,0:T(8,128)S(1)}, u32[]{:S(2)}, u32[]{:S(2)}) collective-permute-start(f32[32,128]{1,0:T(8,128)S(1)} %add.12), channel_id=1, source_target_pairs={{0,3},{1,2},{2,1},{3,0},{4,7},{5,6},{6,5},{7,4},{8,11},{9,10},{10,... | collective-permute-start | bytes 49160 | tf_op jit(solution)/shard_map/ppermute | solution.py:533
  34.5 0.5 %collective-permute-start.5 = (f32[32,128]{1,0:T(8,128)S(1)}, f32[32,128]{1,0:T(8,128)S(1)}, u32[]{:S(2)}, u32[]{:S(2)}) collective-permute-start(f32[32,128]{1,0:T(8,128)S(1)} %add.12), channel_id=1, source_target_pairs={{0,1},{1,0},{2,3},{3,2},{4,5},{5,4},{6,7},{7,6},{8,9},{9,8},{10,11... | collective-permute-start | bytes 49160 | tf_op jit(solution)/shard_map/ppermute | solution.py:533
  35.0 0.2 collective-permute-done.6
  35.3 2.4 %collective-permute-done.7 = f32[32,128]{1,0:T(8,128)S(1)} collective-permute-done((f32[32,128]{1,0:T(8,128)S(1)}, f32[32,128]{1,0:T(8,128)S(1)}, u32[]{:S(2)}, u32[]{:S(2)}) %collective-permute-start.7) | collective-permute-done | bytes 16416 | tf_op jit(solution)/shard_map/ppermute | solution.py:533
  37.7 0.5 %collective-permute-done.5 = f32[32,128]{1,0:T(8,128)S(1)} collective-permute-done((f32[32,128]{1,0:T(8,128)S(1)}, f32[32,128]{1,0:T(8,128)S(1)}, u32[]{:S(2)}, u32[]{:S(2)}) %collective-permute-start.5) | collective-permute-done | bytes 16416 | tf_op jit(solution)/shard_map/ppermute | solution.py:533
  38.2 3.1 %collective-permute-start.8 = (f32[40,128]{1,0:T(8,128)S(1)}, f32[40,128]{1,0:T(8,128)S(1)}, u32[]{:S(2)}, u32[]{:S(2)}) collective-permute-start(f32[40,128]{1,0:T(8,128)S(1)} %pad_maximum_fusion.1), channel_id=1, source_target_pairs={{0,8},{4,12},{8,0},{12,4},{16,24},{20,28},{24,16},{28,20},{1,9},{5... | collective-permute-start | bytes 61448 | tf_op jit(solution)/shard_map/ppermute | solution.py:533
  41.3 1.8 %collective-permute-done.8 = f32[40,128]{1,0:T(8,128)S(1)} collective-permute-done((f32[40,128]{1,0:T(8,128)S(1)}, f32[40,128]{1,0:T(8,128)S(1)}, u32[]{:S(2)}, u32[]{:S(2)}) %collective-permute-start.8) | collective-permute-done | bytes 20512 | tf_op jit(solution)/shard_map/ppermute | solution.py:533
  43.1 0.0 collective-permute-start.9
  43.1 1.2 %collective-permute-done.9.refs_1_ = f32[80,128]{1,0:T(8,128)S(1)} collective-permute-done((f32[80,128]{1,0:T(8,128)S(1)}, f32[80,128]{1,0:T(8,128)S(1)}, u32[]{:S(2)}, u32[]{:S(2)}) %collective-permute-start.9) | collective-permute-done | bytes 40992 | tf_op jit(solution)/shard_map/ppermute | solution.py:533
  44.3 3.3 %shard_map.124 = (f32[4,128]{1,0:T(4,128)}, f32[4,128]{1,0:T(4,128)}, f32[4,64]{1,0:T(4,128)}, f32[4,64]{1,0:T(4,128)}) custom-call(f32[64,128]{1,0:T(8,128)S(1)} %get-tuple-element.37.prior_ref, f32[80,128]{1,0:T(8,128)S(1)} %pad_maximum_fusion.refs_0_, f32[80,128]{1,0:T(8,128)S(1)} %collective-permute-done.9.refs_1_), custom_call_target="tpu_custom_call" | custom-call | tf_op jit(solution)/shard_map/pallas_call | solution.py:521
  (8 shorter events, 0.0 us)
Async XLA Ops:
  1.3 1.0 %copy-start = (f32[1,64,128]{2,1,0:T(8,128)S(1)}, f32[1,64,128]{2,1,0:T(8,128)}, u32[]{:S(2)}) copy-start(f32[1,64,128]{2,1,0:T(8,128)} %param.11) | copy-start | bytes 98308
  2.2 0.7 %copy-start.1 = (f32[1,128]{1,0:T(1,128)S(1)}, f32[1,128]{1,0:T(1,128)}, u32[]{:S(2)}) copy-start(f32[1,128]{1,0:T(1,128)} %param.12) | copy-start | bytes 1540
  2.9 6.2 %copy-start.5 = (f32[4]{0:T(128)S(1)}, f32[4]{0:T(128)}, u32[]{:S(2)}) copy-start(f32[4]{0:T(128)} %param.16) | copy-start | bytes 52
  3.0 6.1 %copy-start.2 = (f32[64]{0:T(128)S(1)}, f32[64]{0:T(128)}, u32[]{:S(2)}) copy-start(f32[64]{0:T(128)} %param.14) | copy-start | bytes 772
  3.0 6.1 %copy-start.3 = (f32[64]{0:T(128)S(1)}, f32[64]{0:T(128)}, u32[]{:S(2)}) copy-start(f32[64]{0:T(128)} %param.13) | copy-start | bytes 772
  3.0 6.1 %copy-start.4 = (f32[4]{0:T(128)S(1)}, f32[4]{0:T(128)}, u32[]{:S(2)}) copy-start(f32[4]{0:T(128)} %param.15) | copy-start | bytes 52
  3.1 6.1 %collective-permute-start.1 = (f32[208,128]{1,0:T(8,128)S(1)}, f32[208,128]{1,0:T(8,128)S(1)}, u32[]{:S(2)}, u32[]{:S(2)}) collective-permute-start(f32[208,128]{1,0:T(8,128)S(1)} %concatenate.14.own_ref), channel_id=1, source_target_pairs={{0,8},{4,12},{8,0},{12,4},{16,24},{20,28},{24,16},{28,20},{1,9},{5... | collective-permute-start | bytes 319496 | tf_op jit(solution)/shard_map/ppermute | solution.py:533
  6.1 3.1 %collective-permute-start = (f32[208,128]{1,0:T(8,128)S(1)}, f32[208,128]{1,0:T(8,128)S(1)}, u32[]{:S(2)}, u32[]{:S(2)}) collective-permute-start(f32[208,128]{1,0:T(8,128)S(1)} %concatenate.14.own_ref), channel_id=1, source_target_pairs={{0,4},{4,0},{8,12},{12,8},{16,20},{20,16},{24,28},{28,24},{1,5},{5... | collective-permute-start | bytes 319496 | tf_op jit(solution)/shard_map/ppermute | solution.py:533
  9.1 1.3 %collective-permute-start.2 = (f32[208,128]{1,0:T(8,128)S(1)}, f32[208,128]{1,0:T(8,128)S(1)}, u32[]{:S(2)}, u32[]{:S(2)}) collective-permute-start(f32[208,128]{1,0:T(8,128)S(1)} %collective-permute-done.1.two_ref), channel_id=1, source_target_pairs={{0,4},{4,0},{8,12},{12,8},{16,20},{20,16},{24,28},{28,24},{1,5},{5... | collective-permute-start | bytes 319496 | tf_op jit(solution)/shard_map/ppermute | solution.py:533
  14.3 7.1 %collective-permute-start.3 = (f32[152,128]{1,0:T(8,128)S(1)}, f32[152,128]{1,0:T(8,128)S(1)}, u32[]{:S(2)}, u32[]{:S(2)}) collective-permute-start(f32[152,128]{1,0:T(8,128)S(1)} %get-tuple-element.38), channel_id=1, source_target_pairs={{0,16},{4,20},{8,24},{12,28},{1,17},{5,21},{9,25},{13,29},{2,18},{... | collective-permute-start | bytes 233480 | tf_op jit(solution)/shard_map/ppermute | solution.py:592
  26.4 5.1 %collective-permute-start.4 = (f32[32,128]{1,0:T(8,128)S(1)}, f32[32,128]{1,0:T(8,128)S(1)}, u32[]{:S(2)}, u32[]{:S(2)}) collective-permute-start(f32[32,128]{1,0:T(8,128)S(1)} %get-tuple-element.48), channel_id=1, source_target_pairs={{0,16},{4,20},{8,24},{12,28},{16,0},{20,4},{24,8},{28,12},{1,17},{... | collective-permute-start | bytes 49160 | tf_op jit(solution)/shard_map/ppermute | solution.py:533
  31.5 3.7 %collective-permute-start.6 = (f32[32,128]{1,0:T(8,128)S(1)}, f32[32,128]{1,0:T(8,128)S(1)}, u32[]{:S(2)}, u32[]{:S(2)}) collective-permute-start(f32[32,128]{1,0:T(8,128)S(1)} %add.12), channel_id=1, source_target_pairs={{0,2},{1,3},{2,0},{3,1},{4,6},{5,7},{6,4},{7,5},{8,10},{9,11},{10,... | collective-permute-start | bytes 49160 | tf_op jit(solution)/shard_map/ppermute | solution.py:533
  33.0 4.6 %collective-permute-start.7 = (f32[32,128]{1,0:T(8,128)S(1)}, f32[32,128]{1,0:T(8,128)S(1)}, u32[]{:S(2)}, u32[]{:S(2)}) collective-permute-start(f32[32,128]{1,0:T(8,128)S(1)} %add.12), channel_id=1, source_target_pairs={{0,3},{1,2},{2,1},{3,0},{4,7},{5,6},{6,5},{7,4},{8,11},{9,10},{10,... | collective-permute-start | bytes 49160 | tf_op jit(solution)/shard_map/ppermute | solution.py:533
  34.5 3.7 %collective-permute-start.5 = (f32[32,128]{1,0:T(8,128)S(1)}, f32[32,128]{1,0:T(8,128)S(1)}, u32[]{:S(2)}, u32[]{:S(2)}) collective-permute-start(f32[32,128]{1,0:T(8,128)S(1)} %add.12), channel_id=1, source_target_pairs={{0,1},{1,0},{2,3},{3,2},{4,5},{5,4},{6,7},{7,6},{8,9},{9,8},{10,11... | collective-permute-start | bytes 49160 | tf_op jit(solution)/shard_map/ppermute | solution.py:533
  38.2 4.9 %collective-permute-start.8 = (f32[40,128]{1,0:T(8,128)S(1)}, f32[40,128]{1,0:T(8,128)S(1)}, u32[]{:S(2)}, u32[]{:S(2)}) collective-permute-start(f32[40,128]{1,0:T(8,128)S(1)} %pad_maximum_fusion.1), channel_id=1, source_target_pairs={{0,8},{4,12},{8,0},{12,4},{16,24},{20,28},{24,16},{28,20},{1,9},{5... | collective-permute-start | bytes 61448 | tf_op jit(solution)/shard_map/ppermute | solution.py:533
  43.1 1.2 %collective-permute-start.9 = (f32[80,128]{1,0:T(8,128)S(1)}, f32[80,128]{1,0:T(8,128)S(1)}, u32[]{:S(2)}, u32[]{:S(2)}) collective-permute-start(f32[80,128]{1,0:T(8,128)S(1)} %pad_maximum_fusion.refs_0_), channel_id=1, source_target_pairs={{0,4},{4,0},{8,12},{12,8},{16,20},{20,16},{24,28},{28,24},{1,5},{5... | collective-permute-start | bytes 122888 | tf_op jit(solution)/shard_map/ppermute | solution.py:533

commit v13 on v11

--- a/solution.py
+++ b/solution.py
@@ -281,35 +281,39 @@
     return jnp.concatenate([rows, jnp.zeros((size - rows.shape[0], size), F32)], axis=0)
 
 
-def joined(state_ref, parts, order, refs, far=None, near=None):
+def joined(state_ref, parts, order, sides, refs, far=None, near=None):
     values = [[third[...] if n == 2 else every[n] for n in order] for every, third in zip(parts[:5], parts[5:])]
-    diags, crosses, backs, sides, lefts = values
+    _, crosses, backs, _, lefts = values
     tile = crosses[0].shape[-1]
     base, came = receive(state_ref)
-    came = padded(came, tile)
+    count = came.shape[0]
     mats = [base + back for back in backs]
-    rights = [
-        jnp.concatenate([cross, came + padded(left, tile)], axis=0) for cross, left in zip(crosses, lefts)
-    ]
+    rights = []
+    for n, cross, left in zip(order, crosses, lefts):
+        tail = came[sides:, :] + left[sides:count, :]
+        if sides:
+            spot = lax.broadcasted_iota(jnp.int32, tail.shape, 0)
+            tail = jnp.where(spot == n, tail[0:1, :], 0.0)
+        rights.append(jnp.concatenate([cross, tail, jnp.zeros((SUB, tile), F32)], axis=0))
     if far is not None:
-        middle = came + padded(near, tile)
+        middle = padded(came + near[0:count, :], tile)
         mats, crosses, rights = mats + [base + far], crosses + [middle], rights + [middle]
     updates, total = quotients(mats, crosses, rights, 5, refs)
-    results = []
-    for diag, side, (update, _) in zip(diags, sides, updates):
-        start = jnp.concatenate([diag, padded(side, tile).T], axis=1)
-        results.append(start - update)
-    return results, updates[-1][0], total
+    return [update for update, _ in updates], total
 
 
 def advance_kernel(state_ref, *refs):
     *parts, out_ref, mat_ref, inv_ref = refs
     tile = state_ref.shape[1]
     position = lax.axis_index("tm")
+    diag, side = parts[0][GROUP - 1], parts[3][GROUP - 1]
 
     def run(refs):
-        (last,), _, total = joined(state_ref, parts, (GROUP - 1,), refs)
-        send(out_ref, last[:, 0:tile], last[:, tile:].T)
+        (update,), total = joined(state_ref, parts, (GROUP - 1,), 0, refs)
+        ends = update[:, tile:]
+        count = ends.shape[1]
+        ends = jnp.concatenate([ends, jnp.zeros((tile, tile - count), F32)], axis=1)
+        send(out_ref, diag - update[:, 0:tile], side[0:count, :] - ends.T[0:count, :])
         return total < SMALL
 
     @pl.when(position >= GROUP)
@@ -322,7 +326,7 @@
 
     @pl.when(position < GROUP)
     def _():
-        send(out_ref, parts[0][GROUP - 1], parts[3][GROUP - 1])
+        send(out_ref, diag, side)
 
 
 def splat(value, lane):
@@ -373,23 +377,32 @@
     return pivots, column
 
 
-def halved(values, refs):
-    tile = values[0].shape[0]
+def halved(squares, sides, refs):
+    tile = squares[0].shape[0]
     half = tile // 2
     col = lax.broadcasted_iota(jnp.int32, (half, tile), 1)
+
+    def beside(rows, side):
+        return jnp.where(col < half, rows, jnp.where(col == half, side, 0.0))
+
+    uppers, overs, lowers = [], [], []
+    for n, square in enumerate(squares):
+        top, bottom = square[0:half, :], square[half:, :]
+        side = sides[:, n : n + 1]
+        uppers.append(beside(top, side[0:half, :]))
+        overs.append(beside(pltpu.roll(top, half, 1), side[0:half, :]))
+        lowers.append(beside(pltpu.roll(bottom, half, 1), side[half:, :]))
     mats, lefts, rights = [], [], []
-    for one, two in zip(values[0::2], values[1::2]):
+    for n in range(0, len(squares), 2):
         for rows, target in ((slice(0, half), mats), (slice(half, tile), lefts)):
-            first = jnp.where(col < half, one[rows, 0:tile], 0.0)
-            second = jnp.where(col < half, two[rows, 0:tile], 0.0)
+            first = jnp.where(col < half, squares[n][rows, :], 0.0)
+            second = jnp.where(col < half, squares[n + 1][rows, :], 0.0)
             target.append(jnp.concatenate([first, pltpu.roll(second, half, 1)], axis=0))
-        rights.append(jnp.concatenate([one[0:half, :], two[0:half, :]], axis=0))
+        rights.append(jnp.concatenate([overs[n], overs[n + 1]], axis=0))
     updates, total = quotients(mats, lefts, rights, 4, refs, NN)
-    uppers = [value[0:half, :] for value in values]
-    lowers = []
-    for place, value in enumerate(values):
+    for place, value in enumerate(lowers):
         first = (place % 2) * half
-        lowers.append(value[half:, :] - updates[place // 2][0][first : first + half, :])
+        lowers[place] = value - updates[place // 2][0][first : first + half, :]
     return uppers, lowers, total
 
 
@@ -414,17 +427,23 @@
 
 
 def merge_kernel(state_ref, *refs):
-    *parts, far_ref, near_ref, part_ref, square_ref, side_ref, sums_ref, small_ref, mat_ref, inv_ref, rows_ref, ends_ref = refs
+    *parts, far_ref, near_ref, part_ref = refs[:-7]
+    square_ref, side_ref, sums_ref, small_ref, mat_ref, inv_ref, rows_ref = refs[-7:]
     tile = state_ref.shape[1]
     tip = part_ref.shape[0]
     position = lax.axis_index("tm")
+    diags = [parts[5][...] if n == 2 else parts[0][n] for n in range(GROUP)]
+    sides = [(parts[8][...] if n == 2 else parts[3][n])[tip : tip + 1, :] for n in range(GROUP)]
+    sides = padded(jnp.concatenate(sides, axis=0), tile).T[:, 0:SUB]
 
     def run(refs):
-        values, share, total = joined(state_ref, parts, range(GROUP), refs, far_ref[...], near_ref[...])
-        for n, value in enumerate(values):
-            square_ref[n] = value[:, 0:tile]
-            side_ref[n] = value[:, tile:]
-        sums_ref[...] = fold(part_ref[...] + share[0:tip, :])
+        updates, total = joined(state_ref, parts, range(GROUP), tip, refs, far_ref[...], near_ref[...])
+        ends = sides
+        for n, diag in enumerate(diags):
+            square_ref[n] = diag - updates[n][:, 0:tile]
+            ends = ends - updates[n][:, tile : tile + SUB]
+        side_ref[...] = ends
+        sums_ref[...] = fold(part_ref[...] + updates[-1][0:tip, :])
         return total < SMALL
 
     @pl.when(position >= GROUP)
@@ -438,25 +457,17 @@
     @pl.when(position < GROUP)
     def _():
         sums_ref[...] = fold(part_ref[...])
-        values = []
-        for n in range(GROUP):
-            diag, side = [third[...] if n == 2 else every[n] for every, third in zip(parts[0:4:3], parts[5:9:3])]
-            values.append(jnp.concatenate([diag, padded(side, tile).T], axis=1))
-        factored(tip, values, small_ref, (mat_ref, inv_ref), rows_ref, ends_ref)
-
-
-def factored(tip, values, small_ref, spare, rows_ref, ends_ref):
-    tile = values[0].shape[0]
+        factored(diags, sides, small_ref, (mat_ref, inv_ref), rows_ref)
+
+
+def factored(squares, sides, small_ref, spare, rows_ref):
+    tile = squares[0].shape[0]
     half = tile // 2
 
     def run(refs):
-        uppers, lowers, total = halved(values, refs)
-        for b, value in enumerate(uppers):
-            rows_ref[pl.ds(b, half, stride=SUB), :] = value[:, 0:tile]
-            ends_ref[pl.ds(b, half, stride=SUB), :] = value[:, tile:]
-        for b, value in enumerate(lowers):
-            rows_ref[pl.ds(GROUP + b, half, stride=SUB), :] = pltpu.roll(value[:, 0:tile], half, 1)
-            ends_ref[pl.ds(GROUP + b, half, stride=SUB), :] = value[:, tile:]
+        uppers, lowers, total = halved(squares, sides, refs)
+        for b, value in enumerate(uppers + lowers):
+            rows_ref[pl.ds(b, half, stride=SUB), :] = value
         return total < SMALL
 
     settled = run(None)
@@ -465,20 +476,20 @@
     def _():
         run(spare)
 
-    pivots, column = factor((rows_ref, ends_ref), half, 2 * GROUP, tip)
+    pivots, column = factor((rows_ref,), half, 2 * GROUP, half)
     for n, value in enumerate((0.5 * jnp.log(pivots), column)):
         spot = slice(n * GROUP, (n + 1) * GROUP)
         small_ref[spot, 0:half] = value[0:GROUP, 0:half]
         small_ref[spot, half:] = value[GROUP:, 0:half]
 
 
-def factor_kernel(tip, square_ref, side_ref, early_ref, small_ref, mat_ref, inv_ref, rows_ref, ends_ref):
+def factor_kernel(square_ref, side_ref, early_ref, small_ref, mat_ref, inv_ref, rows_ref):
     position = lax.axis_index("tm")
 
     @pl.when(position >= GROUP)
     def _():
-        values = [jnp.concatenate([square_ref[n], side_ref[n]], axis=1) for n in range(GROUP)]
-        factored(tip, values, small_ref, (mat_ref, inv_ref), rows_ref, ends_ref)
+        squares = [square_ref[n] for n in range(GROUP)]
+        factored(squares, side_ref[...], small_ref, (mat_ref, inv_ref), rows_ref)
 
     @pl.when(position < GROUP)
     def _():
@@ -587,14 +598,14 @@
     squares, sides, sums, small = call(
         merge_kernel,
         (state, *parts, far, near, part),
-        (square, square, (tip // 2, tile), (2 * GROUP, tile)),
-        (*pair, (half, tile), (half, tile)),
+        (square, (tile, SUB), (tip // 2, tile), (2 * GROUP, tile)),
+        (*pair, (half, tile)),
     )
     (small,) = call(
-        functools.partial(factor_kernel, tip),
+        factor_kernel,
         (squares, sides, small),
         ((2 * GROUP, tile),),
-        (*pair, (half, tile), (half, tile)),
+        (*pair, (half, tile)),
     )
     for axis, first in (("tm", GROUP), ("mesh", 4)):
         step = first

time: 47.2 us -> 47.4 us (level)
  no operation moved by 1% of the time
where the time goes in v13:
time: 47.4 us; the launch traced here: 47.2 us
  starting transfers between devices  17.5 us (37%)
  Pallas kernels  14.3 us (30%)
  waiting for transfers between devices  12.1 us (26%)
  between operations  1.43 us (3%)
  other arithmetic  0.93 us (2%)
  local copies, waits for them, and re-layouts  0.88 us (2%)
    pallas_call x5, Pallas kernels, call(): pl.pallas_call(body, out_shape=tuple((jax.ShapeDtypeStruct(shape, F32) fo...  14.3 us
    ppermute x9, starting transfers between devices, crossed(): lax.ppermute(value, axis, [(source, source ^ step) for source in range(si...  12.9 us
    ppermute x9, waiting for transfers between devices, crossed(): lax.ppermute(value, axis, [(source, source ^ step) for source in range(si...  12.1 us
    ppermute x1, starting transfers between devices, shards(): lax.ppermute(state, 'tm', [(source, source + GROUP) for source in range(g...  4.66 us
  transfers between devices with their start and end apart: 10, of which 8 were waited for; matrix products, arithmetic and copies ran while one was open for 0% of the time, Pallas kernels for 5%

profile of v13, /device:TPU:0, one launch (start us, length us, event | category | flops | bytes accessed | tf_op | source)
XLA Modules:
  0.0 47.2 jit_solution(12677117501318518973)
XLA Ops:
  1.3 0.0 copy-start
  1.3 0.9 %fusion = (f32[128]{0:T(128)S(1)}, f32[128,128]{1,0:T(8,128)S(1)}) fusion(f32[1,128,128]{2,1,0:T(8,128)} %param.10, f32[1,128,128]{2,1,0:T(8,128)} %param.9), kind=kLoop, calls=%fused_computation.2 | loop fusion | flops 81792 | bytes 197120 | tf_op jit(solution)/shard_map/reduce_sum | solution.py:565
  2.2 0.0 copy-start.1
  2.2 0.0 copy-done
  2.2 0.6 %copy-done.1 = f32[1,128]{1,0:T(1,128)S(1)} copy-done((f32[1,128]{1,0:T(1,128)S(1)}, f32[1,128]{1,0:T(1,128)}, u32[]{:S(2)}) %copy-start.1) | copy-done | bytes 536
  2.9 0.0 copy-start.5
  2.9 0.1 concatenate.14.own_ref
  3.0 0.0 copy-start.2
  3.0 0.0 copy-start.3
  3.0 0.0 copy-start.4
  3.1 3.1 %collective-permute-start.1 = (f32[208,128]{1,0:T(8,128)S(1)}, f32[208,128]{1,0:T(8,128)S(1)}, u32[]{:S(2)}, u32[]{:S(2)}) collective-permute-start(f32[208,128]{1,0:T(8,128)S(1)} %concatenate.14.own_ref), channel_id=1, source_target_pairs={{0,8},{4,12},{8,0},{12,4},{16,24},{20,28},{24,16},{28,20},{1,9},{5... | collective-permute-start | bytes 319496 | tf_op jit(solution)/shard_map/ppermute | solution.py:533
  6.1 0.0 collective-permute-start
  6.1 3.0 %collective-permute-done.1.two_ref = f32[208,128]{1,0:T(8,128)S(1)} collective-permute-done((f32[208,128]{1,0:T(8,128)S(1)}, f32[208,128]{1,0:T(8,128)S(1)}, u32[]{:S(2)}, u32[]{:S(2)}) %collective-permute-start.1) | collective-permute-done | bytes 106528 | tf_op jit(solution)/shard_map/ppermute | solution.py:533
  9.1 0.0 collective-permute-start.2
  9.1 0.0 copy-done.5
  9.1 0.0 copy-done.2
  9.1 0.0 copy-done.3
  9.1 0.0 copy-done.4
  9.2 0.1 concatenate.13
  9.2 0.0 collective-permute-done.one_ref
  9.2 1.2 %collective-permute-done.2.three_ref = f32[208,128]{1,0:T(8,128)S(1)} collective-permute-done((f32[208,128]{1,0:T(8,128)S(1)}, f32[208,128]{1,0:T(8,128)S(1)}, u32[]{:S(2)}, u32[]{:S(2)}) %collective-permute-start.2) | collective-permute-done | bytes 106528 | tf_op jit(solution)/shard_map/ppermute | solution.py:533
  10.4 3.9 %shard_map.120 = (f32[4,128,128]{2,1,0:T(8,128)S(1)}, f32[4,128,128]{2,1,0:T(8,128)S(1)}, f32[4,128,128]{2,1,0:T(8,128)S(1)}, f32[4,80,128]{2,1,0:T(8,128)S(1)},...) custom-call(f32[2,128]{1,0:T(2,128)S(1)} %bitcast.17, ...), custom_call_target="tpu_custom_call" | custom-call | tf_op jit(solution)/shard_map/pallas_call | solution.py:521
  14.3 4.7 %collective-permute-start.3 = (f32[152,128]{1,0:T(8,128)S(1)}, f32[152,128]{1,0:T(8,128)S(1)}, u32[]{:S(2)}, u32[]{:S(2)}) collective-permute-start(f32[152,128]{1,0:T(8,128)S(1)} %get-tuple-element.37), channel_id=1, source_target_pairs={{0,16},{4,20},{8,24},{12,28},{1,17},{5,21},{9,25},{13,29},{2,18},{... | collective-permute-start | bytes 233480 | tf_op jit(solution)/shard_map/ppermute | solution.py:592
  19.0 2.3 %shard_map.121 = (f32[128,128]{1,0:T(8,128)S(1)}, f32[128,128]{1,0:T(8,128)S(1)}, f32[128,128]{1,0:T(8,128)S(1)}, f32[80,128]{1,0:T(8,128)S(1)}, f32[80,128]{1,0...) custom-call(f32[2,128]{1,0:T(2,128)S(1)} %bitcast.18, ...), custom_call_target="tpu_custom_call" | custom-call | tf_op jit(solution)/shard_map/pallas_call | solution.py:521
  21.3 0.0 collective-permute-done.3.state_ref
  21.3 4.8 %shard_map.122 = (f32[4,128,128]{2,1,0:T(8,128)S(1)}, f32[128,8]{1,0:T(8,128)S(1)}, f32[32,128]{1,0:T(8,128)S(1)}, f32[8,128]{1,0:T(8,128)S(1)}) custom-call(f32[152,128]{1,0:T(8,128)S(1)} %collective-permute-done.3.state_ref, f32[4,128,128]{2,1,0:T(8,128)S(1)} %get-tuple-element.30.refs_1_.refs_0_, f32[4,128,128]{2,1,0:T(8,128)S(1)} %get-tuple-element.31.refs_2_.refs_1_, ...), custom_call_target="tpu_custom_call" | custom-call | tf_op jit(solution)/shard_map/pallas_call | solution.py:521
  26.2 3.2 %collective-permute-start.4 = (f32[32,128]{1,0:T(8,128)S(1)}, f32[32,128]{1,0:T(8,128)S(1)}, u32[]{:S(2)}, u32[]{:S(2)}) collective-permute-start(f32[32,128]{1,0:T(8,128)S(1)} %get-tuple-element.46), channel_id=1, source_target_pairs={{0,16},{4,20},{8,24},{12,28},{16,0},{20,4},{24,8},{28,12},{1,17},{... | collective-permute-start | bytes 49160 | tf_op jit(solution)/shard_map/ppermute | solution.py:533
  29.3 1.7 %collective-permute-done.4 = f32[32,128]{1,0:T(8,128)S(1)} collective-permute-done((f32[32,128]{1,0:T(8,128)S(1)}, f32[32,128]{1,0:T(8,128)S(1)}, u32[]{:S(2)}, u32[]{:S(2)}) %collective-permute-start.4) | collective-permute-done | bytes 16416 | tf_op jit(solution)/shard_map/ppermute | solution.py:533
  31.1 1.5 %collective-permute-start.6 = (f32[32,128]{1,0:T(8,128)S(1)}, f32[32,128]{1,0:T(8,128)S(1)}, u32[]{:S(2)}, u32[]{:S(2)}) collective-permute-start(f32[32,128]{1,0:T(8,128)S(1)} %add.12), channel_id=1, source_target_pairs={{0,2},{1,3},{2,0},{3,1},{4,6},{5,7},{6,4},{7,5},{8,10},{9,11},{10,... | collective-permute-start | bytes 49160 | tf_op jit(solution)/shard_map/ppermute | solution.py:533
  32.6 1.4 %collective-permute-start.7 = (f32[32,128]{1,0:T(8,128)S(1)}, f32[32,128]{1,0:T(8,128)S(1)}, u32[]{:S(2)}, u32[]{:S(2)}) collective-permute-start(f32[32,128]{1,0:T(8,128)S(1)} %add.12), channel_id=1, source_target_pairs={{0,3},{1,2},{2,1},{3,0},{4,7},{5,6},{6,5},{7,4},{8,11},{9,10},{10,... | collective-permute-start | bytes 49160 | tf_op jit(solution)/shard_map/ppermute | solution.py:533
  34.0 0.5 %collective-permute-start.5 = (f32[32,128]{1,0:T(8,128)S(1)}, f32[32,128]{1,0:T(8,128)S(1)}, u32[]{:S(2)}, u32[]{:S(2)}) collective-permute-start(f32[32,128]{1,0:T(8,128)S(1)} %add.12), channel_id=1, source_target_pairs={{0,1},{1,0},{2,3},{3,2},{4,5},{5,4},{6,7},{7,6},{8,9},{9,8},{10,11... | collective-permute-start | bytes 49160 | tf_op jit(solution)/shard_map/ppermute | solution.py:533
  34.5 0.2 collective-permute-done.6
  34.8 2.4 %collective-permute-done.7 = f32[32,128]{1,0:T(8,128)S(1)} collective-permute-done((f32[32,128]{1,0:T(8,128)S(1)}, f32[32,128]{1,0:T(8,128)S(1)}, u32[]{:S(2)}, u32[]{:S(2)}) %collective-permute-start.7) | collective-permute-done | bytes 16416 | tf_op jit(solution)/shard_map/ppermute | solution.py:533
  37.2 0.5 %collective-permute-done.5 = f32[32,128]{1,0:T(8,128)S(1)} collective-permute-done((f32[32,128]{1,0:T(8,128)S(1)}, f32[32,128]{1,0:T(8,128)S(1)}, u32[]{:S(2)}, u32[]{:S(2)}) %collective-permute-start.5) | collective-permute-done | bytes 16416 | tf_op jit(solution)/shard_map/ppermute | solution.py:533
  37.8 3.1 %collective-permute-start.8 = (f32[40,128]{1,0:T(8,128)S(1)}, f32[40,128]{1,0:T(8,128)S(1)}, u32[]{:S(2)}, u32[]{:S(2)}) collective-permute-start(f32[40,128]{1,0:T(8,128)S(1)} %pad_maximum_fusion.1), channel_id=1, source_target_pairs={{0,8},{4,12},{8,0},{12,4},{16,24},{20,28},{24,16},{28,20},{1,9},{5... | collective-permute-start | bytes 61448 | tf_op jit(solution)/shard_map/ppermute | solution.py:533
  40.9 1.8 %collective-permute-done.8 = f32[40,128]{1,0:T(8,128)S(1)} collective-permute-done((f32[40,128]{1,0:T(8,128)S(1)}, f32[40,128]{1,0:T(8,128)S(1)}, u32[]{:S(2)}, u32[]{:S(2)}) %collective-permute-start.8) | collective-permute-done | bytes 20512 | tf_op jit(solution)/shard_map/ppermute | solution.py:533
  42.6 0.0 collective-permute-start.9
  42.6 1.2 %collective-permute-done.9.refs_1_ = f32[80,128]{1,0:T(8,128)S(1)} collective-permute-done((f32[80,128]{1,0:T(8,128)S(1)}, f32[80,128]{1,0:T(8,128)S(1)}, u32[]{:S(2)}, u32[]{:S(2)}) %collective-permute-start.9) | collective-permute-done | bytes 40992 | tf_op jit(solution)/shard_map/ppermute | solution.py:533
  43.9 3.3 %shard_map.124 = (f32[4,128]{1,0:T(4,128)}, f32[4,128]{1,0:T(4,128)}, f32[4,64]{1,0:T(4,128)}, f32[4,64]{1,0:T(4,128)}) custom-call(f32[64,128]{1,0:T(8,128)S(1)} %get-tuple-element.36.prior_ref, f32[80,128]{1,0:T(8,128)S(1)} %pad_maximum_fusion.refs_0_, f32[80,128]{1,0:T(8,128)S(1)} %collective-permute-done.9.refs_1_), custom_call_target="tpu_custom_call" | custom-call | tf_op jit(solution)/shard_map/pallas_call | solution.py:521
  (8 shorter events, 0.0 us)
Async XLA Ops:
  1.3 1.0 %copy-start = (f32[1,64,128]{2,1,0:T(8,128)S(1)}, f32[1,64,128]{2,1,0:T(8,128)}, u32[]{:S(2)}) copy-start(f32[1,64,128]{2,1,0:T(8,128)} %param.11) | copy-start | bytes 98308
  2.2 0.7 %copy-start.1 = (f32[1,128]{1,0:T(1,128)S(1)}, f32[1,128]{1,0:T(1,128)}, u32[]{:S(2)}) copy-start(f32[1,128]{1,0:T(1,128)} %param.12) | copy-start | bytes 1540
  2.9 6.2 %copy-start.5 = (f32[4]{0:T(128)S(1)}, f32[4]{0:T(128)}, u32[]{:S(2)}) copy-start(f32[4]{0:T(128)} %param.16) | copy-start | bytes 52
  3.0 6.1 %copy-start.2 = (f32[64]{0:T(128)S(1)}, f32[64]{0:T(128)}, u32[]{:S(2)}) copy-start(f32[64]{0:T(128)} %param.14) | copy-start | bytes 772
  3.0 6.1 %copy-start.3 = (f32[64]{0:T(128)S(1)}, f32[64]{0:T(128)}, u32[]{:S(2)}) copy-start(f32[64]{0:T(128)} %param.13) | copy-start | bytes 772
  3.0 6.1 %copy-start.4 = (f32[4]{0:T(128)S(1)}, f32[4]{0:T(128)}, u32[]{:S(2)}) copy-start(f32[4]{0:T(128)} %param.15) | copy-start | bytes 52
  3.1 6.1 %collective-permute-start.1 = (f32[208,128]{1,0:T(8,128)S(1)}, f32[208,128]{1,0:T(8,128)S(1)}, u32[]{:S(2)}, u32[]{:S(2)}) collective-permute-start(f32[208,128]{1,0:T(8,128)S(1)} %concatenate.14.own_ref), channel_id=1, source_target_pairs={{0,8},{4,12},{8,0},{12,4},{16,24},{20,28},{24,16},{28,20},{1,9},{5... | collective-permute-start | bytes 319496 | tf_op jit(solution)/shard_map/ppermute | solution.py:533
  6.1 3.1 %collective-permute-start = (f32[208,128]{1,0:T(8,128)S(1)}, f32[208,128]{1,0:T(8,128)S(1)}, u32[]{:S(2)}, u32[]{:S(2)}) collective-permute-start(f32[208,128]{1,0:T(8,128)S(1)} %concatenate.14.own_ref), channel_id=1, source_target_pairs={{0,4},{4,0},{8,12},{12,8},{16,20},{20,16},{24,28},{28,24},{1,5},{5... | collective-permute-start | bytes 319496 | tf_op jit(solution)/shard_map/ppermute | solution.py:533
  9.1 1.3 %collective-permute-start.2 = (f32[208,128]{1,0:T(8,128)S(1)}, f32[208,128]{1,0:T(8,128)S(1)}, u32[]{:S(2)}, u32[]{:S(2)}) collective-permute-start(f32[208,128]{1,0:T(8,128)S(1)} %collective-permute-done.1.two_ref), channel_id=1, source_target_pairs={{0,4},{4,0},{8,12},{12,8},{16,20},{20,16},{24,28},{28,24},{1,5},{5... | collective-permute-start | bytes 319496 | tf_op jit(solution)/shard_map/ppermute | solution.py:533
  14.3 7.0 %collective-permute-start.3 = (f32[152,128]{1,0:T(8,128)S(1)}, f32[152,128]{1,0:T(8,128)S(1)}, u32[]{:S(2)}, u32[]{:S(2)}) collective-permute-start(f32[152,128]{1,0:T(8,128)S(1)} %get-tuple-element.37), channel_id=1, source_target_pairs={{0,16},{4,20},{8,24},{12,28},{1,17},{5,21},{9,25},{13,29},{2,18},{... | collective-permute-start | bytes 233480 | tf_op jit(solution)/shard_map/ppermute | solution.py:592
  26.2 4.9 %collective-permute-start.4 = (f32[32,128]{1,0:T(8,128)S(1)}, f32[32,128]{1,0:T(8,128)S(1)}, u32[]{:S(2)}, u32[]{:S(2)}) collective-permute-start(f32[32,128]{1,0:T(8,128)S(1)} %get-tuple-element.46), channel_id=1, source_target_pairs={{0,16},{4,20},{8,24},{12,28},{16,0},{20,4},{24,8},{28,12},{1,17},{... | collective-permute-start | bytes 49160 | tf_op jit(solution)/shard_map/ppermute | solution.py:533
  31.1 3.7 %collective-permute-start.6 = (f32[32,128]{1,0:T(8,128)S(1)}, f32[32,128]{1,0:T(8,128)S(1)}, u32[]{:S(2)}, u32[]{:S(2)}) collective-permute-start(f32[32,128]{1,0:T(8,128)S(1)} %add.12), channel_id=1, source_target_pairs={{0,2},{1,3},{2,0},{3,1},{4,6},{5,7},{6,4},{7,5},{8,10},{9,11},{10,... | collective-permute-start | bytes 49160 | tf_op jit(solution)/shard_map/ppermute | solution.py:533
  32.6 4.6 %collective-permute-start.7 = (f32[32,128]{1,0:T(8,128)S(1)}, f32[32,128]{1,0:T(8,128)S(1)}, u32[]{:S(2)}, u32[]{:S(2)}) collective-permute-start(f32[32,128]{1,0:T(8,128)S(1)} %add.12), channel_id=1, source_target_pairs={{0,3},{1,2},{2,1},{3,0},{4,7},{5,6},{6,5},{7,4},{8,11},{9,10},{10,... | collective-permute-start | bytes 49160 | tf_op jit(solution)/shard_map/ppermute | solution.py:533
  34.0 3.7 %collective-permute-start.5 = (f32[32,128]{1,0:T(8,128)S(1)}, f32[32,128]{1,0:T(8,128)S(1)}, u32[]{:S(2)}, u32[]{:S(2)}) collective-permute-start(f32[32,128]{1,0:T(8,128)S(1)} %add.12), channel_id=1, source_target_pairs={{0,1},{1,0},{2,3},{3,2},{4,5},{5,4},{6,7},{7,6},{8,9},{9,8},{10,11... | collective-permute-start | bytes 49160 | tf_op jit(solution)/shard_map/ppermute | solution.py:533
  37.8 4.9 %collective-permute-start.8 = (f32[40,128]{1,0:T(8,128)S(1)}, f32[40,128]{1,0:T(8,128)S(1)}, u32[]{:S(2)}, u32[]{:S(2)}) collective-permute-start(f32[40,128]{1,0:T(8,128)S(1)} %pad_maximum_fusion.1), channel_id=1, source_target_pairs={{0,8},{4,12},{8,0},{12,4},{16,24},{20,28},{24,16},{28,20},{1,9},{5... | collective-permute-start | bytes 61448 | tf_op jit(solution)/shard_map/ppermute | solution.py:533
  42.6 1.2 %collective-permute-start.9 = (f32[80,128]{1,0:T(8,128)S(1)}, f32[80,128]{1,0:T(8,128)S(1)}, u32[]{:S(2)}, u32[]{:S(2)}) collective-permute-start(f32[80,128]{1,0:T(8,128)S(1)} %pad_maximum_fusion.refs_0_), channel_id=1, source_target_pairs={{0,4},{4,0},{8,12},{12,8},{16,20},{20,16},{24,28},{28,24},{1,5},{5... | collective-permute-start | bytes 122888 | tf_op jit(solution)/shard_map/ppermute | solution.py:533

commit v14 on v13

--- a/solution.py
+++ b/solution.py
@@ -75,16 +75,17 @@
     return inv_ref[...]
 
 
-def series(mat, factors):
-    eye = identity(mat.shape[-1])
-    scale = SPAN / largest_sum(mat)
-    error = eye - mat * scale
-    value = eye + error
-    power = error.astype(BF16)
+def series(mats, factors):
+    eye = identity(mats[0].shape[-1])
+    scales = [SPAN / largest_sum(mat) for mat in mats]
+    errors = [eye - mat * scale for mat, scale in zip(mats, scales)]
+    values = [eye + error for error in errors]
+    powers = [error.astype(BF16) for error in errors]
     for _ in range(factors - 1):
-        power = product(power, power).astype(BF16)
-        value = value + product(value.astype(BF16), power)
-    return value * scale
+        powers = [product(power, power).astype(BF16) for power in powers]
+        steps = [product(value.astype(BF16), power) for value, power in zip(values, powers)]
+        values = [value + step for value, step in zip(values, steps)]
+    return [value * scale for value, scale in zip(values, scales)]
 
 
 def quotients(mats, lefts, rights, factors, refs, dims=NT):
@@ -95,15 +96,16 @@
             results.append((fine(first, right, dims), first))
         return results, jnp.float32(0.0)
     eye = identity(mats[0].shape[-1])
-    starts = [series(mat, factors) for mat in mats]
+    starts = series(mats, factors)
+    rests = [eye - fine(mat, start) for mat, start in zip(mats, starts)]
+    firsts = [fine(left, start) for left, start in zip(lefts, starts)]
+    lows = [rest.astype(BF16) for rest in rests]
+    twices = [product(low, low) for low in lows]
+    steps = [fine(first, rest + twice) for first, rest, twice in zip(firsts, rests, twices)]
+    firsts = [first + step for first, step in zip(firsts, steps)]
+    results = [(fine(first, right, dims), first) for first, right in zip(firsts, rights)]
     linear, square = 0.0, 0.0
-    for mat, start, left, right in zip(mats, starts, lefts, rights):
-        rest = eye - fine(mat, start)
-        first = fine(left, start)
-        low = rest.astype(BF16)
-        twice = product(low, low)
-        first = first + fine(first, rest + twice)
-        results.append((fine(first, right, dims), first))
+    for rest, twice in zip(rests, twices):
         linear = linear + rest * rest
         square = square + twice * twice
     return results, jnp.sum(linear) * jnp.sum(square)
@@ -350,7 +352,7 @@
         for panel in range(0, STRIP, SUB):
             base = strip + panel
             block = {
-                (i, m): splat(rows[panel + i][0], base + m) for i in range(SUB) for m in range(i, SUB)
+                (i, m): splat(rows[panel + i][0], base + m) for m in range(SUB) for i in range(m + 1)
             }
             for k in range(SUB):
                 pivot = block[k, k]
@@ -358,7 +360,6 @@
                 pivots = jnp.where(lane == base + k, pivot, pivots)
                 scaled = {m: block[k, m] * root for m in range(k + 1, SUB)}
                 ready = [piece * root for piece in rows[panel + k]]
-                column = jnp.where(lane == base + k, splat(ready[-1], tip), column)
                 rows[panel + k] = ready
                 for i in range(k + 1, SUB):
                     for m in range(i, SUB):
@@ -371,6 +372,8 @@
                     ready = rows[k]
                     weight = splat(ready[0], strip + i)
                     rows[i] = [piece - weight * own for piece, own in zip(rows[i], ready)]
+        for i in range(STRIP):
+            column = jnp.where(lane == strip + i, splat(rows[i][-1], tip), column)
         for i in range(STRIP):
             for p, ref in enumerate(refs):
                 ref[(strip + i) * SUB : (strip + i + 1) * SUB, :] = rows[i][p]

time: 47.4 us -> 45.7 us (0.964)
  Pallas kernels: 14.3 us -> 12.5 us
  waiting for transfers between devices: 12.1 us -> 13.8 us
  starting transfers between devices: 17.5 us -> 15.9 us
    pallas_call x5, Pallas kernels: 14.3 us -> 12.5 us  [call(): pl.pallas_call(body, out_shape=tuple((jax.ShapeDtypeStruct(shape, F32) fo...]
    ppermute x9, starting transfers between devices: 12.9 us -> 11.3 us  [crossed(): lax.ppermute(value, axis, [(source, source ^ step) for source in range(si...]
    ppermute x9, waiting for transfers between devices: 12.1 us -> 13.5 us  [crossed(): lax.ppermute(value, axis, [(source, source ^ step) for source in range(si...]
  transfers between devices with their start and end apart: 10 -> 10, of which waited for: 8 -> 9; matrix products, arithmetic and copies ran while one was open for 0% -> 0% of each run, Pallas kernels for 5% -> 4%
where the time goes in v14:
time: 45.7 us; the launch traced here: 45.5 us
  starting transfers between devices  15.9 us (35%)
  waiting for transfers between devices  13.8 us (30%)
  Pallas kernels  12.5 us (27%)
  between operations  1.42 us (3%)
  other arithmetic  0.93 us (2%)
  local copies, waits for them, and re-layouts  0.88 us (2%)
    ppermute x9, waiting for transfers between devices, crossed(): lax.ppermute(value, axis, [(source, source ^ step) for source in range(si...  13.5 us
    pallas_call x5, Pallas kernels, call(): pl.pallas_call(body, out_shape=tuple((jax.ShapeDtypeStruct(shape, F32) fo...  12.5 us
    ppermute x9, starting transfers between devices, crossed(): lax.ppermute(value, axis, [(source, source ^ step) for source in range(si...  11.3 us
    ppermute x1, starting transfers between devices, shards(): lax.ppermute(state, 'tm', [(source, source + GROUP) for source in range(g...  4.66 us
  transfers between devices with their start and end apart: 10, of which 9 were waited for; matrix products, arithmetic and copies ran while one was open for 0% of the time, Pallas kernels for 4%

profile of v14, /device:TPU:0, one launch (start us, length us, event | category | flops | bytes accessed | tf_op | source)
XLA Modules:
  0.0 45.5 jit_solution(315931034089424688)
XLA Ops:
  1.3 0.0 copy-start
  1.3 0.9 %fusion = (f32[128]{0:T(128)S(1)}, f32[128,128]{1,0:T(8,128)S(1)}) fusion(f32[1,128,128]{2,1,0:T(8,128)} %param.10, f32[1,128,128]{2,1,0:T(8,128)} %param.9), kind=kLoop, calls=%fused_computation.2 | loop fusion | flops 81792 | bytes 197120 | tf_op jit(solution)/shard_map/reduce_sum | solution.py:568
  2.2 0.0 copy-start.1
  2.2 0.0 copy-done
  2.2 0.6 %copy-done.1 = f32[1,128]{1,0:T(1,128)S(1)} copy-done((f32[1,128]{1,0:T(1,128)S(1)}, f32[1,128]{1,0:T(1,128)}, u32[]{:S(2)}) %copy-start.1) | copy-done | bytes 536
  2.9 0.0 copy-start.5
  2.9 0.1 concatenate.14.own_ref
  3.0 0.0 copy-start.2
  3.0 0.0 copy-start.3
  3.0 0.0 copy-start.4
  3.1 3.1 %collective-permute-start.1 = (f32[208,128]{1,0:T(8,128)S(1)}, f32[208,128]{1,0:T(8,128)S(1)}, u32[]{:S(2)}, u32[]{:S(2)}) collective-permute-start(f32[208,128]{1,0:T(8,128)S(1)} %concatenate.14.own_ref), channel_id=1, source_target_pairs={{0,8},{4,12},{8,0},{12,4},{16,24},{20,28},{24,16},{28,20},{1,9},{5... | collective-permute-start | bytes 319496 | tf_op jit(solution)/shard_map/ppermute | solution.py:536
  6.1 0.0 collective-permute-start
  6.1 3.0 %collective-permute-done.1.two_ref = f32[208,128]{1,0:T(8,128)S(1)} collective-permute-done((f32[208,128]{1,0:T(8,128)S(1)}, f32[208,128]{1,0:T(8,128)S(1)}, u32[]{:S(2)}, u32[]{:S(2)}) %collective-permute-start.1) | collective-permute-done | bytes 106528 | tf_op jit(solution)/shard_map/ppermute | solution.py:536
  9.1 0.0 collective-permute-start.2
  9.1 0.0 copy-done.5
  9.1 0.0 copy-done.2
  9.1 0.0 copy-done.3
  9.1 0.0 copy-done.4
  9.2 0.1 concatenate.13
  9.2 0.0 collective-permute-done.one_ref
  9.2 1.2 %collective-permute-done.2.three_ref = f32[208,128]{1,0:T(8,128)S(1)} collective-permute-done((f32[208,128]{1,0:T(8,128)S(1)}, f32[208,128]{1,0:T(8,128)S(1)}, u32[]{:S(2)}, u32[]{:S(2)}) %collective-permute-start.2) | collective-permute-done | bytes 106528 | tf_op jit(solution)/shard_map/ppermute | solution.py:536
  10.4 3.4 %shard_map.120 = (f32[4,128,128]{2,1,0:T(8,128)S(1)}, f32[4,128,128]{2,1,0:T(8,128)S(1)}, f32[4,128,128]{2,1,0:T(8,128)S(1)}, f32[4,80,128]{2,1,0:T(8,128)S(1)},...) custom-call(f32[2,128]{1,0:T(2,128)S(1)} %bitcast.17, ...), custom_call_target="tpu_custom_call" | custom-call | tf_op jit(solution)/shard_map/pallas_call | solution.py:524
  13.8 4.7 %collective-permute-start.3 = (f32[152,128]{1,0:T(8,128)S(1)}, f32[152,128]{1,0:T(8,128)S(1)}, u32[]{:S(2)}, u32[]{:S(2)}) collective-permute-start(f32[152,128]{1,0:T(8,128)S(1)} %get-tuple-element.37), channel_id=1, source_target_pairs={{0,16},{4,20},{8,24},{12,28},{1,17},{5,21},{9,25},{13,29},{2,18},{... | collective-permute-start | bytes 233480 | tf_op jit(solution)/shard_map/ppermute | solution.py:595
  18.5 1.7 %shard_map.121 = (f32[128,128]{1,0:T(8,128)S(1)}, f32[128,128]{1,0:T(8,128)S(1)}, f32[128,128]{1,0:T(8,128)S(1)}, f32[80,128]{1,0:T(8,128)S(1)}, f32[80,128]{1,0...) custom-call(f32[2,128]{1,0:T(2,128)S(1)} %bitcast.18, ...), custom_call_target="tpu_custom_call" | custom-call | tf_op jit(solution)/shard_map/pallas_call | solution.py:524
  20.1 0.3 collective-permute-done.3.state_ref
  20.5 4.3 %shard_map.122 = (f32[4,128,128]{2,1,0:T(8,128)S(1)}, f32[128,8]{1,0:T(8,128)S(1)}, f32[32,128]{1,0:T(8,128)S(1)}, f32[8,128]{1,0:T(8,128)S(1)}) custom-call(f32[152,128]{1,0:T(8,128)S(1)} %collective-permute-done.3.state_ref, f32[4,128,128]{2,1,0:T(8,128)S(1)} %get-tuple-element.30.refs_1_.refs_0_, f32[4,128,128]{2,1,0:T(8,128)S(1)} %get-tuple-element.31.refs_2_.refs_1_, ...), custom_call_target="tpu_custom_call" | custom-call | tf_op jit(solution)/shard_map/pallas_call | solution.py:524
  24.8 1.6 %collective-permute-start.4 = (f32[32,128]{1,0:T(8,128)S(1)}, f32[32,128]{1,0:T(8,128)S(1)}, u32[]{:S(2)}, u32[]{:S(2)}) collective-permute-start(f32[32,128]{1,0:T(8,128)S(1)} %get-tuple-element.46), channel_id=1, source_target_pairs={{0,16},{4,20},{8,24},{12,28},{16,0},{20,4},{24,8},{28,12},{1,17},{... | collective-permute-start | bytes 49160 | tf_op jit(solution)/shard_map/ppermute | solution.py:536
  26.3 3.1 %collective-permute-done.4 = f32[32,128]{1,0:T(8,128)S(1)} collective-permute-done((f32[32,128]{1,0:T(8,128)S(1)}, f32[32,128]{1,0:T(8,128)S(1)}, u32[]{:S(2)}, u32[]{:S(2)}) %collective-permute-start.4) | collective-permute-done | bytes 16416 | tf_op jit(solution)/shard_map/ppermute | solution.py:536
  29.5 1.5 %collective-permute-start.6 = (f32[32,128]{1,0:T(8,128)S(1)}, f32[32,128]{1,0:T(8,128)S(1)}, u32[]{:S(2)}, u32[]{:S(2)}) collective-permute-start(f32[32,128]{1,0:T(8,128)S(1)} %add.12), channel_id=1, source_target_pairs={{0,2},{1,3},{2,0},{3,1},{4,6},{5,7},{6,4},{7,5},{8,10},{9,11},{10,... | collective-permute-start | bytes 49160 | tf_op jit(solution)/shard_map/ppermute | solution.py:536
  31.0 1.4 %collective-permute-start.7 = (f32[32,128]{1,0:T(8,128)S(1)}, f32[32,128]{1,0:T(8,128)S(1)}, u32[]{:S(2)}, u32[]{:S(2)}) collective-permute-start(f32[32,128]{1,0:T(8,128)S(1)} %add.12), channel_id=1, source_target_pairs={{0,3},{1,2},{2,1},{3,0},{4,7},{5,6},{6,5},{7,4},{8,11},{9,10},{10,... | collective-permute-start | bytes 49160 | tf_op jit(solution)/shard_map/ppermute | solution.py:536
  32.4 0.5 %collective-permute-start.5 = (f32[32,128]{1,0:T(8,128)S(1)}, f32[32,128]{1,0:T(8,128)S(1)}, u32[]{:S(2)}, u32[]{:S(2)}) collective-permute-start(f32[32,128]{1,0:T(8,128)S(1)} %add.12), channel_id=1, source_target_pairs={{0,1},{1,0},{2,3},{3,2},{4,5},{5,4},{6,7},{7,6},{8,9},{9,8},{10,11... | collective-permute-start | bytes 49160 | tf_op jit(solution)/shard_map/ppermute | solution.py:536
  33.0 0.2 collective-permute-done.6
  33.2 2.4 %collective-permute-done.7 = f32[32,128]{1,0:T(8,128)S(1)} collective-permute-done((f32[32,128]{1,0:T(8,128)S(1)}, f32[32,128]{1,0:T(8,128)S(1)}, u32[]{:S(2)}, u32[]{:S(2)}) %collective-permute-start.7) | collective-permute-done | bytes 16416 | tf_op jit(solution)/shard_map/ppermute | solution.py:536
  35.6 0.5 %collective-permute-done.5 = f32[32,128]{1,0:T(8,128)S(1)} collective-permute-done((f32[32,128]{1,0:T(8,128)S(1)}, f32[32,128]{1,0:T(8,128)S(1)}, u32[]{:S(2)}, u32[]{:S(2)}) %collective-permute-start.5) | collective-permute-done | bytes 16416 | tf_op jit(solution)/shard_map/ppermute | solution.py:536
  36.2 3.1 %collective-permute-start.8 = (f32[40,128]{1,0:T(8,128)S(1)}, f32[40,128]{1,0:T(8,128)S(1)}, u32[]{:S(2)}, u32[]{:S(2)}) collective-permute-start(f32[40,128]{1,0:T(8,128)S(1)} %pad_maximum_fusion.1), channel_id=1, source_target_pairs={{0,8},{4,12},{8,0},{12,4},{16,24},{20,28},{24,16},{28,20},{1,9},{5... | collective-permute-start | bytes 61448 | tf_op jit(solution)/shard_map/ppermute | solution.py:536
  39.3 1.8 %collective-permute-done.8 = f32[40,128]{1,0:T(8,128)S(1)} collective-permute-done((f32[40,128]{1,0:T(8,128)S(1)}, f32[40,128]{1,0:T(8,128)S(1)}, u32[]{:S(2)}, u32[]{:S(2)}) %collective-permute-start.8) | collective-permute-done | bytes 20512 | tf_op jit(solution)/shard_map/ppermute | solution.py:536
  41.1 0.0 collective-permute-start.9
  41.1 1.2 %collective-permute-done.9.refs_1_ = f32[80,128]{1,0:T(8,128)S(1)} collective-permute-done((f32[80,128]{1,0:T(8,128)S(1)}, f32[80,128]{1,0:T(8,128)S(1)}, u32[]{:S(2)}, u32[]{:S(2)}) %collective-permute-start.9) | collective-permute-done | bytes 40992 | tf_op jit(solution)/shard_map/ppermute | solution.py:536
  42.3 3.2 %shard_map.124 = (f32[4,128]{1,0:T(4,128)}, f32[4,128]{1,0:T(4,128)}, f32[4,64]{1,0:T(4,128)}, f32[4,64]{1,0:T(4,128)}) custom-call(f32[64,128]{1,0:T(8,128)S(1)} %get-tuple-element.36.prior_ref, f32[80,128]{1,0:T(8,128)S(1)} %pad_maximum_fusion.refs_0_, f32[80,128]{1,0:T(8,128)S(1)} %collective-permute-done.9.refs_1_), custom_call_target="tpu_custom_call" | custom-call | tf_op jit(solution)/shard_map/pallas_call | solution.py:524
  (8 shorter events, 0.0 us)
Async XLA Ops:
  1.3 1.0 %copy-start = (f32[1,64,128]{2,1,0:T(8,128)S(1)}, f32[1,64,128]{2,1,0:T(8,128)}, u32[]{:S(2)}) copy-start(f32[1,64,128]{2,1,0:T(8,128)} %param.11) | copy-start | bytes 98308
  2.2 0.7 %copy-start.1 = (f32[1,128]{1,0:T(1,128)S(1)}, f32[1,128]{1,0:T(1,128)}, u32[]{:S(2)}) copy-start(f32[1,128]{1,0:T(1,128)} %param.12) | copy-start | bytes 1540
  2.9 6.2 %copy-start.5 = (f32[4]{0:T(128)S(1)}, f32[4]{0:T(128)}, u32[]{:S(2)}) copy-start(f32[4]{0:T(128)} %param.16) | copy-start | bytes 52
  3.0 6.1 %copy-start.2 = (f32[64]{0:T(128)S(1)}, f32[64]{0:T(128)}, u32[]{:S(2)}) copy-start(f32[64]{0:T(128)} %param.14) | copy-start | bytes 772
  3.0 6.1 %copy-start.3 = (f32[64]{0:T(128)S(1)}, f32[64]{0:T(128)}, u32[]{:S(2)}) copy-start(f32[64]{0:T(128)} %param.13) | copy-start | bytes 772
  3.0 6.1 %copy-start.4 = (f32[4]{0:T(128)S(1)}, f32[4]{0:T(128)}, u32[]{:S(2)}) copy-start(f32[4]{0:T(128)} %param.15) | copy-start | bytes 52
  3.1 6.1 %collective-permute-start.1 = (f32[208,128]{1,0:T(8,128)S(1)}, f32[208,128]{1,0:T(8,128)S(1)}, u32[]{:S(2)}, u32[]{:S(2)}) collective-permute-start(f32[208,128]{1,0:T(8,128)S(1)} %concatenate.14.own_ref), channel_id=1, source_target_pairs={{0,8},{4,12},{8,0},{12,4},{16,24},{20,28},{24,16},{28,20},{1,9},{5... | collective-permute-start | bytes 319496 | tf_op jit(solution)/shard_map/ppermute | solution.py:536
  6.1 3.1 %collective-permute-start = (f32[208,128]{1,0:T(8,128)S(1)}, f32[208,128]{1,0:T(8,128)S(1)}, u32[]{:S(2)}, u32[]{:S(2)}) collective-permute-start(f32[208,128]{1,0:T(8,128)S(1)} %concatenate.14.own_ref), channel_id=1, source_target_pairs={{0,4},{4,0},{8,12},{12,8},{16,20},{20,16},{24,28},{28,24},{1,5},{5... | collective-permute-start | bytes 319496 | tf_op jit(solution)/shard_map/ppermute | solution.py:536
  9.1 1.3 %collective-permute-start.2 = (f32[208,128]{1,0:T(8,128)S(1)}, f32[208,128]{1,0:T(8,128)S(1)}, u32[]{:S(2)}, u32[]{:S(2)}) collective-permute-start(f32[208,128]{1,0:T(8,128)S(1)} %collective-permute-done.1.two_ref), channel_id=1, source_target_pairs={{0,4},{4,0},{8,12},{12,8},{16,20},{20,16},{24,28},{28,24},{1,5},{5... | collective-permute-start | bytes 319496 | tf_op jit(solution)/shard_map/ppermute | solution.py:536
  13.8 6.7 %collective-permute-start.3 = (f32[152,128]{1,0:T(8,128)S(1)}, f32[152,128]{1,0:T(8,128)S(1)}, u32[]{:S(2)}, u32[]{:S(2)}) collective-permute-start(f32[152,128]{1,0:T(8,128)S(1)} %get-tuple-element.37), channel_id=1, source_target_pairs={{0,16},{4,20},{8,24},{12,28},{1,17},{5,21},{9,25},{13,29},{2,18},{... | collective-permute-start | bytes 233480 | tf_op jit(solution)/shard_map/ppermute | solution.py:595
  24.8 4.7 %collective-permute-start.4 = (f32[32,128]{1,0:T(8,128)S(1)}, f32[32,128]{1,0:T(8,128)S(1)}, u32[]{:S(2)}, u32[]{:S(2)}) collective-permute-start(f32[32,128]{1,0:T(8,128)S(1)} %get-tuple-element.46), channel_id=1, source_target_pairs={{0,16},{4,20},{8,24},{12,28},{16,0},{20,4},{24,8},{28,12},{1,17},{... | collective-permute-start | bytes 49160 | tf_op jit(solution)/shard_map/ppermute | solution.py:536
  29.5 3.7 %collective-permute-start.6 = (f32[32,128]{1,0:T(8,128)S(1)}, f32[32,128]{1,0:T(8,128)S(1)}, u32[]{:S(2)}, u32[]{:S(2)}) collective-permute-start(f32[32,128]{1,0:T(8,128)S(1)} %add.12), channel_id=1, source_target_pairs={{0,2},{1,3},{2,0},{3,1},{4,6},{5,7},{6,4},{7,5},{8,10},{9,11},{10,... | collective-permute-start | bytes 49160 | tf_op jit(solution)/shard_map/ppermute | solution.py:536
  31.0 4.6 %collective-permute-start.7 = (f32[32,128]{1,0:T(8,128)S(1)}, f32[32,128]{1,0:T(8,128)S(1)}, u32[]{:S(2)}, u32[]{:S(2)}) collective-permute-start(f32[32,128]{1,0:T(8,128)S(1)} %add.12), channel_id=1, source_target_pairs={{0,3},{1,2},{2,1},{3,0},{4,7},{5,6},{6,5},{7,4},{8,11},{9,10},{10,... | collective-permute-start | bytes 49160 | tf_op jit(solution)/shard_map/ppermute | solution.py:536
  32.4 3.7 %collective-permute-start.5 = (f32[32,128]{1,0:T(8,128)S(1)}, f32[32,128]{1,0:T(8,128)S(1)}, u32[]{:S(2)}, u32[]{:S(2)}) collective-permute-start(f32[32,128]{1,0:T(8,128)S(1)} %add.12), channel_id=1, source_target_pairs={{0,1},{1,0},{2,3},{3,2},{4,5},{5,4},{6,7},{7,6},{8,9},{9,8},{10,11... | collective-permute-start | bytes 49160 | tf_op jit(solution)/shard_map/ppermute | solution.py:536
  36.2 4.9 %collective-permute-start.8 = (f32[40,128]{1,0:T(8,128)S(1)}, f32[40,128]{1,0:T(8,128)S(1)}, u32[]{:S(2)}, u32[]{:S(2)}) collective-permute-start(f32[40,128]{1,0:T(8,128)S(1)} %pad_maximum_fusion.1), channel_id=1, source_target_pairs={{0,8},{4,12},{8,0},{12,4},{16,24},{20,28},{24,16},{28,20},{1,9},{5... | collective-permute-start | bytes 61448 | tf_op jit(solution)/shard_map/ppermute | solution.py:536
  41.1 1.2 %collective-permute-start.9 = (f32[80,128]{1,0:T(8,128)S(1)}, f32[80,128]{1,0:T(8,128)S(1)}, u32[]{:S(2)}, u32[]{:S(2)}) collective-permute-start(f32[80,128]{1,0:T(8,128)S(1)} %pad_maximum_fusion.refs_0_), channel_id=1, source_target_pairs={{0,4},{4,0},{8,12},{12,8},{16,20},{20,16},{24,28},{28,24},{1,5},{5... | collective-permute-start | bytes 122888 | tf_op jit(solution)/shard_map/ppermute | solution.py:536

commit v15 on v14

--- a/solution.py
+++ b/solution.py
@@ -204,9 +204,9 @@
         run((mat_ref, inv_ref))
 
 
-def middle_kernel(tip, start, *refs):
-    extra_ref, diag_ref, cross_ref, back_ref, right_ref, left_ref, part_ref, *refs = refs
-    *out_refs, far_ref, near_ref, share_ref, prior_ref, mat_ref, inv_ref = refs
+def middle(tip, start, parts, part_ref, out_refs, spare):
+    diag_ref, cross_ref, back_ref, right_ref, left_ref = parts
+    *third_refs, far_ref, near_ref, share_ref = out_refs
     tile = diag_ref.shape[-1]
     side = right_ref.shape[1]
     last = jnp.where(lax.axis_index("tm") >= start, 1.0, 0.0).astype(F32)
@@ -224,7 +224,7 @@
             right_ref[2] - gram[end, one],
             left_ref[1] - gram[end, two],
         )
-        for ref, value in zip(out_refs, values):
+        for ref, value in zip(third_refs, values):
             ref[...] = value
         far_ref[...] = back_ref[3] - last * over[one, one]
         near_ref[...] = left_ref[3] - last * over[tile : tile + side, one]
@@ -232,6 +232,25 @@
         return total < SMALL
 
     settled = run(None)
+
+    @pl.when(jnp.logical_not(settled))
+    def _():
+        run(spare)
+
+
+def early_kernel(tip, start, *refs):
+    parts, part_ref, out_refs, spare = refs[:5], refs[5], refs[6:14], refs[14:]
+
+    @pl.when(lax.axis_index("tm") < GROUP)
+    def _():
+        middle(tip, start, parts, part_ref, out_refs, spare)
+
+
+def travel_kernel(tip, start, extra_ref, *refs):
+    parts, part_ref, third_ref, end_ref = refs[:5], refs[5], refs[6], refs[7]
+    out_refs, prior_ref, small_ref = refs[8:16], refs[16], refs[17]
+    mat_ref, inv_ref, rows_ref = refs[18:]
+    tile = third_ref.shape[0]
     tips = extra_ref[0:1, :]
     row = lax.broadcasted_iota(jnp.int32, (tip, 128), 0)
     col = lax.broadcasted_iota(jnp.int32, (tip, 128), 1)
@@ -239,9 +258,16 @@
     column = jnp.sum(jnp.where(row + tip == col, tips, 0.0), axis=1, keepdims=True)
     prior_ref[...] = prior + jnp.where(col == tip, column, 0.0)
 
-    @pl.when(jnp.logical_not(settled))
-    def _():
-        run((mat_ref, inv_ref))
+    @pl.when(lax.axis_index("tm") >= GROUP)
+    def _():
+        middle(tip, start, parts, part_ref, out_refs, (mat_ref, inv_ref))
+
+    @pl.when(lax.axis_index("tm") < GROUP)
+    def _():
+        diags = [third_ref[...] if n == 2 else parts[0][n] for n in range(GROUP)]
+        sides = [(end_ref[...] if n == 2 else parts[3][n])[tip : tip + 1, :] for n in range(GROUP)]
+        sides = padded(jnp.concatenate(sides, axis=0), tile).T[:, 0:SUB]
+        factored(diags, sides, small_ref, (mat_ref, inv_ref), rows_ref)
 
 
 def send(state_ref, diag, right):
@@ -341,13 +367,14 @@
     column = jnp.zeros((SUB, 128), F32)
     for strip in range(0, size, STRIP):
         if strip:
-            for b in range(batch):
-                done = [ref[pl.ds(b, strip, stride=SUB), :] for ref in refs]
-                left = done[0][:, strip : strip + STRIP]
-                update = fine(left, jnp.concatenate(done, axis=1), TN)
-                spot = pl.ds(strip * SUB + b, STRIP, stride=SUB)
+            ready = [[ref[pl.ds(b, strip, stride=SUB), :] for ref in refs] for b in range(batch)]
+            lefts = [done[0][:, strip : strip + STRIP] for done in ready]
+            updates = [fine(left, jnp.concatenate(done, axis=1), TN) for left, done in zip(lefts, ready)]
+            spots = [pl.ds(strip * SUB + b, STRIP, stride=SUB) for b in range(batch)]
+            rests = [[ref[spot, :] for ref in refs] for spot in spots]
+            for spot, rest, update in zip(spots, rests, updates):
                 for p, ref in enumerate(refs):
-                    ref[spot, :] = ref[spot, :] - update[:, 128 * p : 128 * (p + 1)]
+                    ref[spot, :] = rest[p] - update[:, 128 * p : 128 * (p + 1)]
         rows = [[ref[(strip + i) * SUB : (strip + i + 1) * SUB, :] for ref in refs] for i in range(STRIP)]
         for panel in range(0, STRIP, SUB):
             base = strip + panel
@@ -430,8 +457,8 @@
 
 
 def merge_kernel(state_ref, *refs):
-    *parts, far_ref, near_ref, part_ref = refs[:-7]
-    square_ref, side_ref, sums_ref, small_ref, mat_ref, inv_ref, rows_ref = refs[-7:]
+    *parts, far_ref, near_ref, part_ref, early_ref = refs[:-5]
+    square_ref, side_ref, sums_ref, mat_ref, inv_ref = refs[-5:]
     tile = state_ref.shape[1]
     tip = part_ref.shape[0]
     position = lax.axis_index("tm")
@@ -459,8 +486,7 @@
 
     @pl.when(position < GROUP)
     def _():
-        sums_ref[...] = fold(part_ref[...])
-        factored(diags, sides, small_ref, (mat_ref, inv_ref), rows_ref)
+        sums_ref[...] = fold(early_ref[...])
 
 
 def factored(squares, sides, small_ref, spare, rows_ref):
@@ -551,6 +577,7 @@
     tip = arrow_cols.shape[1]
     groups = lax.axis_size("tm")
     spans = groups // GROUP
+    assert spans > 1
     assert config_shift.shape[0] == GROUP and diag_blocks.shape[:2] == (1, tile)
     side = tip + 2 * SUB
     square = (GROUP, tile, tile)
@@ -583,26 +610,27 @@
         (square, square, square, band, band, packed_state, (tip, tile)),
         ((GROUP,) + raw.shape, *pair),
     )
-    *thirds, prior = call(
-        functools.partial(middle_kernel, tip, groups - GROUP),
-        (extra, *parts, part),
-        ((tile, tile),) * 3 + ((side, tile),) * 2 + ((tile, tile), (side, tile), (tip, tile), (tip, tile)),
-        pair,
-    )
-    *thirds, far, near, part = thirds
-    parts = (*parts, *thirds)
+    half = SUB * tile // 2
+    outs = ((tile, tile),) * 3 + ((side, tile),) * 2 + ((tile, tile), (side, tile), (tip, tile))
+    early = call(functools.partial(early_kernel, tip, groups - GROUP), (*parts, part), outs, pair)
+    state, early = lax.optimization_barrier((state, early))
     for span in range(spans - 1):
         state = lax.ppermute(state, "tm", [(source, source + GROUP) for source in range(groups - GROUP)])
+        if span == 0:
+            *later, prior, small = call(
+                functools.partial(travel_kernel, tip, groups - GROUP),
+                (extra, *parts, part, early[0], early[3]),
+                outs + ((tip, tile), (2 * GROUP, tile)),
+                (*pair, (half, tile)),
+            )
+            parts, (far, near, share) = (*parts, *later[:5]), later[5:]
         if span < spans - 2:
             (state,) = call(advance_kernel, (state, *parts), (packed_state,), pair)
-    if spans == 1:
-        state = jnp.zeros_like(state)
-    half = SUB * tile // 2
-    squares, sides, sums, small = call(
+    squares, sides, sums = call(
         merge_kernel,
-        (state, *parts, far, near, part),
-        (square, (tile, SUB), (tip // 2, tile), (2 * GROUP, tile)),
-        (*pair, (half, tile)),
+        (state, *parts, far, near, share, early[7]),
+        (square, (tile, SUB), (tip // 2, tile)),
+        pair,
     )
     (small,) = call(
         factor_kernel,

time: 45.7 us -> 45.2 us (0.989)
  waiting for transfers between devices: 13.8 us -> 12.1 us
  Pallas kernels: 12.5 us -> 13.6 us
    ppermute x9, starting transfers between devices: 11.3 us -> 13.2 us  [crossed(): lax.ppermute(value, axis, [(source, source ^ step) for source in range(si...]
    ppermute x1, starting transfers between devices: 4.66 us -> 2.97 us  [shards(): lax.ppermute(state, 'tm', [(source, source + GROUP) for source in range(g...]
    ppermute x9, waiting for transfers between devices: 13.5 us -> 12.1 us  [crossed(): lax.ppermute(value, axis, [(source, source ^ step) for source in range(si...]
    pallas_call x5 -> x6, Pallas kernels: 12.5 us -> 13.6 us  [call(): pl.pallas_call(body, out_shape=tuple((jax.ShapeDtypeStruct(shape, F32) fo...]
  transfers between devices with their start and end apart: 10 -> 10, of which waited for: 9 -> 8; matrix products, arithmetic and copies ran while one was open for 0% -> 0% of each run, Pallas kernels for 4% -> 9%
where the time goes in v15:
time: 45.2 us; the launch traced here: 45 us
  starting transfers between devices  16.1 us (36%)
  Pallas kernels  13.6 us (30%)
  waiting for transfers between devices  12.1 us (27%)
  between operations  1.41 us (3%)
  other arithmetic  0.93 us (2%)
  local copies, waits for them, and re-layouts  0.88 us (2%)
    pallas_call x6, Pallas kernels, call(): pl.pallas_call(body, out_shape=tuple((jax.ShapeDtypeStruct(shape, F32) fo...  13.6 us
    ppermute x9, starting transfers between devices, crossed(): lax.ppermute(value, axis, [(source, source ^ step) for source in range(si...  13.2 us
    ppermute x9, waiting for transfers between devices, crossed(): lax.ppermute(value, axis, [(source, source ^ step) for source in range(si...  12.1 us
    ppermute x1, starting transfers between devices, shards(): lax.ppermute(state, 'tm', [(source, source + GROUP) for source in range(g...  2.97 us
    reduce_sum x1, other arithmetic, shards(): jnp.sum(jnp.where(row == col, coupling[0], 0.0), axis=0, keepdims=True)  0.91 us
  transfers between devices with their start and end apart: 10, of which 8 were waited for; matrix products, arithmetic and copies ran while one was open for 0% of the time, Pallas kernels for 9%

profile of v15, /device:TPU:0, one launch (start us, length us, event | category | flops | bytes accessed | tf_op | source)
XLA Modules:
  0.0 45.0 jit_solution(1594943433104846605)
XLA Ops:
  1.3 0.0 copy-start
  1.3 0.9 %fusion = (f32[128]{0:T(128)S(1)}, f32[128,128]{1,0:T(8,128)S(1)}) fusion(f32[1,128,128]{2,1,0:T(8,128)} %param.10, f32[1,128,128]{2,1,0:T(8,128)} %param.9), kind=kLoop, calls=%fused_computation.2 | loop fusion | flops 81792 | bytes 197120 | tf_op jit(solution)/shard_map/reduce_sum | solution.py:595
  2.2 0.0 copy-start.1
  2.2 0.0 copy-done
  2.2 0.6 %copy-done.1 = f32[1,128]{1,0:T(1,128)S(1)} copy-done((f32[1,128]{1,0:T(1,128)S(1)}, f32[1,128]{1,0:T(1,128)}, u32[]{:S(2)}) %copy-start.1) | copy-done | bytes 536
  2.9 0.0 copy-start.5
  2.9 0.1 concatenate.14.own_ref
  3.0 0.0 copy-start.2
  3.0 0.0 copy-start.3
  3.0 0.0 copy-start.4
  3.1 3.1 %collective-permute-start.1 = (f32[208,128]{1,0:T(8,128)S(1)}, f32[208,128]{1,0:T(8,128)S(1)}, u32[]{:S(2)}, u32[]{:S(2)}) collective-permute-start(f32[208,128]{1,0:T(8,128)S(1)} %concatenate.14.own_ref), channel_id=1, source_target_pairs={{0,8},{4,12},{8,0},{12,4},{16,24},{20,28},{24,16},{28,20},{1,9},{5... | collective-permute-start | bytes 319496 | tf_op jit(solution)/shard_map/ppermute | solution.py:562
  6.1 0.0 collective-permute-start
  6.1 3.0 %collective-permute-done.1.two_ref = f32[208,128]{1,0:T(8,128)S(1)} collective-permute-done((f32[208,128]{1,0:T(8,128)S(1)}, f32[208,128]{1,0:T(8,128)S(1)}, u32[]{:S(2)}, u32[]{:S(2)}) %collective-permute-start.1) | collective-permute-done | bytes 106528 | tf_op jit(solution)/shard_map/ppermute | solution.py:562
  9.1 0.0 collective-permute-start.2
  9.1 0.0 copy-done.5
  9.1 0.0 copy-done.2
  9.1 0.0 copy-done.3
  9.1 0.0 copy-done.4
  9.2 0.1 concatenate.13
  9.2 0.0 collective-permute-done.one_ref
  9.2 1.2 %collective-permute-done.2.three_ref = f32[208,128]{1,0:T(8,128)S(1)} collective-permute-done((f32[208,128]{1,0:T(8,128)S(1)}, f32[208,128]{1,0:T(8,128)S(1)}, u32[]{:S(2)}, u32[]{:S(2)}) %collective-permute-start.2) | collective-permute-done | bytes 106528 | tf_op jit(solution)/shard_map/ppermute | solution.py:562
  10.4 3.4 %shard_map.120 = (f32[4,128,128]{2,1,0:T(8,128)S(1)}, f32[4,128,128]{2,1,0:T(8,128)S(1)}, f32[4,128,128]{2,1,0:T(8,128)S(1)}, f32[4,80,128]{2,1,0:T(8,128)S(1)},...) custom-call(f32[2,128]{1,0:T(2,128)S(1)} %bitcast.17, ...), custom_call_target="tpu_custom_call" | custom-call | tf_op jit(solution)/shard_map/pallas_call | solution.py:550
  13.8 2.4 %shard_map.121 = (f32[128,128]{1,0:T(8,128)S(1)}, f32[128,128]{1,0:T(8,128)}, f32[128,128]{1,0:T(8,128)}, f32[80,128]{1,0:T(8,128)S(1)}, f32[80,128]{1,0:T(8,128...) custom-call(f32[4,128,128]{2,1,0:T(8,128)S(1)} %get-tuple-element.37.refs_0_, ...), custom_call_target="tpu_custom_call" | custom-call | tf_op jit(solution)/shard_map/pallas_call | solution.py:550
  16.2 3.0 %collective-permute-start.3 = (f32[152,128]{1,0:T(8,128)S(1)}, f32[152,128]{1,0:T(8,128)S(1)}, u32[]{:S(2)}, u32[]{:S(2)}) collective-permute-start(f32[152,128]{1,0:T(8,128)S(1)} %get-tuple-element.50), channel_id=1, source_target_pairs={{0,16},{4,20},{8,24},{12,28},{1,17},{5,21},{9,25},{13,29},{2,18},{... | collective-permute-start | bytes 233480 | tf_op jit(solution)/shard_map/ppermute | solution.py:618
  19.2 4.2 %shard_map.122 = (f32[128,128]{1,0:T(8,128)S(1)}, f32[128,128]{1,0:T(8,128)S(1)}, f32[128,128]{1,0:T(8,128)S(1)}, f32[80,128]{1,0:T(8,128)S(1)}, f32[80,128]{1,0...) custom-call(f32[2,128]{1,0:T(2,128)S(1)} %bitcast.18, ...), custom_call_target="tpu_custom_call" | custom-call | tf_op jit(solution)/shard_map/pallas_call | solution.py:550
  23.4 0.0 collective-permute-done.3.state_ref
  23.4 0.4 shard_map.123
  23.8 3.5 %collective-permute-start.4 = (f32[32,128]{1,0:T(8,128)S(1)}, f32[32,128]{1,0:T(8,128)S(1)}, u32[]{:S(2)}, u32[]{:S(2)}) collective-permute-start(f32[32,128]{1,0:T(8,128)S(1)} %get-tuple-element.60), channel_id=1, source_target_pairs={{0,16},{4,20},{8,24},{12,28},{16,0},{20,4},{24,8},{28,12},{1,17},{... | collective-permute-start | bytes 49160 | tf_op jit(solution)/shard_map/ppermute | solution.py:562
  27.3 1.7 %collective-permute-done.4 = f32[32,128]{1,0:T(8,128)S(1)} collective-permute-done((f32[32,128]{1,0:T(8,128)S(1)}, f32[32,128]{1,0:T(8,128)S(1)}, u32[]{:S(2)}, u32[]{:S(2)}) %collective-permute-start.4) | collective-permute-done | bytes 16416 | tf_op jit(solution)/shard_map/ppermute | solution.py:562
  29.0 2.5 %collective-permute-start.7 = (f32[32,128]{1,0:T(8,128)S(1)}, f32[32,128]{1,0:T(8,128)S(1)}, u32[]{:S(2)}, u32[]{:S(2)}) collective-permute-start(f32[32,128]{1,0:T(8,128)S(1)} %add.12), channel_id=1, source_target_pairs={{0,3},{1,2},{2,1},{3,0},{4,7},{5,6},{6,5},{7,4},{8,11},{9,10},{10,... | collective-permute-start | bytes 49160 | tf_op jit(solution)/shard_map/ppermute | solution.py:562
  31.4 0.5 %collective-permute-start.6 = (f32[32,128]{1,0:T(8,128)S(1)}, f32[32,128]{1,0:T(8,128)S(1)}, u32[]{:S(2)}, u32[]{:S(2)}) collective-permute-start(f32[32,128]{1,0:T(8,128)S(1)} %add.12), channel_id=1, source_target_pairs={{0,2},{1,3},{2,0},{3,1},{4,6},{5,7},{6,4},{7,5},{8,10},{9,11},{10,... | collective-permute-start | bytes 49160 | tf_op jit(solution)/shard_map/ppermute | solution.py:562
  31.9 0.5 %collective-permute-start.5 = (f32[32,128]{1,0:T(8,128)S(1)}, f32[32,128]{1,0:T(8,128)S(1)}, u32[]{:S(2)}, u32[]{:S(2)}) collective-permute-start(f32[32,128]{1,0:T(8,128)S(1)} %add.12), channel_id=1, source_target_pairs={{0,1},{1,0},{2,3},{3,2},{4,5},{5,4},{6,7},{7,6},{8,9},{9,8},{10,11... | collective-permute-start | bytes 49160 | tf_op jit(solution)/shard_map/ppermute | solution.py:562
  32.5 1.2 %collective-permute-done.7 = f32[32,128]{1,0:T(8,128)S(1)} collective-permute-done((f32[32,128]{1,0:T(8,128)S(1)}, f32[32,128]{1,0:T(8,128)S(1)}, u32[]{:S(2)}, u32[]{:S(2)}) %collective-permute-start.7) | collective-permute-done | bytes 16416 | tf_op jit(solution)/shard_map/ppermute | solution.py:562
  33.6 1.5 %collective-permute-done.6 = f32[32,128]{1,0:T(8,128)S(1)} collective-permute-done((f32[32,128]{1,0:T(8,128)S(1)}, f32[32,128]{1,0:T(8,128)S(1)}, u32[]{:S(2)}, u32[]{:S(2)}) %collective-permute-start.6) | collective-permute-done | bytes 16416 | tf_op jit(solution)/shard_map/ppermute | solution.py:562
  35.2 0.5 %collective-permute-done.5 = f32[32,128]{1,0:T(8,128)S(1)} collective-permute-done((f32[32,128]{1,0:T(8,128)S(1)}, f32[32,128]{1,0:T(8,128)S(1)}, u32[]{:S(2)}, u32[]{:S(2)}) %collective-permute-start.5) | collective-permute-done | bytes 16416 | tf_op jit(solution)/shard_map/ppermute | solution.py:562
  35.7 3.1 %collective-permute-start.8 = (f32[40,128]{1,0:T(8,128)S(1)}, f32[40,128]{1,0:T(8,128)S(1)}, u32[]{:S(2)}, u32[]{:S(2)}) collective-permute-start(f32[40,128]{1,0:T(8,128)S(1)} %pad_maximum_fusion.1), channel_id=1, source_target_pairs={{0,8},{4,12},{8,0},{12,4},{16,24},{20,28},{24,16},{28,20},{1,9},{5... | collective-permute-start | bytes 61448 | tf_op jit(solution)/shard_map/ppermute | solution.py:562
  38.8 1.8 %collective-permute-done.8 = f32[40,128]{1,0:T(8,128)S(1)} collective-permute-done((f32[40,128]{1,0:T(8,128)S(1)}, f32[40,128]{1,0:T(8,128)S(1)}, u32[]{:S(2)}, u32[]{:S(2)}) %collective-permute-start.8) | collective-permute-done | bytes 20512 | tf_op jit(solution)/shard_map/ppermute | solution.py:562
  40.6 0.0 collective-permute-start.9
  40.6 1.2 %collective-permute-done.9.refs_1_ = f32[80,128]{1,0:T(8,128)S(1)} collective-permute-done((f32[80,128]{1,0:T(8,128)S(1)}, f32[80,128]{1,0:T(8,128)S(1)}, u32[]{:S(2)}, u32[]{:S(2)}) %collective-permute-start.9) | collective-permute-done | bytes 40992 | tf_op jit(solution)/shard_map/ppermute | solution.py:562
  41.8 3.2 %shard_map.125 = (f32[4,128]{1,0:T(4,128)}, f32[4,128]{1,0:T(4,128)}, f32[4,64]{1,0:T(4,128)}, f32[4,64]{1,0:T(4,128)}) custom-call(f32[64,128]{1,0:T(8,128)S(1)} %get-tuple-element.49.prior_ref, f32[80,128]{1,0:T(8,128)S(1)} %pad_maximum_fusion.refs_0_, f32[80,128]{1,0:T(8,128)S(1)} %collective-permute-done.9.refs_1_), custom_call_target="tpu_custom_call" | custom-call | tf_op jit(solution)/shard_map/pallas_call | solution.py:550
  (8 shorter events, 0.0 us)
Async XLA Ops:
  1.3 1.0 %copy-start = (f32[1,64,128]{2,1,0:T(8,128)S(1)}, f32[1,64,128]{2,1,0:T(8,128)}, u32[]{:S(2)}) copy-start(f32[1,64,128]{2,1,0:T(8,128)} %param.11) | copy-start | bytes 98308
  2.2 0.7 %copy-start.1 = (f32[1,128]{1,0:T(1,128)S(1)}, f32[1,128]{1,0:T(1,128)}, u32[]{:S(2)}) copy-start(f32[1,128]{1,0:T(1,128)} %param.12) | copy-start | bytes 1540
  2.9 6.2 %copy-start.5 = (f32[4]{0:T(128)S(1)}, f32[4]{0:T(128)}, u32[]{:S(2)}) copy-start(f32[4]{0:T(128)} %param.16) | copy-start | bytes 52
  3.0 6.1 %copy-start.2 = (f32[64]{0:T(128)S(1)}, f32[64]{0:T(128)}, u32[]{:S(2)}) copy-start(f32[64]{0:T(128)} %param.14) | copy-start | bytes 772
  3.0 6.1 %copy-start.3 = (f32[64]{0:T(128)S(1)}, f32[64]{0:T(128)}, u32[]{:S(2)}) copy-start(f32[64]{0:T(128)} %param.13) | copy-start | bytes 772
  3.0 6.1 %copy-start.4 = (f32[4]{0:T(128)S(1)}, f32[4]{0:T(128)}, u32[]{:S(2)}) copy-start(f32[4]{0:T(128)} %param.15) | copy-start | bytes 52
  3.1 6.1 %collective-permute-start.1 = (f32[208,128]{1,0:T(8,128)S(1)}, f32[208,128]{1,0:T(8,128)S(1)}, u32[]{:S(2)}, u32[]{:S(2)}) collective-permute-start(f32[208,128]{1,0:T(8,128)S(1)} %concatenate.14.own_ref), channel_id=1, source_target_pairs={{0,8},{4,12},{8,0},{12,4},{16,24},{20,28},{24,16},{28,20},{1,9},{5... | collective-permute-start | bytes 319496 | tf_op jit(solution)/shard_map/ppermute | solution.py:562
  6.1 3.1 %collective-permute-start = (f32[208,128]{1,0:T(8,128)S(1)}, f32[208,128]{1,0:T(8,128)S(1)}, u32[]{:S(2)}, u32[]{:S(2)}) collective-permute-start(f32[208,128]{1,0:T(8,128)S(1)} %concatenate.14.own_ref), channel_id=1, source_target_pairs={{0,4},{4,0},{8,12},{12,8},{16,20},{20,16},{24,28},{28,24},{1,5},{5... | collective-permute-start | bytes 319496 | tf_op jit(solution)/shard_map/ppermute | solution.py:562
  9.1 1.3 %collective-permute-start.2 = (f32[208,128]{1,0:T(8,128)S(1)}, f32[208,128]{1,0:T(8,128)S(1)}, u32[]{:S(2)}, u32[]{:S(2)}) collective-permute-start(f32[208,128]{1,0:T(8,128)S(1)} %collective-permute-done.1.two_ref), channel_id=1, source_target_pairs={{0,4},{4,0},{8,12},{12,8},{16,20},{20,16},{24,28},{28,24},{1,5},{5... | collective-permute-start | bytes 319496 | tf_op jit(solution)/shard_map/ppermute | solution.py:562
  16.2 7.2 %collective-permute-start.3 = (f32[152,128]{1,0:T(8,128)S(1)}, f32[152,128]{1,0:T(8,128)S(1)}, u32[]{:S(2)}, u32[]{:S(2)}) collective-permute-start(f32[152,128]{1,0:T(8,128)S(1)} %get-tuple-element.50), channel_id=1, source_target_pairs={{0,16},{4,20},{8,24},{12,28},{1,17},{5,21},{9,25},{13,29},{2,18},{... | collective-permute-start | bytes 233480 | tf_op jit(solution)/shard_map/ppermute | solution.py:618
  23.8 5.2 %collective-permute-start.4 = (f32[32,128]{1,0:T(8,128)S(1)}, f32[32,128]{1,0:T(8,128)S(1)}, u32[]{:S(2)}, u32[]{:S(2)}) collective-permute-start(f32[32,128]{1,0:T(8,128)S(1)} %get-tuple-element.60), channel_id=1, source_target_pairs={{0,16},{4,20},{8,24},{12,28},{16,0},{20,4},{24,8},{28,12},{1,17},{... | collective-permute-start | bytes 49160 | tf_op jit(solution)/shard_map/ppermute | solution.py:562
  29.0 4.7 %collective-permute-start.7 = (f32[32,128]{1,0:T(8,128)S(1)}, f32[32,128]{1,0:T(8,128)S(1)}, u32[]{:S(2)}, u32[]{:S(2)}) collective-permute-start(f32[32,128]{1,0:T(8,128)S(1)} %add.12), channel_id=1, source_target_pairs={{0,3},{1,2},{2,1},{3,0},{4,7},{5,6},{6,5},{7,4},{8,11},{9,10},{10,... | collective-permute-start | bytes 49160 | tf_op jit(solution)/shard_map/ppermute | solution.py:562
  31.4 3.7 %collective-permute-start.6 = (f32[32,128]{1,0:T(8,128)S(1)}, f32[32,128]{1,0:T(8,128)S(1)}, u32[]{:S(2)}, u32[]{:S(2)}) collective-permute-start(f32[32,128]{1,0:T(8,128)S(1)} %add.12), channel_id=1, source_target_pairs={{0,2},{1,3},{2,0},{3,1},{4,6},{5,7},{6,4},{7,5},{8,10},{9,11},{10,... | collective-permute-start | bytes 49160 | tf_op jit(solution)/shard_map/ppermute | solution.py:562
  31.9 3.7 %collective-permute-start.5 = (f32[32,128]{1,0:T(8,128)S(1)}, f32[32,128]{1,0:T(8,128)S(1)}, u32[]{:S(2)}, u32[]{:S(2)}) collective-permute-start(f32[32,128]{1,0:T(8,128)S(1)} %add.12), channel_id=1, source_target_pairs={{0,1},{1,0},{2,3},{3,2},{4,5},{5,4},{6,7},{7,6},{8,9},{9,8},{10,11... | collective-permute-start | bytes 49160 | tf_op jit(solution)/shard_map/ppermute | solution.py:562
  35.7 4.9 %collective-permute-start.8 = (f32[40,128]{1,0:T(8,128)S(1)}, f32[40,128]{1,0:T(8,128)S(1)}, u32[]{:S(2)}, u32[]{:S(2)}) collective-permute-start(f32[40,128]{1,0:T(8,128)S(1)} %pad_maximum_fusion.1), channel_id=1, source_target_pairs={{0,8},{4,12},{8,0},{12,4},{16,24},{20,28},{24,16},{28,20},{1,9},{5... | collective-permute-start | bytes 61448 | tf_op jit(solution)/shard_map/ppermute | solution.py:562
  40.6 1.2 %collective-permute-start.9 = (f32[80,128]{1,0:T(8,128)S(1)}, f32[80,128]{1,0:T(8,128)S(1)}, u32[]{:S(2)}, u32[]{:S(2)}) collective-permute-start(f32[80,128]{1,0:T(8,128)S(1)} %pad_maximum_fusion.refs_0_), channel_id=1, source_target_pairs={{0,4},{4,0},{8,12},{12,8},{16,20},{20,16},{24,28},{28,24},{1,5},{5... | collective-permute-start | bytes 122888 | tf_op jit(solution)/shard_map/ppermute | solution.py:562

commit v16 on v15

--- a/solution.py
+++ b/solution.py
@@ -239,7 +239,11 @@
 
 
 def early_kernel(tip, start, *refs):
-    parts, part_ref, out_refs, spare = refs[:5], refs[5], refs[6:14], refs[14:]
+    parts, part_ref, refs = refs[:5], refs[5], refs[6:]
+    diag_ref, right_ref, share_ref, mat_ref, inv_ref, *rest_refs = refs
+    cross_ref, back_ref, left_ref, far_ref, near_ref = rest_refs
+    out_refs = (diag_ref, cross_ref, back_ref, right_ref, left_ref, far_ref, near_ref, share_ref)
+    spare = (mat_ref, inv_ref)
 
     @pl.when(lax.axis_index("tm") < GROUP)
     def _():
@@ -376,6 +380,7 @@
                 for p, ref in enumerate(refs):
                     ref[spot, :] = rest[p] - update[:, 128 * p : 128 * (p + 1)]
         rows = [[ref[(strip + i) * SUB : (strip + i + 1) * SUB, :] for ref in refs] for i in range(STRIP)]
+        weights, roots = {}, {}
         for panel in range(0, STRIP, SUB):
             base = strip + panel
             block = {
@@ -383,28 +388,29 @@
             }
             for k in range(SUB):
                 pivot = block[k, k]
-                root = lax.rsqrt(pivot)
+                inverse = pl.reciprocal(pivot, approx=True)
+                inverse = inverse * (2.0 - pivot * inverse)
                 pivots = jnp.where(lane == base + k, pivot, pivots)
-                scaled = {m: block[k, m] * root for m in range(k + 1, SUB)}
-                ready = [piece * root for piece in rows[panel + k]]
-                rows[panel + k] = ready
+                scaled = {m: block[k, m] * inverse for m in range(k + 1, SUB)}
+                own = rows[panel + k]
+                weights[panel + k] = own[0] * inverse
+                roots[panel + k] = pivot
                 for i in range(k + 1, SUB):
                     for m in range(i, SUB):
-                        block[i, m] = block[i, m] - scaled[i] * scaled[m]
-                    rows[panel + i] = [
-                        piece - scaled[i] * own for piece, own in zip(rows[panel + i], ready)
-                    ]
+                        block[i, m] = block[i, m] - scaled[i] * block[k, m]
+                    rows[panel + i] = [piece - scaled[i] * part for piece, part in zip(rows[panel + i], own)]
             for i in range(panel + SUB, STRIP):
                 for k in range(panel, panel + SUB):
-                    ready = rows[k]
-                    weight = splat(ready[0], strip + i)
-                    rows[i] = [piece - weight * own for piece, own in zip(rows[i], ready)]
+                    weight = splat(weights[k], strip + i)
+                    rows[i] = [piece - weight * part for piece, part in zip(rows[i], rows[k])]
         for i in range(STRIP):
             column = jnp.where(lane == strip + i, splat(rows[i][-1], tip), column)
-        for i in range(STRIP):
-            for p, ref in enumerate(refs):
-                ref[(strip + i) * SUB : (strip + i + 1) * SUB, :] = rows[i][p]
-    return pivots, column
+        if strip + STRIP < size:
+            for i in range(STRIP):
+                root = lax.rsqrt(roots[i])
+                for p, ref in enumerate(refs):
+                    ref[(strip + i) * SUB : (strip + i + 1) * SUB, :] = rows[i][p] * root
+    return pivots, column * lax.rsqrt(pivots)
 
 
 def halved(squares, sides, refs):
@@ -612,14 +618,19 @@
     )
     half = SUB * tile // 2
     outs = ((tile, tile),) * 3 + ((side, tile),) * 2 + ((tile, tile), (side, tile), (tip, tile))
-    early = call(functools.partial(early_kernel, tip, groups - GROUP), (*parts, part), outs, pair)
+    early = call(
+        functools.partial(early_kernel, tip, groups - GROUP),
+        (*parts, part),
+        ((tile, tile), (side, tile), (tip, tile)),
+        (*pair, (tile, tile), (tile, tile), (side, tile), (tile, tile), (side, tile)),
+    )
     state, early = lax.optimization_barrier((state, early))
     for span in range(spans - 1):
         state = lax.ppermute(state, "tm", [(source, source + GROUP) for source in range(groups - GROUP)])
         if span == 0:
             *later, prior, small = call(
                 functools.partial(travel_kernel, tip, groups - GROUP),
-                (extra, *parts, part, early[0], early[3]),
+                (extra, *parts, part, early[0], early[1]),
                 outs + ((tip, tile), (2 * GROUP, tile)),
                 (*pair, (half, tile)),
             )
@@ -628,7 +639,7 @@
             (state,) = call(advance_kernel, (state, *parts), (packed_state,), pair)
     squares, sides, sums = call(
         merge_kernel,
-        (state, *parts, far, near, share, early[7]),
+        (state, *parts, far, near, share, early[2]),
         (square, (tile, SUB), (tip // 2, tile)),
         pair,
     )

time: 45.2 us -> 44.5 us (0.985)
  Pallas kernels: 13.6 us -> 13 us
    pallas_call x6, Pallas kernels: 13.6 us -> 13 us  [call(): pl.pallas_call(body, out_shape=tuple((jax.ShapeDtypeStruct(shape, F32) fo...]
  transfers between devices with their start and end apart: 10 -> 10, of which waited for: 8 -> 8; matrix products, arithmetic and copies ran while one was open for 0% -> 0% of each run, Pallas kernels for 9% -> 10%
where the time goes in v16:
time: 44.5 us; the launch traced here: 44.3 us
  starting transfers between devices  16.1 us (36%)
  Pallas kernels  13 us (29%)
  waiting for transfers between devices  12.1 us (27%)
  between operations  1.42 us (3%)
  other arithmetic  0.93 us (2%)
  local copies, waits for them, and re-layouts  0.88 us (2%)
    ppermute x9, starting transfers between devices, crossed(): lax.ppermute(value, axis, [(source, source ^ step) for source in range(si...  13.1 us
    pallas_call x6, Pallas kernels, call(): pl.pallas_call(body, out_shape=tuple((jax.ShapeDtypeStruct(shape, F32) fo...  13 us
    ppermute x9, waiting for transfers between devices, crossed(): lax.ppermute(value, axis, [(source, source ^ step) for source in range(si...  12.1 us
    ppermute x1, starting transfers between devices, shards(): lax.ppermute(state, 'tm', [(source, source + GROUP) for source in range(g...  2.98 us
    reduce_sum x1, other arithmetic, shards(): jnp.sum(jnp.where(row == col, coupling[0], 0.0), axis=0, keepdims=True)  0.91 us
  transfers between devices with their start and end apart: 10, of which 8 were waited for; matrix products, arithmetic and copies ran while one was open for 0% of the time, Pallas kernels for 10%

profile of v16, /device:TPU:0, one launch (start us, length us, event | category | flops | bytes accessed | tf_op | source)
XLA Modules:
  0.0 44.3 jit_solution(16850064978350263737)
XLA Ops:
  1.3 0.0 copy-start
  1.3 0.9 %fusion = (f32[128]{0:T(128)S(1)}, f32[128,128]{1,0:T(8,128)S(1)}) fusion(f32[1,128,128]{2,1,0:T(8,128)} %param.10, f32[1,128,128]{2,1,0:T(8,128)} %param.9), kind=kLoop, calls=%fused_computation.2 | loop fusion | flops 81792 | bytes 197120 | tf_op jit(solution)/shard_map/reduce_sum | solution.py:601
  2.2 0.0 copy-start.1
  2.2 0.0 copy-done
  2.2 0.6 %copy-done.1 = f32[1,128]{1,0:T(1,128)S(1)} copy-done((f32[1,128]{1,0:T(1,128)S(1)}, f32[1,128]{1,0:T(1,128)}, u32[]{:S(2)}) %copy-start.1) | copy-done | bytes 536
  2.9 0.0 copy-start.5
  2.9 0.1 concatenate.14.own_ref
  3.0 0.0 copy-start.2
  3.0 0.0 copy-start.3
  3.0 0.0 copy-start.4
  3.1 3.1 %collective-permute-start.1 = (f32[208,128]{1,0:T(8,128)S(1)}, f32[208,128]{1,0:T(8,128)S(1)}, u32[]{:S(2)}, u32[]{:S(2)}) collective-permute-start(f32[208,128]{1,0:T(8,128)S(1)} %concatenate.14.own_ref), channel_id=1, source_target_pairs={{0,8},{4,12},{8,0},{12,4},{16,24},{20,28},{24,16},{28,20},{1,9},{5... | collective-permute-start | bytes 319496 | tf_op jit(solution)/shard_map/ppermute | solution.py:568
  6.1 0.0 collective-permute-start
  6.1 3.0 %collective-permute-done.1.two_ref = f32[208,128]{1,0:T(8,128)S(1)} collective-permute-done((f32[208,128]{1,0:T(8,128)S(1)}, f32[208,128]{1,0:T(8,128)S(1)}, u32[]{:S(2)}, u32[]{:S(2)}) %collective-permute-start.1) | collective-permute-done | bytes 106528 | tf_op jit(solution)/shard_map/ppermute | solution.py:568
  9.1 0.0 collective-permute-start.2
  9.1 0.0 copy-done.5
  9.1 0.0 copy-done.2
  9.1 0.0 copy-done.3
  9.1 0.0 copy-done.4
  9.2 0.1 concatenate.13
  9.2 0.0 collective-permute-done.one_ref
  9.2 1.2 %collective-permute-done.2.three_ref = f32[208,128]{1,0:T(8,128)S(1)} collective-permute-done((f32[208,128]{1,0:T(8,128)S(1)}, f32[208,128]{1,0:T(8,128)S(1)}, u32[]{:S(2)}, u32[]{:S(2)}) %collective-permute-start.2) | collective-permute-done | bytes 106528 | tf_op jit(solution)/shard_map/ppermute | solution.py:568
  10.4 3.4 %shard_map.120 = (f32[4,128,128]{2,1,0:T(8,128)S(1)}, f32[4,128,128]{2,1,0:T(8,128)S(1)}, f32[4,128,128]{2,1,0:T(8,128)S(1)}, f32[4,80,128]{2,1,0:T(8,128)S(1)},...) custom-call(f32[2,128]{1,0:T(2,128)S(1)} %bitcast.17, ...), custom_call_target="tpu_custom_call" | custom-call | tf_op jit(solution)/shard_map/pallas_call | solution.py:556
  13.8 1.7 %shard_map.121 = (f32[128,128]{1,0:T(8,128)S(1)}, f32[80,128]{1,0:T(8,128)S(1)}, f32[64,128]{1,0:T(8,128)S(1)}) custom-call(f32[4,128,128]{2,1,0:T(8,128)S(1)} %get-tuple-element.37.refs_0_, f32[4,128,128]{2,1,0:T(8,128)S(1)} %get-tuple-element.38.refs_1_, f32[4,128,128]{2,1,0:T(8,128)S(1)} %get-tuple-element.39.refs_2_, ...), custom_call_target="tpu_custom_call" | custom-call | tf_op jit(solution)/shard_map/pallas_call | solution.py:556
  15.5 3.0 %collective-permute-start.3 = (f32[152,128]{1,0:T(8,128)S(1)}, f32[152,128]{1,0:T(8,128)S(1)}, u32[]{:S(2)}, u32[]{:S(2)}) collective-permute-start(f32[152,128]{1,0:T(8,128)S(1)} %get-tuple-element.50), channel_id=1, source_target_pairs={{0,16},{4,20},{8,24},{12,28},{1,17},{5,21},{9,25},{13,29},{2,18},{... | collective-permute-start | bytes 233480 | tf_op jit(solution)/shard_map/ppermute | solution.py:629
  18.5 4.3 %shard_map.122 = (f32[128,128]{1,0:T(8,128)S(1)}, f32[128,128]{1,0:T(8,128)S(1)}, f32[128,128]{1,0:T(8,128)S(1)}, f32[80,128]{1,0:T(8,128)S(1)}, f32[80,128]{1,0...) custom-call(f32[2,128]{1,0:T(2,128)S(1)} %bitcast.18, ...), custom_call_target="tpu_custom_call" | custom-call | tf_op jit(solution)/shard_map/pallas_call | solution.py:556
  22.8 0.0 collective-permute-done.3.state_ref
  22.8 0.4 shard_map.123
  23.2 3.4 %collective-permute-start.4 = (f32[32,128]{1,0:T(8,128)S(1)}, f32[32,128]{1,0:T(8,128)S(1)}, u32[]{:S(2)}, u32[]{:S(2)}) collective-permute-start(f32[32,128]{1,0:T(8,128)S(1)} %get-tuple-element.60), channel_id=1, source_target_pairs={{0,16},{4,20},{8,24},{12,28},{16,0},{20,4},{24,8},{28,12},{1,17},{... | collective-permute-start | bytes 49160 | tf_op jit(solution)/shard_map/ppermute | solution.py:568
  26.6 1.7 %collective-permute-done.4 = f32[32,128]{1,0:T(8,128)S(1)} collective-permute-done((f32[32,128]{1,0:T(8,128)S(1)}, f32[32,128]{1,0:T(8,128)S(1)}, u32[]{:S(2)}, u32[]{:S(2)}) %collective-permute-start.4) | collective-permute-done | bytes 16416 | tf_op jit(solution)/shard_map/ppermute | solution.py:568
  28.3 2.5 %collective-permute-start.7 = (f32[32,128]{1,0:T(8,128)S(1)}, f32[32,128]{1,0:T(8,128)S(1)}, u32[]{:S(2)}, u32[]{:S(2)}) collective-permute-start(f32[32,128]{1,0:T(8,128)S(1)} %add.12), channel_id=1, source_target_pairs={{0,3},{1,2},{2,1},{3,0},{4,7},{5,6},{6,5},{7,4},{8,11},{9,10},{10,... | collective-permute-start | bytes 49160 | tf_op jit(solution)/shard_map/ppermute | solution.py:568
  30.7 0.5 %collective-permute-start.6 = (f32[32,128]{1,0:T(8,128)S(1)}, f32[32,128]{1,0:T(8,128)S(1)}, u32[]{:S(2)}, u32[]{:S(2)}) collective-permute-start(f32[32,128]{1,0:T(8,128)S(1)} %add.12), channel_id=1, source_target_pairs={{0,2},{1,3},{2,0},{3,1},{4,6},{5,7},{6,4},{7,5},{8,10},{9,11},{10,... | collective-permute-start | bytes 49160 | tf_op jit(solution)/shard_map/ppermute | solution.py:568
  31.2 0.5 %collective-permute-start.5 = (f32[32,128]{1,0:T(8,128)S(1)}, f32[32,128]{1,0:T(8,128)S(1)}, u32[]{:S(2)}, u32[]{:S(2)}) collective-permute-start(f32[32,128]{1,0:T(8,128)S(1)} %add.12), channel_id=1, source_target_pairs={{0,1},{1,0},{2,3},{3,2},{4,5},{5,4},{6,7},{7,6},{8,9},{9,8},{10,11... | collective-permute-start | bytes 49160 | tf_op jit(solution)/shard_map/ppermute | solution.py:568
  31.8 1.2 %collective-permute-done.7 = f32[32,128]{1,0:T(8,128)S(1)} collective-permute-done((f32[32,128]{1,0:T(8,128)S(1)}, f32[32,128]{1,0:T(8,128)S(1)}, u32[]{:S(2)}, u32[]{:S(2)}) %collective-permute-start.7) | collective-permute-done | bytes 16416 | tf_op jit(solution)/shard_map/ppermute | solution.py:568
  32.9 1.5 %collective-permute-done.6 = f32[32,128]{1,0:T(8,128)S(1)} collective-permute-done((f32[32,128]{1,0:T(8,128)S(1)}, f32[32,128]{1,0:T(8,128)S(1)}, u32[]{:S(2)}, u32[]{:S(2)}) %collective-permute-start.6) | collective-permute-done | bytes 16416 | tf_op jit(solution)/shard_map/ppermute | solution.py:568
  34.5 0.5 %collective-permute-done.5 = f32[32,128]{1,0:T(8,128)S(1)} collective-permute-done((f32[32,128]{1,0:T(8,128)S(1)}, f32[32,128]{1,0:T(8,128)S(1)}, u32[]{:S(2)}, u32[]{:S(2)}) %collective-permute-start.5) | collective-permute-done | bytes 16416 | tf_op jit(solution)/shard_map/ppermute | solution.py:568
  35.0 3.1 %collective-permute-start.8 = (f32[40,128]{1,0:T(8,128)S(1)}, f32[40,128]{1,0:T(8,128)S(1)}, u32[]{:S(2)}, u32[]{:S(2)}) collective-permute-start(f32[40,128]{1,0:T(8,128)S(1)} %pad_maximum_fusion.1), channel_id=1, source_target_pairs={{0,8},{4,12},{8,0},{12,4},{16,24},{20,28},{24,16},{28,20},{1,9},{5... | collective-permute-start | bytes 61448 | tf_op jit(solution)/shard_map/ppermute | solution.py:568
  38.1 1.8 %collective-permute-done.8 = f32[40,128]{1,0:T(8,128)S(1)} collective-permute-done((f32[40,128]{1,0:T(8,128)S(1)}, f32[40,128]{1,0:T(8,128)S(1)}, u32[]{:S(2)}, u32[]{:S(2)}) %collective-permute-start.8) | collective-permute-done | bytes 20512 | tf_op jit(solution)/shard_map/ppermute | solution.py:568
  39.9 0.0 collective-permute-start.9
  39.9 1.2 %collective-permute-done.9.refs_1_ = f32[80,128]{1,0:T(8,128)S(1)} collective-permute-done((f32[80,128]{1,0:T(8,128)S(1)}, f32[80,128]{1,0:T(8,128)S(1)}, u32[]{:S(2)}, u32[]{:S(2)}) %collective-permute-start.9) | collective-permute-done | bytes 40992 | tf_op jit(solution)/shard_map/ppermute | solution.py:568
  41.1 3.3 %shard_map.125 = (f32[4,128]{1,0:T(4,128)}, f32[4,128]{1,0:T(4,128)}, f32[4,64]{1,0:T(4,128)}, f32[4,64]{1,0:T(4,128)}) custom-call(f32[64,128]{1,0:T(8,128)S(1)} %get-tuple-element.49.prior_ref, f32[80,128]{1,0:T(8,128)S(1)} %pad_maximum_fusion.refs_0_, f32[80,128]{1,0:T(8,128)S(1)} %collective-permute-done.9.refs_1_), custom_call_target="tpu_custom_call" | custom-call | tf_op jit(solution)/shard_map/pallas_call | solution.py:556
  (8 shorter events, 0.0 us)
Async XLA Ops:
  1.3 1.0 %copy-start = (f32[1,64,128]{2,1,0:T(8,128)S(1)}, f32[1,64,128]{2,1,0:T(8,128)}, u32[]{:S(2)}) copy-start(f32[1,64,128]{2,1,0:T(8,128)} %param.11) | copy-start | bytes 98308
  2.2 0.7 %copy-start.1 = (f32[1,128]{1,0:T(1,128)S(1)}, f32[1,128]{1,0:T(1,128)}, u32[]{:S(2)}) copy-start(f32[1,128]{1,0:T(1,128)} %param.12) | copy-start | bytes 1540
  2.9 6.2 %copy-start.5 = (f32[4]{0:T(128)S(1)}, f32[4]{0:T(128)}, u32[]{:S(2)}) copy-start(f32[4]{0:T(128)} %param.16) | copy-start | bytes 52
  3.0 6.1 %copy-start.2 = (f32[64]{0:T(128)S(1)}, f32[64]{0:T(128)}, u32[]{:S(2)}) copy-start(f32[64]{0:T(128)} %param.14) | copy-start | bytes 772
  3.0 6.1 %copy-start.3 = (f32[64]{0:T(128)S(1)}, f32[64]{0:T(128)}, u32[]{:S(2)}) copy-start(f32[64]{0:T(128)} %param.13) | copy-start | bytes 772
  3.0 6.1 %copy-start.4 = (f32[4]{0:T(128)S(1)}, f32[4]{0:T(128)}, u32[]{:S(2)}) copy-start(f32[4]{0:T(128)} %param.15) | copy-start | bytes 52
  3.1 6.1 %collective-permute-start.1 = (f32[208,128]{1,0:T(8,128)S(1)}, f32[208,128]{1,0:T(8,128)S(1)}, u32[]{:S(2)}, u32[]{:S(2)}) collective-permute-start(f32[208,128]{1,0:T(8,128)S(1)} %concatenate.14.own_ref), channel_id=1, source_target_pairs={{0,8},{4,12},{8,0},{12,4},{16,24},{20,28},{24,16},{28,20},{1,9},{5... | collective-permute-start | bytes 319496 | tf_op jit(solution)/shard_map/ppermute | solution.py:568
  6.1 3.1 %collective-permute-start = (f32[208,128]{1,0:T(8,128)S(1)}, f32[208,128]{1,0:T(8,128)S(1)}, u32[]{:S(2)}, u32[]{:S(2)}) collective-permute-start(f32[208,128]{1,0:T(8,128)S(1)} %concatenate.14.own_ref), channel_id=1, source_target_pairs={{0,4},{4,0},{8,12},{12,8},{16,20},{20,16},{24,28},{28,24},{1,5},{5... | collective-permute-start | bytes 319496 | tf_op jit(solution)/shard_map/ppermute | solution.py:568
  9.1 1.3 %collective-permute-start.2 = (f32[208,128]{1,0:T(8,128)S(1)}, f32[208,128]{1,0:T(8,128)S(1)}, u32[]{:S(2)}, u32[]{:S(2)}) collective-permute-start(f32[208,128]{1,0:T(8,128)S(1)} %collective-permute-done.1.two_ref), channel_id=1, source_target_pairs={{0,4},{4,0},{8,12},{12,8},{16,20},{20,16},{24,28},{28,24},{1,5},{5... | collective-permute-start | bytes 319496 | tf_op jit(solution)/shard_map/ppermute | solution.py:568
  15.5 7.3 %collective-permute-start.3 = (f32[152,128]{1,0:T(8,128)S(1)}, f32[152,128]{1,0:T(8,128)S(1)}, u32[]{:S(2)}, u32[]{:S(2)}) collective-permute-start(f32[152,128]{1,0:T(8,128)S(1)} %get-tuple-element.50), channel_id=1, source_target_pairs={{0,16},{4,20},{8,24},{12,28},{1,17},{5,21},{9,25},{13,29},{2,18},{... | collective-permute-start | bytes 233480 | tf_op jit(solution)/shard_map/ppermute | solution.py:629
  23.2 5.1 %collective-permute-start.4 = (f32[32,128]{1,0:T(8,128)S(1)}, f32[32,128]{1,0:T(8,128)S(1)}, u32[]{:S(2)}, u32[]{:S(2)}) collective-permute-start(f32[32,128]{1,0:T(8,128)S(1)} %get-tuple-element.60), channel_id=1, source_target_pairs={{0,16},{4,20},{8,24},{12,28},{16,0},{20,4},{24,8},{28,12},{1,17},{... | collective-permute-start | bytes 49160 | tf_op jit(solution)/shard_map/ppermute | solution.py:568
  28.3 4.7 %collective-permute-start.7 = (f32[32,128]{1,0:T(8,128)S(1)}, f32[32,128]{1,0:T(8,128)S(1)}, u32[]{:S(2)}, u32[]{:S(2)}) collective-permute-start(f32[32,128]{1,0:T(8,128)S(1)} %add.12), channel_id=1, source_target_pairs={{0,3},{1,2},{2,1},{3,0},{4,7},{5,6},{6,5},{7,4},{8,11},{9,10},{10,... | collective-permute-start | bytes 49160 | tf_op jit(solution)/shard_map/ppermute | solution.py:568
  30.7 3.7 %collective-permute-start.6 = (f32[32,128]{1,0:T(8,128)S(1)}, f32[32,128]{1,0:T(8,128)S(1)}, u32[]{:S(2)}, u32[]{:S(2)}) collective-permute-start(f32[32,128]{1,0:T(8,128)S(1)} %add.12), channel_id=1, source_target_pairs={{0,2},{1,3},{2,0},{3,1},{4,6},{5,7},{6,4},{7,5},{8,10},{9,11},{10,... | collective-permute-start | bytes 49160 | tf_op jit(solution)/shard_map/ppermute | solution.py:568
  31.2 3.7 %collective-permute-start.5 = (f32[32,128]{1,0:T(8,128)S(1)}, f32[32,128]{1,0:T(8,128)S(1)}, u32[]{:S(2)}, u32[]{:S(2)}) collective-permute-start(f32[32,128]{1,0:T(8,128)S(1)} %add.12), channel_id=1, source_target_pairs={{0,1},{1,0},{2,3},{3,2},{4,5},{5,4},{6,7},{7,6},{8,9},{9,8},{10,11... | collective-permute-start | bytes 49160 | tf_op jit(solution)/shard_map/ppermute | solution.py:568
  35.0 4.9 %collective-permute-start.8 = (f32[40,128]{1,0:T(8,128)S(1)}, f32[40,128]{1,0:T(8,128)S(1)}, u32[]{:S(2)}, u32[]{:S(2)}) collective-permute-start(f32[40,128]{1,0:T(8,128)S(1)} %pad_maximum_fusion.1), channel_id=1, source_target_pairs={{0,8},{4,12},{8,0},{12,4},{16,24},{20,28},{24,16},{28,20},{1,9},{5... | collective-permute-start | bytes 61448 | tf_op jit(solution)/shard_map/ppermute | solution.py:568
  39.9 1.2 %collective-permute-start.9 = (f32[80,128]{1,0:T(8,128)S(1)}, f32[80,128]{1,0:T(8,128)S(1)}, u32[]{:S(2)}, u32[]{:S(2)}) collective-permute-start(f32[80,128]{1,0:T(8,128)S(1)} %pad_maximum_fusion.refs_0_), channel_id=1, source_target_pairs={{0,4},{4,0},{8,12},{12,8},{16,20},{20,16},{24,28},{28,24},{1,5},{5... | collective-permute-start | bytes 122888 | tf_op jit(solution)/shard_map/ppermute | solution.py:568

commit v17 on v15

--- a/solution.py
+++ b/solution.py
@@ -13,7 +13,7 @@
 NT = (((1,), (1,)), ((), ()))
 TN = (((0,), (0,)), ((), ()))
 SUB = 8
-STRIP = 32
+STRIP = 16
 GROUP = 4
 SPAN = 2.8
 SMALL = 2.5e-9
@@ -239,7 +239,11 @@
 
 
 def early_kernel(tip, start, *refs):
-    parts, part_ref, out_refs, spare = refs[:5], refs[5], refs[6:14], refs[14:]
+    parts, part_ref, refs = refs[:5], refs[5], refs[6:]
+    diag_ref, right_ref, share_ref, mat_ref, inv_ref, *rest_refs = refs
+    cross_ref, back_ref, left_ref, far_ref, near_ref = rest_refs
+    out_refs = (diag_ref, cross_ref, back_ref, right_ref, left_ref, far_ref, near_ref, share_ref)
+    spare = (mat_ref, inv_ref)
 
     @pl.when(lax.axis_index("tm") < GROUP)
     def _():
@@ -612,14 +616,19 @@
     )
     half = SUB * tile // 2
     outs = ((tile, tile),) * 3 + ((side, tile),) * 2 + ((tile, tile), (side, tile), (tip, tile))
-    early = call(functools.partial(early_kernel, tip, groups - GROUP), (*parts, part), outs, pair)
+    early = call(
+        functools.partial(early_kernel, tip, groups - GROUP),
+        (*parts, part),
+        ((tile, tile), (side, tile), (tip, tile)),
+        (*pair, (tile, tile), (tile, tile), (side, tile), (tile, tile), (side, tile)),
+    )
     state, early = lax.optimization_barrier((state, early))
     for span in range(spans - 1):
         state = lax.ppermute(state, "tm", [(source, source + GROUP) for source in range(groups - GROUP)])
         if span == 0:
             *later, prior, small = call(
                 functools.partial(travel_kernel, tip, groups - GROUP),
-                (extra, *parts, part, early[0], early[3]),
+                (extra, *parts, part, early[0], early[1]),
                 outs + ((tip, tile), (2 * GROUP, tile)),
                 (*pair, (half, tile)),
             )
@@ -628,7 +637,7 @@
             (state,) = call(advance_kernel, (state, *parts), (packed_state,), pair)
     squares, sides, sums = call(
         merge_kernel,
-        (state, *parts, far, near, share, early[7]),
+        (state, *parts, far, near, share, early[2]),
         (square, (tile, SUB), (tip // 2, tile)),
         pair,
     )

time: 45.2 us -> 44.3 us (0.980)
  Pallas kernels: 13.6 us -> 12.5 us
    pallas_call x6, Pallas kernels: 13.6 us -> 12.5 us  [call(): pl.pallas_call(body, out_shape=tuple((jax.ShapeDtypeStruct(shape, F32) fo...]
where the time goes in v17:
time: 44.3 us; the launch traced here: 44.1 us
  starting transfers between devices  16.3 us (37%)
  Pallas kernels  12.5 us (28%)
  waiting for transfers between devices  12.1 us (27%)
  between operations  1.42 us (3%)
  other arithmetic  0.93 us (2%)
  local copies, waits for them, and re-layouts  0.88 us (2%)
    ppermute x9, starting transfers between devices, crossed(): lax.ppermute(value, axis, [(source, source ^ step) for source in range(si...  13.3 us
    pallas_call x6, Pallas kernels, call(): pl.pallas_call(body, out_shape=tuple((jax.ShapeDtypeStruct(shape, F32) fo...  12.5 us
    ppermute x9, waiting for transfers between devices, crossed(): lax.ppermute(value, axis, [(source, source ^ step) for source in range(si...  12.1 us
    ppermute x1, starting transfers between devices, shards(): lax.ppermute(state, 'tm', [(source, source + GROUP) for source in range(g...  2.98 us
    reduce_sum x1, other arithmetic, shards(): jnp.sum(jnp.where(row == col, coupling[0], 0.0), axis=0, keepdims=True)  0.91 us
  transfers between devices with their start and end apart: 10, of which 8 were waited for; matrix products, arithmetic and copies ran while one was open for 0% of the time, Pallas kernels for 9%

profile of v17, /device:TPU:0, one launch (start us, length us, event | category | flops | bytes accessed | tf_op | source)
XLA Modules:
  0.0 44.1 jit_solution(7956360773685469488)
XLA Ops:
  1.3 0.0 copy-start
  1.3 0.9 %fusion = (f32[128]{0:T(128)S(1)}, f32[128,128]{1,0:T(8,128)S(1)}) fusion(f32[1,128,128]{2,1,0:T(8,128)} %param.10, f32[1,128,128]{2,1,0:T(8,128)} %param.9), kind=kLoop, calls=%fused_computation.2 | loop fusion | flops 81792 | bytes 197120 | tf_op jit(solution)/shard_map/reduce_sum | solution.py:599
  2.2 0.0 copy-start.1
  2.2 0.0 copy-done
  2.2 0.6 %copy-done.1 = f32[1,128]{1,0:T(1,128)S(1)} copy-done((f32[1,128]{1,0:T(1,128)S(1)}, f32[1,128]{1,0:T(1,128)}, u32[]{:S(2)}) %copy-start.1) | copy-done | bytes 536
  2.9 0.0 copy-start.5
  2.9 0.1 concatenate.14.own_ref
  3.0 0.0 copy-start.2
  3.0 0.0 copy-start.3
  3.0 0.0 copy-start.4
  3.1 3.1 %collective-permute-start.1 = (f32[208,128]{1,0:T(8,128)S(1)}, f32[208,128]{1,0:T(8,128)S(1)}, u32[]{:S(2)}, u32[]{:S(2)}) collective-permute-start(f32[208,128]{1,0:T(8,128)S(1)} %concatenate.14.own_ref), channel_id=1, source_target_pairs={{0,8},{4,12},{8,0},{12,4},{16,24},{20,28},{24,16},{28,20},{1,9},{5... | collective-permute-start | bytes 319496 | tf_op jit(solution)/shard_map/ppermute | solution.py:566
  6.1 0.0 collective-permute-start
  6.1 3.0 %collective-permute-done.1.two_ref = f32[208,128]{1,0:T(8,128)S(1)} collective-permute-done((f32[208,128]{1,0:T(8,128)S(1)}, f32[208,128]{1,0:T(8,128)S(1)}, u32[]{:S(2)}, u32[]{:S(2)}) %collective-permute-start.1) | collective-permute-done | bytes 106528 | tf_op jit(solution)/shard_map/ppermute | solution.py:566
  9.1 0.0 collective-permute-start.2
  9.1 0.0 copy-done.5
  9.1 0.0 copy-done.2
  9.1 0.0 copy-done.3
  9.1 0.0 copy-done.4
  9.2 0.1 concatenate.13
  9.2 0.0 collective-permute-done.one_ref
  9.2 1.2 %collective-permute-done.2.three_ref = f32[208,128]{1,0:T(8,128)S(1)} collective-permute-done((f32[208,128]{1,0:T(8,128)S(1)}, f32[208,128]{1,0:T(8,128)S(1)}, u32[]{:S(2)}, u32[]{:S(2)}) %collective-permute-start.2) | collective-permute-done | bytes 106528 | tf_op jit(solution)/shard_map/ppermute | solution.py:566
  10.4 3.4 %shard_map.120 = (f32[4,128,128]{2,1,0:T(8,128)S(1)}, f32[4,128,128]{2,1,0:T(8,128)S(1)}, f32[4,128,128]{2,1,0:T(8,128)S(1)}, f32[4,80,128]{2,1,0:T(8,128)S(1)},...) custom-call(f32[2,128]{1,0:T(2,128)S(1)} %bitcast.17, ...), custom_call_target="tpu_custom_call" | custom-call | tf_op jit(solution)/shard_map/pallas_call | solution.py:554
  13.8 1.7 %shard_map.121 = (f32[128,128]{1,0:T(8,128)S(1)}, f32[80,128]{1,0:T(8,128)S(1)}, f32[64,128]{1,0:T(8,128)S(1)}) custom-call(f32[4,128,128]{2,1,0:T(8,128)S(1)} %get-tuple-element.37.refs_0_, f32[4,128,128]{2,1,0:T(8,128)S(1)} %get-tuple-element.38.refs_1_, f32[4,128,128]{2,1,0:T(8,128)S(1)} %get-tuple-element.39.refs_2_, ...), custom_call_target="tpu_custom_call" | custom-call | tf_op jit(solution)/shard_map/pallas_call | solution.py:554
  15.5 3.0 %collective-permute-start.3 = (f32[152,128]{1,0:T(8,128)S(1)}, f32[152,128]{1,0:T(8,128)S(1)}, u32[]{:S(2)}, u32[]{:S(2)}) collective-permute-start(f32[152,128]{1,0:T(8,128)S(1)} %get-tuple-element.50), channel_id=1, source_target_pairs={{0,16},{4,20},{8,24},{12,28},{1,17},{5,21},{9,25},{13,29},{2,18},{... | collective-permute-start | bytes 233480 | tf_op jit(solution)/shard_map/ppermute | solution.py:627
  18.5 4.1 %shard_map.122 = (f32[128,128]{1,0:T(8,128)S(1)}, f32[128,128]{1,0:T(8,128)S(1)}, f32[128,128]{1,0:T(8,128)S(1)}, f32[80,128]{1,0:T(8,128)S(1)}, f32[80,128]{1,0...) custom-call(f32[2,128]{1,0:T(2,128)S(1)} %bitcast.18, ...), custom_call_target="tpu_custom_call" | custom-call | tf_op jit(solution)/shard_map/pallas_call | solution.py:554
  22.6 0.0 collective-permute-done.3.state_ref
  22.6 0.4 shard_map.123
  23.0 3.6 %collective-permute-start.4 = (f32[32,128]{1,0:T(8,128)S(1)}, f32[32,128]{1,0:T(8,128)S(1)}, u32[]{:S(2)}, u32[]{:S(2)}) collective-permute-start(f32[32,128]{1,0:T(8,128)S(1)} %get-tuple-element.60), channel_id=1, source_target_pairs={{0,16},{4,20},{8,24},{12,28},{16,0},{20,4},{24,8},{28,12},{1,17},{... | collective-permute-start | bytes 49160 | tf_op jit(solution)/shard_map/ppermute | solution.py:566
  26.6 1.7 %collective-permute-done.4 = f32[32,128]{1,0:T(8,128)S(1)} collective-permute-done((f32[32,128]{1,0:T(8,128)S(1)}, f32[32,128]{1,0:T(8,128)S(1)}, u32[]{:S(2)}, u32[]{:S(2)}) %collective-permute-start.4) | collective-permute-done | bytes 16416 | tf_op jit(solution)/shard_map/ppermute | solution.py:566
  28.3 2.5 %collective-permute-start.7 = (f32[32,128]{1,0:T(8,128)S(1)}, f32[32,128]{1,0:T(8,128)S(1)}, u32[]{:S(2)}, u32[]{:S(2)}) collective-permute-start(f32[32,128]{1,0:T(8,128)S(1)} %add.12), channel_id=1, source_target_pairs={{0,3},{1,2},{2,1},{3,0},{4,7},{5,6},{6,5},{7,4},{8,11},{9,10},{10,... | collective-permute-start | bytes 49160 | tf_op jit(solution)/shard_map/ppermute | solution.py:566
  30.7 0.5 %collective-permute-start.6 = (f32[32,128]{1,0:T(8,128)S(1)}, f32[32,128]{1,0:T(8,128)S(1)}, u32[]{:S(2)}, u32[]{:S(2)}) collective-permute-start(f32[32,128]{1,0:T(8,128)S(1)} %add.12), channel_id=1, source_target_pairs={{0,2},{1,3},{2,0},{3,1},{4,6},{5,7},{6,4},{7,5},{8,10},{9,11},{10,... | collective-permute-start | bytes 49160 | tf_op jit(solution)/shard_map/ppermute | solution.py:566
  31.2 0.5 %collective-permute-start.5 = (f32[32,128]{1,0:T(8,128)S(1)}, f32[32,128]{1,0:T(8,128)S(1)}, u32[]{:S(2)}, u32[]{:S(2)}) collective-permute-start(f32[32,128]{1,0:T(8,128)S(1)} %add.12), channel_id=1, source_target_pairs={{0,1},{1,0},{2,3},{3,2},{4,5},{5,4},{6,7},{7,6},{8,9},{9,8},{10,11... | collective-permute-start | bytes 49160 | tf_op jit(solution)/shard_map/ppermute | solution.py:566
  31.8 1.2 %collective-permute-done.7 = f32[32,128]{1,0:T(8,128)S(1)} collective-permute-done((f32[32,128]{1,0:T(8,128)S(1)}, f32[32,128]{1,0:T(8,128)S(1)}, u32[]{:S(2)}, u32[]{:S(2)}) %collective-permute-start.7) | collective-permute-done | bytes 16416 | tf_op jit(solution)/shard_map/ppermute | solution.py:566
  32.9 1.5 %collective-permute-done.6 = f32[32,128]{1,0:T(8,128)S(1)} collective-permute-done((f32[32,128]{1,0:T(8,128)S(1)}, f32[32,128]{1,0:T(8,128)S(1)}, u32[]{:S(2)}, u32[]{:S(2)}) %collective-permute-start.6) | collective-permute-done | bytes 16416 | tf_op jit(solution)/shard_map/ppermute | solution.py:566
  34.5 0.5 %collective-permute-done.5 = f32[32,128]{1,0:T(8,128)S(1)} collective-permute-done((f32[32,128]{1,0:T(8,128)S(1)}, f32[32,128]{1,0:T(8,128)S(1)}, u32[]{:S(2)}, u32[]{:S(2)}) %collective-permute-start.5) | collective-permute-done | bytes 16416 | tf_op jit(solution)/shard_map/ppermute | solution.py:566
  35.0 3.1 %collective-permute-start.8 = (f32[40,128]{1,0:T(8,128)S(1)}, f32[40,128]{1,0:T(8,128)S(1)}, u32[]{:S(2)}, u32[]{:S(2)}) collective-permute-start(f32[40,128]{1,0:T(8,128)S(1)} %pad_maximum_fusion.1), channel_id=1, source_target_pairs={{0,8},{4,12},{8,0},{12,4},{16,24},{20,28},{24,16},{28,20},{1,9},{5... | collective-permute-start | bytes 61448 | tf_op jit(solution)/shard_map/ppermute | solution.py:566
  38.1 1.8 %collective-permute-done.8 = f32[40,128]{1,0:T(8,128)S(1)} collective-permute-done((f32[40,128]{1,0:T(8,128)S(1)}, f32[40,128]{1,0:T(8,128)S(1)}, u32[]{:S(2)}, u32[]{:S(2)}) %collective-permute-start.8) | collective-permute-done | bytes 20512 | tf_op jit(solution)/shard_map/ppermute | solution.py:566
  39.9 0.0 collective-permute-start.9
  39.9 1.2 %collective-permute-done.9.refs_1_ = f32[80,128]{1,0:T(8,128)S(1)} collective-permute-done((f32[80,128]{1,0:T(8,128)S(1)}, f32[80,128]{1,0:T(8,128)S(1)}, u32[]{:S(2)}, u32[]{:S(2)}) %collective-permute-start.9) | collective-permute-done | bytes 40992 | tf_op jit(solution)/shard_map/ppermute | solution.py:566
  41.1 3.0 %shard_map.125 = (f32[4,128]{1,0:T(4,128)}, f32[4,128]{1,0:T(4,128)}, f32[4,64]{1,0:T(4,128)}, f32[4,64]{1,0:T(4,128)}) custom-call(f32[64,128]{1,0:T(8,128)S(1)} %get-tuple-element.49.prior_ref, f32[80,128]{1,0:T(8,128)S(1)} %pad_maximum_fusion.refs_0_, f32[80,128]{1,0:T(8,128)S(1)} %collective-permute-done.9.refs_1_), custom_call_target="tpu_custom_call" | custom-call | tf_op jit(solution)/shard_map/pallas_call | solution.py:554
  (8 shorter events, 0.0 us)
Async XLA Ops:
  1.3 1.0 %copy-start = (f32[1,64,128]{2,1,0:T(8,128)S(1)}, f32[1,64,128]{2,1,0:T(8,128)}, u32[]{:S(2)}) copy-start(f32[1,64,128]{2,1,0:T(8,128)} %param.11) | copy-start | bytes 98308
  2.2 0.7 %copy-start.1 = (f32[1,128]{1,0:T(1,128)S(1)}, f32[1,128]{1,0:T(1,128)}, u32[]{:S(2)}) copy-start(f32[1,128]{1,0:T(1,128)} %param.12) | copy-start | bytes 1540
  2.9 6.2 %copy-start.5 = (f32[4]{0:T(128)S(1)}, f32[4]{0:T(128)}, u32[]{:S(2)}) copy-start(f32[4]{0:T(128)} %param.16) | copy-start | bytes 52
  3.0 6.1 %copy-start.2 = (f32[64]{0:T(128)S(1)}, f32[64]{0:T(128)}, u32[]{:S(2)}) copy-start(f32[64]{0:T(128)} %param.14) | copy-start | bytes 772
  3.0 6.1 %copy-start.3 = (f32[64]{0:T(128)S(1)}, f32[64]{0:T(128)}, u32[]{:S(2)}) copy-start(f32[64]{0:T(128)} %param.13) | copy-start | bytes 772
  3.0 6.1 %copy-start.4 = (f32[4]{0:T(128)S(1)}, f32[4]{0:T(128)}, u32[]{:S(2)}) copy-start(f32[4]{0:T(128)} %param.15) | copy-start | bytes 52
  3.1 6.1 %collective-permute-start.1 = (f32[208,128]{1,0:T(8,128)S(1)}, f32[208,128]{1,0:T(8,128)S(1)}, u32[]{:S(2)}, u32[]{:S(2)}) collective-permute-start(f32[208,128]{1,0:T(8,128)S(1)} %concatenate.14.own_ref), channel_id=1, source_target_pairs={{0,8},{4,12},{8,0},{12,4},{16,24},{20,28},{24,16},{28,20},{1,9},{5... | collective-permute-start | bytes 319496 | tf_op jit(solution)/shard_map/ppermute | solution.py:566
  6.1 3.1 %collective-permute-start = (f32[208,128]{1,0:T(8,128)S(1)}, f32[208,128]{1,0:T(8,128)S(1)}, u32[]{:S(2)}, u32[]{:S(2)}) collective-permute-start(f32[208,128]{1,0:T(8,128)S(1)} %concatenate.14.own_ref), channel_id=1, source_target_pairs={{0,4},{4,0},{8,12},{12,8},{16,20},{20,16},{24,28},{28,24},{1,5},{5... | collective-permute-start | bytes 319496 | tf_op jit(solution)/shard_map/ppermute | solution.py:566
  9.1 1.3 %collective-permute-start.2 = (f32[208,128]{1,0:T(8,128)S(1)}, f32[208,128]{1,0:T(8,128)S(1)}, u32[]{:S(2)}, u32[]{:S(2)}) collective-permute-start(f32[208,128]{1,0:T(8,128)S(1)} %collective-permute-done.1.two_ref), channel_id=1, source_target_pairs={{0,4},{4,0},{8,12},{12,8},{16,20},{20,16},{24,28},{28,24},{1,5},{5... | collective-permute-start | bytes 319496 | tf_op jit(solution)/shard_map/ppermute | solution.py:566
  15.5 7.1 %collective-permute-start.3 = (f32[152,128]{1,0:T(8,128)S(1)}, f32[152,128]{1,0:T(8,128)S(1)}, u32[]{:S(2)}, u32[]{:S(2)}) collective-permute-start(f32[152,128]{1,0:T(8,128)S(1)} %get-tuple-element.50), channel_id=1, source_target_pairs={{0,16},{4,20},{8,24},{12,28},{1,17},{5,21},{9,25},{13,29},{2,18},{... | collective-permute-start | bytes 233480 | tf_op jit(solution)/shard_map/ppermute | solution.py:627
  23.0 5.3 %collective-permute-start.4 = (f32[32,128]{1,0:T(8,128)S(1)}, f32[32,128]{1,0:T(8,128)S(1)}, u32[]{:S(2)}, u32[]{:S(2)}) collective-permute-start(f32[32,128]{1,0:T(8,128)S(1)} %get-tuple-element.60), channel_id=1, source_target_pairs={{0,16},{4,20},{8,24},{12,28},{16,0},{20,4},{24,8},{28,12},{1,17},{... | collective-permute-start | bytes 49160 | tf_op jit(solution)/shard_map/ppermute | solution.py:566
  28.3 4.7 %collective-permute-start.7 = (f32[32,128]{1,0:T(8,128)S(1)}, f32[32,128]{1,0:T(8,128)S(1)}, u32[]{:S(2)}, u32[]{:S(2)}) collective-permute-start(f32[32,128]{1,0:T(8,128)S(1)} %add.12), channel_id=1, source_target_pairs={{0,3},{1,2},{2,1},{3,0},{4,7},{5,6},{6,5},{7,4},{8,11},{9,10},{10,... | collective-permute-start | bytes 49160 | tf_op jit(solution)/shard_map/ppermute | solution.py:566
  30.7 3.7 %collective-permute-start.6 = (f32[32,128]{1,0:T(8,128)S(1)}, f32[32,128]{1,0:T(8,128)S(1)}, u32[]{:S(2)}, u32[]{:S(2)}) collective-permute-start(f32[32,128]{1,0:T(8,128)S(1)} %add.12), channel_id=1, source_target_pairs={{0,2},{1,3},{2,0},{3,1},{4,6},{5,7},{6,4},{7,5},{8,10},{9,11},{10,... | collective-permute-start | bytes 49160 | tf_op jit(solution)/shard_map/ppermute | solution.py:566
  31.2 3.7 %collective-permute-start.5 = (f32[32,128]{1,0:T(8,128)S(1)}, f32[32,128]{1,0:T(8,128)S(1)}, u32[]{:S(2)}, u32[]{:S(2)}) collective-permute-start(f32[32,128]{1,0:T(8,128)S(1)} %add.12), channel_id=1, source_target_pairs={{0,1},{1,0},{2,3},{3,2},{4,5},{5,4},{6,7},{7,6},{8,9},{9,8},{10,11... | collective-permute-start | bytes 49160 | tf_op jit(solution)/shard_map/ppermute | solution.py:566
  35.0 4.9 %collective-permute-start.8 = (f32[40,128]{1,0:T(8,128)S(1)}, f32[40,128]{1,0:T(8,128)S(1)}, u32[]{:S(2)}, u32[]{:S(2)}) collective-permute-start(f32[40,128]{1,0:T(8,128)S(1)} %pad_maximum_fusion.1), channel_id=1, source_target_pairs={{0,8},{4,12},{8,0},{12,4},{16,24},{20,28},{24,16},{28,20},{1,9},{5... | collective-permute-start | bytes 61448 | tf_op jit(solution)/shard_map/ppermute | solution.py:566
  39.9 1.2 %collective-permute-start.9 = (f32[80,128]{1,0:T(8,128)S(1)}, f32[80,128]{1,0:T(8,128)S(1)}, u32[]{:S(2)}, u32[]{:S(2)}) collective-permute-start(f32[80,128]{1,0:T(8,128)S(1)} %pad_maximum_fusion.refs_0_), channel_id=1, source_target_pairs={{0,4},{4,0},{8,12},{12,8},{16,20},{20,16},{24,28},{28,24},{1,5},{5... | collective-permute-start | bytes 122888 | tf_op jit(solution)/shard_map/ppermute | solution.py:566

commit v18 on v17

--- a/solution.py
+++ b/solution.py
@@ -614,7 +614,7 @@
         (square, square, square, band, band, packed_state, (tip, tile)),
         ((GROUP,) + raw.shape, *pair),
     )
-    half = SUB * tile // 2
+    half = SUB * tile // 2 + SUB
     outs = ((tile, tile),) * 3 + ((side, tile),) * 2 + ((tile, tile), (side, tile), (tip, tile))
     early = call(
         functools.partial(early_kernel, tip, groups - GROUP),
@@ -660,7 +660,7 @@
         tip_kernel,
         (prior, found, crossed(found, "tm", 1)),
         ((GROUP, tile), (GROUP, tile), (GROUP, tip), (GROUP, tip)),
-        ((GROUP, found.shape[0] // 2, tile), (SUB * tip, tile)),
+        ((GROUP, found.shape[0] // 2, tile), (SUB * tip + SUB, tile)),
     )
     return (log_diag[:, None, :], solved[:, None, :], tip_log, tip_forward)
 

time: 44.3 us -> 44.3 us (level)
  no operation moved by 1% of the time
where the time goes in v18:
time: 44.3 us; the launch traced here: 44.1 us
  starting transfers between devices  16.3 us (37%)
  Pallas kernels  12.5 us (28%)
  waiting for transfers between devices  12.1 us (27%)
  between operations  1.42 us (3%)
  other arithmetic  0.93 us (2%)
  local copies, waits for them, and re-layouts  0.88 us (2%)
    ppermute x9, starting transfers between devices, crossed(): lax.ppermute(value, axis, [(source, source ^ step) for source in range(si...  13.3 us
    pallas_call x6, Pallas kernels, call(): pl.pallas_call(body, out_shape=tuple((jax.ShapeDtypeStruct(shape, F32) fo...  12.5 us
    ppermute x9, waiting for transfers between devices, crossed(): lax.ppermute(value, axis, [(source, source ^ step) for source in range(si...  12.1 us
    ppermute x1, starting transfers between devices, shards(): lax.ppermute(state, 'tm', [(source, source + GROUP) for source in range(g...  2.98 us
    reduce_sum x1, other arithmetic, shards(): jnp.sum(jnp.where(row == col, coupling[0], 0.0), axis=0, keepdims=True)  0.91 us
  transfers between devices with their start and end apart: 10, of which 8 were waited for; matrix products, arithmetic and copies ran while one was open for 0% of the time, Pallas kernels for 9%

profile of v18, /device:TPU:0, one launch (start us, length us, event | category | flops | bytes accessed | tf_op | source)
XLA Modules:
  0.0 44.1 jit_solution(2756692244925842637)
XLA Ops:
  1.3 0.0 copy-start
  1.3 0.9 %fusion = (f32[128]{0:T(128)S(1)}, f32[128,128]{1,0:T(8,128)S(1)}) fusion(f32[1,128,128]{2,1,0:T(8,128)} %param.10, f32[1,128,128]{2,1,0:T(8,128)} %param.9), kind=kLoop, calls=%fused_computation.2 | loop fusion | flops 81792 | bytes 197120 | tf_op jit(solution)/shard_map/reduce_sum | solution.py:599
  2.2 0.0 copy-start.1
  2.2 0.0 copy-done
  2.2 0.6 %copy-done.1 = f32[1,128]{1,0:T(1,128)S(1)} copy-done((f32[1,128]{1,0:T(1,128)S(1)}, f32[1,128]{1,0:T(1,128)}, u32[]{:S(2)}) %copy-start.1) | copy-done | bytes 536
  2.9 0.0 copy-start.5
  2.9 0.1 concatenate.14.own_ref
  3.0 0.0 copy-start.2
  3.0 0.0 copy-start.3
  3.0 0.0 copy-start.4
  3.1 3.1 %collective-permute-start.1 = (f32[208,128]{1,0:T(8,128)S(1)}, f32[208,128]{1,0:T(8,128)S(1)}, u32[]{:S(2)}, u32[]{:S(2)}) collective-permute-start(f32[208,128]{1,0:T(8,128)S(1)} %concatenate.14.own_ref), channel_id=1, source_target_pairs={{0,8},{4,12},{8,0},{12,4},{16,24},{20,28},{24,16},{28,20},{1,9},{5... | collective-permute-start | bytes 319496 | tf_op jit(solution)/shard_map/ppermute | solution.py:566
  6.1 0.0 collective-permute-start
  6.1 3.0 %collective-permute-done.1.two_ref = f32[208,128]{1,0:T(8,128)S(1)} collective-permute-done((f32[208,128]{1,0:T(8,128)S(1)}, f32[208,128]{1,0:T(8,128)S(1)}, u32[]{:S(2)}, u32[]{:S(2)}) %collective-permute-start.1) | collective-permute-done | bytes 106528 | tf_op jit(solution)/shard_map/ppermute | solution.py:566
  9.1 0.0 collective-permute-start.2
  9.1 0.0 copy-done.5
  9.1 0.0 copy-done.2
  9.1 0.0 copy-done.3
  9.1 0.0 copy-done.4
  9.2 0.1 concatenate.13
  9.2 0.0 collective-permute-done.one_ref
  9.2 1.2 %collective-permute-done.2.three_ref = f32[208,128]{1,0:T(8,128)S(1)} collective-permute-done((f32[208,128]{1,0:T(8,128)S(1)}, f32[208,128]{1,0:T(8,128)S(1)}, u32[]{:S(2)}, u32[]{:S(2)}) %collective-permute-start.2) | collective-permute-done | bytes 106528 | tf_op jit(solution)/shard_map/ppermute | solution.py:566
  10.4 3.4 %shard_map.120 = (f32[4,128,128]{2,1,0:T(8,128)S(1)}, f32[4,128,128]{2,1,0:T(8,128)S(1)}, f32[4,128,128]{2,1,0:T(8,128)S(1)}, f32[4,80,128]{2,1,0:T(8,128)S(1)},...) custom-call(f32[2,128]{1,0:T(2,128)S(1)} %bitcast.17, ...), custom_call_target="tpu_custom_call" | custom-call | tf_op jit(solution)/shard_map/pallas_call | solution.py:554
  13.8 1.7 %shard_map.121 = (f32[128,128]{1,0:T(8,128)S(1)}, f32[80,128]{1,0:T(8,128)S(1)}, f32[64,128]{1,0:T(8,128)S(1)}) custom-call(f32[4,128,128]{2,1,0:T(8,128)S(1)} %get-tuple-element.37.refs_0_, f32[4,128,128]{2,1,0:T(8,128)S(1)} %get-tuple-element.38.refs_1_, f32[4,128,128]{2,1,0:T(8,128)S(1)} %get-tuple-element.39.refs_2_, ...), custom_call_target="tpu_custom_call" | custom-call | tf_op jit(solution)/shard_map/pallas_call | solution.py:554
  15.5 3.0 %collective-permute-start.3 = (f32[152,128]{1,0:T(8,128)S(1)}, f32[152,128]{1,0:T(8,128)S(1)}, u32[]{:S(2)}, u32[]{:S(2)}) collective-permute-start(f32[152,128]{1,0:T(8,128)S(1)} %get-tuple-element.50), channel_id=1, source_target_pairs={{0,16},{4,20},{8,24},{12,28},{1,17},{5,21},{9,25},{13,29},{2,18},{... | collective-permute-start | bytes 233480 | tf_op jit(solution)/shard_map/ppermute | solution.py:627
  18.5 4.1 %shard_map.122 = (f32[128,128]{1,0:T(8,128)S(1)}, f32[128,128]{1,0:T(8,128)S(1)}, f32[128,128]{1,0:T(8,128)S(1)}, f32[80,128]{1,0:T(8,128)S(1)}, f32[80,128]{1,0...) custom-call(f32[2,128]{1,0:T(2,128)S(1)} %bitcast.18, ...), custom_call_target="tpu_custom_call" | custom-call | tf_op jit(solution)/shard_map/pallas_call | solution.py:554
  22.6 0.0 collective-permute-done.3.state_ref
  22.6 0.4 shard_map.123
  23.0 3.6 %collective-permute-start.4 = (f32[32,128]{1,0:T(8,128)S(1)}, f32[32,128]{1,0:T(8,128)S(1)}, u32[]{:S(2)}, u32[]{:S(2)}) collective-permute-start(f32[32,128]{1,0:T(8,128)S(1)} %get-tuple-element.60), channel_id=1, source_target_pairs={{0,16},{4,20},{8,24},{12,28},{16,0},{20,4},{24,8},{28,12},{1,17},{... | collective-permute-start | bytes 49160 | tf_op jit(solution)/shard_map/ppermute | solution.py:566
  26.6 1.7 %collective-permute-done.4 = f32[32,128]{1,0:T(8,128)S(1)} collective-permute-done((f32[32,128]{1,0:T(8,128)S(1)}, f32[32,128]{1,0:T(8,128)S(1)}, u32[]{:S(2)}, u32[]{:S(2)}) %collective-permute-start.4) | collective-permute-done | bytes 16416 | tf_op jit(solution)/shard_map/ppermute | solution.py:566
  28.3 2.5 %collective-permute-start.7 = (f32[32,128]{1,0:T(8,128)S(1)}, f32[32,128]{1,0:T(8,128)S(1)}, u32[]{:S(2)}, u32[]{:S(2)}) collective-permute-start(f32[32,128]{1,0:T(8,128)S(1)} %add.12), channel_id=1, source_target_pairs={{0,3},{1,2},{2,1},{3,0},{4,7},{5,6},{6,5},{7,4},{8,11},{9,10},{10,... | collective-permute-start | bytes 49160 | tf_op jit(solution)/shard_map/ppermute | solution.py:566
  30.7 0.5 %collective-permute-start.6 = (f32[32,128]{1,0:T(8,128)S(1)}, f32[32,128]{1,0:T(8,128)S(1)}, u32[]{:S(2)}, u32[]{:S(2)}) collective-permute-start(f32[32,128]{1,0:T(8,128)S(1)} %add.12), channel_id=1, source_target_pairs={{0,2},{1,3},{2,0},{3,1},{4,6},{5,7},{6,4},{7,5},{8,10},{9,11},{10,... | collective-permute-start | bytes 49160 | tf_op jit(solution)/shard_map/ppermute | solution.py:566
  31.2 0.5 %collective-permute-start.5 = (f32[32,128]{1,0:T(8,128)S(1)}, f32[32,128]{1,0:T(8,128)S(1)}, u32[]{:S(2)}, u32[]{:S(2)}) collective-permute-start(f32[32,128]{1,0:T(8,128)S(1)} %add.12), channel_id=1, source_target_pairs={{0,1},{1,0},{2,3},{3,2},{4,5},{5,4},{6,7},{7,6},{8,9},{9,8},{10,11... | collective-permute-start | bytes 49160 | tf_op jit(solution)/shard_map/ppermute | solution.py:566
  31.8 1.2 %collective-permute-done.7 = f32[32,128]{1,0:T(8,128)S(1)} collective-permute-done((f32[32,128]{1,0:T(8,128)S(1)}, f32[32,128]{1,0:T(8,128)S(1)}, u32[]{:S(2)}, u32[]{:S(2)}) %collective-permute-start.7) | collective-permute-done | bytes 16416 | tf_op jit(solution)/shard_map/ppermute | solution.py:566
  32.9 1.5 %collective-permute-done.6 = f32[32,128]{1,0:T(8,128)S(1)} collective-permute-done((f32[32,128]{1,0:T(8,128)S(1)}, f32[32,128]{1,0:T(8,128)S(1)}, u32[]{:S(2)}, u32[]{:S(2)}) %collective-permute-start.6) | collective-permute-done | bytes 16416 | tf_op jit(solution)/shard_map/ppermute | solution.py:566
  34.5 0.5 %collective-permute-done.5 = f32[32,128]{1,0:T(8,128)S(1)} collective-permute-done((f32[32,128]{1,0:T(8,128)S(1)}, f32[32,128]{1,0:T(8,128)S(1)}, u32[]{:S(2)}, u32[]{:S(2)}) %collective-permute-start.5) | collective-permute-done | bytes 16416 | tf_op jit(solution)/shard_map/ppermute | solution.py:566
  35.0 3.1 %collective-permute-start.8 = (f32[40,128]{1,0:T(8,128)S(1)}, f32[40,128]{1,0:T(8,128)S(1)}, u32[]{:S(2)}, u32[]{:S(2)}) collective-permute-start(f32[40,128]{1,0:T(8,128)S(1)} %pad_maximum_fusion.1), channel_id=1, source_target_pairs={{0,8},{4,12},{8,0},{12,4},{16,24},{20,28},{24,16},{28,20},{1,9},{5... | collective-permute-start | bytes 61448 | tf_op jit(solution)/shard_map/ppermute | solution.py:566
  38.1 1.8 %collective-permute-done.8 = f32[40,128]{1,0:T(8,128)S(1)} collective-permute-done((f32[40,128]{1,0:T(8,128)S(1)}, f32[40,128]{1,0:T(8,128)S(1)}, u32[]{:S(2)}, u32[]{:S(2)}) %collective-permute-start.8) | collective-permute-done | bytes 20512 | tf_op jit(solution)/shard_map/ppermute | solution.py:566
  39.9 0.0 collective-permute-start.9
  39.9 1.2 %collective-permute-done.9.refs_1_ = f32[80,128]{1,0:T(8,128)S(1)} collective-permute-done((f32[80,128]{1,0:T(8,128)S(1)}, f32[80,128]{1,0:T(8,128)S(1)}, u32[]{:S(2)}, u32[]{:S(2)}) %collective-permute-start.9) | collective-permute-done | bytes 40992 | tf_op jit(solution)/shard_map/ppermute | solution.py:566
  41.1 3.0 %shard_map.125 = (f32[4,128]{1,0:T(4,128)}, f32[4,128]{1,0:T(4,128)}, f32[4,64]{1,0:T(4,128)}, f32[4,64]{1,0:T(4,128)}) custom-call(f32[64,128]{1,0:T(8,128)S(1)} %get-tuple-element.49.prior_ref, f32[80,128]{1,0:T(8,128)S(1)} %pad_maximum_fusion.refs_0_, f32[80,128]{1,0:T(8,128)S(1)} %collective-permute-done.9.refs_1_), custom_call_target="tpu_custom_call" | custom-call | tf_op jit(solution)/shard_map/pallas_call | solution.py:554
  (8 shorter events, 0.0 us)
Async XLA Ops:
  1.3 1.0 %copy-start = (f32[1,64,128]{2,1,0:T(8,128)S(1)}, f32[1,64,128]{2,1,0:T(8,128)}, u32[]{:S(2)}) copy-start(f32[1,64,128]{2,1,0:T(8,128)} %param.11) | copy-start | bytes 98308
  2.2 0.7 %copy-start.1 = (f32[1,128]{1,0:T(1,128)S(1)}, f32[1,128]{1,0:T(1,128)}, u32[]{:S(2)}) copy-start(f32[1,128]{1,0:T(1,128)} %param.12) | copy-start | bytes 1540
  2.9 6.2 %copy-start.5 = (f32[4]{0:T(128)S(1)}, f32[4]{0:T(128)}, u32[]{:S(2)}) copy-start(f32[4]{0:T(128)} %param.16) | copy-start | bytes 52
  3.0 6.1 %copy-start.2 = (f32[64]{0:T(128)S(1)}, f32[64]{0:T(128)}, u32[]{:S(2)}) copy-start(f32[64]{0:T(128)} %param.14) | copy-start | bytes 772
  3.0 6.1 %copy-start.3 = (f32[64]{0:T(128)S(1)}, f32[64]{0:T(128)}, u32[]{:S(2)}) copy-start(f32[64]{0:T(128)} %param.13) | copy-start | bytes 772
  3.0 6.1 %copy-start.4 = (f32[4]{0:T(128)S(1)}, f32[4]{0:T(128)}, u32[]{:S(2)}) copy-start(f32[4]{0:T(128)} %param.15) | copy-start | bytes 52
  3.1 6.1 %collective-permute-start.1 = (f32[208,128]{1,0:T(8,128)S(1)}, f32[208,128]{1,0:T(8,128)S(1)}, u32[]{:S(2)}, u32[]{:S(2)}) collective-permute-start(f32[208,128]{1,0:T(8,128)S(1)} %concatenate.14.own_ref), channel_id=1, source_target_pairs={{0,8},{4,12},{8,0},{12,4},{16,24},{20,28},{24,16},{28,20},{1,9},{5... | collective-permute-start | bytes 319496 | tf_op jit(solution)/shard_map/ppermute | solution.py:566
  6.1 3.1 %collective-permute-start = (f32[208,128]{1,0:T(8,128)S(1)}, f32[208,128]{1,0:T(8,128)S(1)}, u32[]{:S(2)}, u32[]{:S(2)}) collective-permute-start(f32[208,128]{1,0:T(8,128)S(1)} %concatenate.14.own_ref), channel_id=1, source_target_pairs={{0,4},{4,0},{8,12},{12,8},{16,20},{20,16},{24,28},{28,24},{1,5},{5... | collective-permute-start | bytes 319496 | tf_op jit(solution)/shard_map/ppermute | solution.py:566
  9.1 1.3 %collective-permute-start.2 = (f32[208,128]{1,0:T(8,128)S(1)}, f32[208,128]{1,0:T(8,128)S(1)}, u32[]{:S(2)}, u32[]{:S(2)}) collective-permute-start(f32[208,128]{1,0:T(8,128)S(1)} %collective-permute-done.1.two_ref), channel_id=1, source_target_pairs={{0,4},{4,0},{8,12},{12,8},{16,20},{20,16},{24,28},{28,24},{1,5},{5... | collective-permute-start | bytes 319496 | tf_op jit(solution)/shard_map/ppermute | solution.py:566
  15.5 7.1 %collective-permute-start.3 = (f32[152,128]{1,0:T(8,128)S(1)}, f32[152,128]{1,0:T(8,128)S(1)}, u32[]{:S(2)}, u32[]{:S(2)}) collective-permute-start(f32[152,128]{1,0:T(8,128)S(1)} %get-tuple-element.50), channel_id=1, source_target_pairs={{0,16},{4,20},{8,24},{12,28},{1,17},{5,21},{9,25},{13,29},{2,18},{... | collective-permute-start | bytes 233480 | tf_op jit(solution)/shard_map/ppermute | solution.py:627
  23.0 5.3 %collective-permute-start.4 = (f32[32,128]{1,0:T(8,128)S(1)}, f32[32,128]{1,0:T(8,128)S(1)}, u32[]{:S(2)}, u32[]{:S(2)}) collective-permute-start(f32[32,128]{1,0:T(8,128)S(1)} %get-tuple-element.60), channel_id=1, source_target_pairs={{0,16},{4,20},{8,24},{12,28},{16,0},{20,4},{24,8},{28,12},{1,17},{... | collective-permute-start | bytes 49160 | tf_op jit(solution)/shard_map/ppermute | solution.py:566
  28.3 4.7 %collective-permute-start.7 = (f32[32,128]{1,0:T(8,128)S(1)}, f32[32,128]{1,0:T(8,128)S(1)}, u32[]{:S(2)}, u32[]{:S(2)}) collective-permute-start(f32[32,128]{1,0:T(8,128)S(1)} %add.12), channel_id=1, source_target_pairs={{0,3},{1,2},{2,1},{3,0},{4,7},{5,6},{6,5},{7,4},{8,11},{9,10},{10,... | collective-permute-start | bytes 49160 | tf_op jit(solution)/shard_map/ppermute | solution.py:566
  30.7 3.7 %collective-permute-start.6 = (f32[32,128]{1,0:T(8,128)S(1)}, f32[32,128]{1,0:T(8,128)S(1)}, u32[]{:S(2)}, u32[]{:S(2)}) collective-permute-start(f32[32,128]{1,0:T(8,128)S(1)} %add.12), channel_id=1, source_target_pairs={{0,2},{1,3},{2,0},{3,1},{4,6},{5,7},{6,4},{7,5},{8,10},{9,11},{10,... | collective-permute-start | bytes 49160 | tf_op jit(solution)/shard_map/ppermute | solution.py:566
  31.2 3.7 %collective-permute-start.5 = (f32[32,128]{1,0:T(8,128)S(1)}, f32[32,128]{1,0:T(8,128)S(1)}, u32[]{:S(2)}, u32[]{:S(2)}) collective-permute-start(f32[32,128]{1,0:T(8,128)S(1)} %add.12), channel_id=1, source_target_pairs={{0,1},{1,0},{2,3},{3,2},{4,5},{5,4},{6,7},{7,6},{8,9},{9,8},{10,11... | collective-permute-start | bytes 49160 | tf_op jit(solution)/shard_map/ppermute | solution.py:566
  35.0 4.9 %collective-permute-start.8 = (f32[40,128]{1,0:T(8,128)S(1)}, f32[40,128]{1,0:T(8,128)S(1)}, u32[]{:S(2)}, u32[]{:S(2)}) collective-permute-start(f32[40,128]{1,0:T(8,128)S(1)} %pad_maximum_fusion.1), channel_id=1, source_target_pairs={{0,8},{4,12},{8,0},{12,4},{16,24},{20,28},{24,16},{28,20},{1,9},{5... | collective-permute-start | bytes 61448 | tf_op jit(solution)/shard_map/ppermute | solution.py:566
  39.9 1.2 %collective-permute-start.9 = (f32[80,128]{1,0:T(8,128)S(1)}, f32[80,128]{1,0:T(8,128)S(1)}, u32[]{:S(2)}, u32[]{:S(2)}) collective-permute-start(f32[80,128]{1,0:T(8,128)S(1)} %pad_maximum_fusion.refs_0_), channel_id=1, source_target_pairs={{0,4},{4,0},{8,12},{12,8},{16,20},{20,16},{24,28},{28,24},{1,5},{5... | collective-permute-start | bytes 122888 | tf_op jit(solution)/shard_map/ppermute | solution.py:566

commit v19 on v18

--- a/solution.py
+++ b/solution.py
@@ -130,7 +130,7 @@
     inv_ref,
 ):
     tile = own_ref.shape[1]
-    side = own_ref.shape[0] - tile
+    side = own_ref.shape[0] - tile + SUB
     spare = tile + tip + 1
     setting = lax.axis_index("tm") & (GROUP - 1)
     lane = lax.broadcasted_iota(jnp.int32, (1, tile), 1)
@@ -152,7 +152,8 @@
         diag.append(jnp.where(row >= col, both, turned) + shift * eye)
         tie = jnp.where(row < col, both, jnp.where(row > col, turned, middle))
         cross.append(tie * (couple * active))
-        right.append(jnp.where(used, raw_ref[n, tile:, :], 0.0))
+        ends = jnp.concatenate([raw_ref[n, tile:, :], jnp.zeros((SUB, tile), F32)], axis=0)
+        right.append(jnp.where(used, ends, 0.0))
     one, two, end = slice(0, tile), slice(tile, 2 * tile), slice(2 * tile, None)
 
     def share(first, middle):
@@ -598,7 +599,7 @@
             rhs,
             jnp.sum(jnp.where(row == col, coupling[0], 0.0), axis=0, keepdims=True),
             jnp.full((1, tile), active),
-            jnp.zeros((2 * SUB - 3, tile), F32),
+            jnp.zeros((SUB - 3, tile), F32),
         ],
         axis=0,
     )

time: 44.3 us -> 44.1 us (level)
  no operation moved by 1% of the time
where the time goes in v19:
time: 44.1 us; the launch traced here: 43.9 us
  starting transfers between devices  16.3 us (37%)
  Pallas kernels  12.5 us (28%)
  waiting for transfers between devices  12 us (27%)
  between operations  1.4 us (3%)
  other arithmetic  0.93 us (2%)
  local copies, waits for them, and re-layouts  0.77 us (2%)
    ppermute x9, starting transfers between devices, crossed(): lax.ppermute(value, axis, [(source, source ^ step) for source in range(si...  13.3 us
    pallas_call x6, Pallas kernels, call(): pl.pallas_call(body, out_shape=tuple((jax.ShapeDtypeStruct(shape, F32) fo...  12.5 us
    ppermute x9, waiting for transfers between devices, crossed(): lax.ppermute(value, axis, [(source, source ^ step) for source in range(si...  12 us
    ppermute x1, starting transfers between devices, shards(): lax.ppermute(state, 'tm', [(source, source + GROUP) for source in range(g...  3.02 us
    reduce_sum x1, other arithmetic, shards(): jnp.sum(jnp.where(row == col, coupling[0], 0.0), axis=0, keepdims=True)  0.91 us
  transfers between devices with their start and end apart: 10, of which 8 were waited for; matrix products, arithmetic and copies ran while one was open for 0% of the time, Pallas kernels for 9%

profile of v19, /device:TPU:0, one launch (start us, length us, event | category | flops | bytes accessed | tf_op | source)
XLA Modules:
  0.0 43.9 jit_solution(2733985933327243451)
XLA Ops:
  1.3 0.0 copy-start
  1.3 0.9 %fusion = (f32[128]{0:T(128)S(1)}, f32[128,128]{1,0:T(8,128)S(1)}) fusion(f32[1,128,128]{2,1,0:T(8,128)} %param.10, f32[1,128,128]{2,1,0:T(8,128)} %param.9), kind=kLoop, calls=%fused_computation.2 | loop fusion | flops 81792 | bytes 197120 | tf_op jit(solution)/shard_map/reduce_sum | solution.py:600
  2.2 0.0 copy-start.1
  2.2 0.0 copy-done
  2.2 0.6 %copy-done.1 = f32[1,128]{1,0:T(1,128)S(1)} copy-done((f32[1,128]{1,0:T(1,128)S(1)}, f32[1,128]{1,0:T(1,128)}, u32[]{:S(2)}) %copy-start.1) | copy-done | bytes 536
  2.9 0.0 copy-start.5
  2.9 0.0 copy-start.2
  2.9 0.0 copy-start.3
  2.9 0.0 copy-start.4
  2.9 3.1 %collective-permute-start.1 = (f32[200,128]{1,0:T(8,128)S(1)}, f32[200,128]{1,0:T(8,128)S(1)}, u32[]{:S(2)}, u32[]{:S(2)}) collective-permute-start(f32[200,128]{1,0:T(8,128)S(1)} %concatenate.14.own_ref), channel_id=1, source_target_pairs={{0,8},{4,12},{8,0},{12,4},{16,24},{20,28},{24,16},{28,20},{1,9},{5... | collective-permute-start | bytes 307208 | tf_op jit(solution)/shard_map/ppermute | solution.py:567
  6.0 0.0 collective-permute-start
  6.0 2.9 %collective-permute-done.1.two_ref = f32[200,128]{1,0:T(8,128)S(1)} collective-permute-done((f32[200,128]{1,0:T(8,128)S(1)}, f32[200,128]{1,0:T(8,128)S(1)}, u32[]{:S(2)}, u32[]{:S(2)}) %collective-permute-start.1) | collective-permute-done | bytes 102432 | tf_op jit(solution)/shard_map/ppermute | solution.py:567
  8.9 0.0 collective-permute-start.2
  8.9 0.0 copy-done.5
  8.9 0.0 copy-done.2
  8.9 0.0 copy-done.3
  8.9 0.0 copy-done.4
  8.9 0.1 concatenate.13
  9.0 0.0 collective-permute-done.one_ref
  9.0 1.2 %collective-permute-done.2.three_ref = f32[200,128]{1,0:T(8,128)S(1)} collective-permute-done((f32[200,128]{1,0:T(8,128)S(1)}, f32[200,128]{1,0:T(8,128)S(1)}, u32[]{:S(2)}, u32[]{:S(2)}) %collective-permute-start.2) | collective-permute-done | bytes 102432 | tf_op jit(solution)/shard_map/ppermute | solution.py:567
  10.2 3.4 %shard_map.120 = (f32[4,128,128]{2,1,0:T(8,128)S(1)}, f32[4,128,128]{2,1,0:T(8,128)S(1)}, f32[4,128,128]{2,1,0:T(8,128)S(1)}, f32[4,80,128]{2,1,0:T(8,128)S(1)},...) custom-call(f32[2,128]{1,0:T(2,128)S(1)} %bitcast.17, ...), custom_call_target="tpu_custom_call" | custom-call | tf_op jit(solution)/shard_map/pallas_call | solution.py:555
  13.6 1.7 %shard_map.121 = (f32[128,128]{1,0:T(8,128)S(1)}, f32[80,128]{1,0:T(8,128)S(1)}, f32[64,128]{1,0:T(8,128)S(1)}) custom-call(f32[4,128,128]{2,1,0:T(8,128)S(1)} %get-tuple-element.37.refs_0_, f32[4,128,128]{2,1,0:T(8,128)S(1)} %get-tuple-element.38.refs_1_, f32[4,128,128]{2,1,0:T(8,128)S(1)} %get-tuple-element.39.refs_2_, ...), custom_call_target="tpu_custom_call" | custom-call | tf_op jit(solution)/shard_map/pallas_call | solution.py:555
  15.3 3.0 %collective-permute-start.3 = (f32[152,128]{1,0:T(8,128)S(1)}, f32[152,128]{1,0:T(8,128)S(1)}, u32[]{:S(2)}, u32[]{:S(2)}) collective-permute-start(f32[152,128]{1,0:T(8,128)S(1)} %get-tuple-element.50), channel_id=1, source_target_pairs={{0,16},{4,20},{8,24},{12,28},{1,17},{5,21},{9,25},{13,29},{2,18},{... | collective-permute-start | bytes 233480 | tf_op jit(solution)/shard_map/ppermute | solution.py:628
  18.3 4.1 %shard_map.122 = (f32[128,128]{1,0:T(8,128)S(1)}, f32[128,128]{1,0:T(8,128)S(1)}, f32[128,128]{1,0:T(8,128)S(1)}, f32[80,128]{1,0:T(8,128)S(1)}, f32[80,128]{1,0...) custom-call(f32[2,128]{1,0:T(2,128)S(1)} %bitcast.18, ...), custom_call_target="tpu_custom_call" | custom-call | tf_op jit(solution)/shard_map/pallas_call | solution.py:555
  22.4 0.0 collective-permute-done.3.state_ref
  22.4 0.4 shard_map.123
  22.8 3.6 %collective-permute-start.4 = (f32[32,128]{1,0:T(8,128)S(1)}, f32[32,128]{1,0:T(8,128)S(1)}, u32[]{:S(2)}, u32[]{:S(2)}) collective-permute-start(f32[32,128]{1,0:T(8,128)S(1)} %get-tuple-element.60), channel_id=1, source_target_pairs={{0,16},{4,20},{8,24},{12,28},{16,0},{20,4},{24,8},{28,12},{1,17},{... | collective-permute-start | bytes 49160 | tf_op jit(solution)/shard_map/ppermute | solution.py:567
  26.4 1.7 %collective-permute-done.4 = f32[32,128]{1,0:T(8,128)S(1)} collective-permute-done((f32[32,128]{1,0:T(8,128)S(1)}, f32[32,128]{1,0:T(8,128)S(1)}, u32[]{:S(2)}, u32[]{:S(2)}) %collective-permute-start.4) | collective-permute-done | bytes 16416 | tf_op jit(solution)/shard_map/ppermute | solution.py:567
  28.1 2.5 %collective-permute-start.7 = (f32[32,128]{1,0:T(8,128)S(1)}, f32[32,128]{1,0:T(8,128)S(1)}, u32[]{:S(2)}, u32[]{:S(2)}) collective-permute-start(f32[32,128]{1,0:T(8,128)S(1)} %add.12), channel_id=1, source_target_pairs={{0,3},{1,2},{2,1},{3,0},{4,7},{5,6},{6,5},{7,4},{8,11},{9,10},{10,... | collective-permute-start | bytes 49160 | tf_op jit(solution)/shard_map/ppermute | solution.py:567
  30.6 0.5 %collective-permute-start.6 = (f32[32,128]{1,0:T(8,128)S(1)}, f32[32,128]{1,0:T(8,128)S(1)}, u32[]{:S(2)}, u32[]{:S(2)}) collective-permute-start(f32[32,128]{1,0:T(8,128)S(1)} %add.12), channel_id=1, source_target_pairs={{0,2},{1,3},{2,0},{3,1},{4,6},{5,7},{6,4},{7,5},{8,10},{9,11},{10,... | collective-permute-start | bytes 49160 | tf_op jit(solution)/shard_map/ppermute | solution.py:567
  31.1 0.5 %collective-permute-start.5 = (f32[32,128]{1,0:T(8,128)S(1)}, f32[32,128]{1,0:T(8,128)S(1)}, u32[]{:S(2)}, u32[]{:S(2)}) collective-permute-start(f32[32,128]{1,0:T(8,128)S(1)} %add.12), channel_id=1, source_target_pairs={{0,1},{1,0},{2,3},{3,2},{4,5},{5,4},{6,7},{7,6},{8,9},{9,8},{10,11... | collective-permute-start | bytes 49160 | tf_op jit(solution)/shard_map/ppermute | solution.py:567
  31.6 1.2 %collective-permute-done.7 = f32[32,128]{1,0:T(8,128)S(1)} collective-permute-done((f32[32,128]{1,0:T(8,128)S(1)}, f32[32,128]{1,0:T(8,128)S(1)}, u32[]{:S(2)}, u32[]{:S(2)}) %collective-permute-start.7) | collective-permute-done | bytes 16416 | tf_op jit(solution)/shard_map/ppermute | solution.py:567
  32.8 1.5 %collective-permute-done.6 = f32[32,128]{1,0:T(8,128)S(1)} collective-permute-done((f32[32,128]{1,0:T(8,128)S(1)}, f32[32,128]{1,0:T(8,128)S(1)}, u32[]{:S(2)}, u32[]{:S(2)}) %collective-permute-start.6) | collective-permute-done | bytes 16416 | tf_op jit(solution)/shard_map/ppermute | solution.py:567
  34.3 0.5 %collective-permute-done.5 = f32[32,128]{1,0:T(8,128)S(1)} collective-permute-done((f32[32,128]{1,0:T(8,128)S(1)}, f32[32,128]{1,0:T(8,128)S(1)}, u32[]{:S(2)}, u32[]{:S(2)}) %collective-permute-start.5) | collective-permute-done | bytes 16416 | tf_op jit(solution)/shard_map/ppermute | solution.py:567
  34.8 3.1 %collective-permute-start.8 = (f32[40,128]{1,0:T(8,128)S(1)}, f32[40,128]{1,0:T(8,128)S(1)}, u32[]{:S(2)}, u32[]{:S(2)}) collective-permute-start(f32[40,128]{1,0:T(8,128)S(1)} %pad_maximum_fusion.1), channel_id=1, source_target_pairs={{0,8},{4,12},{8,0},{12,4},{16,24},{20,28},{24,16},{28,20},{1,9},{5... | collective-permute-start | bytes 61448 | tf_op jit(solution)/shard_map/ppermute | solution.py:567
  37.9 1.8 %collective-permute-done.8 = f32[40,128]{1,0:T(8,128)S(1)} collective-permute-done((f32[40,128]{1,0:T(8,128)S(1)}, f32[40,128]{1,0:T(8,128)S(1)}, u32[]{:S(2)}, u32[]{:S(2)}) %collective-permute-start.8) | collective-permute-done | bytes 20512 | tf_op jit(solution)/shard_map/ppermute | solution.py:567
  39.7 0.0 collective-permute-start.9
  39.7 1.2 %collective-permute-done.9.refs_1_ = f32[80,128]{1,0:T(8,128)S(1)} collective-permute-done((f32[80,128]{1,0:T(8,128)S(1)}, f32[80,128]{1,0:T(8,128)S(1)}, u32[]{:S(2)}, u32[]{:S(2)}) %collective-permute-start.9) | collective-permute-done | bytes 40992 | tf_op jit(solution)/shard_map/ppermute | solution.py:567
  40.9 3.0 %shard_map.125 = (f32[4,128]{1,0:T(4,128)}, f32[4,128]{1,0:T(4,128)}, f32[4,64]{1,0:T(4,128)}, f32[4,64]{1,0:T(4,128)}) custom-call(f32[64,128]{1,0:T(8,128)S(1)} %get-tuple-element.49.prior_ref, f32[80,128]{1,0:T(8,128)S(1)} %pad_maximum_fusion.refs_0_, f32[80,128]{1,0:T(8,128)S(1)} %collective-permute-done.9.refs_1_), custom_call_target="tpu_custom_call" | custom-call | tf_op jit(solution)/shard_map/pallas_call | solution.py:555
  (9 shorter events, 0.1 us)
Async XLA Ops:
  1.3 1.0 %copy-start = (f32[1,64,128]{2,1,0:T(8,128)S(1)}, f32[1,64,128]{2,1,0:T(8,128)}, u32[]{:S(2)}) copy-start(f32[1,64,128]{2,1,0:T(8,128)} %param.11) | copy-start | bytes 98308
  2.2 0.7 %copy-start.1 = (f32[1,128]{1,0:T(1,128)S(1)}, f32[1,128]{1,0:T(1,128)}, u32[]{:S(2)}) copy-start(f32[1,128]{1,0:T(1,128)} %param.12) | copy-start | bytes 1540
  2.9 6.0 %copy-start.5 = (f32[4]{0:T(128)S(1)}, f32[4]{0:T(128)}, u32[]{:S(2)}) copy-start(f32[4]{0:T(128)} %param.16) | copy-start | bytes 52
  2.9 6.0 %copy-start.2 = (f32[64]{0:T(128)S(1)}, f32[64]{0:T(128)}, u32[]{:S(2)}) copy-start(f32[64]{0:T(128)} %param.14) | copy-start | bytes 772
  2.9 6.0 %copy-start.3 = (f32[64]{0:T(128)S(1)}, f32[64]{0:T(128)}, u32[]{:S(2)}) copy-start(f32[64]{0:T(128)} %param.13) | copy-start | bytes 772
  2.9 6.0 %copy-start.4 = (f32[4]{0:T(128)S(1)}, f32[4]{0:T(128)}, u32[]{:S(2)}) copy-start(f32[4]{0:T(128)} %param.15) | copy-start | bytes 52
  2.9 6.0 %collective-permute-start.1 = (f32[200,128]{1,0:T(8,128)S(1)}, f32[200,128]{1,0:T(8,128)S(1)}, u32[]{:S(2)}, u32[]{:S(2)}) collective-permute-start(f32[200,128]{1,0:T(8,128)S(1)} %concatenate.14.own_ref), channel_id=1, source_target_pairs={{0,8},{4,12},{8,0},{12,4},{16,24},{20,28},{24,16},{28,20},{1,9},{5... | collective-permute-start | bytes 307208 | tf_op jit(solution)/shard_map/ppermute | solution.py:567
  6.0 3.0 %collective-permute-start = (f32[200,128]{1,0:T(8,128)S(1)}, f32[200,128]{1,0:T(8,128)S(1)}, u32[]{:S(2)}, u32[]{:S(2)}) collective-permute-start(f32[200,128]{1,0:T(8,128)S(1)} %concatenate.14.own_ref), channel_id=1, source_target_pairs={{0,4},{4,0},{8,12},{12,8},{16,20},{20,16},{24,28},{28,24},{1,5},{5... | collective-permute-start | bytes 307208 | tf_op jit(solution)/shard_map/ppermute | solution.py:567
  8.9 1.3 %collective-permute-start.2 = (f32[200,128]{1,0:T(8,128)S(1)}, f32[200,128]{1,0:T(8,128)S(1)}, u32[]{:S(2)}, u32[]{:S(2)}) collective-permute-start(f32[200,128]{1,0:T(8,128)S(1)} %collective-permute-done.1.two_ref), channel_id=1, source_target_pairs={{0,4},{4,0},{8,12},{12,8},{16,20},{20,16},{24,28},{28,24},{1,5},{5... | collective-permute-start | bytes 307208 | tf_op jit(solution)/shard_map/ppermute | solution.py:567
  15.3 7.1 %collective-permute-start.3 = (f32[152,128]{1,0:T(8,128)S(1)}, f32[152,128]{1,0:T(8,128)S(1)}, u32[]{:S(2)}, u32[]{:S(2)}) collective-permute-start(f32[152,128]{1,0:T(8,128)S(1)} %get-tuple-element.50), channel_id=1, source_target_pairs={{0,16},{4,20},{8,24},{12,28},{1,17},{5,21},{9,25},{13,29},{2,18},{... | collective-permute-start | bytes 233480 | tf_op jit(solution)/shard_map/ppermute | solution.py:628
  22.8 5.3 %collective-permute-start.4 = (f32[32,128]{1,0:T(8,128)S(1)}, f32[32,128]{1,0:T(8,128)S(1)}, u32[]{:S(2)}, u32[]{:S(2)}) collective-permute-start(f32[32,128]{1,0:T(8,128)S(1)} %get-tuple-element.60), channel_id=1, source_target_pairs={{0,16},{4,20},{8,24},{12,28},{16,0},{20,4},{24,8},{28,12},{1,17},{... | collective-permute-start | bytes 49160 | tf_op jit(solution)/shard_map/ppermute | solution.py:567
  28.1 4.7 %collective-permute-start.7 = (f32[32,128]{1,0:T(8,128)S(1)}, f32[32,128]{1,0:T(8,128)S(1)}, u32[]{:S(2)}, u32[]{:S(2)}) collective-permute-start(f32[32,128]{1,0:T(8,128)S(1)} %add.12), channel_id=1, source_target_pairs={{0,3},{1,2},{2,1},{3,0},{4,7},{5,6},{6,5},{7,4},{8,11},{9,10},{10,... | collective-permute-start | bytes 49160 | tf_op jit(solution)/shard_map/ppermute | solution.py:567
  30.6 3.7 %collective-permute-start.6 = (f32[32,128]{1,0:T(8,128)S(1)}, f32[32,128]{1,0:T(8,128)S(1)}, u32[]{:S(2)}, u32[]{:S(2)}) collective-permute-start(f32[32,128]{1,0:T(8,128)S(1)} %add.12), channel_id=1, source_target_pairs={{0,2},{1,3},{2,0},{3,1},{4,6},{5,7},{6,4},{7,5},{8,10},{9,11},{10,... | collective-permute-start | bytes 49160 | tf_op jit(solution)/shard_map/ppermute | solution.py:567
  31.1 3.7 %collective-permute-start.5 = (f32[32,128]{1,0:T(8,128)S(1)}, f32[32,128]{1,0:T(8,128)S(1)}, u32[]{:S(2)}, u32[]{:S(2)}) collective-permute-start(f32[32,128]{1,0:T(8,128)S(1)} %add.12), channel_id=1, source_target_pairs={{0,1},{1,0},{2,3},{3,2},{4,5},{5,4},{6,7},{7,6},{8,9},{9,8},{10,11... | collective-permute-start | bytes 49160 | tf_op jit(solution)/shard_map/ppermute | solution.py:567
  34.8 4.9 %collective-permute-start.8 = (f32[40,128]{1,0:T(8,128)S(1)}, f32[40,128]{1,0:T(8,128)S(1)}, u32[]{:S(2)}, u32[]{:S(2)}) collective-permute-start(f32[40,128]{1,0:T(8,128)S(1)} %pad_maximum_fusion.1), channel_id=1, source_target_pairs={{0,8},{4,12},{8,0},{12,4},{16,24},{20,28},{24,16},{28,20},{1,9},{5... | collective-permute-start | bytes 61448 | tf_op jit(solution)/shard_map/ppermute | solution.py:567
  39.7 1.2 %collective-permute-start.9 = (f32[80,128]{1,0:T(8,128)S(1)}, f32[80,128]{1,0:T(8,128)S(1)}, u32[]{:S(2)}, u32[]{:S(2)}) collective-permute-start(f32[80,128]{1,0:T(8,128)S(1)} %pad_maximum_fusion.refs_0_), channel_id=1, source_target_pairs={{0,4},{4,0},{8,12},{12,8},{16,20},{20,16},{24,28},{28,24},{1,5},{5... | collective-permute-start | bytes 122888 | tf_op jit(solution)/shard_map/ppermute | solution.py:567
